TPU v7x, 32 devices: a whole 2x2x4 slice. The times are simulated.
32 devices in a mesh: groups: 2 (over x), gx: 4 (over y, core), gz: 4 (over z).
Axes of the slice: x: 2, y: 2, z: 4, core: 2. Of those that a mesh axis runs over, the one named last changes fastest.
Arguments:
- charges: float32 [64, 64, 512], P(('groups', 'gx'), 'gz'), parts along dimension 0, may hold values from -24 to 24
Outputs:
- potential: float32 [64, 64, 512], P(('groups', 'gx'), 'gz'), parts along dimension 0
There are 2 independent parts, one for each index of `groups`. A program takes and returns all parts, laid end to end along the dimension named above; each array names one. Nothing has to cross between parts.
All inputs are finite; a program needn't handle non-finite values.
Results may differ from a plain program's by a relative error of at most 0.0001.
Values sent between devices are 32-bit elements; how exact they have to be, the bound alone decides.
No kernel may reach another device: no remote copies, remote signals or barrier semaphores. Data moves between devices by JAX's collectives and lax.ppermute only.
A program may use at most 128 MiB of HBM per device.

v0:
```python
import jax
import jax.numpy as jnp
from jax import lax
from jax.sharding import PartitionSpec as P

LEVELS = 4
SWEEPS = 2
COARSE_SWEEPS = 8
CYCLES = 2


OMEGA = 0.8


def extended(block, sides, width):
    for axis, dim in sides:
        count = lax.axis_size(axis)
        forward = [(i, i + 1) for i in range(count - 1)]
        backward = [(target, source) for source, target in forward]
        low = lax.ppermute(
            lax.slice_in_dim(block, block.shape[dim] - width, None, axis=dim), axis, forward
        )
        high = lax.ppermute(lax.slice_in_dim(block, 0, width, axis=dim), axis, backward)
        block = jnp.concatenate([low, block, high], axis=dim)
    return block


def mehrstellen(padded, grid_level):
    size_x = padded.shape[0] - 2
    size_z = padded.shape[1] - 2
    size_y = padded.shape[2] - 2

    def window(i, j, k):
        return padded[1 + i : 1 + i + size_x, 1 + j : 1 + j + size_z, 1 + k : 1 + k + size_y]

    face_sum = (
        window(1, 0, 0)
        + window(-1, 0, 0)
        + window(0, 1, 0)
        + window(0, -1, 0)
        + window(0, 0, 1)
        + window(0, 0, -1)
    )
    edge_sum = window(1, 1, 0) + window(1, -1, 0) + window(-1, 1, 0) + window(-1, -1, 0)
    edge_sum = edge_sum + window(1, 0, 1) + window(1, 0, -1) + window(-1, 0, 1) + window(-1, 0, -1)
    edge_sum = edge_sum + window(0, 1, 1) + window(0, 1, -1) + window(0, -1, 1) + window(0, -1, -1)
    return (24.0 * window(0, 0, 0) - 2.0 * face_sum - edge_sum) * (1.0 / (6.0 * 4.0**grid_level))


def charge_source(padded):
    size_x = padded.shape[0] - 2
    size_z = padded.shape[1] - 2
    size_y = padded.shape[2] - 2

    def window(i, j, k):
        return padded[1 + i : 1 + i + size_x, 1 + j : 1 + j + size_z, 1 + k : 1 + k + size_y]

    face_sum = (
        window(1, 0, 0)
        + window(-1, 0, 0)
        + window(0, 1, 0)
        + window(0, -1, 0)
        + window(0, 0, 1)
        + window(0, 0, -1)
    )
    return (6.0 * window(0, 0, 0) + face_sum) * (1.0 / 12.0)


def jacobi(approx, source, applied, grid_level):
    return approx + OMEGA * (source - applied) * (4.0**grid_level / 4.0)


def restrict(residue):
    size_x, size_z, size_y = residue.shape
    return (
        residue.reshape(size_x // 2, 2, size_z // 2, 2, size_y // 2, 2).sum(axis=(1, 3, 5)) * 0.125
    )


def prolong(coarse):
    return jnp.repeat(jnp.repeat(jnp.repeat(coarse, 2, 0), 2, 1), 2, 2)


def whole_cycle(approx, source, grid_level):
    for sweep_index in range(COARSE_SWEEPS):
        approx = jacobi(approx, source, mehrstellen(jnp.pad(approx, 1), grid_level), grid_level)
    return approx


def pad_depth(block):
    return jnp.pad(block, ((0, 0), (0, 0), (1, 1)))


def brick_operator(approx, grid_level):
    padded = extended(approx, (("gx", 0), ("gz", 1)), 1)
    return mehrstellen(pad_depth(padded), grid_level)


def smoothing(approx, source, grid_level):
    for sweep_index in range(SWEEPS):
        approx = jacobi(approx, source, brick_operator(approx, grid_level), grid_level)
    return approx


def brick_cycle(approx, source, grid_level, agg_level):
    if grid_level == agg_level:
        size_x, size_z, size_y = source.shape
        stacked = lax.all_gather(source[None], ("gx", "gz"), axis=0, tiled=True)
        count_x = lax.axis_size("gx")
        count_z = lax.axis_size("gz")
        whole = stacked.reshape(count_x, count_z, size_x, size_z, size_y).transpose(0, 2, 1, 3, 4)
        whole = whole.reshape(count_x * size_x, count_z * size_z, size_y)
        solved = whole_cycle(jnp.zeros_like(whole), whole, grid_level)
        start_x = lax.axis_index("gx") * size_x
        start_z = lax.axis_index("gz") * size_z
        return lax.dynamic_slice(solved, (start_x, start_z, jnp.int32(0)), (size_x, size_z, size_y))
    approx = smoothing(approx, source, grid_level)
    residue = source - brick_operator(approx, grid_level)
    coarse_source = restrict(residue)
    correction = brick_cycle(
        jnp.zeros_like(coarse_source), coarse_source, grid_level + 1, agg_level
    )
    approx = approx + prolong(correction)
    return smoothing(approx, source, grid_level)


def per_device(charges):
    agg_level = LEVELS - 1
    padded = extended(charges, (("gx", 0), ("gz", 1)), 1)
    source = charge_source(pad_depth(padded))
    approx = jnp.zeros_like(charges)
    for cycle_index in range(CYCLES):
        approx = brick_cycle(approx, source, 0, agg_level)
    return approx


def solution(mesh):
    return jax.shard_map(
        per_device,
        mesh=mesh,
        in_specs=(P(("groups", "gx"), "gz", None),),
        out_specs=P(("groups", "gx"), "gz", None),
        check_vma=False,
    )
```

profile of v0, /device:TPU:0, one launch (start us, length us, event | category | flops | bytes accessed | tf_op | source)
XLA Modules:
  0.0 541.3 jit_solution(13216087540982320976)
XLA Ops:
  1.3 3.0 collective-permute-start.5
  5.1 4.5 collective-permute-start.1
  12.4 4.5 collective-permute-start.7
  19.4 4.5 collective-permute-start.3
  27.7 3.0 collective-permute-start.9
  32.1 4.9 collective-permute-start.17
  38.3 4.8 collective-permute-start.11
  44.5 4.5 collective-permute-start.19
  51.4 3.4 collective-permute-start.13
  57.0 4.5 collective-permute-start.15
  64.0 18.1 %reshape.90 = f32[4,2,8,2,256,2]{5,4,3,2,1,0:T(8,128)} reshape(f32[8,16,512]{2,1,0:T(8,128)S(1)} %fusion.67) | data formatting | bytes 524288 | tf_op jit(solution)/shard_map/reshape | solution.py:76
  82.1 7.0 %reduce_sum.68 = f32[4,8,256]{2,1,0:T(8,128)S(1)} reduce(f32[4,2,8,2,256,2]{5,4,3,2,1,0:T(8,128)} %reshape.90, f32[]{:T(128)} %constant.86.clone.1), dimensions={1,3,5}, to_apply=%region_0.1 | reduce | flops 57344 | bytes 294916 | tf_op jit(solution)/shard_map/reduce_sum | solution.py:76
  90.5 3.3 collective-permute-start.21
  96.0 4.6 collective-permute-start.23
  101.8 5.9 %collective-permute-start.29 = (f32[1,4,128]{2,1,0:T(4,128)S(1)}, f32[1,4,128]{2,1,0:T(4,128)S(1)}, u32[]{:S(2)}, u32[]{:S(2)}) collective-permute-start(f32[1,4,128]{2,1,0:T(4,128)S(1)} %broadcast.276), channel_id=1, source_target_pairs={{0,4},{4,8},{8,12},{1,5},{5,9},{9,13},{2,6},{6,10},{10,14},{3,7},{... | collective-permute-start | bytes 6152 | tf_op jit(solution)/shard_map/ppermute | solution.py:20
  109.4 5.1 collective-permute-start.25
  115.9 4.6 collective-permute-start.31
  121.8 4.6 collective-permute-start.27
  131.7 3.0 collective-permute-start.33
  136.8 4.8 collective-permute-start.35
  144.4 3.0 collective-permute-start.37
  149.6 4.8 collective-permute-start.39
  156.1 35.0 %all-gather.2 = f32[16,2,64]{2,1,0:T(2,128)S(1)} all-gather(f32[1,2,64]{2,1,0:T(2,128)S(1)} %multiply_bitcast_fusion.1), channel_id=2, replica_groups=mesh['groups'=2,'gx'=4,'gz'=4] {'gx','gz'}, dimensions={0}, use_global_device_ids=true | all-gather | bytes 8704 | tf_op jit(solution)/shard_map/all_gather | solution.py:108
  193.6 3.0 collective-permute-start.41
  198.8 4.7 collective-permute-start.43
  206.3 3.0 collective-permute-start.45
  211.4 4.8 collective-permute-start.47
  219.6 4.1 collective-permute-start.49
  225.8 4.5 collective-permute-start.51
  233.3 5.0 collective-permute-start.53
  240.5 4.5 collective-permute-start.55
  251.5 5.1 collective-permute-start.57
  258.8 4.5 collective-permute-start.59
  267.1 5.2 collective-permute-start.61
  274.5 4.5 collective-permute-start.63
  282.8 5.3 collective-permute-start.65
  290.3 4.5 collective-permute-start.67
  298.6 5.3 collective-permute-start.69
  306.1 4.5 collective-permute-start.71
  314.4 5.3 collective-permute-start.73
  321.9 4.5 collective-permute-start.75
  328.9 18.1 %reshape.98 = f32[4,2,8,2,256,2]{5,4,3,2,1,0:T(8,128)} reshape(f32[8,16,512]{2,1,0:T(8,128)S(1)} %fusion.29) | data formatting | bytes 524288 | tf_op jit(solution)/shard_map/reshape | solution.py:76
  347.0 7.0 %reduce_sum.73 = f32[4,8,256]{2,1,0:T(8,128)S(1)} reduce(f32[4,2,8,2,256,2]{5,4,3,2,1,0:T(8,128)} %reshape.98, f32[]{:T(128)} %constant.86.clone.1), dimensions={1,3,5}, to_apply=%region_4.5 | reduce | flops 57344 | bytes 294916 | tf_op jit(solution)/shard_map/reduce_sum | solution.py:76
  355.3 5.3 collective-permute-start.77
  362.7 4.8 collective-permute-start.79
  370.2 5.1 collective-permute-start.81
  377.5 4.5 collective-permute-start.83
  387.3 5.0 collective-permute-start.85
  394.4 4.5 collective-permute-start.87
  401.8 5.0 collective-permute-start.89
  408.9 4.5 collective-permute-start.91
  415.2 35.3 %all-gather.3 = f32[16,2,64]{2,1,0:T(2,128)S(1)} all-gather(f32[1,2,64]{2,1,0:T(2,128)S(1)} %multiply_bitcast_fusion), channel_id=3, replica_groups=mesh['groups'=2,'gx'=4,'gz'=4] {'gx','gz'}, dimensions={0}, use_global_device_ids=true | all-gather | bytes 8704 | tf_op jit(solution)/shard_map/all_gather | solution.py:108
  452.9 3.0 collective-permute-start.93
  458.0 4.5 collective-permute-start.95
  465.4 3.0 collective-permute-start.97
  470.5 4.8 collective-permute-start.99
  478.7 4.1 collective-permute-start.101
  484.9 4.5 collective-permute-start.103
  492.4 5.0 collective-permute-start.105
  499.6 4.5 collective-permute-start.107
  510.6 5.1 collective-permute-start.109
  517.9 4.5 collective-permute-start.111
  526.2 5.2 collective-permute-start.113
  533.6 4.5 collective-permute-start.115
  (387 shorter events, 157.8 us)
Async XLA Ops:
  0.0 10.9 %collective-permute-start.4 = (f32[1,16,512]{2,1,0:T(8,128)S(1)}, f32[1,16,512]{2,1,0:T(8,128)S(1)}, u32[]{:S(2)}, u32[]{:S(2)}) collective-permute-start(f32[1,16,512]{2,1,0:T(8,128)S(1)} %broadcast.263), channel_id=1, source_target_pairs={{4,0},{8,4},{12,8},{5,1},{9,5},{13,9},{6,2},{10,6},{14,10},{7,3},{... | collective-permute-start | bytes 98312 | tf_op jit(solution)/shard_map/ppermute | solution.py:23
  1.3 9.6 %collective-permute-start.5 = (f32[1,16,512]{2,1,0:T(8,128)S(1)}, f32[1,16,512]{2,1,0:T(8,128)S(1)}, u32[]{:S(2)}, u32[]{:S(2)}) collective-permute-start(f32[1,16,512]{2,1,0:T(8,128)S(1)} %broadcast.263), channel_id=1, source_target_pairs={{0,4},{4,8},{8,12},{1,5},{5,9},{9,13},{2,6},{6,10},{10,14},{3,7},{... | collective-permute-start | bytes 98312 | tf_op jit(solution)/shard_map/ppermute | solution.py:20
  5.1 11.9 %collective-permute-start.1 = (f32[1,16,512]{2,1,0:T(8,128)S(1)}, f32[1,16,512]{2,1,0:T(8,128)S(1)}, u32[]{:S(2)}, u32[]{:S(2)}) collective-permute-start(f32[1,16,512]{2,1,0:T(8,128)S(1)} %get-tuple-element.79), channel_id=1, source_target_pairs={{0,4},{4,8},{8,12},{1,5},{5,9},{9,13},{2,6},{6,10},{10,14},{3,7},{... | collective-permute-start | bytes 98312 | tf_op jit(solution)/shard_map/ppermute | solution.py:20
  9.6 8.4 %collective-permute-start = (f32[1,16,512]{2,1,0:T(8,128)S(1)}, f32[1,16,512]{2,1,0:T(8,128)S(1)}, u32[]{:S(2)}, u32[]{:S(2)}) collective-permute-start(f32[1,16,512]{2,1,0:T(8,128)S(1)} %get-tuple-element.78), channel_id=1, source_target_pairs={{4,0},{8,4},{12,8},{5,1},{9,5},{13,9},{6,2},{10,6},{14,10},{7,3},{... | collective-permute-start | bytes 98312 | tf_op jit(solution)/shard_map/ppermute | solution.py:23
  11.0 12.9 %collective-permute-start.6 = (f32[10,1,512]{2,1,0:T(1,128)S(1)}, f32[10,1,512]{2,1,0:T(1,128)S(1)}, u32[]{:S(2)}, u32[]{:S(2)}) collective-permute-start(f32[10,1,512]{2,1,0:T(1,128)S(1)} %get-tuple-element.59), channel_id=1, source_target_pairs={{1,0},{2,1},{3,2},{5,4},{6,5},{7,6},{9,8},{10,9},{11,10},{13,12},{... | collective-permute-start | bytes 61448 | tf_op jit(solution)/shard_map/ppermute | solution.py:23
  12.4 11.5 %collective-permute-start.7 = (f32[10,1,512]{2,1,0:T(1,128)S(1)}, f32[10,1,512]{2,1,0:T(1,128)S(1)}, u32[]{:S(2)}, u32[]{:S(2)}) collective-permute-start(f32[10,1,512]{2,1,0:T(1,128)S(1)} %get-tuple-element.58), channel_id=1, source_target_pairs={{0,1},{1,2},{2,3},{4,5},{5,6},{6,7},{8,9},{9,10},{10,11},{12,13},{... | collective-permute-start | bytes 61448 | tf_op jit(solution)/shard_map/ppermute | solution.py:20
  18.1 6.3 %collective-permute-start.2 = (f32[10,1,512]{2,1,0:T(1,128)S(1)}, f32[10,1,512]{2,1,0:T(1,128)S(1)}, u32[]{:S(2)}, u32[]{:S(2)}) collective-permute-start(f32[10,1,512]{2,1,0:T(1,128)S(1)} %get-tuple-element.55), channel_id=1, source_target_pairs={{1,0},{2,1},{3,2},{5,4},{6,5},{7,6},{9,8},{10,9},{11,10},{13,12},{... | collective-permute-start | bytes 61448 | tf_op jit(solution)/shard_map/ppermute | solution.py:23
  19.4 6.0 %collective-permute-start.3 = (f32[10,1,512]{2,1,0:T(1,128)S(1)}, f32[10,1,512]{2,1,0:T(1,128)S(1)}, u32[]{:S(2)}, u32[]{:S(2)}) collective-permute-start(f32[10,1,512]{2,1,0:T(1,128)S(1)} %get-tuple-element.54), channel_id=1, source_target_pairs={{0,1},{1,2},{2,3},{4,5},{5,6},{6,7},{8,9},{9,10},{10,11},{12,13},{... | collective-permute-start | bytes 61448 | tf_op jit(solution)/shard_map/ppermute | solution.py:20
  26.4 10.6 %collective-permute-start.8 = (f32[1,16,512]{2,1,0:T(8,128)S(1)}, f32[1,16,512]{2,1,0:T(8,128)S(1)}, u32[]{:S(2)}, u32[]{:S(2)}) collective-permute-start(f32[1,16,512]{2,1,0:T(8,128)S(1)} %get-tuple-element.77), channel_id=1, source_target_pairs={{4,0},{8,4},{12,8},{5,1},{9,5},{13,9},{6,2},{10,6},{14,10},{7,3},{... | collective-permute-start | bytes 98312 | tf_op jit(solution)/shard_map/ppermute | solution.py:23
  27.7 9.3 %collective-permute-start.9 = (f32[1,16,512]{2,1,0:T(8,128)S(1)}, f32[1,16,512]{2,1,0:T(8,128)S(1)}, u32[]{:S(2)}, u32[]{:S(2)}) collective-permute-start(f32[1,16,512]{2,1,0:T(8,128)S(1)} %get-tuple-element.76), channel_id=1, source_target_pairs={{0,4},{4,8},{8,12},{1,5},{5,9},{9,13},{2,6},{6,10},{10,14},{3,7},{... | collective-permute-start | bytes 98312 | tf_op jit(solution)/shard_map/ppermute | solution.py:20
  30.8 12.4 %collective-permute-start.16 = (f32[1,8,256]{2,1,0:T(8,128)S(1)}, f32[1,8,256]{2,1,0:T(8,128)S(1)}, u32[]{:S(2)}, u32[]{:S(2)}) collective-permute-start(f32[1,8,256]{2,1,0:T(8,128)S(1)} %broadcast.269), channel_id=1, source_target_pairs={{4,0},{8,4},{12,8},{5,1},{9,5},{13,9},{6,2},{10,6},{14,10},{7,3},{... | collective-permute-start | bytes 24584 | tf_op jit(solution)/shard_map/ppermute | solution.py:23
  32.1 11.1 %collective-permute-start.17 = (f32[1,8,256]{2,1,0:T(8,128)S(1)}, f32[1,8,256]{2,1,0:T(8,128)S(1)}, u32[]{:S(2)}, u32[]{:S(2)}) collective-permute-start(f32[1,8,256]{2,1,0:T(8,128)S(1)} %broadcast.269), channel_id=1, source_target_pairs={{0,4},{4,8},{8,12},{1,5},{5,9},{9,13},{2,6},{6,10},{10,14},{3,7},{... | collective-permute-start | bytes 24584 | tf_op jit(solution)/shard_map/ppermute | solution.py:20
  37.0 12.1 %collective-permute-start.10 = (f32[10,1,512]{2,1,0:T(1,128)S(1)}, f32[10,1,512]{2,1,0:T(1,128)S(1)}, u32[]{:S(2)}, u32[]{:S(2)}) collective-permute-start(f32[10,1,512]{2,1,0:T(1,128)S(1)} %get-tuple-element.53), channel_id=1, source_target_pairs={{1,0},{2,1},{3,2},{5,4},{6,5},{7,6},{9,8},{10,9},{11,10},{13,12},{... | collective-permute-start | bytes 61448 | tf_op jit(solution)/shard_map/ppermute | solution.py:23
  38.3 10.8 %collective-permute-start.11 = (f32[10,1,512]{2,1,0:T(1,128)S(1)}, f32[10,1,512]{2,1,0:T(1,128)S(1)}, u32[]{:S(2)}, u32[]{:S(2)}) collective-permute-start(f32[10,1,512]{2,1,0:T(1,128)S(1)} %get-tuple-element.52), channel_id=1, source_target_pairs={{0,1},{1,2},{2,3},{4,5},{5,6},{6,7},{8,9},{9,10},{10,11},{12,13},{... | collective-permute-start | bytes 61448 | tf_op jit(solution)/shard_map/ppermute | solution.py:20
  43.2 11.6 %collective-permute-start.18 = (f32[6,1,256]{2,1,0:T(1,128)S(1)}, f32[6,1,256]{2,1,0:T(1,128)S(1)}, u32[]{:S(2)}, u32[]{:S(2)}) collective-permute-start(f32[6,1,256]{2,1,0:T(1,128)S(1)} %get-tuple-element.115), channel_id=1, source_target_pairs={{1,0},{2,1},{3,2},{5,4},{6,5},{7,6},{9,8},{10,9},{11,10},{13,12},{... | collective-permute-start | bytes 18440 | tf_op jit(solution)/shard_map/ppermute | solution.py:23
  44.5 10.3 %collective-permute-start.19 = (f32[6,1,256]{2,1,0:T(1,128)S(1)}, f32[6,1,256]{2,1,0:T(1,128)S(1)}, u32[]{:S(2)}, u32[]{:S(2)}) collective-permute-start(f32[6,1,256]{2,1,0:T(1,128)S(1)} %get-tuple-element.114), channel_id=1, source_target_pairs={{0,1},{1,2},{2,3},{4,5},{5,6},{6,7},{8,9},{9,10},{10,11},{12,13},{... | collective-permute-start | bytes 18440 | tf_op jit(solution)/shard_map/ppermute | solution.py:20
  55.7 6.0 %collective-permute-start.14 = (f32[10,1,512]{2,1,0:T(1,128)S(1)}, f32[10,1,512]{2,1,0:T(1,128)S(1)}, u32[]{:S(2)}, u32[]{:S(2)}) collective-permute-start(f32[10,1,512]{2,1,0:T(1,128)S(1)} %get-tuple-element.49), channel_id=1, source_target_pairs={{1,0},{2,1},{3,2},{5,4},{6,5},{7,6},{9,8},{10,9},{11,10},{13,12},{... | collective-permute-start | bytes 61448 | tf_op jit(solution)/shard_map/ppermute | solution.py:23
  57.0 6.0 %collective-permute-start.15 = (f32[10,1,512]{2,1,0:T(1,128)S(1)}, f32[10,1,512]{2,1,0:T(1,128)S(1)}, u32[]{:S(2)}, u32[]{:S(2)}) collective-permute-start(f32[10,1,512]{2,1,0:T(1,128)S(1)} %get-tuple-element.48), channel_id=1, source_target_pairs={{0,1},{1,2},{2,3},{4,5},{5,6},{6,7},{8,9},{9,10},{10,11},{12,13},{... | collective-permute-start | bytes 61448 | tf_op jit(solution)/shard_map/ppermute | solution.py:20
  94.7 13.1 %collective-permute-start.22 = (f32[6,1,256]{2,1,0:T(1,128)S(1)}, f32[6,1,256]{2,1,0:T(1,128)S(1)}, u32[]{:S(2)}, u32[]{:S(2)}) collective-permute-start(f32[6,1,256]{2,1,0:T(1,128)S(1)} %get-tuple-element.111), channel_id=1, source_target_pairs={{1,0},{2,1},{3,2},{5,4},{6,5},{7,6},{9,8},{10,9},{11,10},{13,12},{... | collective-permute-start | bytes 18440 | tf_op jit(solution)/shard_map/ppermute | solution.py:23
  96.0 11.8 %collective-permute-start.23 = (f32[6,1,256]{2,1,0:T(1,128)S(1)}, f32[6,1,256]{2,1,0:T(1,128)S(1)}, u32[]{:S(2)}, u32[]{:S(2)}) collective-permute-start(f32[6,1,256]{2,1,0:T(1,128)S(1)} %get-tuple-element.110), channel_id=1, source_target_pairs={{0,1},{1,2},{2,3},{4,5},{5,6},{6,7},{8,9},{9,10},{10,11},{12,13},{... | collective-permute-start | bytes 18440 | tf_op jit(solution)/shard_map/ppermute | solution.py:20
  100.5 14.0 %collective-permute-start.28 = (f32[1,4,128]{2,1,0:T(4,128)S(1)}, f32[1,4,128]{2,1,0:T(4,128)S(1)}, u32[]{:S(2)}, u32[]{:S(2)}) collective-permute-start(f32[1,4,128]{2,1,0:T(4,128)S(1)} %broadcast.276), channel_id=1, source_target_pairs={{4,0},{8,4},{12,8},{5,1},{9,5},{13,9},{6,2},{10,6},{14,10},{7,3},{... | collective-permute-start | bytes 6152 | tf_op jit(solution)/shard_map/ppermute | solution.py:23
  101.8 12.7 %collective-permute-start.29 = (f32[1,4,128]{2,1,0:T(4,128)S(1)}, f32[1,4,128]{2,1,0:T(4,128)S(1)}, u32[]{:S(2)}, u32[]{:S(2)}) collective-permute-start(f32[1,4,128]{2,1,0:T(4,128)S(1)} %broadcast.276), channel_id=1, source_target_pairs={{0,4},{4,8},{8,12},{1,5},{5,9},{9,13},{2,6},{6,10},{10,14},{3,7},{... | collective-permute-start | bytes 6152 | tf_op jit(solution)/shard_map/ppermute | solution.py:20
  108.1 12.3 %collective-permute-start.24 = (f32[1,8,256]{2,1,0:T(8,128)S(1)}, f32[1,8,256]{2,1,0:T(8,128)S(1)}, u32[]{:S(2)}, u32[]{:S(2)}) collective-permute-start(f32[1,8,256]{2,1,0:T(8,128)S(1)} %get-tuple-element.129), channel_id=1, source_target_pairs={{4,0},{8,4},{12,8},{5,1},{9,5},{13,9},{6,2},{10,6},{14,10},{7,3},{... | collective-permute-start | bytes 24584 | tf_op jit(solution)/shard_map/ppermute | solution.py:23
  109.4 11.0 %collective-permute-start.25 = (f32[1,8,256]{2,1,0:T(8,128)S(1)}, f32[1,8,256]{2,1,0:T(8,128)S(1)}, u32[]{:S(2)}, u32[]{:S(2)}) collective-permute-start(f32[1,8,256]{2,1,0:T(8,128)S(1)} %get-tuple-element.128), channel_id=1, source_target_pairs={{0,4},{4,8},{8,12},{1,5},{5,9},{9,13},{2,6},{6,10},{10,14},{3,7},{... | collective-permute-start | bytes 24584 | tf_op jit(solution)/shard_map/ppermute | solution.py:20
  114.6 11.8 %collective-permute-start.30 = (f32[4,1,128]{2,1,0:T(1,128)S(1)}, f32[4,1,128]{2,1,0:T(1,128)S(1)}, u32[]{:S(2)}, u32[]{:S(2)}) collective-permute-start(f32[4,1,128]{2,1,0:T(1,128)S(1)} %get-tuple-element.155), channel_id=1, source_target_pairs={{1,0},{2,1},{3,2},{5,4},{6,5},{7,6},{9,8},{10,9},{11,10},{13,12},{... | collective-permute-start | bytes 6152 | tf_op jit(solution)/shard_map/ppermute | solution.py:23
  115.9 10.5 %collective-permute-start.31 = (f32[4,1,128]{2,1,0:T(1,128)S(1)}, f32[4,1,128]{2,1,0:T(1,128)S(1)}, u32[]{:S(2)}, u32[]{:S(2)}) collective-permute-start(f32[4,1,128]{2,1,0:T(1,128)S(1)} %get-tuple-element.154), channel_id=1, source_target_pairs={{0,1},{1,2},{2,3},{4,5},{5,6},{6,7},{8,9},{9,10},{10,11},{12,13},{... | collective-permute-start | bytes 6152 | tf_op jit(solution)/shard_map/ppermute | solution.py:20
  120.5 6.0 %collective-permute-start.26 = (f32[6,1,256]{2,1,0:T(1,128)S(1)}, f32[6,1,256]{2,1,0:T(1,128)S(1)}, u32[]{:S(2)}, u32[]{:S(2)}) collective-permute-start(f32[6,1,256]{2,1,0:T(1,128)S(1)} %get-tuple-element.107), channel_id=1, source_target_pairs={{1,0},{2,1},{3,2},{5,4},{6,5},{7,6},{9,8},{10,9},{11,10},{13,12},{... | collective-permute-start | bytes 18440 | tf_op jit(solution)/shard_map/ppermute | solution.py:23
  135.5 6.1 %collective-permute-start.34 = (f32[4,1,128]{2,1,0:T(1,128)S(1)}, f32[4,1,128]{2,1,0:T(1,128)S(1)}, u32[]{:S(2)}, u32[]{:S(2)}) collective-permute-start(f32[4,1,128]{2,1,0:T(1,128)S(1)} %get-tuple-element.153), channel_id=1, source_target_pairs={{1,0},{2,1},{3,2},{5,4},{6,5},{7,6},{9,8},{10,9},{11,10},{13,12},{... | collective-permute-start | bytes 6152 | tf_op jit(solution)/shard_map/ppermute | solution.py:23
  136.8 6.1 %collective-permute-start.35 = (f32[4,1,128]{2,1,0:T(1,128)S(1)}, f32[4,1,128]{2,1,0:T(1,128)S(1)}, u32[]{:S(2)}, u32[]{:S(2)}) collective-permute-start(f32[4,1,128]{2,1,0:T(1,128)S(1)} %get-tuple-element.152), channel_id=1, source_target_pairs={{0,1},{1,2},{2,3},{4,5},{5,6},{6,7},{8,9},{9,10},{10,11},{12,13},{... | collective-permute-start | bytes 6152 | tf_op jit(solution)/shard_map/ppermute | solution.py:20
  148.3 6.1 %collective-permute-start.38 = (f32[4,1,128]{2,1,0:T(1,128)S(1)}, f32[4,1,128]{2,1,0:T(1,128)S(1)}, u32[]{:S(2)}, u32[]{:S(2)}) collective-permute-start(f32[4,1,128]{2,1,0:T(1,128)S(1)} %get-tuple-element.151), channel_id=1, source_target_pairs={{1,0},{2,1},{3,2},{5,4},{6,5},{7,6},{9,8},{10,9},{11,10},{13,12},{... | collective-permute-start | bytes 6152 | tf_op jit(solution)/shard_map/ppermute | solution.py:23
  149.6 6.1 %collective-permute-start.39 = (f32[4,1,128]{2,1,0:T(1,128)S(1)}, f32[4,1,128]{2,1,0:T(1,128)S(1)}, u32[]{:S(2)}, u32[]{:S(2)}) collective-permute-start(f32[4,1,128]{2,1,0:T(1,128)S(1)} %get-tuple-element.150), channel_id=1, source_target_pairs={{0,1},{1,2},{2,3},{4,5},{5,6},{6,7},{8,9},{9,10},{10,11},{12,13},{... | collective-permute-start | bytes 6152 | tf_op jit(solution)/shard_map/ppermute | solution.py:20
  197.5 6.0 %collective-permute-start.42 = (f32[4,1,128]{2,1,0:T(1,128)S(1)}, f32[4,1,128]{2,1,0:T(1,128)S(1)}, u32[]{:S(2)}, u32[]{:S(2)}) collective-permute-start(f32[4,1,128]{2,1,0:T(1,128)S(1)} %get-tuple-element.149), channel_id=1, source_target_pairs={{1,0},{2,1},{3,2},{5,4},{6,5},{7,6},{9,8},{10,9},{11,10},{13,12},{... | collective-permute-start | bytes 6152 | tf_op jit(solution)/shard_map/ppermute | solution.py:23
  198.8 6.0 %collective-permute-start.43 = (f32[4,1,128]{2,1,0:T(1,128)S(1)}, f32[4,1,128]{2,1,0:T(1,128)S(1)}, u32[]{:S(2)}, u32[]{:S(2)}) collective-permute-start(f32[4,1,128]{2,1,0:T(1,128)S(1)} %get-tuple-element.148), channel_id=1, source_target_pairs={{0,1},{1,2},{2,3},{4,5},{5,6},{6,7},{8,9},{9,10},{10,11},{12,13},{... | collective-permute-start | bytes 6152 | tf_op jit(solution)/shard_map/ppermute | solution.py:20
  210.1 6.1 %collective-permute-start.46 = (f32[4,1,128]{2,1,0:T(1,128)S(1)}, f32[4,1,128]{2,1,0:T(1,128)S(1)}, u32[]{:S(2)}, u32[]{:S(2)}) collective-permute-start(f32[4,1,128]{2,1,0:T(1,128)S(1)} %get-tuple-element.147), channel_id=1, source_target_pairs={{1,0},{2,1},{3,2},{5,4},{6,5},{7,6},{9,8},{10,9},{11,10},{13,12},{... | collective-permute-start | bytes 6152 | tf_op jit(solution)/shard_map/ppermute | solution.py:23
  211.4 6.1 %collective-permute-start.47 = (f32[4,1,128]{2,1,0:T(1,128)S(1)}, f32[4,1,128]{2,1,0:T(1,128)S(1)}, u32[]{:S(2)}, u32[]{:S(2)}) collective-permute-start(f32[4,1,128]{2,1,0:T(1,128)S(1)} %get-tuple-element.146), channel_id=1, source_target_pairs={{0,1},{1,2},{2,3},{4,5},{5,6},{6,7},{8,9},{9,10},{10,11},{12,13},{... | collective-permute-start | bytes 6152 | tf_op jit(solution)/shard_map/ppermute | solution.py:20
  232.0 6.4 %collective-permute-start.52 = (f32[1,8,256]{2,1,0:T(8,128)S(1)}, f32[1,8,256]{2,1,0:T(8,128)S(1)}, u32[]{:S(2)}, u32[]{:S(2)}) collective-permute-start(f32[1,8,256]{2,1,0:T(8,128)S(1)} %get-tuple-element.125), channel_id=1, source_target_pairs={{4,0},{8,4},{12,8},{5,1},{9,5},{13,9},{6,2},{10,6},{14,10},{7,3},{... | collective-permute-start | bytes 24584 | tf_op jit(solution)/shard_map/ppermute | solution.py:23
  250.2 6.4 %collective-permute-start.56 = (f32[1,16,512]{2,1,0:T(8,128)S(1)}, f32[1,16,512]{2,1,0:T(8,128)S(1)}, u32[]{:S(2)}, u32[]{:S(2)}) collective-permute-start(f32[1,16,512]{2,1,0:T(8,128)S(1)} %get-tuple-element.73), channel_id=1, source_target_pairs={{4,0},{8,4},{12,8},{5,1},{9,5},{13,9},{6,2},{10,6},{14,10},{7,3},{... | collective-permute-start | bytes 98312 | tf_op jit(solution)/shard_map/ppermute | solution.py:23
  258.8 6.0 %collective-permute-start.59 = (f32[10,1,512]{2,1,0:T(1,128)S(1)}, f32[10,1,512]{2,1,0:T(1,128)S(1)}, u32[]{:S(2)}, u32[]{:S(2)}) collective-permute-start(f32[10,1,512]{2,1,0:T(1,128)S(1)} %get-tuple-element.44), channel_id=1, source_target_pairs={{0,1},{1,2},{2,3},{4,5},{5,6},{6,7},{8,9},{9,10},{10,11},{12,13},{... | collective-permute-start | bytes 61448 | tf_op jit(solution)/shard_map/ppermute | solution.py:20
  265.8 6.6 %collective-permute-start.60 = (f32[1,16,512]{2,1,0:T(8,128)S(1)}, f32[1,16,512]{2,1,0:T(8,128)S(1)}, u32[]{:S(2)}, u32[]{:S(2)}) collective-permute-start(f32[1,16,512]{2,1,0:T(8,128)S(1)} %get-tuple-element.71), channel_id=1, source_target_pairs={{4,0},{8,4},{12,8},{5,1},{9,5},{13,9},{6,2},{10,6},{14,10},{7,3},{... | collective-permute-start | bytes 98312 | tf_op jit(solution)/shard_map/ppermute | solution.py:23
  267.1 6.1 %collective-permute-start.61 = (f32[1,16,512]{2,1,0:T(8,128)S(1)}, f32[1,16,512]{2,1,0:T(8,128)S(1)}, u32[]{:S(2)}, u32[]{:S(2)}) collective-permute-start(f32[1,16,512]{2,1,0:T(8,128)S(1)} %get-tuple-element.70), channel_id=1, source_target_pairs={{0,4},{4,8},{8,12},{1,5},{5,9},{9,13},{2,6},{6,10},{10,14},{3,7},{... | collective-permute-start | bytes 98312 | tf_op jit(solution)/shard_map/ppermute | solution.py:20
  274.5 6.0 %collective-permute-start.63 = (f32[10,1,512]{2,1,0:T(1,128)S(1)}, f32[10,1,512]{2,1,0:T(1,128)S(1)}, u32[]{:S(2)}, u32[]{:S(2)}) collective-permute-start(f32[10,1,512]{2,1,0:T(1,128)S(1)} %get-tuple-element.40), channel_id=1, source_target_pairs={{0,1},{1,2},{2,3},{4,5},{5,6},{6,7},{8,9},{9,10},{10,11},{12,13},{... | collective-permute-start | bytes 61448 | tf_op jit(solution)/shard_map/ppermute | solution.py:20
  281.5 6.6 %collective-permute-start.64 = (f32[1,16,512]{2,1,0:T(8,128)S(1)}, f32[1,16,512]{2,1,0:T(8,128)S(1)}, u32[]{:S(2)}, u32[]{:S(2)}) collective-permute-start(f32[1,16,512]{2,1,0:T(8,128)S(1)} %get-tuple-element.69), channel_id=1, source_target_pairs={{4,0},{8,4},{12,8},{5,1},{9,5},{13,9},{6,2},{10,6},{14,10},{7,3},{... | collective-permute-start | bytes 98312 | tf_op jit(solution)/shard_map/ppermute | solution.py:23
  282.8 6.1 %collective-permute-start.65 = (f32[1,16,512]{2,1,0:T(8,128)S(1)}, f32[1,16,512]{2,1,0:T(8,128)S(1)}, u32[]{:S(2)}, u32[]{:S(2)}) collective-permute-start(f32[1,16,512]{2,1,0:T(8,128)S(1)} %get-tuple-element.68), channel_id=1, source_target_pairs={{0,4},{4,8},{8,12},{1,5},{5,9},{9,13},{2,6},{6,10},{10,14},{3,7},{... | collective-permute-start | bytes 98312 | tf_op jit(solution)/shard_map/ppermute | solution.py:20
  290.3 6.0 %collective-permute-start.67 = (f32[10,1,512]{2,1,0:T(1,128)S(1)}, f32[10,1,512]{2,1,0:T(1,128)S(1)}, u32[]{:S(2)}, u32[]{:S(2)}) collective-permute-start(f32[10,1,512]{2,1,0:T(1,128)S(1)} %get-tuple-element.36), channel_id=1, source_target_pairs={{0,1},{1,2},{2,3},{4,5},{5,6},{6,7},{8,9},{9,10},{10,11},{12,13},{... | collective-permute-start | bytes 61448 | tf_op jit(solution)/shard_map/ppermute | solution.py:20
  297.3 6.6 %collective-permute-start.68 = (f32[1,16,512]{2,1,0:T(8,128)S(1)}, f32[1,16,512]{2,1,0:T(8,128)S(1)}, u32[]{:S(2)}, u32[]{:S(2)}) collective-permute-start(f32[1,16,512]{2,1,0:T(8,128)S(1)} %get-tuple-element.67), channel_id=1, source_target_pairs={{4,0},{8,4},{12,8},{5,1},{9,5},{13,9},{6,2},{10,6},{14,10},{7,3},{... | collective-permute-start | bytes 98312 | tf_op jit(solution)/shard_map/ppermute | solution.py:23
  298.6 6.1 %collective-permute-start.69 = (f32[1,16,512]{2,1,0:T(8,128)S(1)}, f32[1,16,512]{2,1,0:T(8,128)S(1)}, u32[]{:S(2)}, u32[]{:S(2)}) collective-permute-start(f32[1,16,512]{2,1,0:T(8,128)S(1)} %get-tuple-element.66), channel_id=1, source_target_pairs={{0,4},{4,8},{8,12},{1,5},{5,9},{9,13},{2,6},{6,10},{10,14},{3,7},{... | collective-permute-start | bytes 98312 | tf_op jit(solution)/shard_map/ppermute | solution.py:20
  306.1 6.0 %collective-permute-start.71 = (f32[10,1,512]{2,1,0:T(1,128)S(1)}, f32[10,1,512]{2,1,0:T(1,128)S(1)}, u32[]{:S(2)}, u32[]{:S(2)}) collective-permute-start(f32[10,1,512]{2,1,0:T(1,128)S(1)} %get-tuple-element.32), channel_id=1, source_target_pairs={{0,1},{1,2},{2,3},{4,5},{5,6},{6,7},{8,9},{9,10},{10,11},{12,13},{... | collective-permute-start | bytes 61448 | tf_op jit(solution)/shard_map/ppermute | solution.py:20
  313.1 6.6 %collective-permute-start.72 = (f32[1,16,512]{2,1,0:T(8,128)S(1)}, f32[1,16,512]{2,1,0:T(8,128)S(1)}, u32[]{:S(2)}, u32[]{:S(2)}) collective-permute-start(f32[1,16,512]{2,1,0:T(8,128)S(1)} %get-tuple-element.65), channel_id=1, source_target_pairs={{4,0},{8,4},{12,8},{5,1},{9,5},{13,9},{6,2},{10,6},{14,10},{7,3},{... | collective-permute-start | bytes 98312 | tf_op jit(solution)/shard_map/ppermute | solution.py:23
  314.4 6.1 %collective-permute-start.73 = (f32[1,16,512]{2,1,0:T(8,128)S(1)}, f32[1,16,512]{2,1,0:T(8,128)S(1)}, u32[]{:S(2)}, u32[]{:S(2)}) collective-permute-start(f32[1,16,512]{2,1,0:T(8,128)S(1)} %get-tuple-element.64), channel_id=1, source_target_pairs={{0,4},{4,8},{8,12},{1,5},{5,9},{9,13},{2,6},{6,10},{10,14},{3,7},{... | collective-permute-start | bytes 98312 | tf_op jit(solution)/shard_map/ppermute | solution.py:20
  321.9 6.0 %collective-permute-start.75 = (f32[10,1,512]{2,1,0:T(1,128)S(1)}, f32[10,1,512]{2,1,0:T(1,128)S(1)}, u32[]{:S(2)}, u32[]{:S(2)}) collective-permute-start(f32[10,1,512]{2,1,0:T(1,128)S(1)} %get-tuple-element.28), channel_id=1, source_target_pairs={{0,1},{1,2},{2,3},{4,5},{5,6},{6,7},{8,9},{9,10},{10,11},{12,13},{... | collective-permute-start | bytes 61448 | tf_op jit(solution)/shard_map/ppermute | solution.py:20
  354.0 6.6 %collective-permute-start.76 = (f32[1,8,256]{2,1,0:T(8,128)S(1)}, f32[1,8,256]{2,1,0:T(8,128)S(1)}, u32[]{:S(2)}, u32[]{:S(2)}) collective-permute-start(f32[1,8,256]{2,1,0:T(8,128)S(1)} %get-tuple-element.123), channel_id=1, source_target_pairs={{4,0},{8,4},{12,8},{5,1},{9,5},{13,9},{6,2},{10,6},{14,10},{7,3},{... | collective-permute-start | bytes 24584 | tf_op jit(solution)/shard_map/ppermute | solution.py:23
  355.3 6.1 %collective-permute-start.77 = (f32[1,8,256]{2,1,0:T(8,128)S(1)}, f32[1,8,256]{2,1,0:T(8,128)S(1)}, u32[]{:S(2)}, u32[]{:S(2)}) collective-permute-start(f32[1,8,256]{2,1,0:T(8,128)S(1)} %get-tuple-element.122), channel_id=1, source_target_pairs={{0,4},{4,8},{8,12},{1,5},{5,9},{9,13},{2,6},{6,10},{10,14},{3,7},{... | collective-permute-start | bytes 24584 | tf_op jit(solution)/shard_map/ppermute | solution.py:20
  361.4 6.1 %collective-permute-start.78 = (f32[6,1,256]{2,1,0:T(1,128)S(1)}, f32[6,1,256]{2,1,0:T(1,128)S(1)}, u32[]{:S(2)}, u32[]{:S(2)}) collective-permute-start(f32[6,1,256]{2,1,0:T(1,128)S(1)} %get-tuple-element.95), channel_id=1, source_target_pairs={{1,0},{2,1},{3,2},{5,4},{6,5},{7,6},{9,8},{10,9},{11,10},{13,12},{... | collective-permute-start | bytes 18440 | tf_op jit(solution)/shard_map/ppermute | solution.py:23
  368.9 6.4 %collective-permute-start.80 = (f32[1,8,256]{2,1,0:T(8,128)S(1)}, f32[1,8,256]{2,1,0:T(8,128)S(1)}, u32[]{:S(2)}, u32[]{:S(2)}) collective-permute-start(f32[1,8,256]{2,1,0:T(8,128)S(1)} %get-tuple-element.121), channel_id=1, source_target_pairs={{4,0},{8,4},{12,8},{5,1},{9,5},{13,9},{6,2},{10,6},{14,10},{7,3},{... | collective-permute-start | bytes 24584 | tf_op jit(solution)/shard_map/ppermute | solution.py:23
  386.0 6.4 %collective-permute-start.84 = (f32[1,4,128]{2,1,0:T(4,128)S(1)}, f32[1,4,128]{2,1,0:T(4,128)S(1)}, u32[]{:S(2)}, u32[]{:S(2)}) collective-permute-start(f32[1,4,128]{2,1,0:T(4,128)S(1)} %get-tuple-element.163), channel_id=1, source_target_pairs={{4,0},{8,4},{12,8},{5,1},{9,5},{13,9},{6,2},{10,6},{14,10},{7,3},{... | collective-permute-start | bytes 6152 | tf_op jit(solution)/shard_map/ppermute | solution.py:23
  400.5 6.3 %collective-permute-start.88 = (f32[1,4,128]{2,1,0:T(4,128)S(1)}, f32[1,4,128]{2,1,0:T(4,128)S(1)}, u32[]{:S(2)}, u32[]{:S(2)}) collective-permute-start(f32[1,4,128]{2,1,0:T(4,128)S(1)} %get-tuple-element.161), channel_id=1, source_target_pairs={{4,0},{8,4},{12,8},{5,1},{9,5},{13,9},{6,2},{10,6},{14,10},{7,3},{... | collective-permute-start | bytes 6152 | tf_op jit(solution)/shard_map/ppermute | solution.py:23
  469.2 6.1 %collective-permute-start.98 = (f32[4,1,128]{2,1,0:T(1,128)S(1)}, f32[4,1,128]{2,1,0:T(1,128)S(1)}, u32[]{:S(2)}, u32[]{:S(2)}) collective-permute-start(f32[4,1,128]{2,1,0:T(1,128)S(1)} %get-tuple-element.139), channel_id=1, source_target_pairs={{1,0},{2,1},{3,2},{5,4},{6,5},{7,6},{9,8},{10,9},{11,10},{13,12},{... | collective-permute-start | bytes 6152 | tf_op jit(solution)/shard_map/ppermute | solution.py:23
  470.5 6.1 %collective-permute-start.99 = (f32[4,1,128]{2,1,0:T(1,128)S(1)}, f32[4,1,128]{2,1,0:T(1,128)S(1)}, u32[]{:S(2)}, u32[]{:S(2)}) collective-permute-start(f32[4,1,128]{2,1,0:T(1,128)S(1)} %get-tuple-element.138), channel_id=1, source_target_pairs={{0,1},{1,2},{2,3},{4,5},{5,6},{6,7},{8,9},{9,10},{10,11},{12,13},{... | collective-permute-start | bytes 6152 | tf_op jit(solution)/shard_map/ppermute | solution.py:20
  491.1 6.4 %collective-permute-start.104 = (f32[1,8,256]{2,1,0:T(8,128)S(1)}, f32[1,8,256]{2,1,0:T(8,128)S(1)}, u32[]{:S(2)}, u32[]{:S(2)}) collective-permute-start(f32[1,8,256]{2,1,0:T(8,128)S(1)} %get-tuple-element.117), channel_id=1, source_target_pairs={{4,0},{8,4},{12,8},{5,1},{9,5},{13,9},{6,2},{10,6},{14,10},{7,3},{... | collective-permute-start | bytes 24584 | tf_op jit(solution)/shard_map/ppermute | solution.py:23
  509.3 6.4 %collective-permute-start.108 = (f32[1,16,512]{2,1,0:T(8,128)S(1)}, f32[1,16,512]{2,1,0:T(8,128)S(1)}, u32[]{:S(2)}, u32[]{:S(2)}) collective-permute-start(f32[1,16,512]{2,1,0:T(8,128)S(1)} %get-tuple-element.63), channel_id=1, source_target_pairs={{4,0},{8,4},{12,8},{5,1},{9,5},{13,9},{6,2},{10,6},{14,10},{7,3},{... | collective-permute-start | bytes 98312 | tf_op jit(solution)/shard_map/ppermute | solution.py:23
  517.9 6.0 %collective-permute-start.111 = (f32[10,1,512]{2,1,0:T(1,128)S(1)}, f32[10,1,512]{2,1,0:T(1,128)S(1)}, u32[]{:S(2)}, u32[]{:S(2)}) collective-permute-start(f32[10,1,512]{2,1,0:T(1,128)S(1)} %get-tuple-element.24), channel_id=1, source_target_pairs={{0,1},{1,2},{2,3},{4,5},{5,6},{6,7},{8,9},{9,10},{10,11},{12,13},{... | collective-permute-start | bytes 61448 | tf_op jit(solution)/shard_map/ppermute | solution.py:20
  524.9 6.6 %collective-permute-start.112 = (f32[1,16,512]{2,1,0:T(8,128)S(1)}, f32[1,16,512]{2,1,0:T(8,128)S(1)}, u32[]{:S(2)}, u32[]{:S(2)}) collective-permute-start(f32[1,16,512]{2,1,0:T(8,128)S(1)} %get-tuple-element.61), channel_id=1, source_target_pairs={{4,0},{8,4},{12,8},{5,1},{9,5},{13,9},{6,2},{10,6},{14,10},{7,3},{... | collective-permute-start | bytes 98312 | tf_op jit(solution)/shard_map/ppermute | solution.py:23
  526.2 6.1 %collective-permute-start.113 = (f32[1,16,512]{2,1,0:T(8,128)S(1)}, f32[1,16,512]{2,1,0:T(8,128)S(1)}, u32[]{:S(2)}, u32[]{:S(2)}) collective-permute-start(f32[1,16,512]{2,1,0:T(8,128)S(1)} %get-tuple-element.60), channel_id=1, source_target_pairs={{0,4},{4,8},{8,12},{1,5},{5,9},{9,13},{2,6},{6,10},{10,14},{3,7},{... | collective-permute-start | bytes 98312 | tf_op jit(solution)/shard_map/ppermute | solution.py:20
  533.6 6.0 %collective-permute-start.115 = (f32[10,1,512]{2,1,0:T(1,128)S(1)}, f32[10,1,512]{2,1,0:T(1,128)S(1)}, u32[]{:S(2)}, u32[]{:S(2)}) collective-permute-start(f32[10,1,512]{2,1,0:T(1,128)S(1)} %get-tuple-element.20), channel_id=1, source_target_pairs={{0,1},{1,2},{2,3},{4,5},{5,6},{6,7},{8,9},{9,10},{10,11},{12,13},{... | collective-permute-start | bytes 61448 | tf_op jit(solution)/shard_map/ppermute | solution.py:20
  (53 other events, 290.1 us)
where the time goes:
time: 549 us; the launch traced here: 541 us
  starting transfers between devices  335 us (61%)
  blocking collectives  70.3 us (13%)
  local copies, waits for them, and re-layouts  50.9 us (9%)
  waiting for transfers between devices  50.3 us (9%)
  other arithmetic  31.8 us (6%)
    ppermute x58, starting transfers between devices, extended(): lax.ppermute(lax.slice_in_dim(block, block.shape[dim] - width, None, axis...  260 us
    ppermute x58, starting transfers between devices, extended(): lax.ppermute(lax.slice_in_dim(block, 0, width, axis=dim), axis, backward)  75 us
    all_gather x2, blocking collectives, brick_cycle(): stacked = lax.all_gather(source[None], ('gx', 'gz'), axis=0, tiled=True)  70.3 us
    ppermute x58, waiting for transfers between devices, extended(): lax.ppermute(lax.slice_in_dim(block, block.shape[dim] - width, None, axis...  50.1 us
    reshape x4, local copies, waits for them, and re-layouts, restrict(): residue.reshape(size_x // 2, 2, size_z // 2, 2, size_y // 2, 2)  40.4 us
    reduce_sum x8, other arithmetic, restrict(): residue.reshape(size_x // 2, 2, size_z // 2, 2, size_y // 2, 2)  14.8 us
  transfers between devices with their start and end apart: 116, of which 47 were waited for; matrix products, arithmetic and copies ran while one was open for 1% of the time, Pallas kernels for 0%

commit v1 on v0

v1 whole, which is shorter than its diff:
```python
import functools

import jax
import jax.numpy as jnp
from jax import lax
from jax.experimental import pallas as pl
from jax.experimental.pallas import tpu as pltpu
from jax.sharding import PartitionSpec as P

COARSE_SWEEPS = 8
LANES = 128
RIM = 8
BRICK_X = 8
BRICK_Z = 16
WIDE_X = BRICK_X + 2 * RIM
WIDE_Z = BRICK_Z + 2 * RIM
VMEM_BYTES = 48 * 1024 * 1024


def lane_of(shape):
    return lax.broadcasted_iota(jnp.int32, shape, len(shape) - 1)


def row_of(shape):
    return lax.broadcasted_iota(jnp.int32, shape, len(shape) - 2)


def next_row(tile, step, cyclic):
    rows = tile.shape[0]
    moved = pltpu.roll(tile, rows - step, 0)
    return moved if cyclic else jnp.where(row_of(tile.shape) < rows - step, moved, 0.0)


def last_row(tile, step, cyclic):
    moved = pltpu.roll(tile, step, 0)
    return moved if cyclic else jnp.where(row_of(tile.shape) >= step, moved, 0.0)


def next_lane(tile, step):
    moved = pltpu.roll(tile, LANES - step, 1)
    return jnp.where(lane_of(tile.shape) < LANES - step, moved, 0.0)


def last_lane(tile, step):
    moved = pltpu.roll(tile, step, 1)
    return jnp.where(lane_of(tile.shape) >= step, moved, 0.0)


def load_plane(ref, x, count_q, count_p):
    return [[ref[x, q, p] for p in range(count_p)] for q in range(count_q)]


def store_plane(ref, x, plane):
    for q, line in enumerate(plane):
        for p, tile in enumerate(line):
            ref[x, q, p] = tile


def along_z(plane, step, cyclic):
    count_q, count_p = len(plane), len(plane[0])
    result = []
    for q in range(count_q):
        line = []
        for p in range(count_p):
            after = plane[q + 1][p] if q + 1 < count_q else next_row(plane[0][p], step, cyclic)
            before = plane[q - 1][p] if q > 0 else last_row(plane[-1][p], step, cyclic)
            line.append(after + before)
        result.append(line)
    return result


def along_y(line, step):
    count_p = len(line)
    result = []
    for p in range(count_p):
        after = line[p + 1] if p + 1 < count_p else next_lane(line[0], step)
        before = line[p - 1] if p > 0 else last_lane(line[-1], step)
        result.append(after + before)
    return result


class Level:
    def __init__(self, count_q, count_p, step, cyclic):
        self.count_q, self.count_p, self.step, self.cyclic = count_q, count_p, step, cyclic

    def load(self, ref, x):
        return load_plane(ref, x, self.count_q, self.count_p)

    def put(self, u_ref, g_ref, x, plane):
        store_plane(u_ref, x, plane)
        sums = along_z(plane, self.step, self.cyclic)
        store_plane(
            g_ref,
            x,
            [
                [s + (v + v) for s, v in zip(sum_line, line)]
                for sum_line, line in zip(sums, plane)
            ],
        )

    def spread(self, u_ref, g_ref, x):
        result = []
        for q in range(self.count_q):
            sides, both = [], []
            for p in range(self.count_p):
                here = g_ref[x, q, p]
                sides.append((u_ref[x - 1, q, p] + u_ref[x + 1, q, p]) + here)
                both.append((g_ref[x - 1, q, p] + g_ref[x + 1, q, p]) + (here + here))
            result.append([a + b for a, b in zip(both, along_y(sides, self.step))])
        return result

    def sweep(self, u_ref, g_ref, b_ref, x, weight):
        wide = self.spread(u_ref, g_ref, x)
        return [
            [
                u_ref[x, q, p] * (1.0 / 15.0) + b_ref[x, q, p] + wide[q][p] * weight
                for p in range(self.count_p)
            ]
            for q in range(self.count_q)
        ]

    def residual(self, u_ref, g_ref, b_ref, x):
        wide = self.spread(u_ref, g_ref, x)
        return [
            [
                b_ref[x, q, p] * 5.0 + (wide[q][p] * (1.0 / 6.0) - u_ref[x, q, p] * (14.0 / 3.0))
                for p in range(self.count_p)
            ]
            for q in range(self.count_q)
        ]


def add_planes(one, other):
    return [[a + b for a, b in zip(l, m)] for l, m in zip(one, other)]


def join(plane):
    lines = [[a + b for a, b in zip(plane[q], plane[q + 1])] for q in range(0, len(plane), 2)]
    return [[line[p] + line[p + 1] for p in range(0, len(line), 2)] for line in lines]


def join_within(tile):
    rows = tile.shape[0]
    even = row_of(tile.shape) % 2 == 0
    tile = tile + jnp.where(even, pltpu.roll(tile, rows - 1, 0), pltpu.roll(tile, 1, 0))
    even = lane_of(tile.shape) % 2 == 0
    return tile + jnp.where(even, pltpu.roll(tile, LANES - 1, 1), pltpu.roll(tile, 1, 1))


def scaled(plane, factor):
    return [[tile * factor for tile in line] for line in plane]


def each(lo, hi, body, chunk):
    count = hi - lo
    whole = count // chunk
    if whole == 1:
        for x in range(lo, lo + chunk):
            body(x)
    elif whole > 1:

        def step(i, carry):
            for d in range(chunk):
                body(lo + i * chunk + d)
            return carry

        lax.fori_loop(0, whole, step, 0)
    for x in range(lo + whole * chunk, hi):
        body(x)


FINE = Level(4, 4, 1, True)
LEVEL_1 = Level(2, 2, 1, False)
LEVEL_2 = Level(1, 1, 1, False)
LEVEL_3 = Level(1, 1, 2, False)
PAD = RIM // 2


def zero_planes(ref, indices):
    for x in indices:
        ref[x] = jnp.zeros(ref.shape[1:], ref.dtype)


def coarse_grids(count_x, count_z):
    rows = count_z * BRICK_Z // 4
    shapes = []
    for planes, count in ((4 * count_x + 2 * PAD, 2), (2 * count_x + 2, 1), (count_x + 2, 1)):
        shapes += [pltpu.VMEM((planes, count, count, rows, LANES), jnp.float32)] * 5
    return shapes


def coarse_solve(count_x, count_z, pieces_ref, grids):
    (ua1, ub1, ga1, gb1, b1), (ua2, ub2, ga2, gb2, b2), (ua3, ub3, ga3, gb3, b3) = (
        grids[0:5],
        grids[5:10],
        grids[10:15],
    )
    size_1, size_2, size_3 = 4 * count_x, 2 * count_x, count_x
    for ref in (ua1, ub1, ga1, gb1):
        zero_planes(ref, list(range(PAD)) + list(range(PAD + size_1, PAD + size_1 + PAD)))
    for ref, size in ((ua2, size_2), (ub2, size_2), (ga2, size_2), (gb2, size_2)):
        zero_planes(ref, (0, size + 1))
    for ref, size in ((ua3, size_3), (ub3, size_3), (ga3, size_3), (gb3, size_3)):
        zero_planes(ref, (0, size + 1))
    third = 1.0 / 30.0

    def gather(at_x):
        for i in range(4):
            x = PAD + at_x * 4 + i
            for q in range(2):
                for p in range(2):
                    for at_z in range(count_z):
                        piece = pieces_ref[at_x * count_z + at_z, i, q, p] * 0.2
                        b1[x, q, p, 4 * at_z : 4 * at_z + 4, :] = piece
            LEVEL_1.put(ub1, gb1, x, LEVEL_1.load(b1, x))

    each(0, count_x, gather, 1)

    def sweep(level, u_in, g_in, u_out, g_out, b):
        return lambda x: level.put(u_out, g_out, x, level.sweep(u_in, g_in, b, x, third))

    each(PAD, PAD + size_1, sweep(LEVEL_1, ub1, gb1, ua1, ga1, b1), 4)

    def restrict_1(x):
        fine = PAD + 2 * (x - 1)
        pair = add_planes(
            LEVEL_1.residual(ua1, ga1, b1, fine), LEVEL_1.residual(ua1, ga1, b1, fine + 1)
        )
        plane = scaled(join(pair), 0.5 * 0.2)
        store_plane(b2, x, plane)
        LEVEL_2.put(ub2, gb2, x, plane)

    each(1, 1 + size_2, restrict_1, 2)
    each(1, 1 + size_2, sweep(LEVEL_2, ub2, gb2, ua2, ga2, b2), 8)

    def restrict_2(x):
        fine = 1 + 2 * (x - 1)
        pair = add_planes(
            LEVEL_2.residual(ua2, ga2, b2, fine), LEVEL_2.residual(ua2, ga2, b2, fine + 1)
        )
        plane = [[join_within(pair[0][0]) * (0.5 * 0.2)]]
        store_plane(b3, x, plane)
        LEVEL_3.put(ub3, gb3, x, plane)

    each(1, 1 + size_3, restrict_2, 4)
    now, later = (ub3, gb3), (ua3, ga3)
    for _ in range(COARSE_SWEEPS - 1):
        each(1, 1 + size_3, sweep(LEVEL_3, *now, *later, b3), 4)
        now, later = later, now

    def prolong_3(x):
        for d in range(2):
            fine = 1 + 2 * (x - 1) + d
            LEVEL_2.put(ua2, ga2, fine, [[ua2[fine, 0, 0] + now[0][x, 0, 0]]])

    each(1, 1 + size_3, prolong_3, 4)
    each(1, 1 + size_2, sweep(LEVEL_2, ua2, ga2, ub2, gb2, b2), 8)
    each(1, 1 + size_2, sweep(LEVEL_2, ub2, gb2, ua2, ga2, b2), 8)

    def prolong_2(x):
        error = ua2[x, 0, 0]
        for d in range(2):
            fine = PAD + 2 * (x - 1) + d
            LEVEL_1.put(
                ua1, ga1, fine, [[t + error for t in line] for line in LEVEL_1.load(ua1, fine)]
            )

    each(1, 1 + size_2, prolong_2, 2)
    each(PAD, PAD + size_1, sweep(LEVEL_1, ua1, ga1, ub1, gb1, b1), 4)
    each(PAD, PAD + size_1, sweep(LEVEL_1, ub1, gb1, ua1, ga1, b1), 4)
    return ua1


def rim_masks(count_x, count_z, where_ref):
    at_x, at_z = where_ref[0], where_ref[1]
    k = row_of((8, LANES))
    low = (at_z > 0).astype(jnp.float32)
    high = (at_z < count_z - 1).astype(jnp.float32)
    rows = jnp.where(k < 4, 1.0, jnp.where(k < 6, high, low))
    below = (at_x > 0).astype(jnp.float32)
    above = (at_x < count_x - 1).astype(jnp.float32)
    return rows, below, above


def in_segments(lo, hi, body, masks, scale, chunk):
    rows, below, above = masks
    inner = rows * scale
    for start, end, weight in (
        (lo, min(hi, RIM), inner * below),
        (max(lo, RIM), min(hi, RIM + BRICK_X), inner),
        (max(lo, RIM + BRICK_X), hi, inner * above),
    ):
        if end > start:
            each(start, end, functools.partial(body, weight=weight), chunk)


def fine_sweep(u_in, g_in, u_out, g_out, b_ref, margin, masks):
    def body(x, weight):
        FINE.put(u_out, g_out, x, FINE.sweep(u_in, g_in, b_ref, x, weight))

    in_segments(margin, WIDE_X - margin, body, masks, 1.0 / 30.0, 2)


def add_correction(coarse_ref, count_z, where_ref, masks, u_in, u_out, g_out, margin):
    at_x, at_z = where_ref[0], where_ref[1]
    rows_1 = coarse_ref.shape[3]
    turn = lax.rem(rows_1 - 4 * at_z, rows_1)
    k = row_of((8, LANES))
    rows = masks[0]

    def body(i):
        error = []
        for q in range(2):
            line = []
            for p in range(2):
                turned = pltpu.roll(coarse_ref[4 * at_x + i, q, p], turn, 0)
                tile = jnp.where(k < 6, turned[0:8], turned[rows_1 - 8 : rows_1])
                line.append(tile * rows)
            error.append(line)
        for d in range(2):
            x = 2 * i + d
            plane = [
                [u_in[x, q, p] + error[q // 2][p // 2] for p in range(4)] for q in range(4)
            ]
            FINE.put(u_out, g_out, x, plane)

    each(margin // 2, (WIDE_X - margin) // 2, body, 1)


def send_residual(u_ref, g_ref, b_ref, out_ref):
    def body(i):
        x = RIM + 2 * i
        pair = add_planes(
            FINE.residual(u_ref, g_ref, b_ref, x), FINE.residual(u_ref, g_ref, b_ref, x + 1)
        )
        for q, line in enumerate(join(pair)):
            for p, tile in enumerate(line):
                out_ref[0, i, q, p] = (tile * 0.5)[0:4]

    each(0, BRICK_X // 2, body, 1)
    piece = out_ref[0]

    def copy(n, carry):
        out_ref[n] = piece
        return carry

    lax.fori_loop(1, out_ref.shape[0], copy, 0)


def swap_blocks(tiles):
    shape = tiles[0].shape
    lane = lane_of(shape)
    half = lane < 64
    even = (lane // 32) % 2 == 0
    a, b, c, d = tiles
    a, c = jnp.where(half, a, pltpu.roll(c, 64, 1)), jnp.where(half, pltpu.roll(a, 64, 1), c)
    b, d = jnp.where(half, b, pltpu.roll(d, 64, 1)), jnp.where(half, pltpu.roll(b, 64, 1), d)
    a, b = jnp.where(even, a, pltpu.roll(b, 32, 1)), jnp.where(even, pltpu.roll(a, 96, 1), b)
    c, d = jnp.where(even, c, pltpu.roll(d, 32, 1)), jnp.where(even, pltpu.roll(c, 96, 1), d)
    return [a, b, c, d]


def pick_lanes(tile, index):
    return jnp.take_along_axis(tile, index, axis=1, mode="promise_in_bounds")


def down_kernel(count_x, count_z, where_ref, low_ref, mid_ref, high_ref, u_ref, b_ref, out_ref,
                c_ref, g_ref, h_ref, rows_ref):
    masks = rim_masks(count_x, count_z, where_ref)
    lane = lane_of((8, LANES))
    index = (lane % 32) * 4 + lane // 32
    for part, ref in enumerate((low_ref, mid_ref, high_ref)):

        def convert(x, part=part, ref=ref):
            for r in range(0, WIDE_Z, 8):
                tiles = []
                for t in range(4):
                    tile = ref[x, r : r + 8, t * LANES : (t + 1) * LANES]
                    tiles.append(pick_lanes(tile, index))
                for p, tile in enumerate(swap_blocks(tiles)):
                    rows_ref[x, p, r : r + 8, :] = tile
            for q in range(4):
                for p in range(4):
                    c_ref[part * BRICK_X + x, q, p] = rows_ref[x, p, pl.ds(q, 8, stride=4), :]

        each(0, BRICK_X, convert, 2)

    def source(x, weight):
        here = FINE.load(c_ref, x)
        sums = along_z(here, 1, True)
        plane = []
        for q in range(4):
            y_sums = along_y(here[q], 1)
            line = []
            for p in range(4):
                face = (c_ref[x - 1, q, p] + c_ref[x + 1, q, p]) + (sums[q][p] + y_sums[p])
                line.append((here[q][p] * 6.0 + face) * weight)
            plane.append(line)
        FINE.put(b_ref, g_ref, x, plane)

    in_segments(1, WIDE_X - 1, source, masks, 0.2 / 12.0, 2)

    def body(x, weight):
        FINE.put(u_ref, h_ref, x, FINE.sweep(b_ref, g_ref, b_ref, x, weight))

    in_segments(2, WIDE_X - 2, body, masks, 1.0 / 30.0, 2)
    send_residual(u_ref, h_ref, b_ref, out_ref)


def middle_kernel(count_x, count_z, where_ref, pieces_ref, u_ref, b_ref, v_ref, out_ref,
                  ga_ref, gb_ref, ua_ref, *grids):
    masks = rim_masks(count_x, count_z, where_ref)
    coarse = coarse_solve(count_x, count_z, pieces_ref, grids)
    add_correction(coarse, count_z, where_ref, masks, u_ref, ua_ref, ga_ref, 2)
    fine_sweep(ua_ref, ga_ref, v_ref, gb_ref, b_ref, 3, masks)
    fine_sweep(v_ref, gb_ref, ua_ref, ga_ref, b_ref, 4, masks)
    fine_sweep(ua_ref, ga_ref, v_ref, gb_ref, b_ref, 5, masks)
    fine_sweep(v_ref, gb_ref, ua_ref, ga_ref, b_ref, 6, masks)

    def keep(x):
        store_plane(v_ref, x, FINE.load(ua_ref, x))

    each(6, WIDE_X - 6, keep, 2)
    send_residual(ua_ref, ga_ref, b_ref, out_ref)


def up_kernel(count_x, count_z, where_ref, pieces_ref, u_ref, b_ref, out_ref,
              ga_ref, gb_ref, ua_ref, ub_ref, rows_ref, *grids):
    masks = rim_masks(count_x, count_z, where_ref)
    coarse = coarse_solve(count_x, count_z, pieces_ref, grids)
    add_correction(coarse, count_z, where_ref, masks, u_ref, ua_ref, ga_ref, 6)
    fine_sweep(ua_ref, ga_ref, ub_ref, gb_ref, b_ref, 7, masks)
    lane = lane_of((8, LANES))
    index = (lane % 4) * 32 + lane // 4

    def body(x):
        plane = FINE.sweep(ub_ref, gb_ref, b_ref, x, 1.0 / 30.0)
        for q in range(4):
            for t, tile in enumerate(swap_blocks(plane[q])):
                rows = pick_lanes(tile, index)[0:4]
                rows_ref[x - RIM, t, pl.ds(q, 4, stride=4), :] = rows
        for t in range(4):
            out_ref[x - RIM, :, t * LANES : (t + 1) * LANES] = rows_ref[x - RIM, t]

    each(RIM, RIM + BRICK_X, body, 2)


def call(kernel, outputs, scratch):
    shapes = [jax.ShapeDtypeStruct(shape, jnp.float32) for shape in outputs]
    return lambda where, *arrays: pl.pallas_call(
        kernel,
        out_shape=shapes,
        in_specs=[pl.BlockSpec(memory_space=pltpu.SMEM)]
        + [pl.BlockSpec(memory_space=pltpu.VMEM)] * len(arrays),
        out_specs=[pl.BlockSpec(memory_space=pltpu.VMEM)] * len(shapes),
        scratch_shapes=scratch,
        compiler_params=pltpu.CompilerParams(vmem_limit_bytes=VMEM_BYTES),
    )(where, *arrays)


def both_ways(axis, to_next, to_last):
    count = lax.axis_size(axis)
    forward = [(i, i + 1) for i in range(count - 1)]
    backward = [(target, source) for source, target in forward]
    return lax.ppermute(to_next, axis, forward), lax.ppermute(to_last, axis, backward)


def per_device(charges):
    count_x, count_z = lax.axis_size("gx"), lax.axis_size("gz")
    where = jnp.stack([lax.axis_index("gx"), lax.axis_index("gz")]).astype(jnp.int32)
    low, high = both_ways("gz", charges[:, BRICK_Z - RIM :], charges[:, :RIM])
    middle = jnp.concatenate([charges, high, low], axis=1)
    below, above = both_ways("gx", middle, middle)

    wide = (WIDE_X, 4, 4, 8, LANES)
    pieces = (count_x * count_z, BRICK_X // 2, 2, 2, 4, LANES)
    fine = pltpu.VMEM(wide, jnp.float32)
    grids = coarse_grids(count_x, count_z)
    rows_in = pltpu.VMEM((BRICK_X, 4, WIDE_Z, LANES), jnp.float32)
    rows_out = pltpu.VMEM((BRICK_X, 4, BRICK_Z, LANES), jnp.float32)

    u, b, piece = call(
        functools.partial(down_kernel, count_x, count_z), [wide, wide, pieces], [fine] * 3 + [rows_in]
    )(where, below, middle, above)
    gathered = lax.all_to_all(piece, ("gx", "gz"), 0, 0)
    u, piece = call(
        functools.partial(middle_kernel, count_x, count_z), [wide, pieces], [fine] * 3 + grids
    )(where, gathered, u, b)
    gathered = lax.all_to_all(piece, ("gx", "gz"), 0, 0)
    (potential,) = call(
        functools.partial(up_kernel, count_x, count_z), [charges.shape], [fine] * 4 + [rows_out] + grids
    )(where, gathered, u, b)
    return potential


def solution(mesh):
    return jax.shard_map(
        per_device,
        mesh=mesh,
        in_specs=(P(("groups", "gx"), "gz", None),),
        out_specs=P(("groups", "gx"), "gz", None),
        check_vma=False,
    )
```

time: 549 us -> 85.5 us (0.16); the launches traced: 541 us -> 85.2 us
  starting transfers between devices: 335 us -> 11.2 us
  local copies, waits for them, and re-layouts: 50.9 us -> 1.98 us
  waiting for transfers between devices: 50.3 us -> 3.15 us
  other arithmetic: 31.8 us -> 0.08 us
  blocking collectives: 70.3 us -> 47.9 us
  Pallas kernels: 0 us -> 20.8 us
    ppermute x116 -> x4, starting transfers between devices: 335 us -> 11.2 us  [the longest x2 8.63 us: both_ways(): lax.ppermute(to_next, axis, forward)]
    all_gather x2 -> x0, blocking collectives: 70.3 us -> none  [brick_cycle(): stacked = lax.all_gather(source[None], ('gx', 'gz'), axis=0, tiled=True)]
    all_to_all x0 -> x2, blocking collectives: none -> 47.9 us  [per_device(): gathered = lax.all_to_all(piece, ('gx', 'gz'), 0, 0)]
    ppermute x116 -> x4, waiting for transfers between devices: 50.3 us -> 3.15 us  [the longest x2 2.57 us: both_ways(): lax.ppermute(to_next, axis, forward)]
    reshape x14 -> x0, local copies, waits for them, and re-layouts: 45.1 us -> none  [the longest x4 40.4 us: restrict(): residue.reshape(size_x // 2, 2, size_z // 2, 2, size_y // 2, 2)]
    pallas_call x0 -> x3, Pallas kernels: none -> 20.8 us  [call(): pl.pallas_call(kernel, out_shape=shapes, in_specs=[pl.BlockSpec(memory_sp...]
    reduce_sum x8 -> x0, other arithmetic: 14.8 us -> none  [restrict(): residue.reshape(size_x // 2, 2, size_z // 2, 2, size_y // 2, 2)]
    concatenate x76 -> x0, other arithmetic: 7.66 us -> none  [extended(): block = jnp.concatenate([low, block, high], axis=dim)]
  transfers between devices with their start and end apart: 116 -> 4, of which waited for: 47 -> 3; matrix products, arithmetic and copies ran while one was open for 1% -> 1% of each run, Pallas kernels for 0% -> 0%
where the time goes in v1:
time: 85.5 us; the launch traced here: 85.2 us
  blocking collectives  47.9 us (56%)
  Pallas kernels  20.8 us (24%)
  starting transfers between devices  11.2 us (13%)
  waiting for transfers between devices  3.15 us (4%)
  local copies, waits for them, and re-layouts  1.98 us (2%)
    all_to_all x2, blocking collectives, per_device(): gathered = lax.all_to_all(piece, ('gx', 'gz'), 0, 0)  47.9 us
    pallas_call x3, Pallas kernels, call(): pl.pallas_call(kernel, out_shape=shapes, in_specs=[pl.BlockSpec(memory_sp...  20.8 us
    ppermute x2, starting transfers between devices, both_ways(): lax.ppermute(to_next, axis, forward)  8.63 us
    ppermute x2, starting transfers between devices, both_ways(): lax.ppermute(to_last, axis, backward)  2.58 us
    ppermute x2, waiting for transfers between devices, both_ways(): lax.ppermute(to_next, axis, forward)  2.57 us
  transfers between devices with their start and end apart: 4, of which 3 were waited for; matrix products, arithmetic and copies ran while one was open for 1% of the time, Pallas kernels for 0%

profile of v1, /device:TPU:0, one launch (start us, length us, event | category | flops | bytes accessed | tf_op | source)
XLA Modules:
  0.0 85.2 jit_solution(6080940421227680125)
XLA Ops:
  0.0 1.0 %fusion = (f32[8,8,512]{2,1,0:T(8,128)S(1)}, f32[8,8,512]{2,1,0:T(8,128)S(1)}) fusion(f32[8,16,512]{2,1,0:T(8,128)} %param.1), kind=kLoop, calls=%fused_computation.4 | loop fusion | bytes 524288 | tf_op jit(solution)/shard_map/slice | solution.py:471
  1.0 1.3 %collective-permute-start = (f32[8,8,512]{2,1,0:T(8,128)S(1)}, f32[8,8,512]{2,1,0:T(8,128)S(1)}, u32[]{:S(2)}, u32[]{:S(2)}) collective-permute-start(f32[8,8,512]{2,1,0:T(8,128)S(1)} %get-tuple-element.16), channel_id=1, source_target_pairs={{1,0},{2,1},{3,2},{5,4},{6,5},{7,6},{9,8},{10,9},{11,10},{13,12},{... | collective-permute-start | bytes 393224 | tf_op jit(solution)/shard_map/ppermute | solution.py:465
  2.3 5.6 %collective-permute-start.1 = (f32[8,8,512]{2,1,0:T(8,128)S(1)}, f32[8,8,512]{2,1,0:T(8,128)S(1)}, u32[]{:S(2)}, u32[]{:S(2)}) collective-permute-start(f32[8,8,512]{2,1,0:T(8,128)S(1)} %get-tuple-element.15), channel_id=1, source_target_pairs={{0,1},{1,2},{2,3},{4,5},{5,6},{6,7},{8,9},{9,10},{10,11},{12,13},{... | collective-permute-start | bytes 393224 | tf_op jit(solution)/shard_map/ppermute | solution.py:465
  7.9 1.0 %constant_dynamic-update-slice_fusion.2 = f32[8,32,512]{2,1,0:T(8,128)S(1)} fusion(f32[8,16,512]{2,1,0:T(8,128)} %param.1), kind=kLoop, calls=%fused_computation.2 | loop fusion | bytes 524288
  8.8 0.6 collective-permute-done
  9.4 1.2 %collective-permute-done.1 = f32[8,8,512]{2,1,0:T(8,128)S(1)} collective-permute-done((f32[8,8,512]{2,1,0:T(8,128)S(1)}, f32[8,8,512]{2,1,0:T(8,128)S(1)}, u32[]{:S(2)}, u32[]{:S(2)}) %collective-permute-start.1) | collective-permute-done | bytes 131104 | tf_op jit(solution)/shard_map/ppermute | solution.py:465
  10.6 1.3 %collective-permute-start.3 = (f32[8,32,512]{2,1,0:T(8,128)S(1)}, f32[8,32,512]{2,1,0:T(8,128)S(1)}, u32[]{:S(2)}, u32[]{:S(2)}) collective-permute-start(f32[8,32,512]{2,1,0:T(8,128)S(1)} %constant_dynamic-update-slice_fusion.mid_ref), channel_id=1, source_target_pairs={{4,0},{8,4},{12,8},{5,1},{9,5},{13,9},{6,2},{10,6},{14,10},{7,3},{... | collective-permute-start | bytes 1572872 | tf_op jit(solution)/shard_map/ppermute | solution.py:465
  11.9 3.1 %collective-permute-start.2 = (f32[8,32,512]{2,1,0:T(8,128)S(1)}, f32[8,32,512]{2,1,0:T(8,128)S(1)}, u32[]{:S(2)}, u32[]{:S(2)}) collective-permute-start(f32[8,32,512]{2,1,0:T(8,128)S(1)} %constant_dynamic-update-slice_fusion.mid_ref), channel_id=1, source_target_pairs={{0,4},{4,8},{8,12},{1,5},{5,9},{9,13},{2,6},{6,10},{10,14},{3,7},{... | collective-permute-start | bytes 1572872 | tf_op jit(solution)/shard_map/ppermute | solution.py:465
  15.0 0.1 pad_add_fusion.where_ref
  15.1 0.0 collective-permute-done.3.high_ref
  15.1 1.4 %collective-permute-done.2.low_ref = f32[8,32,512]{2,1,0:T(8,128)S(1)} collective-permute-done((f32[8,32,512]{2,1,0:T(8,128)S(1)}, f32[8,32,512]{2,1,0:T(8,128)S(1)}, u32[]{:S(2)}, u32[]{:S(2)}) %collective-permute-start.2) | collective-permute-done | bytes 524320 | tf_op jit(solution)/shard_map/ppermute | solution.py:465
  16.5 6.2 %shard_map.17 = (f32[24,4,4,8,128]{4,3,2,1,0:T(8,128)S(1)}, f32[24,4,4,8,128]{4,3,2,1,0:T(8,128)S(1)}, f32[16,4,2,2,4,128]{5,4,3,2,1,0:T(4,128)S(1)}) custom-call(s32[2]{0:T(128)S(1)} %pad_add_fusion.where_ref, f32[8,32,512]{2,1,0:T(8,128)S(1)} %collective-permute-done.2.low_ref, f32[8,32,512]{2,1,0:T(8,128)S(1)} %constant_dynamic-update-slice_fusion.mid_ref, ...), custom_call_target="tpu_custom_call" | custom-call | tf_op jit(solution)/shard_map/pallas_call | solution.py:450
  22.7 29.1 %all_to_all.10.pieces_ref = f32[16,4,2,2,4,128]{5,4,3,2,1,0:T(4,128)S(1)} all-to-all(f32[16,4,2,2,4,128]{5,4,3,2,1,0:T(4,128)S(1)} %get-tuple-element.10), channel_id=1, replica_groups=mesh['groups'=2,'gx'=4,'gz'=4] {'gx','gz'}, dimensions={0} | all-to-all | bytes 1048576 | tf_op jit(solution)/shard_map/all_to_all | solution.py:485
  51.7 7.9 %shard_map.18 = (f32[24,4,4,8,128]{4,3,2,1,0:T(8,128)S(1)}, f32[16,4,2,2,4,128]{5,4,3,2,1,0:T(4,128)S(1)}) custom-call(s32[2]{0:T(128)S(1)} %pad_add_fusion.where_ref, f32[16,4,2,2,4,128]{5,4,3,2,1,0:T(4,128)S(1)} %all_to_all.10.pieces_ref, f32[24,4,4,8,128]{4,3,2,1,0:T(8,128)S(1)} %get-tuple-element.11.u_ref, f32[24,4,4,8,128]{4,3,2,1,0:T(8,128)S(1)} %get-tuple-element.12.b_ref), custom_call_target="tpu_custom_call" | custom-call | tf_op jit(solution)/shard_map/pallas_call | solution.py:450
  59.6 18.9 %all_to_all.11.pieces_ref = f32[16,4,2,2,4,128]{5,4,3,2,1,0:T(4,128)S(1)} all-to-all(f32[16,4,2,2,4,128]{5,4,3,2,1,0:T(4,128)S(1)} %get-tuple-element.13), channel_id=1, replica_groups=mesh['groups'=2,'gx'=4,'gz'=4] {'gx','gz'}, dimensions={0} | all-to-all | bytes 1048576 | tf_op jit(solution)/shard_map/all_to_all | solution.py:489
  78.5 6.7 %shard_map.19 = f32[8,16,512]{2,1,0:T(8,128)} custom-call(s32[2]{0:T(128)S(1)} %pad_add_fusion.where_ref, f32[16,4,2,2,4,128]{5,4,3,2,1,0:T(4,128)S(1)} %all_to_all.11.pieces_ref, f32[24,4,4,8,128]{4,3,2,1,0:T(8,128)S(1)} %get-tuple-element.14.u_ref, f32[24,4,4,8,128]{4,3,2,1,0:T(8,128)S(1)} %get-tuple-element.12.b_ref), custom_call_target="tpu_custom_call" | custom-call | tf_op jit(solution)/shard_map/pallas_call | solution.py:450
  (2 shorter events, 0.0 us)
Async XLA Ops:
  1.0 8.4 %collective-permute-start = (f32[8,8,512]{2,1,0:T(8,128)S(1)}, f32[8,8,512]{2,1,0:T(8,128)S(1)}, u32[]{:S(2)}, u32[]{:S(2)}) collective-permute-start(f32[8,8,512]{2,1,0:T(8,128)S(1)} %get-tuple-element.16), channel_id=1, source_target_pairs={{1,0},{2,1},{3,2},{5,4},{6,5},{7,6},{9,8},{10,9},{11,10},{13,12},{... | collective-permute-start | bytes 393224 | tf_op jit(solution)/shard_map/ppermute | solution.py:465
  2.3 8.3 %collective-permute-start.1 = (f32[8,8,512]{2,1,0:T(8,128)S(1)}, f32[8,8,512]{2,1,0:T(8,128)S(1)}, u32[]{:S(2)}, u32[]{:S(2)}) collective-permute-start(f32[8,8,512]{2,1,0:T(8,128)S(1)} %get-tuple-element.15), channel_id=1, source_target_pairs={{0,1},{1,2},{2,3},{4,5},{5,6},{6,7},{8,9},{9,10},{10,11},{12,13},{... | collective-permute-start | bytes 393224 | tf_op jit(solution)/shard_map/ppermute | solution.py:465
  10.6 4.5 %collective-permute-start.3 = (f32[8,32,512]{2,1,0:T(8,128)S(1)}, f32[8,32,512]{2,1,0:T(8,128)S(1)}, u32[]{:S(2)}, u32[]{:S(2)}) collective-permute-start(f32[8,32,512]{2,1,0:T(8,128)S(1)} %constant_dynamic-update-slice_fusion.mid_ref), channel_id=1, source_target_pairs={{4,0},{8,4},{12,8},{5,1},{9,5},{13,9},{6,2},{10,6},{14,10},{7,3},{... | collective-permute-start | bytes 1572872 | tf_op jit(solution)/shard_map/ppermute | solution.py:465
  11.9 4.6 %collective-permute-start.2 = (f32[8,32,512]{2,1,0:T(8,128)S(1)}, f32[8,32,512]{2,1,0:T(8,128)S(1)}, u32[]{:S(2)}, u32[]{:S(2)}) collective-permute-start(f32[8,32,512]{2,1,0:T(8,128)S(1)} %constant_dynamic-update-slice_fusion.mid_ref), channel_id=1, source_target_pairs={{0,4},{4,8},{8,12},{1,5},{5,9},{9,13},{2,6},{6,10},{10,14},{3,7},{... | collective-permute-start | bytes 1572872 | tf_op jit(solution)/shard_map/ppermute | solution.py:465

commit v2 on v1

--- a/solution.py
+++ b/solution.py
@@ -123,7 +123,7 @@
         wide = self.spread(u_ref, g_ref, x)
         return [
             [
-                b_ref[x, q, p] * 5.0 + (wide[q][p] * (1.0 / 6.0) - u_ref[x, q, p] * (14.0 / 3.0))
+                b_ref[x, q, p] * 5.0 + (wide[q][p] - u_ref[x, q, p] * 28.0) * (1.0 / 6.0)
                 for p in range(self.count_p)
             ]
             for q in range(self.count_q)
@@ -208,18 +208,20 @@
         for i in range(4):
             x = PAD + at_x * 4 + i
             for q in range(2):
-                for p in range(2):
-                    for at_z in range(count_z):
-                        piece = pieces_ref[at_x * count_z + at_z, i, q, p] * 0.2
-                        b1[x, q, p, 4 * at_z : 4 * at_z + 4, :] = piece
+                for at_z in range(0, count_z, 2):
+                    one, two = (pieces_ref[at_x * count_z + at_z + d, i, q] for d in range(2))
+                    first = row_of(one.shape) < 4
+                    rows = slice(4 * at_z, 4 * at_z + 8)
+                    b1[x, q, 0, rows] = jnp.where(first, one, pltpu.roll(two, 4, 0))
+                    b1[x, q, 1, rows] = jnp.where(first, pltpu.roll(one, 4, 0), two)
             LEVEL_1.put(ub1, gb1, x, LEVEL_1.load(b1, x))
 
-    each(0, count_x, gather, 1)
+    each(0, count_x, gather, 4)
 
     def sweep(level, u_in, g_in, u_out, g_out, b):
         return lambda x: level.put(u_out, g_out, x, level.sweep(u_in, g_in, b, x, third))
 
-    each(PAD, PAD + size_1, sweep(LEVEL_1, ub1, gb1, ua1, ga1, b1), 4)
+    each(PAD, PAD + size_1, sweep(LEVEL_1, ub1, gb1, ua1, ga1, b1), 16)
 
     def restrict_1(x):
         fine = PAD + 2 * (x - 1)
@@ -230,7 +232,7 @@
         store_plane(b2, x, plane)
         LEVEL_2.put(ub2, gb2, x, plane)
 
-    each(1, 1 + size_2, restrict_1, 2)
+    each(1, 1 + size_2, restrict_1, 8)
     each(1, 1 + size_2, sweep(LEVEL_2, ub2, gb2, ua2, ga2, b2), 8)
 
     def restrict_2(x):
@@ -265,9 +267,9 @@
                 ua1, ga1, fine, [[t + error for t in line] for line in LEVEL_1.load(ua1, fine)]
             )
 
-    each(1, 1 + size_2, prolong_2, 2)
-    each(PAD, PAD + size_1, sweep(LEVEL_1, ua1, ga1, ub1, gb1, b1), 4)
-    each(PAD, PAD + size_1, sweep(LEVEL_1, ub1, gb1, ua1, ga1, b1), 4)
+    each(1, 1 + size_2, prolong_2, 8)
+    each(PAD, PAD + size_1, sweep(LEVEL_1, ua1, ga1, ub1, gb1, b1), 16)
+    each(PAD, PAD + size_1, sweep(LEVEL_1, ub1, gb1, ua1, ga1, b1), 16)
     return ua1
 
 
@@ -298,7 +300,7 @@
     def body(x, weight):
         FINE.put(u_out, g_out, x, FINE.sweep(u_in, g_in, b_ref, x, weight))
 
-    in_segments(margin, WIDE_X - margin, body, masks, 1.0 / 30.0, 2)
+    in_segments(margin, WIDE_X - margin, body, masks, 1.0 / 30.0, 4)
 
 
 def add_correction(coarse_ref, count_z, where_ref, masks, u_in, u_out, g_out, margin):
@@ -324,7 +326,7 @@
             ]
             FINE.put(u_out, g_out, x, plane)
 
-    each(margin // 2, (WIDE_X - margin) // 2, body, 1)
+    each(margin // 2, (WIDE_X - margin) // 2, body, 3)
 
 
 def send_residual(u_ref, g_ref, b_ref, out_ref):
@@ -333,18 +335,10 @@
         pair = add_planes(
             FINE.residual(u_ref, g_ref, b_ref, x), FINE.residual(u_ref, g_ref, b_ref, x + 1)
         )
-        for q, line in enumerate(join(pair)):
-            for p, tile in enumerate(line):
-                out_ref[0, i, q, p] = (tile * 0.5)[0:4]
-
-    each(0, BRICK_X // 2, body, 1)
-    piece = out_ref[0]
-
-    def copy(n, carry):
-        out_ref[n] = piece
-        return carry
-
-    lax.fori_loop(1, out_ref.shape[0], copy, 0)
+        for q, (even, odd) in enumerate(join(pair)):
+            out_ref[i, q] = 0.1 * jnp.where(row_of(even.shape) < 4, even, pltpu.roll(odd, 4, 0))
+
+    each(0, BRICK_X // 2, body, BRICK_X // 2)
 
 
 def swap_blocks(tiles):
@@ -383,7 +377,7 @@
                 for p in range(4):
                     c_ref[part * BRICK_X + x, q, p] = rows_ref[x, p, pl.ds(q, 8, stride=4), :]
 
-        each(0, BRICK_X, convert, 2)
+        each(0, BRICK_X, convert, 8)
 
     def source(x, weight):
         here = FINE.load(c_ref, x)
@@ -398,12 +392,12 @@
             plane.append(line)
         FINE.put(b_ref, g_ref, x, plane)
 
-    in_segments(1, WIDE_X - 1, source, masks, 0.2 / 12.0, 2)
+    in_segments(1, WIDE_X - 1, source, masks, 0.2 / 12.0, 4)
 
     def body(x, weight):
         FINE.put(u_ref, h_ref, x, FINE.sweep(b_ref, g_ref, b_ref, x, weight))
 
-    in_segments(2, WIDE_X - 2, body, masks, 1.0 / 30.0, 2)
+    in_segments(2, WIDE_X - 2, body, masks, 1.0 / 30.0, 4)
     send_residual(u_ref, h_ref, b_ref, out_ref)
 
 
@@ -442,7 +436,7 @@
         for t in range(4):
             out_ref[x - RIM, :, t * LANES : (t + 1) * LANES] = rows_ref[x - RIM, t]
 
-    each(RIM, RIM + BRICK_X, body, 2)
+    each(RIM, RIM + BRICK_X, body, 4)
 
 
 def call(kernel, outputs, scratch):
@@ -465,6 +459,16 @@
     return lax.ppermute(to_next, axis, forward), lax.ppermute(to_last, axis, backward)
 
 
+def every_piece_by_axes(piece):
+    line = lax.all_to_all(
+        jnp.broadcast_to(piece[None], (lax.axis_size("gz"),) + piece.shape), "gz", 0, 0
+    )
+    grid = lax.all_to_all(
+        jnp.broadcast_to(line[None], (lax.axis_size("gx"),) + line.shape), "gx", 0, 0
+    )
+    return grid.reshape((-1,) + piece.shape)
+
+
 def per_device(charges):
     count_x, count_z = lax.axis_size("gx"), lax.axis_size("gz")
     where = jnp.stack([lax.axis_index("gx"), lax.axis_index("gz")]).astype(jnp.int32)
@@ -473,20 +477,20 @@
     below, above = both_ways("gx", middle, middle)
 
     wide = (WIDE_X, 4, 4, 8, LANES)
-    pieces = (count_x * count_z, BRICK_X // 2, 2, 2, 4, LANES)
+    piece_shape = (BRICK_X // 2, 2, 8, LANES)
     fine = pltpu.VMEM(wide, jnp.float32)
     grids = coarse_grids(count_x, count_z)
     rows_in = pltpu.VMEM((BRICK_X, 4, WIDE_Z, LANES), jnp.float32)
     rows_out = pltpu.VMEM((BRICK_X, 4, BRICK_Z, LANES), jnp.float32)
 
     u, b, piece = call(
-        functools.partial(down_kernel, count_x, count_z), [wide, wide, pieces], [fine] * 3 + [rows_in]
+        functools.partial(down_kernel, count_x, count_z), [wide, wide, piece_shape], [fine] * 3 + [rows_in]
     )(where, below, middle, above)
-    gathered = lax.all_to_all(piece, ("gx", "gz"), 0, 0)
+    gathered = every_piece_by_axes(piece)
     u, piece = call(
-        functools.partial(middle_kernel, count_x, count_z), [wide, pieces], [fine] * 3 + grids
+        functools.partial(middle_kernel, count_x, count_z), [wide, piece_shape], [fine] * 3 + grids
     )(where, gathered, u, b)
-    gathered = lax.all_to_all(piece, ("gx", "gz"), 0, 0)
+    gathered = lax.all_gather(piece, ("gx", "gz"), axis=0)
     (potential,) = call(
         functools.partial(up_kernel, count_x, count_z), [charges.shape], [fine] * 4 + [rows_out] + grids
     )(where, gathered, u, b)

time: 85.5 us -> 107 us (1.25)
  blocking collectives: 47.9 us -> 63.9 us
  Pallas kernels: 20.8 us -> 25.8 us
    all_gather x0 -> x1, blocking collectives: none -> 34.2 us  [per_device(): gathered = lax.all_gather(piece, ('gx', 'gz'), axis=0)]
    all_to_all x2, blocking collectives: 47.9 us -> 29.7 us  [the longest x1 18 us: every_piece_by_axes(): lax.all_to_all(jnp.broadcast_to(line[None], (lax.axis_size('gx'),) + line...]
    pallas_call x3, Pallas kernels: 20.8 us -> 25.8 us  [call(): pl.pallas_call(kernel, out_shape=shapes, in_specs=[pl.BlockSpec(memory_sp...]
where the time goes in v2:
time: 107 us; the launch traced here: 106 us
  blocking collectives  63.9 us (60%)
  Pallas kernels  25.8 us (24%)
  starting transfers between devices  11.2 us (10%)
  waiting for transfers between devices  3.14 us (3%)
  local copies, waits for them, and re-layouts  2.03 us (2%)
    all_gather x1, blocking collectives, per_device(): gathered = lax.all_gather(piece, ('gx', 'gz'), axis=0)  34.2 us
    pallas_call x3, Pallas kernels, call(): pl.pallas_call(kernel, out_shape=shapes, in_specs=[pl.BlockSpec(memory_sp...  25.8 us
    all_to_all x1, blocking collectives, every_piece_by_axes(): lax.all_to_all(jnp.broadcast_to(line[None], (lax.axis_size('gx'),) + line...  18 us
    all_to_all x1, blocking collectives, every_piece_by_axes(): lax.all_to_all(jnp.broadcast_to(piece[None], (lax.axis_size('gz'),) + pie...  11.7 us
    ppermute x2, starting transfers between devices, both_ways(): lax.ppermute(to_next, axis, forward)  8.63 us
    ppermute x2, starting transfers between devices, both_ways(): lax.ppermute(to_last, axis, backward)  2.58 us
    ppermute x2, waiting for transfers between devices, both_ways(): lax.ppermute(to_next, axis, forward)  2.57 us
  transfers between devices with their start and end apart: 4, of which 3 were waited for; matrix products, arithmetic and copies ran while one was open for 1% of the time, Pallas kernels for 0%

profile of v2, /device:TPU:0, one launch (start us, length us, event | category | flops | bytes accessed | tf_op | source)
XLA Modules:
  0.0 106.2 jit_solution(2351457236971939189)
XLA Ops:
  0.0 1.0 fusion
  1.0 1.3 %collective-permute-start = (f32[8,8,512]{2,1,0:T(8,128)S(1)}, f32[8,8,512]{2,1,0:T(8,128)S(1)}, u32[]{:S(2)}, u32[]{:S(2)}) collective-permute-start(f32[8,8,512]{2,1,0:T(8,128)S(1)} %get-tuple-element.16), channel_id=1, source_target_pairs={{1,0},{2,1},{3,2},{5,4},{6,5},{7,6},{9,8},{10,9},{11,10},{13,12},{... | collective-permute-start | bytes 393224 | tf_op jit(solution)/shard_map/ppermute | solution.py:459
  2.3 5.6 %collective-permute-start.1 = (f32[8,8,512]{2,1,0:T(8,128)S(1)}, f32[8,8,512]{2,1,0:T(8,128)S(1)}, u32[]{:S(2)}, u32[]{:S(2)}) collective-permute-start(f32[8,8,512]{2,1,0:T(8,128)S(1)} %get-tuple-element.15), channel_id=1, source_target_pairs={{0,1},{1,2},{2,3},{4,5},{5,6},{6,7},{8,9},{9,10},{10,11},{12,13},{... | collective-permute-start | bytes 393224 | tf_op jit(solution)/shard_map/ppermute | solution.py:459
  7.9 1.0 constant_dynamic-update-slice_fusion.2
  8.8 0.6 collective-permute-done
  9.4 1.2 %collective-permute-done.1 = f32[8,8,512]{2,1,0:T(8,128)S(1)} collective-permute-done((f32[8,8,512]{2,1,0:T(8,128)S(1)}, f32[8,8,512]{2,1,0:T(8,128)S(1)}, u32[]{:S(2)}, u32[]{:S(2)}) %collective-permute-start.1) | collective-permute-done | bytes 131104 | tf_op jit(solution)/shard_map/ppermute | solution.py:459
  10.6 1.3 %collective-permute-start.3 = (f32[8,32,512]{2,1,0:T(8,128)S(1)}, f32[8,32,512]{2,1,0:T(8,128)S(1)}, u32[]{:S(2)}, u32[]{:S(2)}) collective-permute-start(f32[8,32,512]{2,1,0:T(8,128)S(1)} %constant_dynamic-update-slice_fusion.mid_ref), channel_id=1, source_target_pairs={{4,0},{8,4},{12,8},{5,1},{9,5},{13,9},{6,2},{10,6},{14,10},{7,3},{... | collective-permute-start | bytes 1572872 | tf_op jit(solution)/shard_map/ppermute | solution.py:459
  11.9 3.1 %collective-permute-start.2 = (f32[8,32,512]{2,1,0:T(8,128)S(1)}, f32[8,32,512]{2,1,0:T(8,128)S(1)}, u32[]{:S(2)}, u32[]{:S(2)}) collective-permute-start(f32[8,32,512]{2,1,0:T(8,128)S(1)} %constant_dynamic-update-slice_fusion.mid_ref), channel_id=1, source_target_pairs={{0,4},{4,8},{8,12},{1,5},{5,9},{9,13},{2,6},{6,10},{10,14},{3,7},{... | collective-permute-start | bytes 1572872 | tf_op jit(solution)/shard_map/ppermute | solution.py:459
  15.0 0.1 pad_add_fusion.where_ref
  15.1 0.0 collective-permute-done.3.high_ref
  15.1 1.4 %collective-permute-done.2.low_ref = f32[8,32,512]{2,1,0:T(8,128)S(1)} collective-permute-done((f32[8,32,512]{2,1,0:T(8,128)S(1)}, f32[8,32,512]{2,1,0:T(8,128)S(1)}, u32[]{:S(2)}, u32[]{:S(2)}) %collective-permute-start.2) | collective-permute-done | bytes 524320 | tf_op jit(solution)/shard_map/ppermute | solution.py:459
  16.5 14.5 %shard_map.17 = (f32[24,4,4,8,128]{4,3,2,1,0:T(8,128)S(1)}, f32[24,4,4,8,128]{4,3,2,1,0:T(8,128)S(1)}, f32[4,2,8,128]{3,2,1,0:T(8,128)S(1)}) custom-call(s32[2]{0:T(128)S(1)} %pad_add_fusion.where_ref, f32[8,32,512]{2,1,0:T(8,128)S(1)} %collective-permute-done.2.low_ref, f32[8,32,512]{2,1,0:T(8,128)S(1)} %constant_dynamic-update-slice_fusion.mid_ref, ...), custom_call_target="tpu_custom_call" | custom-call | tf_op jit(solution)/shard_map/pallas_call | solution.py:444
  31.0 11.7 %all_to_all.10 = f32[4,4,2,8,128]{4,3,2,1,0:T(8,128)S(1)} all-to-all(f32[4,4,2,8,128]{4,3,2,1,0:T(8,128)S(1)} %broadcast_in_dim.4), channel_id=1, replica_groups=mesh['groups'=2,'gx'=4,'gz'=4] {'gz'}, dimensions={0} | all-to-all | bytes 262144 | tf_op jit(solution)/shard_map/all_to_all | solution.py:463
  42.7 18.0 %all_to_all.11 = f32[4,4,4,2,8,128]{5,4,3,2,1,0:T(8,128)S(1)} all-to-all(f32[4,4,4,2,8,128]{5,4,3,2,1,0:T(8,128)S(1)} %broadcast_in_dim.5), channel_id=1, replica_groups=mesh['groups'=2,'gx'=4,'gz'=4] {'gx'}, dimensions={0} | all-to-all | bytes 1048576 | tf_op jit(solution)/shard_map/all_to_all | solution.py:466
  60.7 5.9 %shard_map.18 = (f32[24,4,4,8,128]{4,3,2,1,0:T(8,128)S(1)}, f32[4,2,8,128]{3,2,1,0:T(8,128)S(1)}) custom-call(s32[2]{0:T(128)S(1)} %pad_add_fusion.where_ref, f32[16,4,2,8,128]{4,3,2,1,0:T(8,128)S(1)} %bitcast.5, f32[24,4,4,8,128]{4,3,2,1,0:T(8,128)S(1)} %get-tuple-element.11.u_ref, f32[24,4,4,8,128]{4,3,2,1,0:T(8,128)S(1)} %get-tuple-element.12.b_ref), custom_call_target="tpu_custom_call" | custom-call | tf_op jit(solution)/shard_map/pallas_call | solution.py:444
  66.6 34.2 %all-gather = f32[64,2,8,128]{3,2,1,0:T(8,128)S(1)} all-gather(f32[4,2,8,128]{3,2,1,0:T(8,128)S(1)} %get-tuple-element.13), channel_id=2, replica_groups=mesh['groups'=2,'gx'=4,'gz'=4] {'gx','gz'}, dimensions={0}, use_global_device_ids=true | all-gather | bytes 557056 | tf_op jit(solution)/shard_map/all_gather | solution.py:493
  100.8 5.4 %shard_map.19 = f32[8,16,512]{2,1,0:T(8,128)} custom-call(s32[2]{0:T(128)S(1)} %pad_add_fusion.where_ref, f32[16,4,2,8,128]{4,3,2,1,0:T(8,128)S(1)} %bitcast.4, f32[24,4,4,8,128]{4,3,2,1,0:T(8,128)S(1)} %get-tuple-element.14.u_ref, f32[24,4,4,8,128]{4,3,2,1,0:T(8,128)S(1)} %get-tuple-element.12.b_ref), custom_call_target="tpu_custom_call" | custom-call | tf_op jit(solution)/shard_map/pallas_call | solution.py:444
  (4 shorter events, 0.1 us)
Async XLA Ops:
  1.0 8.4 %collective-permute-start = (f32[8,8,512]{2,1,0:T(8,128)S(1)}, f32[8,8,512]{2,1,0:T(8,128)S(1)}, u32[]{:S(2)}, u32[]{:S(2)}) collective-permute-start(f32[8,8,512]{2,1,0:T(8,128)S(1)} %get-tuple-element.16), channel_id=1, source_target_pairs={{1,0},{2,1},{3,2},{5,4},{6,5},{7,6},{9,8},{10,9},{11,10},{13,12},{... | collective-permute-start | bytes 393224 | tf_op jit(solution)/shard_map/ppermute | solution.py:459
  2.3 8.3 %collective-permute-start.1 = (f32[8,8,512]{2,1,0:T(8,128)S(1)}, f32[8,8,512]{2,1,0:T(8,128)S(1)}, u32[]{:S(2)}, u32[]{:S(2)}) collective-permute-start(f32[8,8,512]{2,1,0:T(8,128)S(1)} %get-tuple-element.15), channel_id=1, source_target_pairs={{0,1},{1,2},{2,3},{4,5},{5,6},{6,7},{8,9},{9,10},{10,11},{12,13},{... | collective-permute-start | bytes 393224 | tf_op jit(solution)/shard_map/ppermute | solution.py:459
  10.6 4.5 %collective-permute-start.3 = (f32[8,32,512]{2,1,0:T(8,128)S(1)}, f32[8,32,512]{2,1,0:T(8,128)S(1)}, u32[]{:S(2)}, u32[]{:S(2)}) collective-permute-start(f32[8,32,512]{2,1,0:T(8,128)S(1)} %constant_dynamic-update-slice_fusion.mid_ref), channel_id=1, source_target_pairs={{4,0},{8,4},{12,8},{5,1},{9,5},{13,9},{6,2},{10,6},{14,10},{7,3},{... | collective-permute-start | bytes 1572872 | tf_op jit(solution)/shard_map/ppermute | solution.py:459
  11.9 4.6 %collective-permute-start.2 = (f32[8,32,512]{2,1,0:T(8,128)S(1)}, f32[8,32,512]{2,1,0:T(8,128)S(1)}, u32[]{:S(2)}, u32[]{:S(2)}) collective-permute-start(f32[8,32,512]{2,1,0:T(8,128)S(1)} %constant_dynamic-update-slice_fusion.mid_ref), channel_id=1, source_target_pairs={{0,4},{4,8},{8,12},{1,5},{5,9},{9,13},{2,6},{6,10},{10,14},{3,7},{... | collective-permute-start | bytes 1572872 | tf_op jit(solution)/shard_map/ppermute | solution.py:459

commit v3 on v2

--- a/solution.py
+++ b/solution.py
@@ -189,7 +189,7 @@
     return shapes
 
 
-def coarse_solve(count_x, count_z, pieces_ref, grids):
+def coarse_solve(count_x, count_z, where_ref, pieces, grids):
     (ua1, ub1, ga1, gb1, b1), (ua2, ub2, ga2, gb2, b2), (ua3, ub3, ga3, gb3, b3) = (
         grids[0:5],
         grids[5:10],
@@ -204,24 +204,38 @@
         zero_planes(ref, (0, size + 1))
     third = 1.0 / 30.0
 
-    def gather(at_x):
+    at_x, at_z = where_ref[0], where_ref[1]
+
+    def place(x, load):
         for i in range(4):
-            x = PAD + at_x * 4 + i
             for q in range(2):
-                for at_z in range(0, count_z, 2):
-                    one, two = (pieces_ref[at_x * count_z + at_z + d, i, q] for d in range(2))
+                for z in range(0, count_z, 2):
+                    one, two = load(z, i, q), load(z + 1, i, q)
                     first = row_of(one.shape) < 4
-                    rows = slice(4 * at_z, 4 * at_z + 8)
-                    b1[x, q, 0, rows] = jnp.where(first, one, pltpu.roll(two, 4, 0))
-                    b1[x, q, 1, rows] = jnp.where(first, pltpu.roll(one, 4, 0), two)
-            LEVEL_1.put(ub1, gb1, x, LEVEL_1.load(b1, x))
-
-    each(0, count_x, gather, 4)
+                    rows = slice(4 * z, 4 * z + 8)
+                    b1[x + i, q, 0, rows] = jnp.where(first, one, pltpu.roll(two, 4, 0))
+                    b1[x + i, q, 1, rows] = jnp.where(first, pltpu.roll(one, 4, 0), two)
+            LEVEL_1.put(ub1, gb1, x + i, LEVEL_1.load(b1, x + i))
+
+    if len(pieces) == 1:
+
+        def gather(n):
+            place(PAD + 4 * n, lambda z, i, q: pieces[0][n * count_z + z, i, q])
+
+        each(0, count_x, gather, 1)
+    else:
+
+        def gather(n):
+            for core in range(2):
+                x = PAD + 4 * ((2 * n + core) ^ at_x)
+                place(x, lambda z, i, q: pieces[core][n * count_z + (z ^ at_z), i, q])
+
+        each(0, count_x // 2, gather, 1)
 
     def sweep(level, u_in, g_in, u_out, g_out, b):
         return lambda x: level.put(u_out, g_out, x, level.sweep(u_in, g_in, b, x, third))
 
-    each(PAD, PAD + size_1, sweep(LEVEL_1, ub1, gb1, ua1, ga1, b1), 16)
+    each(PAD, PAD + size_1, sweep(LEVEL_1, ub1, gb1, ua1, ga1, b1), 8)
 
     def restrict_1(x):
         fine = PAD + 2 * (x - 1)
@@ -268,8 +282,8 @@
             )
 
     each(1, 1 + size_2, prolong_2, 8)
-    each(PAD, PAD + size_1, sweep(LEVEL_1, ua1, ga1, ub1, gb1, b1), 16)
-    each(PAD, PAD + size_1, sweep(LEVEL_1, ub1, gb1, ua1, ga1, b1), 16)
+    each(PAD, PAD + size_1, sweep(LEVEL_1, ua1, ga1, ub1, gb1, b1), 8)
+    each(PAD, PAD + size_1, sweep(LEVEL_1, ub1, gb1, ua1, ga1, b1), 8)
     return ua1
 
 
@@ -358,14 +372,15 @@
     return jnp.take_along_axis(tile, index, axis=1, mode="promise_in_bounds")
 
 
-def down_kernel(count_x, count_z, where_ref, low_ref, mid_ref, high_ref, u_ref, b_ref, out_ref,
+def down_kernel(count_x, count_z, where_ref, mid_ref, one_ref, two_ref, u_ref, b_ref, out_ref,
                 c_ref, g_ref, h_ref, rows_ref):
     masks = rim_masks(count_x, count_z, where_ref)
     lane = lane_of((8, LANES))
     index = (lane % 32) * 4 + lane // 32
-    for part, ref in enumerate((low_ref, mid_ref, high_ref)):
-
-        def convert(x, part=part, ref=ref):
+    odd = where_ref[0] % 2
+
+    def convert_from(ref, part):
+        def convert(x):
             for r in range(0, WIDE_Z, 8):
                 tiles = []
                 for t in range(4):
@@ -377,7 +392,11 @@
                 for p in range(4):
                     c_ref[part * BRICK_X + x, q, p] = rows_ref[x, p, pl.ds(q, 8, stride=4), :]
 
-        each(0, BRICK_X, convert, 8)
+        each(0, BRICK_X, convert, 2)
+
+    convert_from(mid_ref, 1)
+    convert_from(one_ref, 2 - 2 * odd)
+    convert_from(two_ref, 2 * odd)
 
     def source(x, weight):
         here = FINE.load(c_ref, x)
@@ -401,10 +420,11 @@
     send_residual(u_ref, h_ref, b_ref, out_ref)
 
 
-def middle_kernel(count_x, count_z, where_ref, pieces_ref, u_ref, b_ref, v_ref, out_ref,
-                  ga_ref, gb_ref, ua_ref, *grids):
+def middle_kernel(count_x, count_z, count_pieces, where_ref, *refs):
+    pieces, refs = refs[:count_pieces], refs[count_pieces:]
+    u_ref, b_ref, v_ref, out_ref, ga_ref, gb_ref, ua_ref, *grids = refs
     masks = rim_masks(count_x, count_z, where_ref)
-    coarse = coarse_solve(count_x, count_z, pieces_ref, grids)
+    coarse = coarse_solve(count_x, count_z, where_ref, pieces, grids)
     add_correction(coarse, count_z, where_ref, masks, u_ref, ua_ref, ga_ref, 2)
     fine_sweep(ua_ref, ga_ref, v_ref, gb_ref, b_ref, 3, masks)
     fine_sweep(v_ref, gb_ref, ua_ref, ga_ref, b_ref, 4, masks)
@@ -418,10 +438,11 @@
     send_residual(ua_ref, ga_ref, b_ref, out_ref)
 
 
-def up_kernel(count_x, count_z, where_ref, pieces_ref, u_ref, b_ref, out_ref,
-              ga_ref, gb_ref, ua_ref, ub_ref, rows_ref, *grids):
+def up_kernel(count_x, count_z, count_pieces, where_ref, *refs):
+    pieces, refs = refs[:count_pieces], refs[count_pieces:]
+    u_ref, b_ref, out_ref, ga_ref, gb_ref, ua_ref, ub_ref, rows_ref, *grids = refs
     masks = rim_masks(count_x, count_z, where_ref)
-    coarse = coarse_solve(count_x, count_z, pieces_ref, grids)
+    coarse = coarse_solve(count_x, count_z, where_ref, pieces, grids)
     add_correction(coarse, count_z, where_ref, masks, u_ref, ua_ref, ga_ref, 6)
     fine_sweep(ua_ref, ga_ref, ub_ref, gb_ref, b_ref, 7, masks)
     lane = lane_of((8, LANES))
@@ -452,29 +473,47 @@
     )(where, *arrays)
 
 
-def both_ways(axis, to_next, to_last):
+def swap(axis, values, distance):
     count = lax.axis_size(axis)
-    forward = [(i, i + 1) for i in range(count - 1)]
-    backward = [(target, source) for source, target in forward]
-    return lax.ppermute(to_next, axis, forward), lax.ppermute(to_last, axis, backward)
-
-
-def every_piece_by_axes(piece):
-    line = lax.all_to_all(
-        jnp.broadcast_to(piece[None], (lax.axis_size("gz"),) + piece.shape), "gz", 0, 0
-    )
-    grid = lax.all_to_all(
-        jnp.broadcast_to(line[None], (lax.axis_size("gx"),) + line.shape), "gx", 0, 0
-    )
-    return grid.reshape((-1,) + piece.shape)
+    return lax.ppermute(values, axis, [(i, i ^ distance) for i in range(count)])
+
+
+def swap_shifted(axis, values):
+    pairs = [(i, i + 1) for i in range(1, lax.axis_size(axis) - 1, 2)]
+    return lax.ppermute(values, axis, pairs + [(target, source) for source, target in pairs])
+
+
+def every_piece(piece):
+    count = lax.axis_size("gx") * lax.axis_size("gz")
+    return (lax.all_to_all(jnp.broadcast_to(piece[None], (count,) + piece.shape), ("gx", "gz"), 0, 0),)
+
+
+def every_piece_by_doubling(piece):
+    held = piece[None]
+    distance = 1
+    while distance < lax.axis_size("gz"):
+        held = jnp.concatenate([held, swap("gz", held, distance)])
+        distance *= 2
+    distance = 2
+    while distance < lax.axis_size("gx"):
+        held = jnp.concatenate([held, swap("gx", held, distance)])
+        distance *= 2
+    return held, swap("gx", held, 1)
 
 
 def per_device(charges):
     count_x, count_z = lax.axis_size("gx"), lax.axis_size("gz")
-    where = jnp.stack([lax.axis_index("gx"), lax.axis_index("gz")]).astype(jnp.int32)
-    low, high = both_ways("gz", charges[:, BRICK_Z - RIM :], charges[:, :RIM])
-    middle = jnp.concatenate([charges, high, low], axis=1)
-    below, above = both_ways("gx", middle, middle)
+    at_x, at_z = lax.axis_index("gx"), lax.axis_index("gz")
+    where = jnp.stack([at_x, at_z]).astype(jnp.int32)
+    even = at_z % 2 == 0
+    first, last = charges[:, :RIM], charges[:, BRICK_Z - RIM :]
+    one = swap("gz", jnp.where(even, last, first), 1)
+    two = swap_shifted("gz", jnp.where(even, first, last))
+    middle = jnp.concatenate(
+        [charges, jnp.where(even, one, two), jnp.where(even, two, one)], axis=1
+    )
+    far = swap_shifted("gx", middle)
+    near = swap("gx", middle, 1)
 
     wide = (WIDE_X, 4, 4, 8, LANES)
     piece_shape = (BRICK_X // 2, 2, 8, LANES)
@@ -484,16 +523,22 @@
     rows_out = pltpu.VMEM((BRICK_X, 4, BRICK_Z, LANES), jnp.float32)
 
     u, b, piece = call(
-        functools.partial(down_kernel, count_x, count_z), [wide, wide, piece_shape], [fine] * 3 + [rows_in]
-    )(where, below, middle, above)
-    gathered = every_piece_by_axes(piece)
+        functools.partial(down_kernel, count_x, count_z),
+        [wide, wide, piece_shape],
+        [fine] * 3 + [rows_in],
+    )(where, middle, near, far)
+    pieces = every_piece(piece)
     u, piece = call(
-        functools.partial(middle_kernel, count_x, count_z), [wide, piece_shape], [fine] * 3 + grids
-    )(where, gathered, u, b)
-    gathered = lax.all_gather(piece, ("gx", "gz"), axis=0)
+        functools.partial(middle_kernel, count_x, count_z, len(pieces)),
+        [wide, piece_shape],
+        [fine] * 3 + grids,
+    )(where, *pieces, u, b)
+    pieces = every_piece_by_doubling(piece)
     (potential,) = call(
-        functools.partial(up_kernel, count_x, count_z), [charges.shape], [fine] * 4 + [rows_out] + grids
-    )(where, gathered, u, b)
+        functools.partial(up_kernel, count_x, count_z, len(pieces)),
+        [charges.shape],
+        [fine] * 4 + [rows_out] + grids,
+    )(where, *pieces, u, b)
     return potential
 
 

time: 107 us -> 76.7 us (0.72)
  blocking collectives: 63.9 us -> 28.9 us
  waiting for transfers between devices: 3.14 us -> 18.9 us
  Pallas kernels: 25.8 us -> 17.6 us
  starting transfers between devices: 11.2 us -> 8.85 us
  other arithmetic: 0.08 us -> 2.1 us
  local copies, waits for them, and re-layouts: 2.03 us -> 0.04 us
    all_gather x1 -> x0, blocking collectives: 34.2 us -> none  [per_device(): gathered = lax.all_gather(piece, ('gx', 'gz'), axis=0)]
    ppermute x4 -> x8, waiting for transfers between devices: 3.14 us -> 18.9 us  [the longest x6 18.9 us: swap(): return lax.ppermute(values, axis, [(i, i ^ distance) for i in range(count)])]
    pallas_call x3, Pallas kernels: 25.8 us -> 17.6 us  [call(): pl.pallas_call(kernel, out_shape=shapes, in_specs=[pl.BlockSpec(memory_sp...]
    ppermute x4 -> x8, starting transfers between devices: 11.2 us -> 8.85 us  [the longest x6 7.49 us: swap(): return lax.ppermute(values, axis, [(i, i ^ distance) for i in range(count)])]
    all_to_all x2 -> x1, blocking collectives: 29.7 us -> 28.9 us  [every_piece(): lax.all_to_all(jnp.broadcast_to(piece[None], (count,) + piece.shape), ('g...]
  transfers between devices with their start and end apart: 4 -> 8, of which waited for: 3 -> 6; matrix products, arithmetic and copies ran while one was open for 1% -> 0% of each run, Pallas kernels for 0% -> 0%
where the time goes in v3:
time: 76.7 us; the launch traced here: 76.5 us
  blocking collectives  28.9 us (38%)
  waiting for transfers between devices  18.9 us (25%)
  Pallas kernels  17.6 us (23%)
  starting transfers between devices  8.85 us (12%)
  other arithmetic  2.1 us (3%)
    all_to_all x1, blocking collectives, every_piece(): lax.all_to_all(jnp.broadcast_to(piece[None], (count,) + piece.shape), ('g...  28.9 us
    ppermute x6, waiting for transfers between devices, swap(): return lax.ppermute(values, axis, [(i, i ^ distance) for i in range(count)])  18.9 us
    pallas_call x3, Pallas kernels, call(): pl.pallas_call(kernel, out_shape=shapes, in_specs=[pl.BlockSpec(memory_sp...  17.6 us
    ppermute x6, starting transfers between devices, swap(): return lax.ppermute(values, axis, [(i, i ^ distance) for i in range(count)])  7.49 us
  transfers between devices with their start and end apart: 8, of which 6 were waited for; matrix products, arithmetic and copies ran while one was open for 0% of the time, Pallas kernels for 0%

profile of v3, /device:TPU:0, one launch (start us, length us, event | category | flops | bytes accessed | tf_op | source)
XLA Modules:
  0.0 76.5 jit_solution(14616334002635440254)
XLA Ops:
  0.0 1.0 %slice_select_fusion.1 = (f32[8,8,512]{2,1,0:T(8,128)S(1)}, f32[8,8,512]{2,1,0:T(8,128)S(1)}) fusion(f32[8,16,512]{2,1,0:T(8,128)} %param.1, pred[]{:T(512)S(6)} %eq.5), kind=kLoop, calls=%fused_computation.4 | loop fusion | flops 65536 | bytes 524289 | tf_op jit(solution)/shard_map/jit(_where)/select_n | solution.py:510
  1.0 3.1 %collective-permute-start = (f32[8,8,512]{2,1,0:T(8,128)S(1)}, f32[8,8,512]{2,1,0:T(8,128)S(1)}, u32[]{:S(2)}, u32[]{:S(2)}) collective-permute-start(f32[8,8,512]{2,1,0:T(8,128)S(1)} %get-tuple-element.17), channel_id=1, source_target_pairs={{0,1},{1,0},{2,3},{3,2},{4,5},{5,4},{6,7},{7,6},{8,9},{9,8},{10,11... | collective-permute-start | bytes 393224 | tf_op jit(solution)/shard_map/ppermute | solution.py:478
  4.1 0.7 collective-permute-start.1
  4.7 2.8 %collective-permute-done = f32[8,8,512]{2,1,0:T(8,128)S(1)} collective-permute-done((f32[8,8,512]{2,1,0:T(8,128)S(1)}, f32[8,8,512]{2,1,0:T(8,128)S(1)}, u32[]{:S(2)}, u32[]{:S(2)}) %collective-permute-start) | collective-permute-done | bytes 131104 | tf_op jit(solution)/shard_map/ppermute | solution.py:478
  7.6 0.0 collective-permute-done.1
  7.6 1.0 %pad_maximum_fusion.mid_ref = f32[8,32,512]{2,1,0:T(8,128)S(1)} fusion(f32[8,8,512]{2,1,0:T(8,128)S(1)} %get-tuple-element.16, f32[8,8,512]{2,1,0:T(8,128)S(1)} %get-tuple-element.15, f32[8,16,512]{2,1,0:T(8,128)} %param.1), kind=kLoop, calls=%fused_computation | loop fusion | flops 262144 | bytes 1048576 | tf_op jit(solution)/shard_map/concatenate | solution.py:512
  8.6 0.7 collective-permute-start.3
  9.3 3.1 %collective-permute-start.2 = (f32[8,32,512]{2,1,0:T(8,128)S(1)}, f32[8,32,512]{2,1,0:T(8,128)S(1)}, u32[]{:S(2)}, u32[]{:S(2)}) collective-permute-start(f32[8,32,512]{2,1,0:T(8,128)S(1)} %pad_maximum_fusion.mid_ref), channel_id=1, source_target_pairs={{0,4},{4,0},{8,12},{12,8},{1,5},{5,1},{9,13},{13,9},{2,6},{6,2},{1... | collective-permute-start | bytes 1572872 | tf_op jit(solution)/shard_map/ppermute | solution.py:478
  12.4 0.1 pad_add_fusion.where_ref
  12.5 0.0 collective-permute-done.3.two_ref
  12.5 1.5 %collective-permute-done.2.one_ref = f32[8,32,512]{2,1,0:T(8,128)S(1)} collective-permute-done((f32[8,32,512]{2,1,0:T(8,128)S(1)}, f32[8,32,512]{2,1,0:T(8,128)S(1)}, u32[]{:S(2)}, u32[]{:S(2)}) %collective-permute-start.2) | collective-permute-done | bytes 524320 | tf_op jit(solution)/shard_map/ppermute | solution.py:478
  13.9 5.3 %shard_map.17 = (f32[24,4,4,8,128]{4,3,2,1,0:T(8,128)S(1)}, f32[24,4,4,8,128]{4,3,2,1,0:T(8,128)S(1)}, f32[4,2,8,128]{3,2,1,0:T(8,128)S(1)}) custom-call(s32[2]{0:T(128)S(1)} %pad_add_fusion.where_ref, f32[8,32,512]{2,1,0:T(8,128)S(1)} %pad_maximum_fusion.mid_ref, f32[8,32,512]{2,1,0:T(8,128)S(1)} %collective-permute-done.2.one_ref, ...), custom_call_target="tpu_custom_call" | custom-call | tf_op jit(solution)/shard_map/pallas_call | solution.py:465
  19.2 28.9 %all_to_all.5.refs_0_ = f32[16,4,2,8,128]{4,3,2,1,0:T(8,128)S(1)} all-to-all(f32[16,4,2,8,128]{4,3,2,1,0:T(8,128)S(1)} %broadcast_in_dim.4), channel_id=1, replica_groups=mesh['groups'=2,'gx'=4,'gz'=4] {'gx','gz'}, dimensions={0} | all-to-all | bytes 1048576 | tf_op jit(solution)/shard_map/all_to_all | solution.py:488
  48.2 6.4 %shard_map.18 = (f32[24,4,4,8,128]{4,3,2,1,0:T(8,128)S(1)}, f32[4,2,8,128]{3,2,1,0:T(8,128)S(1)}) custom-call(s32[2]{0:T(128)S(1)} %pad_add_fusion.where_ref, f32[16,4,2,8,128]{4,3,2,1,0:T(8,128)S(1)} %all_to_all.5.refs_0_, f32[24,4,4,8,128]{4,3,2,1,0:T(8,128)S(1)} %get-tuple-element.11.refs_1_, f32[24,4,4,8,128]{4,3,2,1,0:T(8,128)S(1)} %get-tuple-element.12.refs_2_.refs_3_), custom_call_target="tpu_custom_call" | custom-call | tf_op jit(solution)/shard_map/pallas_call | solution.py:465
  54.6 0.1 collective-permute-start.4
  54.7 3.9 %collective-permute-done.4 = f32[1,4,2,8,128]{4,3,2,1,0:T(8,128)S(1)} collective-permute-done((f32[1,4,2,8,128]{4,3,2,1,0:T(8,128)S(1)}, f32[1,4,2,8,128]{4,3,2,1,0:T(8,128)S(1)}, u32[]{:S(2)}, u32[]{:S(2)}) %collective-permute-start.4) | collective-permute-done | bytes 32800 | tf_op jit(solution)/shard_map/ppermute | solution.py:478
  58.6 0.0 collective-permute-start.5
  58.6 5.3 %collective-permute-done.5 = f32[2,4,2,8,128]{4,3,2,1,0:T(8,128)S(1)} collective-permute-done((f32[2,4,2,8,128]{4,3,2,1,0:T(8,128)S(1)}, f32[2,4,2,8,128]{4,3,2,1,0:T(8,128)S(1)}, u32[]{:S(2)}, u32[]{:S(2)}) %collective-permute-start.5) | collective-permute-done | bytes 65568 | tf_op jit(solution)/shard_map/ppermute | solution.py:478
  63.9 1.2 %collective-permute-start.6 = (f32[4,4,2,8,128]{4,3,2,1,0:T(8,128)S(1)}, f32[4,4,2,8,128]{4,3,2,1,0:T(8,128)S(1)}, u32[]{:S(2)}, u32[]{:S(2)}) collective-permute-start(f32[4,4,2,8,128]{4,3,2,1,0:T(8,128)S(1)} %pad_maximum_fusion.2), channel_id=1, source_target_pairs={{0,8},{4,12},{8,0},{12,4},{1,9},{5,13},{9,1},{13,5},{2,10},{6,14},... | collective-permute-start | bytes 393224 | tf_op jit(solution)/shard_map/ppermute | solution.py:478
  65.1 3.9 %collective-permute-done.6 = f32[4,4,2,8,128]{4,3,2,1,0:T(8,128)S(1)} collective-permute-done((f32[4,4,2,8,128]{4,3,2,1,0:T(8,128)S(1)}, f32[4,4,2,8,128]{4,3,2,1,0:T(8,128)S(1)}, u32[]{:S(2)}, u32[]{:S(2)}) %collective-permute-start.6) | collective-permute-done | bytes 131104 | tf_op jit(solution)/shard_map/ppermute | solution.py:478
  69.0 0.1 collective-permute-start.7
  69.1 1.5 %collective-permute-done.7.refs_1_ = f32[8,4,2,8,128]{4,3,2,1,0:T(8,128)S(1)} collective-permute-done((f32[8,4,2,8,128]{4,3,2,1,0:T(8,128)S(1)}, f32[8,4,2,8,128]{4,3,2,1,0:T(8,128)S(1)}, u32[]{:S(2)}, u32[]{:S(2)}) %collective-permute-start.7) | collective-permute-done | bytes 262176 | tf_op jit(solution)/shard_map/ppermute | solution.py:478
  70.6 5.9 %shard_map.19 = f32[8,16,512]{2,1,0:T(8,128)} custom-call(s32[2]{0:T(128)S(1)} %pad_add_fusion.where_ref, f32[8,4,2,8,128]{4,3,2,1,0:T(8,128)S(1)} %pad_maximum_fusion.1.refs_0_, f32[8,4,2,8,128]{4,3,2,1,0:T(8,128)S(1)} %collective-permute-done.7.refs_1_, f32[24,4,4,8,128]{4,3,2,1,0:T(8,128)S(1)} %get-tuple-element.14.refs_2_, ...), custom_call_target="tpu_custom_call" | custom-call | tf_op jit(solution)/shard_map/pallas_call | solution.py:465
  (5 shorter events, 0.1 us)
Async XLA Ops:
  1.0 6.6 %collective-permute-start = (f32[8,8,512]{2,1,0:T(8,128)S(1)}, f32[8,8,512]{2,1,0:T(8,128)S(1)}, u32[]{:S(2)}, u32[]{:S(2)}) collective-permute-start(f32[8,8,512]{2,1,0:T(8,128)S(1)} %get-tuple-element.17), channel_id=1, source_target_pairs={{0,1},{1,0},{2,3},{3,2},{4,5},{5,4},{6,7},{7,6},{8,9},{9,8},{10,11... | collective-permute-start | bytes 393224 | tf_op jit(solution)/shard_map/ppermute | solution.py:478
  4.1 3.5 %collective-permute-start.1 = (f32[8,8,512]{2,1,0:T(8,128)S(1)}, f32[8,8,512]{2,1,0:T(8,128)S(1)}, u32[]{:S(2)}, u32[]{:S(2)}) collective-permute-start(f32[8,8,512]{2,1,0:T(8,128)S(1)} %get-tuple-element.18), channel_id=1, source_target_pairs={{1,2},{2,1},{5,6},{6,5},{9,10},{10,9},{13,14},{14,13},{17,18},{18,... | collective-permute-start | bytes 393224 | tf_op jit(solution)/shard_map/ppermute | solution.py:483
  8.6 3.9 %collective-permute-start.3 = (f32[8,32,512]{2,1,0:T(8,128)S(1)}, f32[8,32,512]{2,1,0:T(8,128)S(1)}, u32[]{:S(2)}, u32[]{:S(2)}) collective-permute-start(f32[8,32,512]{2,1,0:T(8,128)S(1)} %pad_maximum_fusion.mid_ref), channel_id=1, source_target_pairs={{4,8},{8,4},{5,9},{9,5},{6,10},{10,6},{7,11},{11,7},{20,24},{24,20... | collective-permute-start | bytes 1572872 | tf_op jit(solution)/shard_map/ppermute | solution.py:483
  9.3 4.6 %collective-permute-start.2 = (f32[8,32,512]{2,1,0:T(8,128)S(1)}, f32[8,32,512]{2,1,0:T(8,128)S(1)}, u32[]{:S(2)}, u32[]{:S(2)}) collective-permute-start(f32[8,32,512]{2,1,0:T(8,128)S(1)} %pad_maximum_fusion.mid_ref), channel_id=1, source_target_pairs={{0,4},{4,0},{8,12},{12,8},{1,5},{5,1},{9,13},{13,9},{2,6},{6,2},{1... | collective-permute-start | bytes 1572872 | tf_op jit(solution)/shard_map/ppermute | solution.py:478
  54.6 4.0 %collective-permute-start.4 = (f32[1,4,2,8,128]{4,3,2,1,0:T(8,128)S(1)}, f32[1,4,2,8,128]{4,3,2,1,0:T(8,128)S(1)}, u32[]{:S(2)}, u32[]{:S(2)}) collective-permute-start(f32[1,4,2,8,128]{4,3,2,1,0:T(8,128)S(1)} %bitcast.3), channel_id=1, source_target_pairs={{0,1},{1,0},{2,3},{3,2},{4,5},{5,4},{6,7},{7,6},{8,9},{9,8},{10,11... | collective-permute-start | bytes 98312 | tf_op jit(solution)/shard_map/ppermute | solution.py:478
  58.6 5.3 %collective-permute-start.5 = (f32[2,4,2,8,128]{4,3,2,1,0:T(8,128)S(1)}, f32[2,4,2,8,128]{4,3,2,1,0:T(8,128)S(1)}, u32[]{:S(2)}, u32[]{:S(2)}) collective-permute-start(f32[2,4,2,8,128]{4,3,2,1,0:T(8,128)S(1)} %pad_maximum_fusion.3), channel_id=1, source_target_pairs={{0,2},{1,3},{2,0},{3,1},{4,6},{5,7},{6,4},{7,5},{8,10},{9,11},{10,... | collective-permute-start | bytes 196616 | tf_op jit(solution)/shard_map/ppermute | solution.py:478
  63.9 5.0 %collective-permute-start.6 = (f32[4,4,2,8,128]{4,3,2,1,0:T(8,128)S(1)}, f32[4,4,2,8,128]{4,3,2,1,0:T(8,128)S(1)}, u32[]{:S(2)}, u32[]{:S(2)}) collective-permute-start(f32[4,4,2,8,128]{4,3,2,1,0:T(8,128)S(1)} %pad_maximum_fusion.2), channel_id=1, source_target_pairs={{0,8},{4,12},{8,0},{12,4},{1,9},{5,13},{9,1},{13,5},{2,10},{6,14},... | collective-permute-start | bytes 393224 | tf_op jit(solution)/shard_map/ppermute | solution.py:478
  69.0 1.6 %collective-permute-start.7 = (f32[8,4,2,8,128]{4,3,2,1,0:T(8,128)S(1)}, f32[8,4,2,8,128]{4,3,2,1,0:T(8,128)S(1)}, u32[]{:S(2)}, u32[]{:S(2)}) collective-permute-start(f32[8,4,2,8,128]{4,3,2,1,0:T(8,128)S(1)} %pad_maximum_fusion.1.refs_0_), channel_id=1, source_target_pairs={{0,4},{4,0},{8,12},{12,8},{1,5},{5,1},{9,13},{13,9},{2,6},{6,2},{1... | collective-permute-start | bytes 786440 | tf_op jit(solution)/shard_map/ppermute | solution.py:478

commit v4 on v3

--- a/solution.py
+++ b/solution.py
@@ -1,4 +1,5 @@
 import functools
+import math
 
 import jax
 import jax.numpy as jnp
@@ -14,7 +15,7 @@
 BRICK_Z = 16
 WIDE_X = BRICK_X + 2 * RIM
 WIDE_Z = BRICK_Z + 2 * RIM
-VMEM_BYTES = 48 * 1024 * 1024
+SPARE_BYTES = 4 * 1024 * 1024
 
 
 def lane_of(shape):
@@ -372,31 +373,46 @@
     return jnp.take_along_axis(tile, index, axis=1, mode="promise_in_bounds")
 
 
-def down_kernel(count_x, count_z, where_ref, mid_ref, one_ref, two_ref, u_ref, b_ref, out_ref,
-                c_ref, g_ref, h_ref, rows_ref):
-    masks = rim_masks(count_x, count_z, where_ref)
+def lanes_kernel(where_ref, charges_ref, rows_ref, one_ref, two_ref):
     lane = lane_of((8, LANES))
     index = (lane % 32) * 4 + lane // 32
+    odd = where_ref[1] % 2
+
+    def body(x):
+        for part in range(2):
+            rows = slice(8 * part, 8 * part + 8)
+            tiles = [
+                pick_lanes(charges_ref[x, rows, t * LANES : (t + 1) * LANES], index)
+                for t in range(4)
+            ]
+            for p, tile in enumerate(swap_blocks(tiles)):
+                rows_ref[x, p, rows] = tile
+        for p in range(4):
+            first, last = rows_ref[x, p, 0:8], rows_ref[x, p, 8:16]
+            one_ref[x, p] = jnp.where(odd == 0, last, first)
+            two_ref[x, p] = jnp.where(odd == 0, first, last)
+
+    each(0, BRICK_X, body, 2)
+
+
+def down_kernel(count_x, count_z, where_ref, mid_ref, mid_rim_ref, one_ref, one_rim_ref, two_ref,
+                two_rim_ref, u_ref, b_ref, out_ref, c_ref, g_ref, h_ref, rows_ref):
+    masks = rim_masks(count_x, count_z, where_ref)
     odd = where_ref[0] % 2
 
-    def convert_from(ref, part):
-        def convert(x):
-            for r in range(0, WIDE_Z, 8):
-                tiles = []
-                for t in range(4):
-                    tile = ref[x, r : r + 8, t * LANES : (t + 1) * LANES]
-                    tiles.append(pick_lanes(tile, index))
-                for p, tile in enumerate(swap_blocks(tiles)):
-                    rows_ref[x, p, r : r + 8, :] = tile
-            for q in range(4):
-                for p in range(4):
+    def split_rows(ref, rim_ref, part):
+        def split(x):
+            for p in range(4):
+                rows_ref[x, p, 0:BRICK_Z] = ref[x, p]
+                rows_ref[x, p, BRICK_Z:WIDE_Z] = rim_ref[x, p]
+                for q in range(4):
                     c_ref[part * BRICK_X + x, q, p] = rows_ref[x, p, pl.ds(q, 8, stride=4), :]
 
-        each(0, BRICK_X, convert, 2)
-
-    convert_from(mid_ref, 1)
-    convert_from(one_ref, 2 - 2 * odd)
-    convert_from(two_ref, 2 * odd)
+        each(0, BRICK_X, split, 2)
+
+    split_rows(mid_ref, mid_rim_ref, 1)
+    split_rows(one_ref, one_rim_ref, 2 - 2 * odd)
+    split_rows(two_ref, two_rim_ref, 2 * odd)
 
     def source(x, weight):
         here = FINE.load(c_ref, x)
@@ -462,15 +478,21 @@
 
 def call(kernel, outputs, scratch):
     shapes = [jax.ShapeDtypeStruct(shape, jnp.float32) for shape in outputs]
-    return lambda where, *arrays: pl.pallas_call(
-        kernel,
-        out_shape=shapes,
-        in_specs=[pl.BlockSpec(memory_space=pltpu.SMEM)]
-        + [pl.BlockSpec(memory_space=pltpu.VMEM)] * len(arrays),
-        out_specs=[pl.BlockSpec(memory_space=pltpu.VMEM)] * len(shapes),
-        scratch_shapes=scratch,
-        compiler_params=pltpu.CompilerParams(vmem_limit_bytes=VMEM_BYTES),
-    )(where, *arrays)
+    held = sum(4 * math.prod(shape.shape) for shape in scratch)
+
+    def run(where, *arrays):
+        moved = sum(4 * math.prod(array.shape) for array in arrays + tuple(shapes))
+        return pl.pallas_call(
+            kernel,
+            out_shape=shapes,
+            in_specs=[pl.BlockSpec(memory_space=pltpu.SMEM)]
+            + [pl.BlockSpec(memory_space=pltpu.VMEM)] * len(arrays),
+            out_specs=[pl.BlockSpec(memory_space=pltpu.VMEM)] * len(shapes),
+            scratch_shapes=scratch,
+            compiler_params=pltpu.CompilerParams(vmem_limit_bytes=held + moved + SPARE_BYTES),
+        )(where, *arrays)
+
+    return run
 
 
 def swap(axis, values, distance):
@@ -484,11 +506,6 @@
 
 
 def every_piece(piece):
-    count = lax.axis_size("gx") * lax.axis_size("gz")
-    return (lax.all_to_all(jnp.broadcast_to(piece[None], (count,) + piece.shape), ("gx", "gz"), 0, 0),)
-
-
-def every_piece_by_doubling(piece):
     held = piece[None]
     distance = 1
     while distance < lax.axis_size("gz"):
@@ -505,15 +522,16 @@
     count_x, count_z = lax.axis_size("gx"), lax.axis_size("gz")
     at_x, at_z = lax.axis_index("gx"), lax.axis_index("gz")
     where = jnp.stack([at_x, at_z]).astype(jnp.int32)
-    even = at_z % 2 == 0
-    first, last = charges[:, :RIM], charges[:, BRICK_Z - RIM :]
-    one = swap("gz", jnp.where(even, last, first), 1)
-    two = swap_shifted("gz", jnp.where(even, first, last))
-    middle = jnp.concatenate(
-        [charges, jnp.where(even, one, two), jnp.where(even, two, one)], axis=1
-    )
+    brick, rim = (BRICK_X, 4, BRICK_Z, LANES), (BRICK_X, 4, RIM, LANES)
+    middle, one, two = call(lanes_kernel, [brick, rim, rim], [])(where, charges)
     far = swap_shifted("gx", middle)
     near = swap("gx", middle, 1)
+    one = swap("gz", one, 1)
+    two = swap_shifted("gz", two)
+    even = at_z % 2 == 0
+    middle_rim = jnp.concatenate([jnp.where(even, one, two), jnp.where(even, two, one)], axis=2)
+    far_rim = swap_shifted("gx", middle_rim)
+    near_rim = swap("gx", middle_rim, 1)
 
     wide = (WIDE_X, 4, 4, 8, LANES)
     piece_shape = (BRICK_X // 2, 2, 8, LANES)
@@ -526,14 +544,14 @@
         functools.partial(down_kernel, count_x, count_z),
         [wide, wide, piece_shape],
         [fine] * 3 + [rows_in],
-    )(where, middle, near, far)
+    )(where, middle, middle_rim, near, near_rim, far, far_rim)
     pieces = every_piece(piece)
     u, piece = call(
         functools.partial(middle_kernel, count_x, count_z, len(pieces)),
         [wide, piece_shape],
         [fine] * 3 + grids,
     )(where, *pieces, u, b)
-    pieces = every_piece_by_doubling(piece)
+    pieces = every_piece(piece)
     (potential,) = call(
         functools.partial(up_kernel, count_x, count_z, len(pieces)),
         [charges.shape],

time: 76.7 us -> 66.4 us (0.87)
  blocking collectives: 28.9 us -> 0 us
  starting transfers between devices: 8.85 us -> 28.4 us
  other arithmetic: 2.1 us -> 0.18 us
  waiting for transfers between devices: 18.9 us -> 20.3 us
  Pallas kernels: 17.6 us -> 16.3 us
  local copies, waits for them, and re-layouts: 0.04 us -> 0.95 us
    all_to_all x1 -> x0, blocking collectives: 28.9 us -> none  [every_piece(): lax.all_to_all(jnp.broadcast_to(piece[None], (count,) + piece.shape), ('g...]
    ppermute x6 -> x11, starting transfers between devices: 7.49 us -> 26.4 us  [swap(): return lax.ppermute(values, axis, [(i, i ^ distance) for i in range(count)])]
    ppermute x6 -> x11, waiting for transfers between devices: 18.9 us -> 20.3 us  [swap(): return lax.ppermute(values, axis, [(i, i ^ distance) for i in range(count)])]
    pallas_call x3 -> x4, Pallas kernels: 17.6 us -> 16.3 us  [run(): pl.pallas_call(kernel, out_shape=shapes, in_specs=[pl.BlockSpec(memory_sp...]
    select_n x1 -> x0, other arithmetic: 0.99 us -> none  [per_device(): one = swap('gz', jnp.where(even, last, first), 1)]
    unnamed x0 -> x2, local copies, waits for them, and re-layouts: none -> 0.95 us
    concatenate x4 -> x7, other arithmetic: 1.02 us -> 0.08 us  [the longest x2 0.04 us: every_piece(): held = jnp.concatenate([held, swap('gx', held, distance)])]
    ppermute x2 -> x3, starting transfers between devices: 1.35 us -> 2.01 us  [swap_shifted(): lax.ppermute(values, axis, pairs + [(target, source) for source, target i...]
  transfers between devices with their start and end apart: 8 -> 14, of which waited for: 6 -> 9; matrix products, arithmetic and copies ran while one was open for 0% -> 0% of each run, Pallas kernels for 0% -> 0%
where the time goes in v4:
time: 66.4 us; the launch traced here: 66.3 us
  starting transfers between devices  28.4 us (43%)
  waiting for transfers between devices  20.3 us (31%)
  Pallas kernels  16.3 us (25%)
  local copies, waits for them, and re-layouts  0.95 us (1%)
    ppermute x11, starting transfers between devices, swap(): return lax.ppermute(values, axis, [(i, i ^ distance) for i in range(count)])  26.4 us
    ppermute x11, waiting for transfers between devices, swap(): return lax.ppermute(values, axis, [(i, i ^ distance) for i in range(count)])  20.3 us
    pallas_call x4, Pallas kernels, run(): pl.pallas_call(kernel, out_shape=shapes, in_specs=[pl.BlockSpec(memory_sp...  16.3 us
    ppermute x3, starting transfers between devices, swap_shifted(): lax.ppermute(values, axis, pairs + [(target, source) for source, target i...  2.01 us
  transfers between devices with their start and end apart: 14, of which 9 were waited for; matrix products, arithmetic and copies ran while one was open for 0% of the time, Pallas kernels for 0%

profile of v4, /device:TPU:0, one launch (start us, length us, event | category | flops | bytes accessed | tf_op | source)
XLA Modules:
  0.0 66.3 jit_solution(17975773575946602798)
XLA Ops:
  0.0 0.1 pad_add_fusion.where_ref
  0.1 0.0 copy-start
  0.1 0.9 %copy-done = f32[8,16,512]{2,1,0:T(8,128)S(1)} copy-done((f32[8,16,512]{2,1,0:T(8,128)S(1)}, f32[8,16,512]{2,1,0:T(8,128)}, u32[]{:S(2)}) %copy-start) | copy-done | bytes 262168
  1.0 1.4 %shard_map.17 = (f32[8,4,16,128]{3,2,1,0:T(8,128)S(1)}, f32[8,4,8,128]{3,2,1,0:T(8,128)S(1)}, f32[8,4,8,128]{3,2,1,0:T(8,128)S(1)}) custom-call(s32[2]{0:T(128)S(1)} %pad_add_fusion.where_ref, f32[8,16,512]{2,1,0:T(8,128)S(1)} %copy-done), custom_call_target="tpu_custom_call" | custom-call | tf_op jit(solution)/shard_map/pallas_call | solution.py:485
  2.5 3.1 %collective-permute-start = (f32[8,4,8,128]{3,2,1,0:T(8,128)S(1)}, f32[8,4,8,128]{3,2,1,0:T(8,128)S(1)}, u32[]{:S(2)}, u32[]{:S(2)}) collective-permute-start(f32[8,4,8,128]{3,2,1,0:T(8,128)S(1)} %get-tuple-element.14), channel_id=1, source_target_pairs={{0,1},{1,0},{2,3},{3,2},{4,5},{5,4},{6,7},{7,6},{8,9},{9,8},{10,11... | collective-permute-start | bytes 393224 | tf_op jit(solution)/shard_map/ppermute | solution.py:500
  5.6 0.7 collective-permute-start.1
  6.2 0.7 %collective-permute-start.4 = (f32[8,4,16,128]{3,2,1,0:T(8,128)S(1)}, f32[8,4,16,128]{3,2,1,0:T(8,128)S(1)}, u32[]{:S(2)}, u32[]{:S(2)}) collective-permute-start(f32[8,4,16,128]{3,2,1,0:T(8,128)S(1)} %get-tuple-element.13.mid_ref), channel_id=1, source_target_pairs={{4,8},{8,4},{5,9},{9,5},{6,10},{10,6},{7,11},{11,7},{20,24},{24,20... | collective-permute-start | bytes 786440 | tf_op jit(solution)/shard_map/ppermute | solution.py:505
  6.9 2.9 %collective-permute-start.2 = (f32[8,4,16,128]{3,2,1,0:T(8,128)S(1)}, f32[8,4,16,128]{3,2,1,0:T(8,128)S(1)}, u32[]{:S(2)}, u32[]{:S(2)}) collective-permute-start(f32[8,4,16,128]{3,2,1,0:T(8,128)S(1)} %get-tuple-element.13.mid_ref), channel_id=1, source_target_pairs={{0,4},{4,0},{8,12},{12,8},{1,5},{5,1},{9,13},{13,9},{2,6},{6,2},{1... | collective-permute-start | bytes 786440 | tf_op jit(solution)/shard_map/ppermute | solution.py:500
  9.9 0.0 collective-permute-done
  9.9 0.0 collective-permute-done.1
  9.9 0.7 %collective-permute-start.5 = (f32[8,4,16,128]{3,2,1,0:T(8,128)S(1)}, f32[8,4,16,128]{3,2,1,0:T(8,128)S(1)}, u32[]{:S(2)}, u32[]{:S(2)}) collective-permute-start(f32[8,4,16,128]{3,2,1,0:T(8,128)S(1)} %pad_maximum_fusion.mid_rim_ref), channel_id=1, source_target_pairs={{4,8},{8,4},{5,9},{9,5},{6,10},{10,6},{7,11},{11,7},{20,24},{24,20... | collective-permute-start | bytes 786440 | tf_op jit(solution)/shard_map/ppermute | solution.py:505
  10.6 2.3 %collective-permute-start.3 = (f32[8,4,16,128]{3,2,1,0:T(8,128)S(1)}, f32[8,4,16,128]{3,2,1,0:T(8,128)S(1)}, u32[]{:S(2)}, u32[]{:S(2)}) collective-permute-start(f32[8,4,16,128]{3,2,1,0:T(8,128)S(1)} %pad_maximum_fusion.mid_rim_ref), channel_id=1, source_target_pairs={{0,4},{4,0},{8,12},{12,8},{1,5},{5,1},{9,13},{13,9},{2,6},{6,2},{1... | collective-permute-start | bytes 786440 | tf_op jit(solution)/shard_map/ppermute | solution.py:500
  12.9 0.0 collective-permute-done.4.two_ref
  12.9 0.0 collective-permute-done.2.one_ref
  12.9 0.0 collective-permute-done.5.two_rim_ref
  12.9 1.1 %collective-permute-done.3.one_rim_ref = f32[8,4,16,128]{3,2,1,0:T(8,128)S(1)} collective-permute-done((f32[8,4,16,128]{3,2,1,0:T(8,128)S(1)}, f32[8,4,16,128]{3,2,1,0:T(8,128)S(1)}, u32[]{:S(2)}, u32[]{:S(2)}) %collective-permute-start.3) | collective-permute-done | bytes 262176 | tf_op jit(solution)/shard_map/ppermute | solution.py:500
  14.1 2.6 %shard_map.18 = (f32[24,4,4,8,128]{4,3,2,1,0:T(8,128)S(1)}, f32[24,4,4,8,128]{4,3,2,1,0:T(8,128)S(1)}, f32[4,2,8,128]{3,2,1,0:T(8,128)S(1)}) custom-call(s32[2]{0:T(128)S(1)} %pad_add_fusion.where_ref, f32[8,4,16,128]{3,2,1,0:T(8,128)S(1)} %get-tuple-element.13.mid_ref, f32[8,4,16,128]{3,2,1,0:T(8,128)S(1)} %pad_maximum_fusion.mid_rim_ref, ...), custom_call_target="tpu_custom_call" | custom-call | tf_op jit(solution)/shard_map/pallas_call | solution.py:485
  16.6 4.7 %collective-permute-start.6 = (f32[1,4,2,8,128]{4,3,2,1,0:T(8,128)S(1)}, f32[1,4,2,8,128]{4,3,2,1,0:T(8,128)S(1)}, u32[]{:S(2)}, u32[]{:S(2)}) collective-permute-start(f32[1,4,2,8,128]{4,3,2,1,0:T(8,128)S(1)} %bitcast.4), channel_id=1, source_target_pairs={{0,1},{1,0},{2,3},{3,2},{4,5},{5,4},{6,7},{7,6},{8,9},{9,8},{10,11... | collective-permute-start | bytes 98312 | tf_op jit(solution)/shard_map/ppermute | solution.py:500
  21.3 1.9 %collective-permute-done.6 = f32[1,4,2,8,128]{4,3,2,1,0:T(8,128)S(1)} collective-permute-done((f32[1,4,2,8,128]{4,3,2,1,0:T(8,128)S(1)}, f32[1,4,2,8,128]{4,3,2,1,0:T(8,128)S(1)}, u32[]{:S(2)}, u32[]{:S(2)}) %collective-permute-start.6) | collective-permute-done | bytes 32800 | tf_op jit(solution)/shard_map/ppermute | solution.py:500
  23.2 3.2 %collective-permute-start.7 = (f32[2,4,2,8,128]{4,3,2,1,0:T(8,128)S(1)}, f32[2,4,2,8,128]{4,3,2,1,0:T(8,128)S(1)}, u32[]{:S(2)}, u32[]{:S(2)}) collective-permute-start(f32[2,4,2,8,128]{4,3,2,1,0:T(8,128)S(1)} %pad_maximum_fusion.5), channel_id=1, source_target_pairs={{0,2},{1,3},{2,0},{3,1},{4,6},{5,7},{6,4},{7,5},{8,10},{9,11},{10,... | collective-permute-start | bytes 196616 | tf_op jit(solution)/shard_map/ppermute | solution.py:500
  26.4 2.2 %collective-permute-done.7 = f32[2,4,2,8,128]{4,3,2,1,0:T(8,128)S(1)} collective-permute-done((f32[2,4,2,8,128]{4,3,2,1,0:T(8,128)S(1)}, f32[2,4,2,8,128]{4,3,2,1,0:T(8,128)S(1)}, u32[]{:S(2)}, u32[]{:S(2)}) %collective-permute-start.7) | collective-permute-done | bytes 65568 | tf_op jit(solution)/shard_map/ppermute | solution.py:500
  28.7 4.5 %collective-permute-start.8 = (f32[4,4,2,8,128]{4,3,2,1,0:T(8,128)S(1)}, f32[4,4,2,8,128]{4,3,2,1,0:T(8,128)S(1)}, u32[]{:S(2)}, u32[]{:S(2)}) collective-permute-start(f32[4,4,2,8,128]{4,3,2,1,0:T(8,128)S(1)} %pad_maximum_fusion.3), channel_id=1, source_target_pairs={{0,8},{4,12},{8,0},{12,4},{1,9},{5,13},{9,1},{13,5},{2,10},{6,14},... | collective-permute-start | bytes 393224 | tf_op jit(solution)/shard_map/ppermute | solution.py:500
  33.2 3.4 %collective-permute-done.8 = f32[4,4,2,8,128]{4,3,2,1,0:T(8,128)S(1)} collective-permute-done((f32[4,4,2,8,128]{4,3,2,1,0:T(8,128)S(1)}, f32[4,4,2,8,128]{4,3,2,1,0:T(8,128)S(1)}, u32[]{:S(2)}, u32[]{:S(2)}) %collective-permute-start.8) | collective-permute-done | bytes 131104 | tf_op jit(solution)/shard_map/ppermute | solution.py:500
  36.6 0.1 collective-permute-start.9
  36.6 1.5 %collective-permute-done.9.refs_1_ = f32[8,4,2,8,128]{4,3,2,1,0:T(8,128)S(1)} collective-permute-done((f32[8,4,2,8,128]{4,3,2,1,0:T(8,128)S(1)}, f32[8,4,2,8,128]{4,3,2,1,0:T(8,128)S(1)}, u32[]{:S(2)}, u32[]{:S(2)}) %collective-permute-start.9) | collective-permute-done | bytes 262176 | tf_op jit(solution)/shard_map/ppermute | solution.py:500
  38.2 6.4 %shard_map.19 = (f32[24,4,4,8,128]{4,3,2,1,0:T(8,128)S(1)}, f32[4,2,8,128]{3,2,1,0:T(8,128)S(1)}) custom-call(s32[2]{0:T(128)S(1)} %pad_add_fusion.where_ref, f32[8,4,2,8,128]{4,3,2,1,0:T(8,128)S(1)} %pad_maximum_fusion.1.refs_0_, f32[8,4,2,8,128]{4,3,2,1,0:T(8,128)S(1)} %collective-permute-done.9.refs_1_, ...), custom_call_target="tpu_custom_call" | custom-call | tf_op jit(solution)/shard_map/pallas_call | solution.py:485
  44.6 1.4 %collective-permute-start.10 = (f32[1,4,2,8,128]{4,3,2,1,0:T(8,128)S(1)}, f32[1,4,2,8,128]{4,3,2,1,0:T(8,128)S(1)}, u32[]{:S(2)}, u32[]{:S(2)}) collective-permute-start(f32[1,4,2,8,128]{4,3,2,1,0:T(8,128)S(1)} %bitcast.8), channel_id=1, source_target_pairs={{0,1},{1,0},{2,3},{3,2},{4,5},{5,4},{6,7},{7,6},{8,9},{9,8},{10,11... | collective-permute-start | bytes 98312 | tf_op jit(solution)/shard_map/ppermute | solution.py:500
  46.0 2.6 %collective-permute-done.10 = f32[1,4,2,8,128]{4,3,2,1,0:T(8,128)S(1)} collective-permute-done((f32[1,4,2,8,128]{4,3,2,1,0:T(8,128)S(1)}, f32[1,4,2,8,128]{4,3,2,1,0:T(8,128)S(1)}, u32[]{:S(2)}, u32[]{:S(2)}) %collective-permute-start.10) | collective-permute-done | bytes 32800 | tf_op jit(solution)/shard_map/ppermute | solution.py:500
  48.6 2.5 %collective-permute-start.11 = (f32[2,4,2,8,128]{4,3,2,1,0:T(8,128)S(1)}, f32[2,4,2,8,128]{4,3,2,1,0:T(8,128)S(1)}, u32[]{:S(2)}, u32[]{:S(2)}) collective-permute-start(f32[2,4,2,8,128]{4,3,2,1,0:T(8,128)S(1)} %pad_maximum_fusion.6), channel_id=1, source_target_pairs={{0,2},{1,3},{2,0},{3,1},{4,6},{5,7},{6,4},{7,5},{8,10},{9,11},{10,... | collective-permute-start | bytes 196616 | tf_op jit(solution)/shard_map/ppermute | solution.py:500
  51.1 2.7 %collective-permute-done.11 = f32[2,4,2,8,128]{4,3,2,1,0:T(8,128)S(1)} collective-permute-done((f32[2,4,2,8,128]{4,3,2,1,0:T(8,128)S(1)}, f32[2,4,2,8,128]{4,3,2,1,0:T(8,128)S(1)}, u32[]{:S(2)}, u32[]{:S(2)}) %collective-permute-start.11) | collective-permute-done | bytes 65568 | tf_op jit(solution)/shard_map/ppermute | solution.py:500
  53.7 1.7 %collective-permute-start.12 = (f32[4,4,2,8,128]{4,3,2,1,0:T(8,128)S(1)}, f32[4,4,2,8,128]{4,3,2,1,0:T(8,128)S(1)}, u32[]{:S(2)}, u32[]{:S(2)}) collective-permute-start(f32[4,4,2,8,128]{4,3,2,1,0:T(8,128)S(1)} %pad_maximum_fusion.4), channel_id=1, source_target_pairs={{0,8},{4,12},{8,0},{12,4},{1,9},{5,13},{9,1},{13,5},{2,10},{6,14},... | collective-permute-start | bytes 393224 | tf_op jit(solution)/shard_map/ppermute | solution.py:500
  55.4 3.4 %collective-permute-done.12 = f32[4,4,2,8,128]{4,3,2,1,0:T(8,128)S(1)} collective-permute-done((f32[4,4,2,8,128]{4,3,2,1,0:T(8,128)S(1)}, f32[4,4,2,8,128]{4,3,2,1,0:T(8,128)S(1)}, u32[]{:S(2)}, u32[]{:S(2)}) %collective-permute-start.12) | collective-permute-done | bytes 131104 | tf_op jit(solution)/shard_map/ppermute | solution.py:500
  58.8 0.1 collective-permute-start.13
  58.9 1.5 %collective-permute-done.13.refs_1_ = f32[8,4,2,8,128]{4,3,2,1,0:T(8,128)S(1)} collective-permute-done((f32[8,4,2,8,128]{4,3,2,1,0:T(8,128)S(1)}, f32[8,4,2,8,128]{4,3,2,1,0:T(8,128)S(1)}, u32[]{:S(2)}, u32[]{:S(2)}) %collective-permute-start.13) | collective-permute-done | bytes 262176 | tf_op jit(solution)/shard_map/ppermute | solution.py:500
  60.4 5.9 %shard_map.20 = f32[8,16,512]{2,1,0:T(8,128)} custom-call(s32[2]{0:T(128)S(1)} %pad_add_fusion.where_ref, f32[8,4,2,8,128]{4,3,2,1,0:T(8,128)S(1)} %pad_maximum_fusion.2.refs_0_, f32[8,4,2,8,128]{4,3,2,1,0:T(8,128)S(1)} %collective-permute-done.13.refs_1_, f32[24,4,4,8,128]{4,3,2,1,0:T(8,128)S(1)} %get-tuple-element.20.refs_2_, ...), custom_call_target="tpu_custom_call" | custom-call | tf_op jit(solution)/shard_map/pallas_call | solution.py:485
  (8 shorter events, 0.1 us)
Async XLA Ops:
  0.1 0.9 %copy-start = (f32[8,16,512]{2,1,0:T(8,128)S(1)}, f32[8,16,512]{2,1,0:T(8,128)}, u32[]{:S(2)}) copy-start(f32[8,16,512]{2,1,0:T(8,128)} %charges_ref.1) | copy-start | bytes 786436
  2.5 7.4 %collective-permute-start = (f32[8,4,8,128]{3,2,1,0:T(8,128)S(1)}, f32[8,4,8,128]{3,2,1,0:T(8,128)S(1)}, u32[]{:S(2)}, u32[]{:S(2)}) collective-permute-start(f32[8,4,8,128]{3,2,1,0:T(8,128)S(1)} %get-tuple-element.14), channel_id=1, source_target_pairs={{0,1},{1,0},{2,3},{3,2},{4,5},{5,4},{6,7},{7,6},{8,9},{9,8},{10,11... | collective-permute-start | bytes 393224 | tf_op jit(solution)/shard_map/ppermute | solution.py:500
  5.6 4.3 %collective-permute-start.1 = (f32[8,4,8,128]{3,2,1,0:T(8,128)S(1)}, f32[8,4,8,128]{3,2,1,0:T(8,128)S(1)}, u32[]{:S(2)}, u32[]{:S(2)}) collective-permute-start(f32[8,4,8,128]{3,2,1,0:T(8,128)S(1)} %get-tuple-element.15), channel_id=1, source_target_pairs={{1,2},{2,1},{5,6},{6,5},{9,10},{10,9},{13,14},{14,13},{17,18},{18,... | collective-permute-start | bytes 393224 | tf_op jit(solution)/shard_map/ppermute | solution.py:505
  6.2 6.7 %collective-permute-start.4 = (f32[8,4,16,128]{3,2,1,0:T(8,128)S(1)}, f32[8,4,16,128]{3,2,1,0:T(8,128)S(1)}, u32[]{:S(2)}, u32[]{:S(2)}) collective-permute-start(f32[8,4,16,128]{3,2,1,0:T(8,128)S(1)} %get-tuple-element.13.mid_ref), channel_id=1, source_target_pairs={{4,8},{8,4},{5,9},{9,5},{6,10},{10,6},{7,11},{11,7},{20,24},{24,20... | collective-permute-start | bytes 786440 | tf_op jit(solution)/shard_map/ppermute | solution.py:505
  6.9 6.0 %collective-permute-start.2 = (f32[8,4,16,128]{3,2,1,0:T(8,128)S(1)}, f32[8,4,16,128]{3,2,1,0:T(8,128)S(1)}, u32[]{:S(2)}, u32[]{:S(2)}) collective-permute-start(f32[8,4,16,128]{3,2,1,0:T(8,128)S(1)} %get-tuple-element.13.mid_ref), channel_id=1, source_target_pairs={{0,4},{4,0},{8,12},{12,8},{1,5},{5,1},{9,13},{13,9},{2,6},{6,2},{1... | collective-permute-start | bytes 786440 | tf_op jit(solution)/shard_map/ppermute | solution.py:500
  9.9 3.0 %collective-permute-start.5 = (f32[8,4,16,128]{3,2,1,0:T(8,128)S(1)}, f32[8,4,16,128]{3,2,1,0:T(8,128)S(1)}, u32[]{:S(2)}, u32[]{:S(2)}) collective-permute-start(f32[8,4,16,128]{3,2,1,0:T(8,128)S(1)} %pad_maximum_fusion.mid_rim_ref), channel_id=1, source_target_pairs={{4,8},{8,4},{5,9},{9,5},{6,10},{10,6},{7,11},{11,7},{20,24},{24,20... | collective-permute-start | bytes 786440 | tf_op jit(solution)/shard_map/ppermute | solution.py:505
  10.6 3.5 %collective-permute-start.3 = (f32[8,4,16,128]{3,2,1,0:T(8,128)S(1)}, f32[8,4,16,128]{3,2,1,0:T(8,128)S(1)}, u32[]{:S(2)}, u32[]{:S(2)}) collective-permute-start(f32[8,4,16,128]{3,2,1,0:T(8,128)S(1)} %pad_maximum_fusion.mid_rim_ref), channel_id=1, source_target_pairs={{0,4},{4,0},{8,12},{12,8},{1,5},{5,1},{9,13},{13,9},{2,6},{6,2},{1... | collective-permute-start | bytes 786440 | tf_op jit(solution)/shard_map/ppermute | solution.py:500
  16.6 6.6 %collective-permute-start.6 = (f32[1,4,2,8,128]{4,3,2,1,0:T(8,128)S(1)}, f32[1,4,2,8,128]{4,3,2,1,0:T(8,128)S(1)}, u32[]{:S(2)}, u32[]{:S(2)}) collective-permute-start(f32[1,4,2,8,128]{4,3,2,1,0:T(8,128)S(1)} %bitcast.4), channel_id=1, source_target_pairs={{0,1},{1,0},{2,3},{3,2},{4,5},{5,4},{6,7},{7,6},{8,9},{9,8},{10,11... | collective-permute-start | bytes 98312 | tf_op jit(solution)/shard_map/ppermute | solution.py:500
  23.2 5.4 %collective-permute-start.7 = (f32[2,4,2,8,128]{4,3,2,1,0:T(8,128)S(1)}, f32[2,4,2,8,128]{4,3,2,1,0:T(8,128)S(1)}, u32[]{:S(2)}, u32[]{:S(2)}) collective-permute-start(f32[2,4,2,8,128]{4,3,2,1,0:T(8,128)S(1)} %pad_maximum_fusion.5), channel_id=1, source_target_pairs={{0,2},{1,3},{2,0},{3,1},{4,6},{5,7},{6,4},{7,5},{8,10},{9,11},{10,... | collective-permute-start | bytes 196616 | tf_op jit(solution)/shard_map/ppermute | solution.py:500
  28.7 7.9 %collective-permute-start.8 = (f32[4,4,2,8,128]{4,3,2,1,0:T(8,128)S(1)}, f32[4,4,2,8,128]{4,3,2,1,0:T(8,128)S(1)}, u32[]{:S(2)}, u32[]{:S(2)}) collective-permute-start(f32[4,4,2,8,128]{4,3,2,1,0:T(8,128)S(1)} %pad_maximum_fusion.3), channel_id=1, source_target_pairs={{0,8},{4,12},{8,0},{12,4},{1,9},{5,13},{9,1},{13,5},{2,10},{6,14},... | collective-permute-start | bytes 393224 | tf_op jit(solution)/shard_map/ppermute | solution.py:500
  36.6 1.6 %collective-permute-start.9 = (f32[8,4,2,8,128]{4,3,2,1,0:T(8,128)S(1)}, f32[8,4,2,8,128]{4,3,2,1,0:T(8,128)S(1)}, u32[]{:S(2)}, u32[]{:S(2)}) collective-permute-start(f32[8,4,2,8,128]{4,3,2,1,0:T(8,128)S(1)} %pad_maximum_fusion.1.refs_0_), channel_id=1, source_target_pairs={{0,4},{4,0},{8,12},{12,8},{1,5},{5,1},{9,13},{13,9},{2,6},{6,2},{1... | collective-permute-start | bytes 786440 | tf_op jit(solution)/shard_map/ppermute | solution.py:500
  44.6 4.0 %collective-permute-start.10 = (f32[1,4,2,8,128]{4,3,2,1,0:T(8,128)S(1)}, f32[1,4,2,8,128]{4,3,2,1,0:T(8,128)S(1)}, u32[]{:S(2)}, u32[]{:S(2)}) collective-permute-start(f32[1,4,2,8,128]{4,3,2,1,0:T(8,128)S(1)} %bitcast.8), channel_id=1, source_target_pairs={{0,1},{1,0},{2,3},{3,2},{4,5},{5,4},{6,7},{7,6},{8,9},{9,8},{10,11... | collective-permute-start | bytes 98312 | tf_op jit(solution)/shard_map/ppermute | solution.py:500
  48.6 5.2 %collective-permute-start.11 = (f32[2,4,2,8,128]{4,3,2,1,0:T(8,128)S(1)}, f32[2,4,2,8,128]{4,3,2,1,0:T(8,128)S(1)}, u32[]{:S(2)}, u32[]{:S(2)}) collective-permute-start(f32[2,4,2,8,128]{4,3,2,1,0:T(8,128)S(1)} %pad_maximum_fusion.6), channel_id=1, source_target_pairs={{0,2},{1,3},{2,0},{3,1},{4,6},{5,7},{6,4},{7,5},{8,10},{9,11},{10,... | collective-permute-start | bytes 196616 | tf_op jit(solution)/shard_map/ppermute | solution.py:500
  53.7 5.0 %collective-permute-start.12 = (f32[4,4,2,8,128]{4,3,2,1,0:T(8,128)S(1)}, f32[4,4,2,8,128]{4,3,2,1,0:T(8,128)S(1)}, u32[]{:S(2)}, u32[]{:S(2)}) collective-permute-start(f32[4,4,2,8,128]{4,3,2,1,0:T(8,128)S(1)} %pad_maximum_fusion.4), channel_id=1, source_target_pairs={{0,8},{4,12},{8,0},{12,4},{1,9},{5,13},{9,1},{13,5},{2,10},{6,14},... | collective-permute-start | bytes 393224 | tf_op jit(solution)/shard_map/ppermute | solution.py:500
  58.8 1.6 %collective-permute-start.13 = (f32[8,4,2,8,128]{4,3,2,1,0:T(8,128)S(1)}, f32[8,4,2,8,128]{4,3,2,1,0:T(8,128)S(1)}, u32[]{:S(2)}, u32[]{:S(2)}) collective-permute-start(f32[8,4,2,8,128]{4,3,2,1,0:T(8,128)S(1)} %pad_maximum_fusion.2.refs_0_), channel_id=1, source_target_pairs={{0,4},{4,0},{8,12},{12,8},{1,5},{5,1},{9,13},{13,9},{2,6},{6,2},{1... | collective-permute-start | bytes 786440 | tf_op jit(solution)/shard_map/ppermute | solution.py:500

commit v5 on v4

--- a/solution.py
+++ b/solution.py
@@ -99,29 +99,28 @@
             ],
         )
 
-    def spread(self, u_ref, g_ref, x):
+    def spread(self, u_ref, g_ref, x, with_u):
         result = []
         for q in range(self.count_q):
             sides, both = [], []
             for p in range(self.count_p):
                 here = g_ref[x, q, p]
                 sides.append((u_ref[x - 1, q, p] + u_ref[x + 1, q, p]) + here)
+                if with_u:
+                    here = here + u_ref[x, q, p]
                 both.append((g_ref[x - 1, q, p] + g_ref[x + 1, q, p]) + (here + here))
             result.append([a + b for a, b in zip(both, along_y(sides, self.step))])
         return result
 
     def sweep(self, u_ref, g_ref, b_ref, x, weight):
-        wide = self.spread(u_ref, g_ref, x)
+        wide = self.spread(u_ref, g_ref, x, True)
         return [
-            [
-                u_ref[x, q, p] * (1.0 / 15.0) + b_ref[x, q, p] + wide[q][p] * weight
-                for p in range(self.count_p)
-            ]
+            [b_ref[x, q, p] + wide[q][p] * weight for p in range(self.count_p)]
             for q in range(self.count_q)
         ]
 
     def residual(self, u_ref, g_ref, b_ref, x):
-        wide = self.spread(u_ref, g_ref, x)
+        wide = self.spread(u_ref, g_ref, x, False)
         return [
             [
                 b_ref[x, q, p] * 5.0 + (wide[q][p] - u_ref[x, q, p] * 28.0) * (1.0 / 6.0)
@@ -172,9 +171,11 @@
 
 FINE = Level(4, 4, 1, True)
 LEVEL_1 = Level(2, 2, 1, False)
+NEAR_1 = Level(2, 2, 1, True)
 LEVEL_2 = Level(1, 1, 1, False)
 LEVEL_3 = Level(1, 1, 2, False)
 PAD = RIM // 2
+PAD_2 = RIM // 4
 
 
 def zero_planes(ref, indices):
@@ -185,7 +186,7 @@
 def coarse_grids(count_x, count_z):
     rows = count_z * BRICK_Z // 4
     shapes = []
-    for planes, count in ((4 * count_x + 2 * PAD, 2), (2 * count_x + 2, 1), (count_x + 2, 1)):
+    for planes, count in ((4 * count_x + 2 * PAD, 2), (2 * count_x + 2 * PAD_2, 1), (count_x + 2, 1)):
         shapes += [pltpu.VMEM((planes, count, count, rows, LANES), jnp.float32)] * 5
     return shapes
 
@@ -197,12 +198,13 @@
         grids[10:15],
     )
     size_1, size_2, size_3 = 4 * count_x, 2 * count_x, count_x
-    for ref in (ua1, ub1, ga1, gb1):
-        zero_planes(ref, list(range(PAD)) + list(range(PAD + size_1, PAD + size_1 + PAD)))
-    for ref, size in ((ua2, size_2), (ub2, size_2), (ga2, size_2), (gb2, size_2)):
-        zero_planes(ref, (0, size + 1))
-    for ref, size in ((ua3, size_3), (ub3, size_3), (ga3, size_3), (gb3, size_3)):
-        zero_planes(ref, (0, size + 1))
+    for refs, pad, size in (
+        ((ua1, ub1, ga1, gb1, b1), PAD, size_1),
+        ((ua2, ub2, ga2, gb2), PAD_2, size_2),
+        ((ua3, ub3, ga3, gb3), 1, size_3),
+    ):
+        for ref in refs:
+            zero_planes(ref, list(range(pad)) + list(range(pad + size, pad + size + pad)))
     third = 1.0 / 30.0
 
     at_x, at_z = where_ref[0], where_ref[1]
@@ -239,27 +241,28 @@
     each(PAD, PAD + size_1, sweep(LEVEL_1, ub1, gb1, ua1, ga1, b1), 8)
 
     def restrict_1(x):
-        fine = PAD + 2 * (x - 1)
+        fine = PAD + 2 * x
         pair = add_planes(
             LEVEL_1.residual(ua1, ga1, b1, fine), LEVEL_1.residual(ua1, ga1, b1, fine + 1)
         )
         plane = scaled(join(pair), 0.5 * 0.2)
-        store_plane(b2, x, plane)
-        LEVEL_2.put(ub2, gb2, x, plane)
-
-    each(1, 1 + size_2, restrict_1, 8)
-    each(1, 1 + size_2, sweep(LEVEL_2, ub2, gb2, ua2, ga2, b2), 8)
+        store_plane(b2, PAD_2 + x, plane)
+        LEVEL_2.put(ub2, gb2, PAD_2 + x, plane)
+
+    each(0, size_2, restrict_1, 8)
+    all_2 = (PAD_2, PAD_2 + size_2)
+    each(*all_2, sweep(LEVEL_2, ub2, gb2, ua2, ga2, b2), 8)
 
     def restrict_2(x):
-        fine = 1 + 2 * (x - 1)
+        fine = PAD_2 + 2 * x
         pair = add_planes(
             LEVEL_2.residual(ua2, ga2, b2, fine), LEVEL_2.residual(ua2, ga2, b2, fine + 1)
         )
         plane = [[join_within(pair[0][0]) * (0.5 * 0.2)]]
-        store_plane(b3, x, plane)
-        LEVEL_3.put(ub3, gb3, x, plane)
-
-    each(1, 1 + size_3, restrict_2, 4)
+        store_plane(b3, 1 + x, plane)
+        LEVEL_3.put(ub3, gb3, 1 + x, plane)
+
+    each(0, size_3, restrict_2, 4)
     now, later = (ub3, gb3), (ua3, ga3)
     for _ in range(COARSE_SWEEPS - 1):
         each(1, 1 + size_3, sweep(LEVEL_3, *now, *later, b3), 4)
@@ -267,25 +270,70 @@
 
     def prolong_3(x):
         for d in range(2):
-            fine = 1 + 2 * (x - 1) + d
-            LEVEL_2.put(ua2, ga2, fine, [[ua2[fine, 0, 0] + now[0][x, 0, 0]]])
-
-    each(1, 1 + size_3, prolong_3, 4)
-    each(1, 1 + size_2, sweep(LEVEL_2, ua2, ga2, ub2, gb2, b2), 8)
-    each(1, 1 + size_2, sweep(LEVEL_2, ub2, gb2, ua2, ga2, b2), 8)
+            fine = PAD_2 + 2 * x + d
+            LEVEL_2.put(ua2, ga2, fine, [[ua2[fine, 0, 0] + now[0][1 + x, 0, 0]]])
+
+    each(0, size_3, prolong_3, 4)
+    each(*all_2, sweep(LEVEL_2, ua2, ga2, ub2, gb2, b2), 8)
+    each(*all_2, sweep(LEVEL_2, ub2, gb2, ua2, ga2, b2), 8)
+    return ua1, ua2, b1
+
+
+def coarse_finish(count_x, grids):
+    ua1, ub1, ga1, gb1, b1 = grids[0:5]
+    ua2 = grids[5]
+    size_1, size_2 = 4 * count_x, 2 * count_x
 
     def prolong_2(x):
-        error = ua2[x, 0, 0]
+        error = ua2[PAD_2 + x, 0, 0]
         for d in range(2):
-            fine = PAD + 2 * (x - 1) + d
+            fine = PAD + 2 * x + d
             LEVEL_1.put(
                 ua1, ga1, fine, [[t + error for t in line] for line in LEVEL_1.load(ua1, fine)]
             )
 
-    each(1, 1 + size_2, prolong_2, 8)
-    each(PAD, PAD + size_1, sweep(LEVEL_1, ua1, ga1, ub1, gb1, b1), 8)
-    each(PAD, PAD + size_1, sweep(LEVEL_1, ub1, gb1, ua1, ga1, b1), 8)
+    def sweep(u_in, g_in, u_out, g_out):
+        return lambda x: LEVEL_1.put(
+            u_out, g_out, x, LEVEL_1.sweep(u_in, g_in, b1, x, 1.0 / 30.0)
+        )
+
+    each(0, size_2, prolong_2, 8)
+    each(PAD, PAD + size_1, sweep(ua1, ga1, ub1, gb1), 8)
+    each(PAD, PAD + size_1, sweep(ub1, gb1, ua1, ga1), 8)
     return ua1
+
+
+def turned_tile(tile, at_z, rows):
+    count = tile.shape[0]
+    turned = pltpu.roll(tile, lax.rem(count - 4 * at_z, count), 0)
+    return jnp.where(row_of((8, LANES)) < 6, turned[0:8], turned[count - 8 : count]) * rows
+
+
+def near_finish(coarse, where_ref, masks, near):
+    ua1, ua2, b1 = coarse
+    ua, ga, ub, gb, b = near
+    at_x, at_z = where_ref[0], where_ref[1]
+    rows = masks[0]
+
+    def take(i):
+        error = ua2[2 * at_x + i // 2, 0, 0]
+        plane = [[t + error for t in line] for line in LEVEL_1.load(ua1, 4 * at_x + i)]
+        plane = [[turned_tile(t, at_z, rows) for t in line] for line in plane]
+        NEAR_1.put(ua, ga, i, plane)
+        plane = LEVEL_1.load(b1, 4 * at_x + i)
+        store_plane(b, i, [[turned_tile(t, at_z, rows) for t in line] for line in plane])
+
+    each(1, 11, take, 5)
+
+    def sweep(u_in, g_in, u_out, g_out):
+        def body(i, weight):
+            NEAR_1.put(u_out, g_out, i, NEAR_1.sweep(u_in, g_in, b, i, weight))
+
+        return body
+
+    in_segments(2, 10, sweep(ua, ga, ub, gb), masks, 1.0 / 30.0, 4, PAD, BRICK_X // 2)
+    in_segments(3, 9, sweep(ub, gb, ua, ga), masks, 1.0 / 30.0, 4, PAD, BRICK_X // 2)
+    return ua
 
 
 def rim_masks(count_x, count_z, where_ref):
@@ -299,13 +347,13 @@
     return rows, below, above
 
 
-def in_segments(lo, hi, body, masks, scale, chunk):
+def in_segments(lo, hi, body, masks, scale, chunk, rim=RIM, brick=BRICK_X):
     rows, below, above = masks
     inner = rows * scale
     for start, end, weight in (
-        (lo, min(hi, RIM), inner * below),
-        (max(lo, RIM), min(hi, RIM + BRICK_X), inner),
-        (max(lo, RIM + BRICK_X), hi, inner * above),
+        (lo, min(hi, rim), inner * below),
+        (max(lo, rim), min(hi, rim + brick), inner),
+        (max(lo, rim + brick), hi, inner * above),
     ):
         if end > start:
             each(start, end, functools.partial(body, weight=weight), chunk)
@@ -318,22 +366,9 @@
     in_segments(margin, WIDE_X - margin, body, masks, 1.0 / 30.0, 4)
 
 
-def add_correction(coarse_ref, count_z, where_ref, masks, u_in, u_out, g_out, margin):
-    at_x, at_z = where_ref[0], where_ref[1]
-    rows_1 = coarse_ref.shape[3]
-    turn = lax.rem(rows_1 - 4 * at_z, rows_1)
-    k = row_of((8, LANES))
-    rows = masks[0]
-
+def add_correction(error_of, u_in, u_out, g_out, margin):
     def body(i):
-        error = []
-        for q in range(2):
-            line = []
-            for p in range(2):
-                turned = pltpu.roll(coarse_ref[4 * at_x + i, q, p], turn, 0)
-                tile = jnp.where(k < 6, turned[0:8], turned[rows_1 - 8 : rows_1])
-                line.append(tile * rows)
-            error.append(line)
+        error = error_of(i)
         for d in range(2):
             x = 2 * i + d
             plane = [
@@ -341,7 +376,7 @@
             ]
             FINE.put(u_out, g_out, x, plane)
 
-    each(margin // 2, (WIDE_X - margin) // 2, body, 3)
+    each(margin // 2, (WIDE_X - margin) // 2, body, 2)
 
 
 def send_residual(u_ref, g_ref, b_ref, out_ref):
@@ -356,43 +391,30 @@
     each(0, BRICK_X // 2, body, BRICK_X // 2)
 
 
-def swap_blocks(tiles):
-    shape = tiles[0].shape
-    lane = lane_of(shape)
-    half = lane < 64
-    even = (lane // 32) % 2 == 0
-    a, b, c, d = tiles
-    a, c = jnp.where(half, a, pltpu.roll(c, 64, 1)), jnp.where(half, pltpu.roll(a, 64, 1), c)
-    b, d = jnp.where(half, b, pltpu.roll(d, 64, 1)), jnp.where(half, pltpu.roll(b, 64, 1), d)
-    a, b = jnp.where(even, a, pltpu.roll(b, 32, 1)), jnp.where(even, pltpu.roll(a, 96, 1), b)
-    c, d = jnp.where(even, c, pltpu.roll(d, 32, 1)), jnp.where(even, pltpu.roll(c, 96, 1), d)
-    return [a, b, c, d]
-
-
-def pick_lanes(tile, index):
-    return jnp.take_along_axis(tile, index, axis=1, mode="promise_in_bounds")
+def permuted(values, places):
+    shape = (values.shape[1], values.shape[1])
+    row, column = (lax.broadcasted_iota(jnp.int32, shape, d) for d in range(2))
+    matrix = places(row, column).astype(jnp.float32).astype(jnp.bfloat16)
+    total, rest = None, values
+    terms = []
+    for _ in range(3):
+        term = rest.astype(jnp.bfloat16)
+        rest = rest - term.astype(jnp.float32)
+        terms.append(jnp.dot(term, matrix, preferred_element_type=jnp.float32))
+    return terms[0] + (terms[1] + terms[2])
 
 
 def lanes_kernel(where_ref, charges_ref, rows_ref, one_ref, two_ref):
-    lane = lane_of((8, LANES))
-    index = (lane % 32) * 4 + lane // 32
     odd = where_ref[1] % 2
-
-    def body(x):
-        for part in range(2):
-            rows = slice(8 * part, 8 * part + 8)
-            tiles = [
-                pick_lanes(charges_ref[x, rows, t * LANES : (t + 1) * LANES], index)
-                for t in range(4)
-            ]
-            for p, tile in enumerate(swap_blocks(tiles)):
-                rows_ref[x, p, rows] = tile
-        for p in range(4):
-            first, last = rows_ref[x, p, 0:8], rows_ref[x, p, 8:16]
-            one_ref[x, p] = jnp.where(odd == 0, last, first)
-            two_ref[x, p] = jnp.where(odd == 0, first, last)
-
-    each(0, BRICK_X, body, 2)
+    width = charges_ref.shape[2]
+    flat = charges_ref[...].reshape(BRICK_X * BRICK_Z, width)
+    split = permuted(flat, lambda y, l: y == (l % LANES) * 4 + l // LANES)
+    for p in range(4):
+        tile = split[:, p * LANES : (p + 1) * LANES].reshape(BRICK_X, BRICK_Z, LANES)
+        rows_ref[:, p] = tile
+        first, last = tile[:, 0:8], tile[:, 8:16]
+        one_ref[:, p] = jnp.where(odd == 0, last, first)
+        two_ref[:, p] = jnp.where(odd == 0, first, last)
 
 
 def down_kernel(count_x, count_z, where_ref, mid_ref, mid_rim_ref, one_ref, one_rim_ref, two_ref,
@@ -440,40 +462,44 @@
     pieces, refs = refs[:count_pieces], refs[count_pieces:]
     u_ref, b_ref, v_ref, out_ref, ga_ref, gb_ref, ua_ref, *grids = refs
     masks = rim_masks(count_x, count_z, where_ref)
-    coarse = coarse_solve(count_x, count_z, where_ref, pieces, grids)
-    add_correction(coarse, count_z, where_ref, masks, u_ref, ua_ref, ga_ref, 2)
-    fine_sweep(ua_ref, ga_ref, v_ref, gb_ref, b_ref, 3, masks)
-    fine_sweep(v_ref, gb_ref, ua_ref, ga_ref, b_ref, 4, masks)
-    fine_sweep(ua_ref, ga_ref, v_ref, gb_ref, b_ref, 5, masks)
-    fine_sweep(v_ref, gb_ref, ua_ref, ga_ref, b_ref, 6, masks)
-
-    def keep(x):
-        store_plane(v_ref, x, FINE.load(ua_ref, x))
-
-    each(6, WIDE_X - 6, keep, 2)
-    send_residual(ua_ref, ga_ref, b_ref, out_ref)
+    coarse_solve(count_x, count_z, where_ref, pieces, grids)
+    coarse_ref = coarse_finish(count_x, grids)
+    at_x, at_z = where_ref[0], where_ref[1]
+
+    def error_of(i):
+        plane = LEVEL_1.load(coarse_ref, 4 * at_x + i)
+        return [[turned_tile(t, at_z, masks[0]) for t in line] for line in plane]
+
+    add_correction(error_of, u_ref, v_ref, ga_ref, 2)
+    fine_sweep(v_ref, ga_ref, ua_ref, gb_ref, b_ref, 3, masks)
+    fine_sweep(ua_ref, gb_ref, v_ref, ga_ref, b_ref, 4, masks)
+    fine_sweep(v_ref, ga_ref, ua_ref, gb_ref, b_ref, 5, masks)
+    fine_sweep(ua_ref, gb_ref, v_ref, ga_ref, b_ref, 6, masks)
+    send_residual(v_ref, ga_ref, b_ref, out_ref)
 
 
 def up_kernel(count_x, count_z, count_pieces, where_ref, *refs):
     pieces, refs = refs[:count_pieces], refs[count_pieces:]
-    u_ref, b_ref, out_ref, ga_ref, gb_ref, ua_ref, ub_ref, rows_ref, *grids = refs
+    u_ref, b_ref, out_ref, ga_ref, gb_ref, ua_ref, ub_ref, rows_ref, *refs = refs
+    near, grids = refs[:5], refs[5:]
     masks = rim_masks(count_x, count_z, where_ref)
     coarse = coarse_solve(count_x, count_z, where_ref, pieces, grids)
-    add_correction(coarse, count_z, where_ref, masks, u_ref, ua_ref, ga_ref, 6)
+    error_ref = near_finish(coarse, where_ref, masks, near)
+    add_correction(lambda i: NEAR_1.load(error_ref, i), u_ref, ua_ref, ga_ref, 6)
     fine_sweep(ua_ref, ga_ref, ub_ref, gb_ref, b_ref, 7, masks)
-    lane = lane_of((8, LANES))
-    index = (lane % 4) * 32 + lane // 4
 
     def body(x):
         plane = FINE.sweep(ub_ref, gb_ref, b_ref, x, 1.0 / 30.0)
         for q in range(4):
-            for t, tile in enumerate(swap_blocks(plane[q])):
-                rows = pick_lanes(tile, index)[0:4]
-                rows_ref[x - RIM, t, pl.ds(q, 4, stride=4), :] = rows
-        for t in range(4):
-            out_ref[x - RIM, :, t * LANES : (t + 1) * LANES] = rows_ref[x - RIM, t]
-
-    each(RIM, RIM + BRICK_X, body, 4)
+            for p in range(4):
+                rows_ref[x - RIM, p, pl.ds(q, 4, stride=4), :] = plane[q][p][0:4]
+
+    each(RIM, RIM + BRICK_X, body, 2)
+    tiles = [rows_ref[:, p].reshape(BRICK_X * BRICK_Z, LANES) for p in range(4)]
+    whole = permuted(
+        jnp.concatenate(tiles, axis=1), lambda l, y: y == (l % LANES) * 4 + l // LANES
+    )
+    out_ref[...] = whole.reshape(out_ref.shape)
 
 
 def call(kernel, outputs, scratch):
@@ -507,10 +533,9 @@
 
 def every_piece(piece):
     held = piece[None]
-    distance = 1
-    while distance < lax.axis_size("gz"):
-        held = jnp.concatenate([held, swap("gz", held, distance)])
-        distance *= 2
+    held = jnp.concatenate(
+        [held] + [swap("gz", held, distance) for distance in range(1, lax.axis_size("gz"))]
+    )
     distance = 2
     while distance < lax.axis_size("gx"):
         held = jnp.concatenate([held, swap("gx", held, distance)])
@@ -538,6 +563,7 @@
     fine = pltpu.VMEM(wide, jnp.float32)
     grids = coarse_grids(count_x, count_z)
     rows_in = pltpu.VMEM((BRICK_X, 4, WIDE_Z, LANES), jnp.float32)
+    close = pltpu.VMEM((WIDE_X // 2, 2, 2, 8, LANES), jnp.float32)
     rows_out = pltpu.VMEM((BRICK_X, 4, BRICK_Z, LANES), jnp.float32)
 
     u, b, piece = call(
@@ -555,7 +581,7 @@
     (potential,) = call(
         functools.partial(up_kernel, count_x, count_z, len(pieces)),
         [charges.shape],
-        [fine] * 4 + [rows_out] + grids,
+        [fine] * 4 + [rows_out] + [close] * 5 + grids,
     )(where, *pieces, u, b)
     return potential
 

time: 66.4 us -> 60.7 us (0.914)
  waiting for transfers between devices: 20.3 us -> 16.7 us
  Pallas kernels: 16.3 us -> 14.6 us
    ppermute x11 -> x13, waiting for transfers between devices: 20.3 us -> 16.7 us  [swap(): return lax.ppermute(values, axis, [(i, i ^ distance) for i in range(count)])]
    pallas_call x4, Pallas kernels: 16.3 us -> 14.6 us  [run(): pl.pallas_call(kernel, out_shape=shapes, in_specs=[pl.BlockSpec(memory_sp...]
    ppermute x11 -> x13, starting transfers between devices: 26.4 us -> 25.9 us  [swap(): return lax.ppermute(values, axis, [(i, i ^ distance) for i in range(count)])]
  transfers between devices with their start and end apart: 14 -> 16, of which waited for: 9 -> 9; matrix products, arithmetic and copies ran while one was open for 0% -> 0% of each run, Pallas kernels for 0% -> 0%
where the time goes in v5:
time: 60.7 us; the launch traced here: 60.5 us
  starting transfers between devices  27.9 us (46%)
  waiting for transfers between devices  16.7 us (28%)
  Pallas kernels  14.6 us (24%)
  local copies, waits for them, and re-layouts  1 us (2%)
    ppermute x13, starting transfers between devices, swap(): return lax.ppermute(values, axis, [(i, i ^ distance) for i in range(count)])  25.9 us
    ppermute x13, waiting for transfers between devices, swap(): return lax.ppermute(values, axis, [(i, i ^ distance) for i in range(count)])  16.7 us
    pallas_call x4, Pallas kernels, run(): pl.pallas_call(kernel, out_shape=shapes, in_specs=[pl.BlockSpec(memory_sp...  14.6 us
    ppermute x3, starting transfers between devices, swap_shifted(): lax.ppermute(values, axis, pairs + [(target, source) for source, target i...  2.01 us
  transfers between devices with their start and end apart: 16, of which 9 were waited for; matrix products, arithmetic and copies ran while one was open for 0% of the time, Pallas kernels for 0%

profile of v5, /device:TPU:0, one launch (start us, length us, event | category | flops | bytes accessed | tf_op | source)
XLA Modules:
  0.0 60.5 jit_solution(14199284366681513351)
XLA Ops:
  0.0 0.1 pad_add_fusion.where_ref
  0.1 0.0 copy-start
  0.1 0.9 %copy-done = f32[8,16,512]{2,1,0:T(8,128)S(1)} copy-done((f32[8,16,512]{2,1,0:T(8,128)S(1)}, f32[8,16,512]{2,1,0:T(8,128)}, u32[]{:S(2)}) %copy-start) | copy-done | bytes 262168
  1.0 1.0 %shard_map.17 = (f32[8,4,16,128]{3,2,1,0:T(8,128)S(1)}, f32[8,4,8,128]{3,2,1,0:T(8,128)S(1)}, f32[8,4,8,128]{3,2,1,0:T(8,128)S(1)}) custom-call(s32[2]{0:T(128)S(1)} %pad_add_fusion.where_ref, f32[8,16,512]{2,1,0:T(8,128)S(1)} %copy-done), custom_call_target="tpu_custom_call" | custom-call | tf_op jit(solution)/shard_map/pallas_call | solution.py:511
  2.0 3.1 %collective-permute-start = (f32[8,4,8,128]{3,2,1,0:T(8,128)S(1)}, f32[8,4,8,128]{3,2,1,0:T(8,128)S(1)}, u32[]{:S(2)}, u32[]{:S(2)}) collective-permute-start(f32[8,4,8,128]{3,2,1,0:T(8,128)S(1)} %get-tuple-element.14), channel_id=1, source_target_pairs={{0,1},{1,0},{2,3},{3,2},{4,5},{5,4},{6,7},{7,6},{8,9},{9,8},{10,11... | collective-permute-start | bytes 393224 | tf_op jit(solution)/shard_map/ppermute | solution.py:526
  5.1 0.7 %collective-permute-start.1 = (f32[8,4,8,128]{3,2,1,0:T(8,128)S(1)}, f32[8,4,8,128]{3,2,1,0:T(8,128)S(1)}, u32[]{:S(2)}, u32[]{:S(2)}) collective-permute-start(f32[8,4,8,128]{3,2,1,0:T(8,128)S(1)} %get-tuple-element.15), channel_id=1, source_target_pairs={{1,2},{2,1},{5,6},{6,5},{9,10},{10,9},{13,14},{14,13},{17,18},{18,... | collective-permute-start | bytes 393224 | tf_op jit(solution)/shard_map/ppermute | solution.py:531
  5.8 0.7 %collective-permute-start.4 = (f32[8,4,16,128]{3,2,1,0:T(8,128)S(1)}, f32[8,4,16,128]{3,2,1,0:T(8,128)S(1)}, u32[]{:S(2)}, u32[]{:S(2)}) collective-permute-start(f32[8,4,16,128]{3,2,1,0:T(8,128)S(1)} %get-tuple-element.13.mid_ref), channel_id=1, source_target_pairs={{4,8},{8,4},{5,9},{9,5},{6,10},{10,6},{7,11},{11,7},{20,24},{24,20... | collective-permute-start | bytes 786440 | tf_op jit(solution)/shard_map/ppermute | solution.py:531
  6.5 2.9 %collective-permute-start.2 = (f32[8,4,16,128]{3,2,1,0:T(8,128)S(1)}, f32[8,4,16,128]{3,2,1,0:T(8,128)S(1)}, u32[]{:S(2)}, u32[]{:S(2)}) collective-permute-start(f32[8,4,16,128]{3,2,1,0:T(8,128)S(1)} %get-tuple-element.13.mid_ref), channel_id=1, source_target_pairs={{0,4},{4,0},{8,12},{12,8},{1,5},{5,1},{9,13},{13,9},{2,6},{6,2},{1... | collective-permute-start | bytes 786440 | tf_op jit(solution)/shard_map/ppermute | solution.py:526
  9.4 0.0 collective-permute-done
  9.4 0.0 collective-permute-done.1
  9.4 0.7 %collective-permute-start.5 = (f32[8,4,16,128]{3,2,1,0:T(8,128)S(1)}, f32[8,4,16,128]{3,2,1,0:T(8,128)S(1)}, u32[]{:S(2)}, u32[]{:S(2)}) collective-permute-start(f32[8,4,16,128]{3,2,1,0:T(8,128)S(1)} %pad_maximum_fusion.mid_rim_ref), channel_id=1, source_target_pairs={{4,8},{8,4},{5,9},{9,5},{6,10},{10,6},{7,11},{11,7},{20,24},{24,20... | collective-permute-start | bytes 786440 | tf_op jit(solution)/shard_map/ppermute | solution.py:531
  10.1 2.3 %collective-permute-start.3 = (f32[8,4,16,128]{3,2,1,0:T(8,128)S(1)}, f32[8,4,16,128]{3,2,1,0:T(8,128)S(1)}, u32[]{:S(2)}, u32[]{:S(2)}) collective-permute-start(f32[8,4,16,128]{3,2,1,0:T(8,128)S(1)} %pad_maximum_fusion.mid_rim_ref), channel_id=1, source_target_pairs={{0,4},{4,0},{8,12},{12,8},{1,5},{5,1},{9,13},{13,9},{2,6},{6,2},{1... | collective-permute-start | bytes 786440 | tf_op jit(solution)/shard_map/ppermute | solution.py:526
  12.4 0.0 collective-permute-done.4.two_ref
  12.4 0.0 collective-permute-done.2.one_ref
  12.4 0.0 collective-permute-done.5.two_rim_ref
  12.5 1.1 %collective-permute-done.3.one_rim_ref = f32[8,4,16,128]{3,2,1,0:T(8,128)S(1)} collective-permute-done((f32[8,4,16,128]{3,2,1,0:T(8,128)S(1)}, f32[8,4,16,128]{3,2,1,0:T(8,128)S(1)}, u32[]{:S(2)}, u32[]{:S(2)}) %collective-permute-start.3) | collective-permute-done | bytes 262176 | tf_op jit(solution)/shard_map/ppermute | solution.py:526
  13.6 2.5 %shard_map.18 = (f32[24,4,4,8,128]{4,3,2,1,0:T(8,128)S(1)}, f32[24,4,4,8,128]{4,3,2,1,0:T(8,128)S(1)}, f32[4,2,8,128]{3,2,1,0:T(8,128)S(1)}) custom-call(s32[2]{0:T(128)S(1)} %pad_add_fusion.where_ref, f32[8,4,16,128]{3,2,1,0:T(8,128)S(1)} %get-tuple-element.13.mid_ref, f32[8,4,16,128]{3,2,1,0:T(8,128)S(1)} %pad_maximum_fusion.mid_rim_ref, ...), custom_call_target="tpu_custom_call" | custom-call | tf_op jit(solution)/shard_map/pallas_call | solution.py:511
  16.1 3.7 %collective-permute-start.8 = (f32[1,4,2,8,128]{4,3,2,1,0:T(8,128)S(1)}, f32[1,4,2,8,128]{4,3,2,1,0:T(8,128)S(1)}, u32[]{:S(2)}, u32[]{:S(2)}) collective-permute-start(f32[1,4,2,8,128]{4,3,2,1,0:T(8,128)S(1)} %bitcast.6), channel_id=1, source_target_pairs={{0,3},{1,2},{2,1},{3,0},{4,7},{5,6},{6,5},{7,4},{8,11},{9,10},{10,... | collective-permute-start | bytes 98312 | tf_op jit(solution)/shard_map/ppermute | solution.py:526
  19.8 2.5 %collective-permute-start.7 = (f32[1,4,2,8,128]{4,3,2,1,0:T(8,128)S(1)}, f32[1,4,2,8,128]{4,3,2,1,0:T(8,128)S(1)}, u32[]{:S(2)}, u32[]{:S(2)}) collective-permute-start(f32[1,4,2,8,128]{4,3,2,1,0:T(8,128)S(1)} %bitcast.7), channel_id=1, source_target_pairs={{0,2},{1,3},{2,0},{3,1},{4,6},{5,7},{6,4},{7,5},{8,10},{9,11},{10,... | collective-permute-start | bytes 98312 | tf_op jit(solution)/shard_map/ppermute | solution.py:526
  22.3 0.3 collective-permute-start.6
  22.6 0.0 collective-permute-done.8
  22.6 2.3 %collective-permute-done.7 = f32[1,4,2,8,128]{4,3,2,1,0:T(8,128)S(1)} collective-permute-done((f32[1,4,2,8,128]{4,3,2,1,0:T(8,128)S(1)}, f32[1,4,2,8,128]{4,3,2,1,0:T(8,128)S(1)}, u32[]{:S(2)}, u32[]{:S(2)}) %collective-permute-start.7) | collective-permute-done | bytes 32800 | tf_op jit(solution)/shard_map/ppermute | solution.py:526
  24.9 1.3 %collective-permute-done.6 = f32[1,4,2,8,128]{4,3,2,1,0:T(8,128)S(1)} collective-permute-done((f32[1,4,2,8,128]{4,3,2,1,0:T(8,128)S(1)}, f32[1,4,2,8,128]{4,3,2,1,0:T(8,128)S(1)}, u32[]{:S(2)}, u32[]{:S(2)}) %collective-permute-start.6) | collective-permute-done | bytes 32800 | tf_op jit(solution)/shard_map/ppermute | solution.py:526
  26.2 4.5 %collective-permute-start.9 = (f32[4,4,2,8,128]{4,3,2,1,0:T(8,128)S(1)}, f32[4,4,2,8,128]{4,3,2,1,0:T(8,128)S(1)}, u32[]{:S(2)}, u32[]{:S(2)}) collective-permute-start(f32[4,4,2,8,128]{4,3,2,1,0:T(8,128)S(1)} %pad_maximum_fusion.1), channel_id=1, source_target_pairs={{0,8},{4,12},{8,0},{12,4},{1,9},{5,13},{9,1},{13,5},{2,10},{6,14},... | collective-permute-start | bytes 393224 | tf_op jit(solution)/shard_map/ppermute | solution.py:526
  30.7 2.9 %collective-permute-done.9 = f32[4,4,2,8,128]{4,3,2,1,0:T(8,128)S(1)} collective-permute-done((f32[4,4,2,8,128]{4,3,2,1,0:T(8,128)S(1)}, f32[4,4,2,8,128]{4,3,2,1,0:T(8,128)S(1)}, u32[]{:S(2)}, u32[]{:S(2)}) %collective-permute-start.9) | collective-permute-done | bytes 131104 | tf_op jit(solution)/shard_map/ppermute | solution.py:526
  33.7 0.1 collective-permute-start.10
  33.7 1.5 %collective-permute-done.10.refs_1_ = f32[8,4,2,8,128]{4,3,2,1,0:T(8,128)S(1)} collective-permute-done((f32[8,4,2,8,128]{4,3,2,1,0:T(8,128)S(1)}, f32[8,4,2,8,128]{4,3,2,1,0:T(8,128)S(1)}, u32[]{:S(2)}, u32[]{:S(2)}) %collective-permute-start.10) | collective-permute-done | bytes 262176 | tf_op jit(solution)/shard_map/ppermute | solution.py:526
  35.3 6.1 %shard_map.19 = (f32[24,4,4,8,128]{4,3,2,1,0:T(8,128)S(1)}, f32[4,2,8,128]{3,2,1,0:T(8,128)S(1)}) custom-call(s32[2]{0:T(128)S(1)} %pad_add_fusion.where_ref, f32[8,4,2,8,128]{4,3,2,1,0:T(8,128)S(1)} %constant_dynamic-update-slice_fusion.refs_0_, f32[8,4,2,8,128]{4,3,2,1,0:T(8,128)S(1)} %collective-permute-done.10.refs_1_, ...), custom_call_target="tpu_custom_call" | custom-call | tf_op jit(solution)/shard_map/pallas_call | solution.py:511
  41.4 2.7 %collective-permute-start.13 = (f32[1,4,2,8,128]{4,3,2,1,0:T(8,128)S(1)}, f32[1,4,2,8,128]{4,3,2,1,0:T(8,128)S(1)}, u32[]{:S(2)}, u32[]{:S(2)}) collective-permute-start(f32[1,4,2,8,128]{4,3,2,1,0:T(8,128)S(1)} %bitcast.10), channel_id=1, source_target_pairs={{0,3},{1,2},{2,1},{3,0},{4,7},{5,6},{6,5},{7,4},{8,11},{9,10},{10,... | collective-permute-start | bytes 98312 | tf_op jit(solution)/shard_map/ppermute | solution.py:526
  44.1 0.0 collective-permute-start.12
  44.1 1.7 %collective-permute-start.11 = (f32[1,4,2,8,128]{4,3,2,1,0:T(8,128)S(1)}, f32[1,4,2,8,128]{4,3,2,1,0:T(8,128)S(1)}, u32[]{:S(2)}, u32[]{:S(2)}) collective-permute-start(f32[1,4,2,8,128]{4,3,2,1,0:T(8,128)S(1)} %bitcast.12), channel_id=1, source_target_pairs={{0,1},{1,0},{2,3},{3,2},{4,5},{5,4},{6,7},{7,6},{8,9},{9,8},{10,11... | collective-permute-start | bytes 98312 | tf_op jit(solution)/shard_map/ppermute | solution.py:526
  45.9 1.4 %collective-permute-done.13 = f32[1,4,2,8,128]{4,3,2,1,0:T(8,128)S(1)} collective-permute-done((f32[1,4,2,8,128]{4,3,2,1,0:T(8,128)S(1)}, f32[1,4,2,8,128]{4,3,2,1,0:T(8,128)S(1)}, u32[]{:S(2)}, u32[]{:S(2)}) %collective-permute-start.13) | collective-permute-done | bytes 32800 | tf_op jit(solution)/shard_map/ppermute | solution.py:526
  47.3 1.7 %collective-permute-done.12 = f32[1,4,2,8,128]{4,3,2,1,0:T(8,128)S(1)} collective-permute-done((f32[1,4,2,8,128]{4,3,2,1,0:T(8,128)S(1)}, f32[1,4,2,8,128]{4,3,2,1,0:T(8,128)S(1)}, u32[]{:S(2)}, u32[]{:S(2)}) %collective-permute-start.12) | collective-permute-done | bytes 32800 | tf_op jit(solution)/shard_map/ppermute | solution.py:526
  48.9 0.0 collective-permute-done.11
  48.9 2.1 %collective-permute-start.14 = (f32[4,4,2,8,128]{4,3,2,1,0:T(8,128)S(1)}, f32[4,4,2,8,128]{4,3,2,1,0:T(8,128)S(1)}, u32[]{:S(2)}, u32[]{:S(2)}) collective-permute-start(f32[4,4,2,8,128]{4,3,2,1,0:T(8,128)S(1)} %pad_maximum_fusion.2), channel_id=1, source_target_pairs={{0,8},{4,12},{8,0},{12,4},{1,9},{5,13},{9,1},{13,5},{2,10},{6,14},... | collective-permute-start | bytes 393224 | tf_op jit(solution)/shard_map/ppermute | solution.py:526
  51.1 2.9 %collective-permute-done.14 = f32[4,4,2,8,128]{4,3,2,1,0:T(8,128)S(1)} collective-permute-done((f32[4,4,2,8,128]{4,3,2,1,0:T(8,128)S(1)}, f32[4,4,2,8,128]{4,3,2,1,0:T(8,128)S(1)}, u32[]{:S(2)}, u32[]{:S(2)}) %collective-permute-start.14) | collective-permute-done | bytes 131104 | tf_op jit(solution)/shard_map/ppermute | solution.py:526
  54.0 0.1 collective-permute-start.15
  54.1 1.5 %collective-permute-done.15.refs_1_ = f32[8,4,2,8,128]{4,3,2,1,0:T(8,128)S(1)} collective-permute-done((f32[8,4,2,8,128]{4,3,2,1,0:T(8,128)S(1)}, f32[8,4,2,8,128]{4,3,2,1,0:T(8,128)S(1)}, u32[]{:S(2)}, u32[]{:S(2)}) %collective-permute-start.15) | collective-permute-done | bytes 262176 | tf_op jit(solution)/shard_map/ppermute | solution.py:526
  55.6 5.0 %shard_map.20 = f32[8,16,512]{2,1,0:T(8,128)} custom-call(s32[2]{0:T(128)S(1)} %pad_add_fusion.where_ref, f32[8,4,2,8,128]{4,3,2,1,0:T(8,128)S(1)} %constant_dynamic-update-slice_fusion.5.refs_0_, f32[8,4,2,8,128]{4,3,2,1,0:T(8,128)S(1)} %collective-permute-done.15.refs_1_, f32[24,4,4,8,128]{4,3,2,1,0:T(8,128)S(1)} %get-tuple-element.20.refs_2_, ...), custom_call_target="tpu_custom_call" | custom-call | tf_op jit(solution)/shard_map/pallas_call | solution.py:511
  (14 shorter events, 0.1 us)
Async XLA Ops:
  0.1 0.9 %copy-start = (f32[8,16,512]{2,1,0:T(8,128)S(1)}, f32[8,16,512]{2,1,0:T(8,128)}, u32[]{:S(2)}) copy-start(f32[8,16,512]{2,1,0:T(8,128)} %charges_ref.1) | copy-start | bytes 786436
  2.0 7.4 %collective-permute-start = (f32[8,4,8,128]{3,2,1,0:T(8,128)S(1)}, f32[8,4,8,128]{3,2,1,0:T(8,128)S(1)}, u32[]{:S(2)}, u32[]{:S(2)}) collective-permute-start(f32[8,4,8,128]{3,2,1,0:T(8,128)S(1)} %get-tuple-element.14), channel_id=1, source_target_pairs={{0,1},{1,0},{2,3},{3,2},{4,5},{5,4},{6,7},{7,6},{8,9},{9,8},{10,11... | collective-permute-start | bytes 393224 | tf_op jit(solution)/shard_map/ppermute | solution.py:526
  5.1 4.3 %collective-permute-start.1 = (f32[8,4,8,128]{3,2,1,0:T(8,128)S(1)}, f32[8,4,8,128]{3,2,1,0:T(8,128)S(1)}, u32[]{:S(2)}, u32[]{:S(2)}) collective-permute-start(f32[8,4,8,128]{3,2,1,0:T(8,128)S(1)} %get-tuple-element.15), channel_id=1, source_target_pairs={{1,2},{2,1},{5,6},{6,5},{9,10},{10,9},{13,14},{14,13},{17,18},{18,... | collective-permute-start | bytes 393224 | tf_op jit(solution)/shard_map/ppermute | solution.py:531
  5.8 6.7 %collective-permute-start.4 = (f32[8,4,16,128]{3,2,1,0:T(8,128)S(1)}, f32[8,4,16,128]{3,2,1,0:T(8,128)S(1)}, u32[]{:S(2)}, u32[]{:S(2)}) collective-permute-start(f32[8,4,16,128]{3,2,1,0:T(8,128)S(1)} %get-tuple-element.13.mid_ref), channel_id=1, source_target_pairs={{4,8},{8,4},{5,9},{9,5},{6,10},{10,6},{7,11},{11,7},{20,24},{24,20... | collective-permute-start | bytes 786440 | tf_op jit(solution)/shard_map/ppermute | solution.py:531
  6.5 6.0 %collective-permute-start.2 = (f32[8,4,16,128]{3,2,1,0:T(8,128)S(1)}, f32[8,4,16,128]{3,2,1,0:T(8,128)S(1)}, u32[]{:S(2)}, u32[]{:S(2)}) collective-permute-start(f32[8,4,16,128]{3,2,1,0:T(8,128)S(1)} %get-tuple-element.13.mid_ref), channel_id=1, source_target_pairs={{0,4},{4,0},{8,12},{12,8},{1,5},{5,1},{9,13},{13,9},{2,6},{6,2},{1... | collective-permute-start | bytes 786440 | tf_op jit(solution)/shard_map/ppermute | solution.py:526
  9.4 3.0 %collective-permute-start.5 = (f32[8,4,16,128]{3,2,1,0:T(8,128)S(1)}, f32[8,4,16,128]{3,2,1,0:T(8,128)S(1)}, u32[]{:S(2)}, u32[]{:S(2)}) collective-permute-start(f32[8,4,16,128]{3,2,1,0:T(8,128)S(1)} %pad_maximum_fusion.mid_rim_ref), channel_id=1, source_target_pairs={{4,8},{8,4},{5,9},{9,5},{6,10},{10,6},{7,11},{11,7},{20,24},{24,20... | collective-permute-start | bytes 786440 | tf_op jit(solution)/shard_map/ppermute | solution.py:531
  10.1 3.5 %collective-permute-start.3 = (f32[8,4,16,128]{3,2,1,0:T(8,128)S(1)}, f32[8,4,16,128]{3,2,1,0:T(8,128)S(1)}, u32[]{:S(2)}, u32[]{:S(2)}) collective-permute-start(f32[8,4,16,128]{3,2,1,0:T(8,128)S(1)} %pad_maximum_fusion.mid_rim_ref), channel_id=1, source_target_pairs={{0,4},{4,0},{8,12},{12,8},{1,5},{5,1},{9,13},{13,9},{2,6},{6,2},{1... | collective-permute-start | bytes 786440 | tf_op jit(solution)/shard_map/ppermute | solution.py:526
  16.1 6.4 %collective-permute-start.8 = (f32[1,4,2,8,128]{4,3,2,1,0:T(8,128)S(1)}, f32[1,4,2,8,128]{4,3,2,1,0:T(8,128)S(1)}, u32[]{:S(2)}, u32[]{:S(2)}) collective-permute-start(f32[1,4,2,8,128]{4,3,2,1,0:T(8,128)S(1)} %bitcast.6), channel_id=1, source_target_pairs={{0,3},{1,2},{2,1},{3,0},{4,7},{5,6},{6,5},{7,4},{8,11},{9,10},{10,... | collective-permute-start | bytes 98312 | tf_op jit(solution)/shard_map/ppermute | solution.py:526
  19.8 5.1 %collective-permute-start.7 = (f32[1,4,2,8,128]{4,3,2,1,0:T(8,128)S(1)}, f32[1,4,2,8,128]{4,3,2,1,0:T(8,128)S(1)}, u32[]{:S(2)}, u32[]{:S(2)}) collective-permute-start(f32[1,4,2,8,128]{4,3,2,1,0:T(8,128)S(1)} %bitcast.7), channel_id=1, source_target_pairs={{0,2},{1,3},{2,0},{3,1},{4,6},{5,7},{6,4},{7,5},{8,10},{9,11},{10,... | collective-permute-start | bytes 98312 | tf_op jit(solution)/shard_map/ppermute | solution.py:526
  22.3 3.9 %collective-permute-start.6 = (f32[1,4,2,8,128]{4,3,2,1,0:T(8,128)S(1)}, f32[1,4,2,8,128]{4,3,2,1,0:T(8,128)S(1)}, u32[]{:S(2)}, u32[]{:S(2)}) collective-permute-start(f32[1,4,2,8,128]{4,3,2,1,0:T(8,128)S(1)} %bitcast.8), channel_id=1, source_target_pairs={{0,1},{1,0},{2,3},{3,2},{4,5},{5,4},{6,7},{7,6},{8,9},{9,8},{10,11... | collective-permute-start | bytes 98312 | tf_op jit(solution)/shard_map/ppermute | solution.py:526
  26.2 7.4 %collective-permute-start.9 = (f32[4,4,2,8,128]{4,3,2,1,0:T(8,128)S(1)}, f32[4,4,2,8,128]{4,3,2,1,0:T(8,128)S(1)}, u32[]{:S(2)}, u32[]{:S(2)}) collective-permute-start(f32[4,4,2,8,128]{4,3,2,1,0:T(8,128)S(1)} %pad_maximum_fusion.1), channel_id=1, source_target_pairs={{0,8},{4,12},{8,0},{12,4},{1,9},{5,13},{9,1},{13,5},{2,10},{6,14},... | collective-permute-start | bytes 393224 | tf_op jit(solution)/shard_map/ppermute | solution.py:526
  33.7 1.6 %collective-permute-start.10 = (f32[8,4,2,8,128]{4,3,2,1,0:T(8,128)S(1)}, f32[8,4,2,8,128]{4,3,2,1,0:T(8,128)S(1)}, u32[]{:S(2)}, u32[]{:S(2)}) collective-permute-start(f32[8,4,2,8,128]{4,3,2,1,0:T(8,128)S(1)} %constant_dynamic-update-slice_fusion.refs_0_), channel_id=1, source_target_pairs={{0,4},{4,0},{8,12},{12,8},{1,5},{5,1},{9,13},{13,9},{2,6},{6,2},{1... | collective-permute-start | bytes 786440 | tf_op jit(solution)/shard_map/ppermute | solution.py:526
  41.4 5.9 %collective-permute-start.13 = (f32[1,4,2,8,128]{4,3,2,1,0:T(8,128)S(1)}, f32[1,4,2,8,128]{4,3,2,1,0:T(8,128)S(1)}, u32[]{:S(2)}, u32[]{:S(2)}) collective-permute-start(f32[1,4,2,8,128]{4,3,2,1,0:T(8,128)S(1)} %bitcast.10), channel_id=1, source_target_pairs={{0,3},{1,2},{2,1},{3,0},{4,7},{5,6},{6,5},{7,4},{8,11},{9,10},{10,... | collective-permute-start | bytes 98312 | tf_op jit(solution)/shard_map/ppermute | solution.py:526
  44.1 4.8 %collective-permute-start.12 = (f32[1,4,2,8,128]{4,3,2,1,0:T(8,128)S(1)}, f32[1,4,2,8,128]{4,3,2,1,0:T(8,128)S(1)}, u32[]{:S(2)}, u32[]{:S(2)}) collective-permute-start(f32[1,4,2,8,128]{4,3,2,1,0:T(8,128)S(1)} %bitcast.11), channel_id=1, source_target_pairs={{0,2},{1,3},{2,0},{3,1},{4,6},{5,7},{6,4},{7,5},{8,10},{9,11},{10,... | collective-permute-start | bytes 98312 | tf_op jit(solution)/shard_map/ppermute | solution.py:526
  44.1 4.8 %collective-permute-start.11 = (f32[1,4,2,8,128]{4,3,2,1,0:T(8,128)S(1)}, f32[1,4,2,8,128]{4,3,2,1,0:T(8,128)S(1)}, u32[]{:S(2)}, u32[]{:S(2)}) collective-permute-start(f32[1,4,2,8,128]{4,3,2,1,0:T(8,128)S(1)} %bitcast.12), channel_id=1, source_target_pairs={{0,1},{1,0},{2,3},{3,2},{4,5},{5,4},{6,7},{7,6},{8,9},{9,8},{10,11... | collective-permute-start | bytes 98312 | tf_op jit(solution)/shard_map/ppermute | solution.py:526
  48.9 5.0 %collective-permute-start.14 = (f32[4,4,2,8,128]{4,3,2,1,0:T(8,128)S(1)}, f32[4,4,2,8,128]{4,3,2,1,0:T(8,128)S(1)}, u32[]{:S(2)}, u32[]{:S(2)}) collective-permute-start(f32[4,4,2,8,128]{4,3,2,1,0:T(8,128)S(1)} %pad_maximum_fusion.2), channel_id=1, source_target_pairs={{0,8},{4,12},{8,0},{12,4},{1,9},{5,13},{9,1},{13,5},{2,10},{6,14},... | collective-permute-start | bytes 393224 | tf_op jit(solution)/shard_map/ppermute | solution.py:526
  54.0 1.6 %collective-permute-start.15 = (f32[8,4,2,8,128]{4,3,2,1,0:T(8,128)S(1)}, f32[8,4,2,8,128]{4,3,2,1,0:T(8,128)S(1)}, u32[]{:S(2)}, u32[]{:S(2)}) collective-permute-start(f32[8,4,2,8,128]{4,3,2,1,0:T(8,128)S(1)} %constant_dynamic-update-slice_fusion.5.refs_0_), channel_id=1, source_target_pairs={{0,4},{4,0},{8,12},{12,8},{1,5},{5,1},{9,13},{13,9},{2,6},{6,2},{1... | collective-permute-start | bytes 786440 | tf_op jit(solution)/shard_map/ppermute | solution.py:526

commit v6 on v5

--- a/solution.py
+++ b/solution.py
@@ -231,14 +231,14 @@
         def gather(n):
             for core in range(2):
                 x = PAD + 4 * ((2 * n + core) ^ at_x)
-                place(x, lambda z, i, q: pieces[core][n * count_z + (z ^ at_z), i, q])
+                place(x, lambda z, i, q: pieces[core][n * count_z + (z ^ at_z ^ (count_z - 1)), i, q])
 
         each(0, count_x // 2, gather, 1)
 
     def sweep(level, u_in, g_in, u_out, g_out, b):
         return lambda x: level.put(u_out, g_out, x, level.sweep(u_in, g_in, b, x, third))
 
-    each(PAD, PAD + size_1, sweep(LEVEL_1, ub1, gb1, ua1, ga1, b1), 8)
+    each(PAD, PAD + size_1, sweep(LEVEL_1, ub1, gb1, ua1, ga1, b1), 2)
 
     def restrict_1(x):
         fine = PAD + 2 * x
@@ -249,7 +249,7 @@
         store_plane(b2, PAD_2 + x, plane)
         LEVEL_2.put(ub2, gb2, PAD_2 + x, plane)
 
-    each(0, size_2, restrict_1, 8)
+    each(0, size_2, restrict_1, 1)
     all_2 = (PAD_2, PAD_2 + size_2)
     each(*all_2, sweep(LEVEL_2, ub2, gb2, ua2, ga2, b2), 8)
 
@@ -263,10 +263,18 @@
         LEVEL_3.put(ub3, gb3, 1 + x, plane)
 
     each(0, size_3, restrict_2, 4)
-    now, later = (ub3, gb3), (ua3, ga3)
-    for _ in range(COARSE_SWEEPS - 1):
-        each(1, 1 + size_3, sweep(LEVEL_3, *now, *later, b3), 4)
-        now, later = later, now
+    first, second = (ub3, gb3), (ua3, ga3)
+
+    def two_sweeps(n, carry):
+        each(1, 1 + size_3, sweep(LEVEL_3, *first, *second, b3), 4)
+        each(1, 1 + size_3, sweep(LEVEL_3, *second, *first, b3), 4)
+        return carry
+
+    pairs, rest = divmod(COARSE_SWEEPS - 1, 2)
+    lax.fori_loop(0, pairs, two_sweeps, 0)
+    if rest:
+        each(1, 1 + size_3, sweep(LEVEL_3, *first, *second, b3), 4)
+    now = second if rest else first
 
     def prolong_3(x):
         for d in range(2):
@@ -297,9 +305,9 @@
             u_out, g_out, x, LEVEL_1.sweep(u_in, g_in, b1, x, 1.0 / 30.0)
         )
 
-    each(0, size_2, prolong_2, 8)
-    each(PAD, PAD + size_1, sweep(ua1, ga1, ub1, gb1), 8)
-    each(PAD, PAD + size_1, sweep(ub1, gb1, ua1, ga1), 8)
+    each(0, size_2, prolong_2, 1)
+    each(PAD, PAD + size_1, sweep(ua1, ga1, ub1, gb1), 2)
+    each(PAD, PAD + size_1, sweep(ub1, gb1, ua1, ga1), 2)
     return ua1
 
 
@@ -309,11 +317,11 @@
     return jnp.where(row_of((8, LANES)) < 6, turned[0:8], turned[count - 8 : count]) * rows
 
 
-def near_finish(coarse, where_ref, masks, near):
+def near_finish(coarse, where_ref, masks_ref, near):
     ua1, ua2, b1 = coarse
     ua, ga, ub, gb, b = near
     at_x, at_z = where_ref[0], where_ref[1]
-    rows = masks[0]
+    rows = masks_ref[1]
 
     def take(i):
         error = ua2[2 * at_x + i // 2, 0, 0]
@@ -323,7 +331,7 @@
         plane = LEVEL_1.load(b1, 4 * at_x + i)
         store_plane(b, i, [[turned_tile(t, at_z, rows) for t in line] for line in plane])
 
-    each(1, 11, take, 5)
+    each(1, 11, take, 2)
 
     def sweep(u_in, g_in, u_out, g_out):
         def body(i, weight):
@@ -331,39 +339,46 @@
 
         return body
 
-    in_segments(2, 10, sweep(ua, ga, ub, gb), masks, 1.0 / 30.0, 4, PAD, BRICK_X // 2)
-    in_segments(3, 9, sweep(ub, gb, ua, ga), masks, 1.0 / 30.0, 4, PAD, BRICK_X // 2)
+    each(2, 10, masked(sweep(ua, ga, ub, gb), masks_ref, 1.0 / 30.0, PAD), 2)
+    each(3, 9, masked(sweep(ub, gb, ua, ga), masks_ref, 1.0 / 30.0, PAD), 2)
     return ua
 
 
-def rim_masks(count_x, count_z, where_ref):
+def rim_masks(count_x, count_z, where_ref, masks_ref):
     at_x, at_z = where_ref[0], where_ref[1]
     k = row_of((8, LANES))
     low = (at_z > 0).astype(jnp.float32)
     high = (at_z < count_z - 1).astype(jnp.float32)
     rows = jnp.where(k < 4, 1.0, jnp.where(k < 6, high, low))
-    below = (at_x > 0).astype(jnp.float32)
-    above = (at_x < count_x - 1).astype(jnp.float32)
-    return rows, below, above
-
-
-def in_segments(lo, hi, body, masks, scale, chunk, rim=RIM, brick=BRICK_X):
-    rows, below, above = masks
-    inner = rows * scale
-    for start, end, weight in (
-        (lo, min(hi, rim), inner * below),
-        (max(lo, rim), min(hi, rim + brick), inner),
-        (max(lo, rim + brick), hi, inner * above),
-    ):
-        if end > start:
-            each(start, end, functools.partial(body, weight=weight), chunk)
-
-
-def fine_sweep(u_in, g_in, u_out, g_out, b_ref, margin, masks):
-    def body(x, weight):
-        FINE.put(u_out, g_out, x, FINE.sweep(u_in, g_in, b_ref, x, weight))
-
-    in_segments(margin, WIDE_X - margin, body, masks, 1.0 / 30.0, 4)
+    masks_ref[0] = rows * (at_x > 0).astype(jnp.float32)
+    masks_ref[1] = rows
+    masks_ref[2] = rows * (at_x < count_x - 1).astype(jnp.float32)
+
+
+def masked(body, masks_ref, scale, brick):
+    return lambda x: body(x, masks_ref[lax.div(jnp.int32(x), jnp.int32(brick))] * scale)
+
+
+def fine_sweeps(u_refs, g_refs, b_ref, first, count, masks_ref):
+    def sweep(n, carry):
+        now, later = n % 2, (n + 1) % 2
+        u_in, g_in, u_out, g_out = u_refs.at[now], g_refs.at[now], u_refs.at[later], g_refs.at[later]
+
+        def body(x, weight):
+            FINE.put(u_out, g_out, x, FINE.sweep(u_in, g_in, b_ref, x, weight))
+
+        body = masked(body, masks_ref, 1.0 / 30.0, BRICK_X)
+        margin = first + n
+
+        def step(i, carry):
+            for d in range(2):
+                body(margin + 2 * i + d)
+            return carry
+
+        lax.fori_loop(0, WIDE_X // 2 - margin, step, 0)
+        return carry
+
+    lax.fori_loop(0, count, sweep, 0)
 
 
 def add_correction(error_of, u_in, u_out, g_out, margin):
@@ -376,7 +391,7 @@
             ]
             FINE.put(u_out, g_out, x, plane)
 
-    each(margin // 2, (WIDE_X - margin) // 2, body, 2)
+    each(margin // 2, (WIDE_X - margin) // 2, body, 1)
 
 
 def send_residual(u_ref, g_ref, b_ref, out_ref):
@@ -388,7 +403,7 @@
         for q, (even, odd) in enumerate(join(pair)):
             out_ref[i, q] = 0.1 * jnp.where(row_of(even.shape) < 4, even, pltpu.roll(odd, 4, 0))
 
-    each(0, BRICK_X // 2, body, BRICK_X // 2)
+    each(0, BRICK_X // 2, body, 1)
 
 
 def permuted(values, places):
@@ -418,8 +433,8 @@
 
 
 def down_kernel(count_x, count_z, where_ref, mid_ref, mid_rim_ref, one_ref, one_rim_ref, two_ref,
-                two_rim_ref, u_ref, b_ref, out_ref, c_ref, g_ref, h_ref, rows_ref):
-    masks = rim_masks(count_x, count_z, where_ref)
+                two_rim_ref, u_ref, b_ref, out_ref, c_ref, g_ref, h_ref, rows_ref, masks_ref):
+    rim_masks(count_x, count_z, where_ref, masks_ref)
     odd = where_ref[0] % 2
 
     def split_rows(ref, rim_ref, part):
@@ -430,7 +445,7 @@
                 for q in range(4):
                     c_ref[part * BRICK_X + x, q, p] = rows_ref[x, p, pl.ds(q, 8, stride=4), :]
 
-        each(0, BRICK_X, split, 2)
+        each(0, BRICK_X, split, 1)
 
     split_rows(mid_ref, mid_rim_ref, 1)
     split_rows(one_ref, one_rim_ref, 2 - 2 * odd)
@@ -449,47 +464,49 @@
             plane.append(line)
         FINE.put(b_ref, g_ref, x, plane)
 
-    in_segments(1, WIDE_X - 1, source, masks, 0.2 / 12.0, 4)
+    each(1, WIDE_X - 1, masked(source, masks_ref, 0.2 / 12.0, BRICK_X), 2)
 
     def body(x, weight):
         FINE.put(u_ref, h_ref, x, FINE.sweep(b_ref, g_ref, b_ref, x, weight))
 
-    in_segments(2, WIDE_X - 2, body, masks, 1.0 / 30.0, 4)
+    each(2, WIDE_X - 2, masked(body, masks_ref, 1.0 / 30.0, BRICK_X), 2)
     send_residual(u_ref, h_ref, b_ref, out_ref)
 
 
 def middle_kernel(count_x, count_z, count_pieces, where_ref, *refs):
     pieces, refs = refs[:count_pieces], refs[count_pieces:]
-    u_ref, b_ref, v_ref, out_ref, ga_ref, gb_ref, ua_ref, *grids = refs
-    masks = rim_masks(count_x, count_z, where_ref)
+    u_ref, b_ref, v_ref, out_ref, u_refs, g_refs, masks_ref, *grids = refs
+    rim_masks(count_x, count_z, where_ref, masks_ref)
     coarse_solve(count_x, count_z, where_ref, pieces, grids)
     coarse_ref = coarse_finish(count_x, grids)
     at_x, at_z = where_ref[0], where_ref[1]
 
     def error_of(i):
         plane = LEVEL_1.load(coarse_ref, 4 * at_x + i)
-        return [[turned_tile(t, at_z, masks[0]) for t in line] for line in plane]
-
-    add_correction(error_of, u_ref, v_ref, ga_ref, 2)
-    fine_sweep(v_ref, ga_ref, ua_ref, gb_ref, b_ref, 3, masks)
-    fine_sweep(ua_ref, gb_ref, v_ref, ga_ref, b_ref, 4, masks)
-    fine_sweep(v_ref, ga_ref, ua_ref, gb_ref, b_ref, 5, masks)
-    fine_sweep(ua_ref, gb_ref, v_ref, ga_ref, b_ref, 6, masks)
-    send_residual(v_ref, ga_ref, b_ref, out_ref)
+        return [[turned_tile(t, at_z, masks_ref[1]) for t in line] for line in plane]
+
+    add_correction(error_of, u_ref, u_refs.at[0], g_refs.at[0], 2)
+    fine_sweeps(u_refs, g_refs, b_ref, 3, 4, masks_ref)
+
+    def keep(x):
+        store_plane(v_ref, x, FINE.load(u_refs.at[0], x))
+
+    each(6, WIDE_X - 6, keep, 1)
+    send_residual(u_refs.at[0], g_refs.at[0], b_ref, out_ref)
 
 
 def up_kernel(count_x, count_z, count_pieces, where_ref, *refs):
     pieces, refs = refs[:count_pieces], refs[count_pieces:]
-    u_ref, b_ref, out_ref, ga_ref, gb_ref, ua_ref, ub_ref, rows_ref, *refs = refs
+    u_ref, b_ref, out_ref, u_refs, g_refs, rows_ref, masks_ref, *refs = refs
     near, grids = refs[:5], refs[5:]
-    masks = rim_masks(count_x, count_z, where_ref)
+    rim_masks(count_x, count_z, where_ref, masks_ref)
     coarse = coarse_solve(count_x, count_z, where_ref, pieces, grids)
-    error_ref = near_finish(coarse, where_ref, masks, near)
-    add_correction(lambda i: NEAR_1.load(error_ref, i), u_ref, ua_ref, ga_ref, 6)
-    fine_sweep(ua_ref, ga_ref, ub_ref, gb_ref, b_ref, 7, masks)
+    error_ref = near_finish(coarse, where_ref, masks_ref, near)
+    add_correction(lambda i: NEAR_1.load(error_ref, i), u_ref, u_refs.at[0], g_refs.at[0], 6)
+    fine_sweeps(u_refs, g_refs, b_ref, 7, 1, masks_ref)
 
     def body(x):
-        plane = FINE.sweep(ub_ref, gb_ref, b_ref, x, 1.0 / 30.0)
+        plane = FINE.sweep(u_refs.at[1], g_refs.at[1], b_ref, x, 1.0 / 30.0)
         for q in range(4):
             for p in range(4):
                 rows_ref[x - RIM, p, pl.ds(q, 4, stride=4), :] = plane[q][p][0:4]
@@ -532,12 +549,12 @@
 
 
 def every_piece(piece):
-    held = piece[None]
-    held = jnp.concatenate(
-        [held] + [swap("gz", held, distance) for distance in range(1, lax.axis_size("gz"))]
-    )
-    distance = 2
-    while distance < lax.axis_size("gx"):
+    count_x, count_z = lax.axis_size("gx"), lax.axis_size("gz")
+    line = [swap("gz", piece[None], count_z - 1 - n) for n in range(count_z - 1)] + [piece[None]]
+    halves = [jnp.concatenate(half) for half in (line[: count_z // 2], line[count_z // 2 :])]
+    held = jnp.concatenate(halves + [swap("gx", half, 2) for half in halves])
+    distance = 4
+    while distance < count_x:
         held = jnp.concatenate([held, swap("gx", held, distance)])
         distance *= 2
     return held, swap("gx", held, 1)
@@ -562,6 +579,8 @@
     piece_shape = (BRICK_X // 2, 2, 8, LANES)
     fine = pltpu.VMEM(wide, jnp.float32)
     grids = coarse_grids(count_x, count_z)
+    both = pltpu.VMEM((2,) + wide, jnp.float32)
+    masks = pltpu.VMEM((3, 8, LANES), jnp.float32)
     rows_in = pltpu.VMEM((BRICK_X, 4, WIDE_Z, LANES), jnp.float32)
     close = pltpu.VMEM((WIDE_X // 2, 2, 2, 8, LANES), jnp.float32)
     rows_out = pltpu.VMEM((BRICK_X, 4, BRICK_Z, LANES), jnp.float32)
@@ -569,19 +588,19 @@
     u, b, piece = call(
         functools.partial(down_kernel, count_x, count_z),
         [wide, wide, piece_shape],
-        [fine] * 3 + [rows_in],
+        [fine] * 3 + [rows_in, masks],
     )(where, middle, middle_rim, near, near_rim, far, far_rim)
     pieces = every_piece(piece)
     u, piece = call(
         functools.partial(middle_kernel, count_x, count_z, len(pieces)),
         [wide, piece_shape],
-        [fine] * 3 + grids,
+        [both, both, masks] + grids,
     )(where, *pieces, u, b)
     pieces = every_piece(piece)
     (potential,) = call(
         functools.partial(up_kernel, count_x, count_z, len(pieces)),
         [charges.shape],
-        [fine] * 4 + [rows_out] + [close] * 5 + grids,
+        [both, both, rows_out, masks] + [close] * 5 + grids,
     )(where, *pieces, u, b)
     return potential
 

time: 60.7 us -> 68.4 us (1.13)
  Pallas kernels: 14.6 us -> 22 us
  starting transfers between devices: 27.9 us -> 35.1 us
  waiting for transfers between devices: 16.7 us -> 9.85 us
    pallas_call x4, Pallas kernels: 14.6 us -> 22 us  [run(): pl.pallas_call(kernel, out_shape=shapes, in_specs=[pl.BlockSpec(memory_sp...]
    ppermute x13 -> x15, starting transfers between devices: 25.9 us -> 33.1 us  [swap(): return lax.ppermute(values, axis, [(i, i ^ distance) for i in range(count)])]
    ppermute x13 -> x15, waiting for transfers between devices: 16.7 us -> 9.84 us  [swap(): return lax.ppermute(values, axis, [(i, i ^ distance) for i in range(count)])]
  transfers between devices with their start and end apart: 16 -> 18, of which waited for: 9 -> 6; matrix products, arithmetic and copies ran while one was open for 0% -> 0% of each run, Pallas kernels for 0% -> 0%
where the time goes in v6:
time: 68.4 us; the launch traced here: 68.2 us
  starting transfers between devices  35.1 us (51%)
  Pallas kernels  22 us (32%)
  waiting for transfers between devices  9.85 us (14%)
  local copies, waits for them, and re-layouts  1.01 us (1%)
    ppermute x15, starting transfers between devices, swap(): return lax.ppermute(values, axis, [(i, i ^ distance) for i in range(count)])  33.1 us
    pallas_call x4, Pallas kernels, run(): pl.pallas_call(kernel, out_shape=shapes, in_specs=[pl.BlockSpec(memory_sp...  22 us
    ppermute x15, waiting for transfers between devices, swap(): return lax.ppermute(values, axis, [(i, i ^ distance) for i in range(count)])  9.84 us
    ppermute x3, starting transfers between devices, swap_shifted(): lax.ppermute(values, axis, pairs + [(target, source) for source, target i...  2.01 us
  transfers between devices with their start and end apart: 18, of which 6 were waited for; matrix products, arithmetic and copies ran while one was open for 0% of the time, Pallas kernels for 0%

profile of v6, /device:TPU:0, one launch (start us, length us, event | category | flops | bytes accessed | tf_op | source)
XLA Modules:
  0.0 68.2 jit_solution(16148016489607516420)
XLA Ops:
  0.0 0.1 pad_add_fusion.where_ref
  0.1 0.0 copy-start
  0.1 0.9 %copy-done = f32[8,16,512]{2,1,0:T(8,128)S(1)} copy-done((f32[8,16,512]{2,1,0:T(8,128)S(1)}, f32[8,16,512]{2,1,0:T(8,128)}, u32[]{:S(2)}) %copy-start) | copy-done | bytes 262168
  1.0 1.0 %shard_map.17 = (f32[8,4,16,128]{3,2,1,0:T(8,128)S(1)}, f32[8,4,8,128]{3,2,1,0:T(8,128)S(1)}, f32[8,4,8,128]{3,2,1,0:T(8,128)S(1)}) custom-call(s32[2]{0:T(128)S(1)} %pad_add_fusion.where_ref, f32[8,16,512]{2,1,0:T(8,128)S(1)} %copy-done), custom_call_target="tpu_custom_call" | custom-call | tf_op jit(solution)/shard_map/pallas_call | solution.py:528
  2.0 3.1 %collective-permute-start = (f32[8,4,8,128]{3,2,1,0:T(8,128)S(1)}, f32[8,4,8,128]{3,2,1,0:T(8,128)S(1)}, u32[]{:S(2)}, u32[]{:S(2)}) collective-permute-start(f32[8,4,8,128]{3,2,1,0:T(8,128)S(1)} %get-tuple-element.14), channel_id=1, source_target_pairs={{0,1},{1,0},{2,3},{3,2},{4,5},{5,4},{6,7},{7,6},{8,9},{9,8},{10,11... | collective-permute-start | bytes 393224 | tf_op jit(solution)/shard_map/ppermute | solution.py:543
  5.1 0.7 collective-permute-start.1
  5.8 0.7 collective-permute-start.4
  6.5 2.9 %collective-permute-start.2 = (f32[8,4,16,128]{3,2,1,0:T(8,128)S(1)}, f32[8,4,16,128]{3,2,1,0:T(8,128)S(1)}, u32[]{:S(2)}, u32[]{:S(2)}) collective-permute-start(f32[8,4,16,128]{3,2,1,0:T(8,128)S(1)} %get-tuple-element.13.mid_ref), channel_id=1, source_target_pairs={{0,4},{4,0},{8,12},{12,8},{1,5},{5,1},{9,13},{13,9},{2,6},{6,2},{1... | collective-permute-start | bytes 786440 | tf_op jit(solution)/shard_map/ppermute | solution.py:543
  9.4 0.0 collective-permute-done
  9.4 0.0 collective-permute-done.1
  9.4 0.7 collective-permute-start.5
  10.1 2.3 %collective-permute-start.3 = (f32[8,4,16,128]{3,2,1,0:T(8,128)S(1)}, f32[8,4,16,128]{3,2,1,0:T(8,128)S(1)}, u32[]{:S(2)}, u32[]{:S(2)}) collective-permute-start(f32[8,4,16,128]{3,2,1,0:T(8,128)S(1)} %pad_maximum_fusion.mid_rim_ref), channel_id=1, source_target_pairs={{0,4},{4,0},{8,12},{12,8},{1,5},{5,1},{9,13},{13,9},{2,6},{6,2},{1... | collective-permute-start | bytes 786440 | tf_op jit(solution)/shard_map/ppermute | solution.py:543
  12.4 0.0 collective-permute-done.4.two_ref
  12.4 0.0 collective-permute-done.2.one_ref
  12.4 0.0 collective-permute-done.5.two_rim_ref
  12.5 1.1 %collective-permute-done.3.one_rim_ref = f32[8,4,16,128]{3,2,1,0:T(8,128)S(1)} collective-permute-done((f32[8,4,16,128]{3,2,1,0:T(8,128)S(1)}, f32[8,4,16,128]{3,2,1,0:T(8,128)S(1)}, u32[]{:S(2)}, u32[]{:S(2)}) %collective-permute-start.3) | collective-permute-done | bytes 262176 | tf_op jit(solution)/shard_map/ppermute | solution.py:543
  13.6 3.3 %shard_map.18 = (f32[24,4,4,8,128]{4,3,2,1,0:T(8,128)S(1)}, f32[24,4,4,8,128]{4,3,2,1,0:T(8,128)S(1)}, f32[4,2,8,128]{3,2,1,0:T(8,128)S(1)}) custom-call(s32[2]{0:T(128)S(1)} %pad_add_fusion.where_ref, f32[8,4,16,128]{3,2,1,0:T(8,128)S(1)} %get-tuple-element.13.mid_ref, f32[8,4,16,128]{3,2,1,0:T(8,128)S(1)} %pad_maximum_fusion.mid_rim_ref, ...), custom_call_target="tpu_custom_call" | custom-call | tf_op jit(solution)/shard_map/pallas_call | solution.py:528
  16.9 4.7 %collective-permute-start.8 = (f32[1,4,2,8,128]{4,3,2,1,0:T(8,128)S(1)}, f32[1,4,2,8,128]{4,3,2,1,0:T(8,128)S(1)}, u32[]{:S(2)}, u32[]{:S(2)}) collective-permute-start(f32[1,4,2,8,128]{4,3,2,1,0:T(8,128)S(1)} %bitcast.6), channel_id=1, source_target_pairs={{0,1},{1,0},{2,3},{3,2},{4,5},{5,4},{6,7},{7,6},{8,9},{9,8},{10,11... | collective-permute-start | bytes 98312 | tf_op jit(solution)/shard_map/ppermute | solution.py:543
  21.6 1.3 %collective-permute-start.7 = (f32[1,4,2,8,128]{4,3,2,1,0:T(8,128)S(1)}, f32[1,4,2,8,128]{4,3,2,1,0:T(8,128)S(1)}, u32[]{:S(2)}, u32[]{:S(2)}) collective-permute-start(f32[1,4,2,8,128]{4,3,2,1,0:T(8,128)S(1)} %bitcast.7), channel_id=1, source_target_pairs={{0,2},{1,3},{2,0},{3,1},{4,6},{5,7},{6,4},{7,5},{8,10},{9,11},{10,... | collective-permute-start | bytes 98312 | tf_op jit(solution)/shard_map/ppermute | solution.py:543
  22.8 1.4 %collective-permute-start.6 = (f32[1,4,2,8,128]{4,3,2,1,0:T(8,128)S(1)}, f32[1,4,2,8,128]{4,3,2,1,0:T(8,128)S(1)}, u32[]{:S(2)}, u32[]{:S(2)}) collective-permute-start(f32[1,4,2,8,128]{4,3,2,1,0:T(8,128)S(1)} %bitcast.8), channel_id=1, source_target_pairs={{0,3},{1,2},{2,1},{3,0},{4,7},{5,6},{6,5},{7,4},{8,11},{9,10},{10,... | collective-permute-start | bytes 98312 | tf_op jit(solution)/shard_map/ppermute | solution.py:543
  24.2 0.0 collective-permute-done.8
  24.2 4.5 %collective-permute-start.10 = (f32[2,4,2,8,128]{4,3,2,1,0:T(8,128)S(1)}, f32[2,4,2,8,128]{4,3,2,1,0:T(8,128)S(1)}, u32[]{:S(2)}, u32[]{:S(2)}) collective-permute-start(f32[2,4,2,8,128]{4,3,2,1,0:T(8,128)S(1)} %pad_maximum_fusion.2), channel_id=1, source_target_pairs={{0,8},{4,12},{8,0},{12,4},{1,9},{5,13},{9,1},{13,5},{2,10},{6,14},... | collective-permute-start | bytes 196616 | tf_op jit(solution)/shard_map/ppermute | solution.py:543
  28.7 0.0 collective-permute-done.7
  28.7 0.0 collective-permute-done.6
  28.8 4.2 %collective-permute-start.9 = (f32[2,4,2,8,128]{4,3,2,1,0:T(8,128)S(1)}, f32[2,4,2,8,128]{4,3,2,1,0:T(8,128)S(1)}, u32[]{:S(2)}, u32[]{:S(2)}) collective-permute-start(f32[2,4,2,8,128]{4,3,2,1,0:T(8,128)S(1)} %pad_maximum_fusion.1), channel_id=1, source_target_pairs={{0,8},{4,12},{8,0},{12,4},{1,9},{5,13},{9,1},{13,5},{2,10},{6,14},... | collective-permute-start | bytes 196616 | tf_op jit(solution)/shard_map/ppermute | solution.py:543
  33.0 2.2 %collective-permute-done.9 = f32[2,4,2,8,128]{4,3,2,1,0:T(8,128)S(1)} collective-permute-done((f32[2,4,2,8,128]{4,3,2,1,0:T(8,128)S(1)}, f32[2,4,2,8,128]{4,3,2,1,0:T(8,128)S(1)}, u32[]{:S(2)}, u32[]{:S(2)}) %collective-permute-start.9) | collective-permute-done | bytes 65568 | tf_op jit(solution)/shard_map/ppermute | solution.py:543
  35.2 0.0 collective-permute-done.10
  35.3 0.1 collective-permute-start.11
  35.3 1.5 %collective-permute-done.11.refs_1_ = f32[8,4,2,8,128]{4,3,2,1,0:T(8,128)S(1)} collective-permute-done((f32[8,4,2,8,128]{4,3,2,1,0:T(8,128)S(1)}, f32[8,4,2,8,128]{4,3,2,1,0:T(8,128)S(1)}, u32[]{:S(2)}, u32[]{:S(2)}) %collective-permute-start.11) | collective-permute-done | bytes 262176 | tf_op jit(solution)/shard_map/ppermute | solution.py:543
  36.9 11.3 %shard_map.19 = (f32[24,4,4,8,128]{4,3,2,1,0:T(8,128)S(1)}, f32[4,2,8,128]{3,2,1,0:T(8,128)S(1)}) custom-call(s32[2]{0:T(128)S(1)} %pad_add_fusion.where_ref, f32[8,4,2,8,128]{4,3,2,1,0:T(8,128)S(1)} %constant_dynamic-update-slice_fusion.refs_0_, f32[8,4,2,8,128]{4,3,2,1,0:T(8,128)S(1)} %collective-permute-done.11.refs_1_, ...), custom_call_target="tpu_custom_call" | custom-call | tf_op jit(solution)/shard_map/pallas_call | solution.py:528
  48.2 0.2 collective-permute-start.14
  48.4 1.8 %collective-permute-start.13 = (f32[1,4,2,8,128]{4,3,2,1,0:T(8,128)S(1)}, f32[1,4,2,8,128]{4,3,2,1,0:T(8,128)S(1)}, u32[]{:S(2)}, u32[]{:S(2)}) collective-permute-start(f32[1,4,2,8,128]{4,3,2,1,0:T(8,128)S(1)} %bitcast.11), channel_id=1, source_target_pairs={{0,2},{1,3},{2,0},{3,1},{4,6},{5,7},{6,4},{7,5},{8,10},{9,11},{10,... | collective-permute-start | bytes 98312 | tf_op jit(solution)/shard_map/ppermute | solution.py:543
  50.2 2.4 %collective-permute-start.12 = (f32[1,4,2,8,128]{4,3,2,1,0:T(8,128)S(1)}, f32[1,4,2,8,128]{4,3,2,1,0:T(8,128)S(1)}, u32[]{:S(2)}, u32[]{:S(2)}) collective-permute-start(f32[1,4,2,8,128]{4,3,2,1,0:T(8,128)S(1)} %bitcast.12), channel_id=1, source_target_pairs={{0,3},{1,2},{2,1},{3,0},{4,7},{5,6},{6,5},{7,4},{8,11},{9,10},{10,... | collective-permute-start | bytes 98312 | tf_op jit(solution)/shard_map/ppermute | solution.py:543
  52.6 0.0 collective-permute-done.14
  52.6 2.1 %collective-permute-start.16 = (f32[2,4,2,8,128]{4,3,2,1,0:T(8,128)S(1)}, f32[2,4,2,8,128]{4,3,2,1,0:T(8,128)S(1)}, u32[]{:S(2)}, u32[]{:S(2)}) collective-permute-start(f32[2,4,2,8,128]{4,3,2,1,0:T(8,128)S(1)} %pad_maximum_fusion.4), channel_id=1, source_target_pairs={{0,8},{4,12},{8,0},{12,4},{1,9},{5,13},{9,1},{13,5},{2,10},{6,14},... | collective-permute-start | bytes 196616 | tf_op jit(solution)/shard_map/ppermute | solution.py:543
  54.7 0.0 collective-permute-done.13
  54.7 1.2 %collective-permute-done.12 = f32[1,4,2,8,128]{4,3,2,1,0:T(8,128)S(1)} collective-permute-done((f32[1,4,2,8,128]{4,3,2,1,0:T(8,128)S(1)}, f32[1,4,2,8,128]{4,3,2,1,0:T(8,128)S(1)}, u32[]{:S(2)}, u32[]{:S(2)}) %collective-permute-start.12) | collective-permute-done | bytes 32800 | tf_op jit(solution)/shard_map/ppermute | solution.py:543
  55.9 2.0 %collective-permute-start.15 = (f32[2,4,2,8,128]{4,3,2,1,0:T(8,128)S(1)}, f32[2,4,2,8,128]{4,3,2,1,0:T(8,128)S(1)}, u32[]{:S(2)}, u32[]{:S(2)}) collective-permute-start(f32[2,4,2,8,128]{4,3,2,1,0:T(8,128)S(1)} %pad_maximum_fusion.3), channel_id=1, source_target_pairs={{0,8},{4,12},{8,0},{12,4},{1,9},{5,13},{9,1},{13,5},{2,10},{6,14},... | collective-permute-start | bytes 196616 | tf_op jit(solution)/shard_map/ppermute | solution.py:543
  57.9 2.2 %collective-permute-done.15 = f32[2,4,2,8,128]{4,3,2,1,0:T(8,128)S(1)} collective-permute-done((f32[2,4,2,8,128]{4,3,2,1,0:T(8,128)S(1)}, f32[2,4,2,8,128]{4,3,2,1,0:T(8,128)S(1)}, u32[]{:S(2)}, u32[]{:S(2)}) %collective-permute-start.15) | collective-permute-done | bytes 65568 | tf_op jit(solution)/shard_map/ppermute | solution.py:543
  60.2 0.0 collective-permute-done.16
  60.2 0.1 collective-permute-start.17
  60.3 1.5 %collective-permute-done.17.refs_1_ = f32[8,4,2,8,128]{4,3,2,1,0:T(8,128)S(1)} collective-permute-done((f32[8,4,2,8,128]{4,3,2,1,0:T(8,128)S(1)}, f32[8,4,2,8,128]{4,3,2,1,0:T(8,128)S(1)}, u32[]{:S(2)}, u32[]{:S(2)}) %collective-permute-start.17) | collective-permute-done | bytes 262176 | tf_op jit(solution)/shard_map/ppermute | solution.py:543
  61.8 6.4 %shard_map.20 = f32[8,16,512]{2,1,0:T(8,128)} custom-call(s32[2]{0:T(128)S(1)} %pad_add_fusion.where_ref, f32[8,4,2,8,128]{4,3,2,1,0:T(8,128)S(1)} %constant_dynamic-update-slice_fusion.6.refs_0_, f32[8,4,2,8,128]{4,3,2,1,0:T(8,128)S(1)} %collective-permute-done.17.refs_1_, f32[24,4,4,8,128]{4,3,2,1,0:T(8,128)S(1)} %get-tuple-element.20.refs_2_, ...), custom_call_target="tpu_custom_call" | custom-call | tf_op jit(solution)/shard_map/pallas_call | solution.py:528
  (18 shorter events, 0.1 us)
Async XLA Ops:
  0.1 0.9 %copy-start = (f32[8,16,512]{2,1,0:T(8,128)S(1)}, f32[8,16,512]{2,1,0:T(8,128)}, u32[]{:S(2)}) copy-start(f32[8,16,512]{2,1,0:T(8,128)} %charges_ref.1) | copy-start | bytes 786436
  2.0 7.4 %collective-permute-start = (f32[8,4,8,128]{3,2,1,0:T(8,128)S(1)}, f32[8,4,8,128]{3,2,1,0:T(8,128)S(1)}, u32[]{:S(2)}, u32[]{:S(2)}) collective-permute-start(f32[8,4,8,128]{3,2,1,0:T(8,128)S(1)} %get-tuple-element.14), channel_id=1, source_target_pairs={{0,1},{1,0},{2,3},{3,2},{4,5},{5,4},{6,7},{7,6},{8,9},{9,8},{10,11... | collective-permute-start | bytes 393224 | tf_op jit(solution)/shard_map/ppermute | solution.py:543
  5.1 4.3 %collective-permute-start.1 = (f32[8,4,8,128]{3,2,1,0:T(8,128)S(1)}, f32[8,4,8,128]{3,2,1,0:T(8,128)S(1)}, u32[]{:S(2)}, u32[]{:S(2)}) collective-permute-start(f32[8,4,8,128]{3,2,1,0:T(8,128)S(1)} %get-tuple-element.15), channel_id=1, source_target_pairs={{1,2},{2,1},{5,6},{6,5},{9,10},{10,9},{13,14},{14,13},{17,18},{18,... | collective-permute-start | bytes 393224 | tf_op jit(solution)/shard_map/ppermute | solution.py:548
  5.8 6.7 %collective-permute-start.4 = (f32[8,4,16,128]{3,2,1,0:T(8,128)S(1)}, f32[8,4,16,128]{3,2,1,0:T(8,128)S(1)}, u32[]{:S(2)}, u32[]{:S(2)}) collective-permute-start(f32[8,4,16,128]{3,2,1,0:T(8,128)S(1)} %get-tuple-element.13.mid_ref), channel_id=1, source_target_pairs={{4,8},{8,4},{5,9},{9,5},{6,10},{10,6},{7,11},{11,7},{20,24},{24,20... | collective-permute-start | bytes 786440 | tf_op jit(solution)/shard_map/ppermute | solution.py:548
  6.5 6.0 %collective-permute-start.2 = (f32[8,4,16,128]{3,2,1,0:T(8,128)S(1)}, f32[8,4,16,128]{3,2,1,0:T(8,128)S(1)}, u32[]{:S(2)}, u32[]{:S(2)}) collective-permute-start(f32[8,4,16,128]{3,2,1,0:T(8,128)S(1)} %get-tuple-element.13.mid_ref), channel_id=1, source_target_pairs={{0,4},{4,0},{8,12},{12,8},{1,5},{5,1},{9,13},{13,9},{2,6},{6,2},{1... | collective-permute-start | bytes 786440 | tf_op jit(solution)/shard_map/ppermute | solution.py:543
  9.4 3.0 %collective-permute-start.5 = (f32[8,4,16,128]{3,2,1,0:T(8,128)S(1)}, f32[8,4,16,128]{3,2,1,0:T(8,128)S(1)}, u32[]{:S(2)}, u32[]{:S(2)}) collective-permute-start(f32[8,4,16,128]{3,2,1,0:T(8,128)S(1)} %pad_maximum_fusion.mid_rim_ref), channel_id=1, source_target_pairs={{4,8},{8,4},{5,9},{9,5},{6,10},{10,6},{7,11},{11,7},{20,24},{24,20... | collective-permute-start | bytes 786440 | tf_op jit(solution)/shard_map/ppermute | solution.py:548
  10.1 3.5 %collective-permute-start.3 = (f32[8,4,16,128]{3,2,1,0:T(8,128)S(1)}, f32[8,4,16,128]{3,2,1,0:T(8,128)S(1)}, u32[]{:S(2)}, u32[]{:S(2)}) collective-permute-start(f32[8,4,16,128]{3,2,1,0:T(8,128)S(1)} %pad_maximum_fusion.mid_rim_ref), channel_id=1, source_target_pairs={{0,4},{4,0},{8,12},{12,8},{1,5},{5,1},{9,13},{13,9},{2,6},{6,2},{1... | collective-permute-start | bytes 786440 | tf_op jit(solution)/shard_map/ppermute | solution.py:543
  16.9 7.3 %collective-permute-start.8 = (f32[1,4,2,8,128]{4,3,2,1,0:T(8,128)S(1)}, f32[1,4,2,8,128]{4,3,2,1,0:T(8,128)S(1)}, u32[]{:S(2)}, u32[]{:S(2)}) collective-permute-start(f32[1,4,2,8,128]{4,3,2,1,0:T(8,128)S(1)} %bitcast.6), channel_id=1, source_target_pairs={{0,1},{1,0},{2,3},{3,2},{4,5},{5,4},{6,7},{7,6},{8,9},{9,8},{10,11... | collective-permute-start | bytes 98312 | tf_op jit(solution)/shard_map/ppermute | solution.py:543
  21.6 7.2 %collective-permute-start.7 = (f32[1,4,2,8,128]{4,3,2,1,0:T(8,128)S(1)}, f32[1,4,2,8,128]{4,3,2,1,0:T(8,128)S(1)}, u32[]{:S(2)}, u32[]{:S(2)}) collective-permute-start(f32[1,4,2,8,128]{4,3,2,1,0:T(8,128)S(1)} %bitcast.7), channel_id=1, source_target_pairs={{0,2},{1,3},{2,0},{3,1},{4,6},{5,7},{6,4},{7,5},{8,10},{9,11},{10,... | collective-permute-start | bytes 98312 | tf_op jit(solution)/shard_map/ppermute | solution.py:543
  22.8 5.9 %collective-permute-start.6 = (f32[1,4,2,8,128]{4,3,2,1,0:T(8,128)S(1)}, f32[1,4,2,8,128]{4,3,2,1,0:T(8,128)S(1)}, u32[]{:S(2)}, u32[]{:S(2)}) collective-permute-start(f32[1,4,2,8,128]{4,3,2,1,0:T(8,128)S(1)} %bitcast.8), channel_id=1, source_target_pairs={{0,3},{1,2},{2,1},{3,0},{4,7},{5,6},{6,5},{7,4},{8,11},{9,10},{10,... | collective-permute-start | bytes 98312 | tf_op jit(solution)/shard_map/ppermute | solution.py:543
  24.2 11.0 %collective-permute-start.10 = (f32[2,4,2,8,128]{4,3,2,1,0:T(8,128)S(1)}, f32[2,4,2,8,128]{4,3,2,1,0:T(8,128)S(1)}, u32[]{:S(2)}, u32[]{:S(2)}) collective-permute-start(f32[2,4,2,8,128]{4,3,2,1,0:T(8,128)S(1)} %pad_maximum_fusion.2), channel_id=1, source_target_pairs={{0,8},{4,12},{8,0},{12,4},{1,9},{5,13},{9,1},{13,5},{2,10},{6,14},... | collective-permute-start | bytes 196616 | tf_op jit(solution)/shard_map/ppermute | solution.py:543
  28.8 6.5 %collective-permute-start.9 = (f32[2,4,2,8,128]{4,3,2,1,0:T(8,128)S(1)}, f32[2,4,2,8,128]{4,3,2,1,0:T(8,128)S(1)}, u32[]{:S(2)}, u32[]{:S(2)}) collective-permute-start(f32[2,4,2,8,128]{4,3,2,1,0:T(8,128)S(1)} %pad_maximum_fusion.1), channel_id=1, source_target_pairs={{0,8},{4,12},{8,0},{12,4},{1,9},{5,13},{9,1},{13,5},{2,10},{6,14},... | collective-permute-start | bytes 196616 | tf_op jit(solution)/shard_map/ppermute | solution.py:543
  35.3 1.6 %collective-permute-start.11 = (f32[8,4,2,8,128]{4,3,2,1,0:T(8,128)S(1)}, f32[8,4,2,8,128]{4,3,2,1,0:T(8,128)S(1)}, u32[]{:S(2)}, u32[]{:S(2)}) collective-permute-start(f32[8,4,2,8,128]{4,3,2,1,0:T(8,128)S(1)} %constant_dynamic-update-slice_fusion.refs_0_), channel_id=1, source_target_pairs={{0,4},{4,0},{8,12},{12,8},{1,5},{5,1},{9,13},{13,9},{2,6},{6,2},{1... | collective-permute-start | bytes 786440 | tf_op jit(solution)/shard_map/ppermute | solution.py:543
  48.2 4.5 %collective-permute-start.14 = (f32[1,4,2,8,128]{4,3,2,1,0:T(8,128)S(1)}, f32[1,4,2,8,128]{4,3,2,1,0:T(8,128)S(1)}, u32[]{:S(2)}, u32[]{:S(2)}) collective-permute-start(f32[1,4,2,8,128]{4,3,2,1,0:T(8,128)S(1)} %bitcast.10), channel_id=1, source_target_pairs={{0,1},{1,0},{2,3},{3,2},{4,5},{5,4},{6,7},{7,6},{8,9},{9,8},{10,11... | collective-permute-start | bytes 98312 | tf_op jit(solution)/shard_map/ppermute | solution.py:543
  48.4 6.3 %collective-permute-start.13 = (f32[1,4,2,8,128]{4,3,2,1,0:T(8,128)S(1)}, f32[1,4,2,8,128]{4,3,2,1,0:T(8,128)S(1)}, u32[]{:S(2)}, u32[]{:S(2)}) collective-permute-start(f32[1,4,2,8,128]{4,3,2,1,0:T(8,128)S(1)} %bitcast.11), channel_id=1, source_target_pairs={{0,2},{1,3},{2,0},{3,1},{4,6},{5,7},{6,4},{7,5},{8,10},{9,11},{10,... | collective-permute-start | bytes 98312 | tf_op jit(solution)/shard_map/ppermute | solution.py:543
  50.2 5.7 %collective-permute-start.12 = (f32[1,4,2,8,128]{4,3,2,1,0:T(8,128)S(1)}, f32[1,4,2,8,128]{4,3,2,1,0:T(8,128)S(1)}, u32[]{:S(2)}, u32[]{:S(2)}) collective-permute-start(f32[1,4,2,8,128]{4,3,2,1,0:T(8,128)S(1)} %bitcast.12), channel_id=1, source_target_pairs={{0,3},{1,2},{2,1},{3,0},{4,7},{5,6},{6,5},{7,4},{8,11},{9,10},{10,... | collective-permute-start | bytes 98312 | tf_op jit(solution)/shard_map/ppermute | solution.py:543
  52.6 7.5 %collective-permute-start.16 = (f32[2,4,2,8,128]{4,3,2,1,0:T(8,128)S(1)}, f32[2,4,2,8,128]{4,3,2,1,0:T(8,128)S(1)}, u32[]{:S(2)}, u32[]{:S(2)}) collective-permute-start(f32[2,4,2,8,128]{4,3,2,1,0:T(8,128)S(1)} %pad_maximum_fusion.4), channel_id=1, source_target_pairs={{0,8},{4,12},{8,0},{12,4},{1,9},{5,13},{9,1},{13,5},{2,10},{6,14},... | collective-permute-start | bytes 196616 | tf_op jit(solution)/shard_map/ppermute | solution.py:543
  55.9 4.3 %collective-permute-start.15 = (f32[2,4,2,8,128]{4,3,2,1,0:T(8,128)S(1)}, f32[2,4,2,8,128]{4,3,2,1,0:T(8,128)S(1)}, u32[]{:S(2)}, u32[]{:S(2)}) collective-permute-start(f32[2,4,2,8,128]{4,3,2,1,0:T(8,128)S(1)} %pad_maximum_fusion.3), channel_id=1, source_target_pairs={{0,8},{4,12},{8,0},{12,4},{1,9},{5,13},{9,1},{13,5},{2,10},{6,14},... | collective-permute-start | bytes 196616 | tf_op jit(solution)/shard_map/ppermute | solution.py:543
  60.2 1.6 %collective-permute-start.17 = (f32[8,4,2,8,128]{4,3,2,1,0:T(8,128)S(1)}, f32[8,4,2,8,128]{4,3,2,1,0:T(8,128)S(1)}, u32[]{:S(2)}, u32[]{:S(2)}) collective-permute-start(f32[8,4,2,8,128]{4,3,2,1,0:T(8,128)S(1)} %constant_dynamic-update-slice_fusion.6.refs_0_), channel_id=1, source_target_pairs={{0,4},{4,0},{8,12},{12,8},{1,5},{5,1},{9,13},{13,9},{2,6},{6,2},{1... | collective-permute-start | bytes 786440 | tf_op jit(solution)/shard_map/ppermute | solution.py:543

commit v7 on v5

--- a/solution.py
+++ b/solution.py
@@ -211,14 +211,17 @@
 
     def place(x, load):
         for i in range(4):
+            plane = []
             for q in range(2):
+                even, odd = [], []
                 for z in range(0, count_z, 2):
                     one, two = load(z, i, q), load(z + 1, i, q)
                     first = row_of(one.shape) < 4
-                    rows = slice(4 * z, 4 * z + 8)
-                    b1[x + i, q, 0, rows] = jnp.where(first, one, pltpu.roll(two, 4, 0))
-                    b1[x + i, q, 1, rows] = jnp.where(first, pltpu.roll(one, 4, 0), two)
-            LEVEL_1.put(ub1, gb1, x + i, LEVEL_1.load(b1, x + i))
+                    even.append(jnp.where(first, one, pltpu.roll(two, 4, 0)))
+                    odd.append(jnp.where(first, pltpu.roll(one, 4, 0), two))
+                plane.append([jnp.concatenate(even, axis=0), jnp.concatenate(odd, axis=0)])
+            store_plane(b1, x + i, plane)
+            LEVEL_1.put(ub1, gb1, x + i, plane)
 
     if len(pieces) == 1:
 
@@ -231,14 +234,14 @@
         def gather(n):
             for core in range(2):
                 x = PAD + 4 * ((2 * n + core) ^ at_x)
-                place(x, lambda z, i, q: pieces[core][n * count_z + (z ^ at_z), i, q])
+                place(x, lambda z, i, q: pieces[core][n * count_z + (z ^ at_z ^ (count_z - 1)), i, q])
 
         each(0, count_x // 2, gather, 1)
 
     def sweep(level, u_in, g_in, u_out, g_out, b):
         return lambda x: level.put(u_out, g_out, x, level.sweep(u_in, g_in, b, x, third))
 
-    each(PAD, PAD + size_1, sweep(LEVEL_1, ub1, gb1, ua1, ga1, b1), 8)
+    each(PAD, PAD + size_1, sweep(LEVEL_1, ub1, gb1, ua1, ga1, b1), 16)
 
     def restrict_1(x):
         fine = PAD + 2 * x
@@ -298,8 +301,8 @@
         )
 
     each(0, size_2, prolong_2, 8)
-    each(PAD, PAD + size_1, sweep(ua1, ga1, ub1, gb1), 8)
-    each(PAD, PAD + size_1, sweep(ub1, gb1, ua1, ga1), 8)
+    each(PAD, PAD + size_1, sweep(ua1, ga1, ub1, gb1), 16)
+    each(PAD, PAD + size_1, sweep(ub1, gb1, ua1, ga1), 16)
     return ua1
 
 
@@ -521,23 +524,34 @@
     return run
 
 
+def pairs_apart(count, distance):
+    return [(i, i ^ distance) for i in range(count)]
+
+
+def pairs_shifted(count):
+    pairs = [(i, i + 1) for i in range(1, count - 1, 2)]
+    return pairs + [(target, source) for source, target in pairs]
+
+
+def across(pairs_x, pairs_z, count_z):
+    return [
+        (x_from * count_z + z_from, x_to * count_z + z_to)
+        for x_from, x_to in pairs_x
+        for z_from, z_to in pairs_z
+    ]
+
+
 def swap(axis, values, distance):
-    count = lax.axis_size(axis)
-    return lax.ppermute(values, axis, [(i, i ^ distance) for i in range(count)])
-
-
-def swap_shifted(axis, values):
-    pairs = [(i, i + 1) for i in range(1, lax.axis_size(axis) - 1, 2)]
-    return lax.ppermute(values, axis, pairs + [(target, source) for source, target in pairs])
+    return lax.ppermute(values, axis, pairs_apart(lax.axis_size(axis), distance))
 
 
 def every_piece(piece):
-    held = piece[None]
-    held = jnp.concatenate(
-        [held] + [swap("gz", held, distance) for distance in range(1, lax.axis_size("gz"))]
-    )
-    distance = 2
-    while distance < lax.axis_size("gx"):
+    count_x, count_z = lax.axis_size("gx"), lax.axis_size("gz")
+    line = [swap("gz", piece[None], count_z - 1 - n) for n in range(count_z - 1)] + [piece[None]]
+    halves = [jnp.concatenate(half) for half in (line[: count_z // 2], line[count_z // 2 :])]
+    held = jnp.concatenate(halves + [swap("gx", half, 2) for half in halves])
+    distance = 4
+    while distance < count_x:
         held = jnp.concatenate([held, swap("gx", held, distance)])
         distance *= 2
     return held, swap("gx", held, 1)
@@ -549,13 +563,22 @@
     where = jnp.stack([at_x, at_z]).astype(jnp.int32)
     brick, rim = (BRICK_X, 4, BRICK_Z, LANES), (BRICK_X, 4, RIM, LANES)
     middle, one, two = call(lanes_kernel, [brick, rim, rim], [])(where, charges)
-    far = swap_shifted("gx", middle)
+    z_one = pairs_apart(count_z, 1)
+    z_two = pairs_shifted(count_z)
+    x_far = pairs_shifted(count_x)
+    even = at_z % 2 == 0
+
+    def both_rims(from_one, from_two):
+        after, before = jnp.where(even, from_one, from_two), jnp.where(even, from_two, from_one)
+        return jnp.concatenate([after, before], axis=2)
+
+    far = lax.ppermute(middle, "gx", x_far)
+    far_rim = both_rims(
+        lax.ppermute(one, ("gx", "gz"), across(x_far, z_one, count_z)),
+        lax.ppermute(two, ("gx", "gz"), across(x_far, z_two, count_z)),
+    )
+    middle_rim = both_rims(lax.ppermute(one, "gz", z_one), lax.ppermute(two, "gz", z_two))
     near = swap("gx", middle, 1)
-    one = swap("gz", one, 1)
-    two = swap_shifted("gz", two)
-    even = at_z % 2 == 0
-    middle_rim = jnp.concatenate([jnp.where(even, one, two), jnp.where(even, two, one)], axis=2)
-    far_rim = swap_shifted("gx", middle_rim)
     near_rim = swap("gx", middle_rim, 1)
 
     wide = (WIDE_X, 4, 4, 8, LANES)

time: 60.7 us -> 61.5 us (1.013)
  starting transfers between devices: 27.9 us -> 33.8 us
  waiting for transfers between devices: 16.7 us -> 11.8 us
    ppermute x16 -> x19, starting transfers between devices: 27.9 us -> 33.8 us  [the longest x14 28.1 us: swap(): lax.ppermute(values, axis, pairs_apart(lax.axis_size(axis), distance))]
    ppermute x16 -> x19, waiting for transfers between devices: 16.7 us -> 11.8 us  [the longest x14 11 us: swap(): lax.ppermute(values, axis, pairs_apart(lax.axis_size(axis), distance))]
  transfers between devices with their start and end apart: 16 -> 19, of which waited for: 9 -> 8; matrix products, arithmetic and copies ran while one was open for 0% -> 0% of each run, Pallas kernels for 0% -> 0%
where the time goes in v7:
time: 61.5 us; the launch traced here: 61.3 us
  starting transfers between devices  33.8 us (55%)
  Pallas kernels  14.4 us (23%)
  waiting for transfers between devices  11.8 us (19%)
  local copies, waits for them, and re-layouts  1.01 us (2%)
    ppermute x14, starting transfers between devices, swap(): lax.ppermute(values, axis, pairs_apart(lax.axis_size(axis), distance))  28.1 us
    pallas_call x4, Pallas kernels, run(): pl.pallas_call(kernel, out_shape=shapes, in_specs=[pl.BlockSpec(memory_sp...  14.4 us
    ppermute x14, waiting for transfers between devices, swap(): lax.ppermute(values, axis, pairs_apart(lax.axis_size(axis), distance))  11 us
    ppermute x1, starting transfers between devices, per_device(): lax.ppermute(one, 'gz', z_one)  3.09 us
  transfers between devices with their start and end apart: 19, of which 8 were waited for; matrix products, arithmetic and copies ran while one was open for 0% of the time, Pallas kernels for 0%

profile of v7, /device:TPU:0, one launch (start us, length us, event | category | flops | bytes accessed | tf_op | source)
XLA Modules:
  0.0 61.3 jit_solution(11073990103573225291)
XLA Ops:
  0.0 0.1 pad_add_fusion.where_ref
  0.1 0.0 copy-start
  0.1 0.9 %copy-done = f32[8,16,512]{2,1,0:T(8,128)S(1)} copy-done((f32[8,16,512]{2,1,0:T(8,128)S(1)}, f32[8,16,512]{2,1,0:T(8,128)}, u32[]{:S(2)}) %copy-start) | copy-done | bytes 262168
  1.0 1.0 %shard_map.17 = (f32[8,4,16,128]{3,2,1,0:T(8,128)S(1)}, f32[8,4,8,128]{3,2,1,0:T(8,128)S(1)}, f32[8,4,8,128]{3,2,1,0:T(8,128)S(1)}) custom-call(s32[2]{0:T(128)S(1)} %pad_add_fusion.where_ref, f32[8,16,512]{2,1,0:T(8,128)S(1)} %copy-done), custom_call_target="tpu_custom_call" | custom-call | tf_op jit(solution)/shard_map/pallas_call | solution.py:514
  2.0 3.1 %collective-permute-start = (f32[8,4,8,128]{3,2,1,0:T(8,128)S(1)}, f32[8,4,8,128]{3,2,1,0:T(8,128)S(1)}, u32[]{:S(2)}, u32[]{:S(2)}) collective-permute-start(f32[8,4,8,128]{3,2,1,0:T(8,128)S(1)} %get-tuple-element.14), channel_id=1, source_target_pairs={{0,1},{1,0},{2,3},{3,2},{4,5},{5,4},{6,7},{7,6},{8,9},{9,8},{10,11... | collective-permute-start | bytes 393224 | tf_op jit(solution)/shard_map/ppermute | solution.py:580
  5.1 0.7 %collective-permute-start.1 = (f32[8,4,8,128]{3,2,1,0:T(8,128)S(1)}, f32[8,4,8,128]{3,2,1,0:T(8,128)S(1)}, u32[]{:S(2)}, u32[]{:S(2)}) collective-permute-start(f32[8,4,8,128]{3,2,1,0:T(8,128)S(1)} %get-tuple-element.15), channel_id=1, source_target_pairs={{1,2},{2,1},{5,6},{6,5},{9,10},{10,9},{13,14},{14,13},{17,18},{18,... | collective-permute-start | bytes 393224 | tf_op jit(solution)/shard_map/ppermute | solution.py:580
  5.8 0.7 %collective-permute-start.5 = (f32[8,4,8,128]{3,2,1,0:T(8,128)S(1)}, f32[8,4,8,128]{3,2,1,0:T(8,128)S(1)}, u32[]{:S(2)}, u32[]{:S(2)}) collective-permute-start(f32[8,4,8,128]{3,2,1,0:T(8,128)S(1)} %get-tuple-element.14), channel_id=1, source_target_pairs={{4,9},{5,8},{6,11},{7,10},{8,5},{9,4},{10,7},{11,6},{20,25},{21,24... | collective-permute-start | bytes 393224 | tf_op jit(solution)/shard_map/ppermute | solution.py:577
  6.5 0.7 %collective-permute-start.6 = (f32[8,4,8,128]{3,2,1,0:T(8,128)S(1)}, f32[8,4,8,128]{3,2,1,0:T(8,128)S(1)}, u32[]{:S(2)}, u32[]{:S(2)}) collective-permute-start(f32[8,4,8,128]{3,2,1,0:T(8,128)S(1)} %get-tuple-element.15), channel_id=1, source_target_pairs={{5,10},{6,9},{9,6},{10,5},{21,26},{22,25},{25,22},{26,21}} | collective-permute-start | bytes 393224 | tf_op jit(solution)/shard_map/ppermute | solution.py:578
  7.1 0.7 %collective-permute-start.4 = (f32[8,4,16,128]{3,2,1,0:T(8,128)S(1)}, f32[8,4,16,128]{3,2,1,0:T(8,128)S(1)}, u32[]{:S(2)}, u32[]{:S(2)}) collective-permute-start(f32[8,4,16,128]{3,2,1,0:T(8,128)S(1)} %get-tuple-element.13.mid_ref), channel_id=1, source_target_pairs={{4,8},{8,4},{5,9},{9,5},{6,10},{10,6},{7,11},{11,7},{20,24},{24,20... | collective-permute-start | bytes 786440 | tf_op jit(solution)/shard_map/ppermute | solution.py:575
  7.8 0.8 %collective-permute-done = f32[8,4,8,128]{3,2,1,0:T(8,128)S(1)} collective-permute-done((f32[8,4,8,128]{3,2,1,0:T(8,128)S(1)}, f32[8,4,8,128]{3,2,1,0:T(8,128)S(1)}, u32[]{:S(2)}, u32[]{:S(2)}) %collective-permute-start) | collective-permute-done | bytes 131104 | tf_op jit(solution)/shard_map/ppermute | solution.py:580
  8.6 7.2 %collective-permute-start.2 = (f32[8,4,16,128]{3,2,1,0:T(8,128)S(1)}, f32[8,4,16,128]{3,2,1,0:T(8,128)S(1)}, u32[]{:S(2)}, u32[]{:S(2)}) collective-permute-start(f32[8,4,16,128]{3,2,1,0:T(8,128)S(1)} %get-tuple-element.13.mid_ref), channel_id=1, source_target_pairs={{0,4},{4,0},{8,12},{12,8},{1,5},{5,1},{9,13},{13,9},{2,6},{6,2},{1... | collective-permute-start | bytes 786440 | tf_op jit(solution)/shard_map/ppermute | solution.py:545
  15.8 0.0 collective-permute-done.1
  15.9 0.1 collective-permute-start.3
  16.0 0.0 collective-permute-done.5
  16.0 0.0 collective-permute-done.6
  16.1 0.0 collective-permute-done.4.two_ref
  16.1 0.9 %collective-permute-done.2.one_ref = f32[8,4,16,128]{3,2,1,0:T(8,128)S(1)} collective-permute-done((f32[8,4,16,128]{3,2,1,0:T(8,128)S(1)}, f32[8,4,16,128]{3,2,1,0:T(8,128)S(1)}, u32[]{:S(2)}, u32[]{:S(2)}) %collective-permute-start.2) | collective-permute-done | bytes 262176 | tf_op jit(solution)/shard_map/ppermute | solution.py:545
  17.0 0.5 collective-permute-done.3.one_rim_ref
  17.5 2.5 %shard_map.18 = (f32[24,4,4,8,128]{4,3,2,1,0:T(8,128)S(1)}, f32[24,4,4,8,128]{4,3,2,1,0:T(8,128)S(1)}, f32[4,2,8,128]{3,2,1,0:T(8,128)S(1)}) custom-call(s32[2]{0:T(128)S(1)} %pad_add_fusion.where_ref, f32[8,4,16,128]{3,2,1,0:T(8,128)S(1)} %get-tuple-element.13.mid_ref, f32[8,4,16,128]{3,2,1,0:T(8,128)S(1)} %pad_maximum_fusion.mid_rim_ref, ...), custom_call_target="tpu_custom_call" | custom-call | tf_op jit(solution)/shard_map/pallas_call | solution.py:514
  20.0 1.9 %collective-permute-start.9 = (f32[1,4,2,8,128]{4,3,2,1,0:T(8,128)S(1)}, f32[1,4,2,8,128]{4,3,2,1,0:T(8,128)S(1)}, u32[]{:S(2)}, u32[]{:S(2)}) collective-permute-start(f32[1,4,2,8,128]{4,3,2,1,0:T(8,128)S(1)} %bitcast.6), channel_id=1, source_target_pairs={{0,1},{1,0},{2,3},{3,2},{4,5},{5,4},{6,7},{7,6},{8,9},{9,8},{10,11... | collective-permute-start | bytes 98312 | tf_op jit(solution)/shard_map/ppermute | solution.py:545
  21.9 1.0 %collective-permute-start.8 = (f32[1,4,2,8,128]{4,3,2,1,0:T(8,128)S(1)}, f32[1,4,2,8,128]{4,3,2,1,0:T(8,128)S(1)}, u32[]{:S(2)}, u32[]{:S(2)}) collective-permute-start(f32[1,4,2,8,128]{4,3,2,1,0:T(8,128)S(1)} %bitcast.7), channel_id=1, source_target_pairs={{0,2},{1,3},{2,0},{3,1},{4,6},{5,7},{6,4},{7,5},{8,10},{9,11},{10,... | collective-permute-start | bytes 98312 | tf_op jit(solution)/shard_map/ppermute | solution.py:545
  22.9 1.6 %collective-permute-start.7 = (f32[1,4,2,8,128]{4,3,2,1,0:T(8,128)S(1)}, f32[1,4,2,8,128]{4,3,2,1,0:T(8,128)S(1)}, u32[]{:S(2)}, u32[]{:S(2)}) collective-permute-start(f32[1,4,2,8,128]{4,3,2,1,0:T(8,128)S(1)} %bitcast.8), channel_id=1, source_target_pairs={{0,3},{1,2},{2,1},{3,0},{4,7},{5,6},{6,5},{7,4},{8,11},{9,10},{10,... | collective-permute-start | bytes 98312 | tf_op jit(solution)/shard_map/ppermute | solution.py:545
  24.5 0.0 collective-permute-done.9
  24.5 4.2 %collective-permute-start.11 = (f32[2,4,2,8,128]{4,3,2,1,0:T(8,128)S(1)}, f32[2,4,2,8,128]{4,3,2,1,0:T(8,128)S(1)}, u32[]{:S(2)}, u32[]{:S(2)}) collective-permute-start(f32[2,4,2,8,128]{4,3,2,1,0:T(8,128)S(1)} %pad_maximum_fusion.3), channel_id=1, source_target_pairs={{0,8},{4,12},{8,0},{12,4},{1,9},{5,13},{9,1},{13,5},{2,10},{6,14},... | collective-permute-start | bytes 196616 | tf_op jit(solution)/shard_map/ppermute | solution.py:545
  28.7 0.0 collective-permute-done.8
  28.7 0.0 collective-permute-done.7
  28.7 3.8 %collective-permute-start.10 = (f32[2,4,2,8,128]{4,3,2,1,0:T(8,128)S(1)}, f32[2,4,2,8,128]{4,3,2,1,0:T(8,128)S(1)}, u32[]{:S(2)}, u32[]{:S(2)}) collective-permute-start(f32[2,4,2,8,128]{4,3,2,1,0:T(8,128)S(1)} %pad_maximum_fusion.2), channel_id=1, source_target_pairs={{0,8},{4,12},{8,0},{12,4},{1,9},{5,13},{9,1},{13,5},{2,10},{6,14},... | collective-permute-start | bytes 196616 | tf_op jit(solution)/shard_map/ppermute | solution.py:545
  32.6 2.6 %collective-permute-done.10 = f32[2,4,2,8,128]{4,3,2,1,0:T(8,128)S(1)} collective-permute-done((f32[2,4,2,8,128]{4,3,2,1,0:T(8,128)S(1)}, f32[2,4,2,8,128]{4,3,2,1,0:T(8,128)S(1)}, u32[]{:S(2)}, u32[]{:S(2)}) %collective-permute-start.10) | collective-permute-done | bytes 65568 | tf_op jit(solution)/shard_map/ppermute | solution.py:545
  35.2 0.0 collective-permute-done.11
  35.2 0.1 collective-permute-start.12
  35.3 1.5 %collective-permute-done.12.refs_1_ = f32[8,4,2,8,128]{4,3,2,1,0:T(8,128)S(1)} collective-permute-done((f32[8,4,2,8,128]{4,3,2,1,0:T(8,128)S(1)}, f32[8,4,2,8,128]{4,3,2,1,0:T(8,128)S(1)}, u32[]{:S(2)}, u32[]{:S(2)}) %collective-permute-start.12) | collective-permute-done | bytes 262176 | tf_op jit(solution)/shard_map/ppermute | solution.py:545
  36.8 6.0 %shard_map.19 = (f32[24,4,4,8,128]{4,3,2,1,0:T(8,128)S(1)}, f32[4,2,8,128]{3,2,1,0:T(8,128)S(1)}) custom-call(s32[2]{0:T(128)S(1)} %pad_add_fusion.where_ref, f32[8,4,2,8,128]{4,3,2,1,0:T(8,128)S(1)} %constant_dynamic-update-slice_fusion.refs_0_, f32[8,4,2,8,128]{4,3,2,1,0:T(8,128)S(1)} %collective-permute-done.12.refs_1_, ...), custom_call_target="tpu_custom_call" | custom-call | tf_op jit(solution)/shard_map/pallas_call | solution.py:514
  42.8 0.1 collective-permute-start.15
  42.9 2.0 %collective-permute-start.14 = (f32[1,4,2,8,128]{4,3,2,1,0:T(8,128)S(1)}, f32[1,4,2,8,128]{4,3,2,1,0:T(8,128)S(1)}, u32[]{:S(2)}, u32[]{:S(2)}) collective-permute-start(f32[1,4,2,8,128]{4,3,2,1,0:T(8,128)S(1)} %bitcast.11), channel_id=1, source_target_pairs={{0,2},{1,3},{2,0},{3,1},{4,6},{5,7},{6,4},{7,5},{8,10},{9,11},{10,... | collective-permute-start | bytes 98312 | tf_op jit(solution)/shard_map/ppermute | solution.py:545
  44.8 2.4 %collective-permute-start.13 = (f32[1,4,2,8,128]{4,3,2,1,0:T(8,128)S(1)}, f32[1,4,2,8,128]{4,3,2,1,0:T(8,128)S(1)}, u32[]{:S(2)}, u32[]{:S(2)}) collective-permute-start(f32[1,4,2,8,128]{4,3,2,1,0:T(8,128)S(1)} %bitcast.12), channel_id=1, source_target_pairs={{0,3},{1,2},{2,1},{3,0},{4,7},{5,6},{6,5},{7,4},{8,11},{9,10},{10,... | collective-permute-start | bytes 98312 | tf_op jit(solution)/shard_map/ppermute | solution.py:545
  47.3 0.0 collective-permute-done.15
  47.3 1.7 %collective-permute-start.17 = (f32[2,4,2,8,128]{4,3,2,1,0:T(8,128)S(1)}, f32[2,4,2,8,128]{4,3,2,1,0:T(8,128)S(1)}, u32[]{:S(2)}, u32[]{:S(2)}) collective-permute-start(f32[2,4,2,8,128]{4,3,2,1,0:T(8,128)S(1)} %pad_maximum_fusion.5), channel_id=1, source_target_pairs={{0,8},{4,12},{8,0},{12,4},{1,9},{5,13},{9,1},{13,5},{2,10},{6,14},... | collective-permute-start | bytes 196616 | tf_op jit(solution)/shard_map/ppermute | solution.py:545
  48.9 0.0 collective-permute-done.14
  48.9 1.6 %collective-permute-done.13 = f32[1,4,2,8,128]{4,3,2,1,0:T(8,128)S(1)} collective-permute-done((f32[1,4,2,8,128]{4,3,2,1,0:T(8,128)S(1)}, f32[1,4,2,8,128]{4,3,2,1,0:T(8,128)S(1)}, u32[]{:S(2)}, u32[]{:S(2)}) %collective-permute-start.13) | collective-permute-done | bytes 32800 | tf_op jit(solution)/shard_map/ppermute | solution.py:545
  50.6 2.0 %collective-permute-start.16 = (f32[2,4,2,8,128]{4,3,2,1,0:T(8,128)S(1)}, f32[2,4,2,8,128]{4,3,2,1,0:T(8,128)S(1)}, u32[]{:S(2)}, u32[]{:S(2)}) collective-permute-start(f32[2,4,2,8,128]{4,3,2,1,0:T(8,128)S(1)} %pad_maximum_fusion.4), channel_id=1, source_target_pairs={{0,8},{4,12},{8,0},{12,4},{1,9},{5,13},{9,1},{13,5},{2,10},{6,14},... | collective-permute-start | bytes 196616 | tf_op jit(solution)/shard_map/ppermute | solution.py:545
  52.6 2.2 %collective-permute-done.16 = f32[2,4,2,8,128]{4,3,2,1,0:T(8,128)S(1)} collective-permute-done((f32[2,4,2,8,128]{4,3,2,1,0:T(8,128)S(1)}, f32[2,4,2,8,128]{4,3,2,1,0:T(8,128)S(1)}, u32[]{:S(2)}, u32[]{:S(2)}) %collective-permute-start.16) | collective-permute-done | bytes 65568 | tf_op jit(solution)/shard_map/ppermute | solution.py:545
  54.8 0.0 collective-permute-done.17
  54.9 0.1 collective-permute-start.18
  54.9 1.5 %collective-permute-done.18.refs_1_ = f32[8,4,2,8,128]{4,3,2,1,0:T(8,128)S(1)} collective-permute-done((f32[8,4,2,8,128]{4,3,2,1,0:T(8,128)S(1)}, f32[8,4,2,8,128]{4,3,2,1,0:T(8,128)S(1)}, u32[]{:S(2)}, u32[]{:S(2)}) %collective-permute-start.18) | collective-permute-done | bytes 262176 | tf_op jit(solution)/shard_map/ppermute | solution.py:545
  56.5 4.9 %shard_map.20 = f32[8,16,512]{2,1,0:T(8,128)} custom-call(s32[2]{0:T(128)S(1)} %pad_add_fusion.where_ref, f32[8,4,2,8,128]{4,3,2,1,0:T(8,128)S(1)} %constant_dynamic-update-slice_fusion.6.refs_0_, f32[8,4,2,8,128]{4,3,2,1,0:T(8,128)S(1)} %collective-permute-done.18.refs_1_, f32[24,4,4,8,128]{4,3,2,1,0:T(8,128)S(1)} %get-tuple-element.20.refs_2_, ...), custom_call_target="tpu_custom_call" | custom-call | tf_op jit(solution)/shard_map/pallas_call | solution.py:514
  (20 shorter events, 0.2 us)
Async XLA Ops:
  0.1 0.9 %copy-start = (f32[8,16,512]{2,1,0:T(8,128)S(1)}, f32[8,16,512]{2,1,0:T(8,128)}, u32[]{:S(2)}) copy-start(f32[8,16,512]{2,1,0:T(8,128)} %charges_ref.1) | copy-start | bytes 786436
  2.0 6.6 %collective-permute-start = (f32[8,4,8,128]{3,2,1,0:T(8,128)S(1)}, f32[8,4,8,128]{3,2,1,0:T(8,128)S(1)}, u32[]{:S(2)}, u32[]{:S(2)}) collective-permute-start(f32[8,4,8,128]{3,2,1,0:T(8,128)S(1)} %get-tuple-element.14), channel_id=1, source_target_pairs={{0,1},{1,0},{2,3},{3,2},{4,5},{5,4},{6,7},{7,6},{8,9},{9,8},{10,11... | collective-permute-start | bytes 393224 | tf_op jit(solution)/shard_map/ppermute | solution.py:580
  5.1 10.7 %collective-permute-start.1 = (f32[8,4,8,128]{3,2,1,0:T(8,128)S(1)}, f32[8,4,8,128]{3,2,1,0:T(8,128)S(1)}, u32[]{:S(2)}, u32[]{:S(2)}) collective-permute-start(f32[8,4,8,128]{3,2,1,0:T(8,128)S(1)} %get-tuple-element.15), channel_id=1, source_target_pairs={{1,2},{2,1},{5,6},{6,5},{9,10},{10,9},{13,14},{14,13},{17,18},{18,... | collective-permute-start | bytes 393224 | tf_op jit(solution)/shard_map/ppermute | solution.py:580
  5.8 10.2 %collective-permute-start.5 = (f32[8,4,8,128]{3,2,1,0:T(8,128)S(1)}, f32[8,4,8,128]{3,2,1,0:T(8,128)S(1)}, u32[]{:S(2)}, u32[]{:S(2)}) collective-permute-start(f32[8,4,8,128]{3,2,1,0:T(8,128)S(1)} %get-tuple-element.14), channel_id=1, source_target_pairs={{4,9},{5,8},{6,11},{7,10},{8,5},{9,4},{10,7},{11,6},{20,25},{21,24... | collective-permute-start | bytes 393224 | tf_op jit(solution)/shard_map/ppermute | solution.py:577
  6.5 9.5 %collective-permute-start.6 = (f32[8,4,8,128]{3,2,1,0:T(8,128)S(1)}, f32[8,4,8,128]{3,2,1,0:T(8,128)S(1)}, u32[]{:S(2)}, u32[]{:S(2)}) collective-permute-start(f32[8,4,8,128]{3,2,1,0:T(8,128)S(1)} %get-tuple-element.15), channel_id=1, source_target_pairs={{5,10},{6,9},{9,6},{10,5},{21,26},{22,25},{25,22},{26,21}} | collective-permute-start | bytes 393224 | tf_op jit(solution)/shard_map/ppermute | solution.py:578
  7.1 8.9 %collective-permute-start.4 = (f32[8,4,16,128]{3,2,1,0:T(8,128)S(1)}, f32[8,4,16,128]{3,2,1,0:T(8,128)S(1)}, u32[]{:S(2)}, u32[]{:S(2)}) collective-permute-start(f32[8,4,16,128]{3,2,1,0:T(8,128)S(1)} %get-tuple-element.13.mid_ref), channel_id=1, source_target_pairs={{4,8},{8,4},{5,9},{9,5},{6,10},{10,6},{7,11},{11,7},{20,24},{24,20... | collective-permute-start | bytes 786440 | tf_op jit(solution)/shard_map/ppermute | solution.py:575
  8.6 8.4 %collective-permute-start.2 = (f32[8,4,16,128]{3,2,1,0:T(8,128)S(1)}, f32[8,4,16,128]{3,2,1,0:T(8,128)S(1)}, u32[]{:S(2)}, u32[]{:S(2)}) collective-permute-start(f32[8,4,16,128]{3,2,1,0:T(8,128)S(1)} %get-tuple-element.13.mid_ref), channel_id=1, source_target_pairs={{0,4},{4,0},{8,12},{12,8},{1,5},{5,1},{9,13},{13,9},{2,6},{6,2},{1... | collective-permute-start | bytes 786440 | tf_op jit(solution)/shard_map/ppermute | solution.py:545
  15.9 1.6 %collective-permute-start.3 = (f32[8,4,16,128]{3,2,1,0:T(8,128)S(1)}, f32[8,4,16,128]{3,2,1,0:T(8,128)S(1)}, u32[]{:S(2)}, u32[]{:S(2)}) collective-permute-start(f32[8,4,16,128]{3,2,1,0:T(8,128)S(1)} %pad_maximum_fusion.mid_rim_ref), channel_id=1, source_target_pairs={{0,4},{4,0},{8,12},{12,8},{1,5},{5,1},{9,13},{13,9},{2,6},{6,2},{1... | collective-permute-start | bytes 786440 | tf_op jit(solution)/shard_map/ppermute | solution.py:545
  20.0 4.5 %collective-permute-start.9 = (f32[1,4,2,8,128]{4,3,2,1,0:T(8,128)S(1)}, f32[1,4,2,8,128]{4,3,2,1,0:T(8,128)S(1)}, u32[]{:S(2)}, u32[]{:S(2)}) collective-permute-start(f32[1,4,2,8,128]{4,3,2,1,0:T(8,128)S(1)} %bitcast.6), channel_id=1, source_target_pairs={{0,1},{1,0},{2,3},{3,2},{4,5},{5,4},{6,7},{7,6},{8,9},{9,8},{10,11... | collective-permute-start | bytes 98312 | tf_op jit(solution)/shard_map/ppermute | solution.py:545
  21.9 6.8 %collective-permute-start.8 = (f32[1,4,2,8,128]{4,3,2,1,0:T(8,128)S(1)}, f32[1,4,2,8,128]{4,3,2,1,0:T(8,128)S(1)}, u32[]{:S(2)}, u32[]{:S(2)}) collective-permute-start(f32[1,4,2,8,128]{4,3,2,1,0:T(8,128)S(1)} %bitcast.7), channel_id=1, source_target_pairs={{0,2},{1,3},{2,0},{3,1},{4,6},{5,7},{6,4},{7,5},{8,10},{9,11},{10,... | collective-permute-start | bytes 98312 | tf_op jit(solution)/shard_map/ppermute | solution.py:545
  22.9 5.8 %collective-permute-start.7 = (f32[1,4,2,8,128]{4,3,2,1,0:T(8,128)S(1)}, f32[1,4,2,8,128]{4,3,2,1,0:T(8,128)S(1)}, u32[]{:S(2)}, u32[]{:S(2)}) collective-permute-start(f32[1,4,2,8,128]{4,3,2,1,0:T(8,128)S(1)} %bitcast.8), channel_id=1, source_target_pairs={{0,3},{1,2},{2,1},{3,0},{4,7},{5,6},{6,5},{7,4},{8,11},{9,10},{10,... | collective-permute-start | bytes 98312 | tf_op jit(solution)/shard_map/ppermute | solution.py:545
  24.5 10.7 %collective-permute-start.11 = (f32[2,4,2,8,128]{4,3,2,1,0:T(8,128)S(1)}, f32[2,4,2,8,128]{4,3,2,1,0:T(8,128)S(1)}, u32[]{:S(2)}, u32[]{:S(2)}) collective-permute-start(f32[2,4,2,8,128]{4,3,2,1,0:T(8,128)S(1)} %pad_maximum_fusion.3), channel_id=1, source_target_pairs={{0,8},{4,12},{8,0},{12,4},{1,9},{5,13},{9,1},{13,5},{2,10},{6,14},... | collective-permute-start | bytes 196616 | tf_op jit(solution)/shard_map/ppermute | solution.py:545
  28.7 6.5 %collective-permute-start.10 = (f32[2,4,2,8,128]{4,3,2,1,0:T(8,128)S(1)}, f32[2,4,2,8,128]{4,3,2,1,0:T(8,128)S(1)}, u32[]{:S(2)}, u32[]{:S(2)}) collective-permute-start(f32[2,4,2,8,128]{4,3,2,1,0:T(8,128)S(1)} %pad_maximum_fusion.2), channel_id=1, source_target_pairs={{0,8},{4,12},{8,0},{12,4},{1,9},{5,13},{9,1},{13,5},{2,10},{6,14},... | collective-permute-start | bytes 196616 | tf_op jit(solution)/shard_map/ppermute | solution.py:545
  35.2 1.6 %collective-permute-start.12 = (f32[8,4,2,8,128]{4,3,2,1,0:T(8,128)S(1)}, f32[8,4,2,8,128]{4,3,2,1,0:T(8,128)S(1)}, u32[]{:S(2)}, u32[]{:S(2)}) collective-permute-start(f32[8,4,2,8,128]{4,3,2,1,0:T(8,128)S(1)} %constant_dynamic-update-slice_fusion.refs_0_), channel_id=1, source_target_pairs={{0,4},{4,0},{8,12},{12,8},{1,5},{5,1},{9,13},{13,9},{2,6},{6,2},{1... | collective-permute-start | bytes 786440 | tf_op jit(solution)/shard_map/ppermute | solution.py:545
  42.8 4.5 %collective-permute-start.15 = (f32[1,4,2,8,128]{4,3,2,1,0:T(8,128)S(1)}, f32[1,4,2,8,128]{4,3,2,1,0:T(8,128)S(1)}, u32[]{:S(2)}, u32[]{:S(2)}) collective-permute-start(f32[1,4,2,8,128]{4,3,2,1,0:T(8,128)S(1)} %bitcast.10), channel_id=1, source_target_pairs={{0,1},{1,0},{2,3},{3,2},{4,5},{5,4},{6,7},{7,6},{8,9},{9,8},{10,11... | collective-permute-start | bytes 98312 | tf_op jit(solution)/shard_map/ppermute | solution.py:545
  42.9 6.0 %collective-permute-start.14 = (f32[1,4,2,8,128]{4,3,2,1,0:T(8,128)S(1)}, f32[1,4,2,8,128]{4,3,2,1,0:T(8,128)S(1)}, u32[]{:S(2)}, u32[]{:S(2)}) collective-permute-start(f32[1,4,2,8,128]{4,3,2,1,0:T(8,128)S(1)} %bitcast.11), channel_id=1, source_target_pairs={{0,2},{1,3},{2,0},{3,1},{4,6},{5,7},{6,4},{7,5},{8,10},{9,11},{10,... | collective-permute-start | bytes 98312 | tf_op jit(solution)/shard_map/ppermute | solution.py:545
  44.8 5.7 %collective-permute-start.13 = (f32[1,4,2,8,128]{4,3,2,1,0:T(8,128)S(1)}, f32[1,4,2,8,128]{4,3,2,1,0:T(8,128)S(1)}, u32[]{:S(2)}, u32[]{:S(2)}) collective-permute-start(f32[1,4,2,8,128]{4,3,2,1,0:T(8,128)S(1)} %bitcast.12), channel_id=1, source_target_pairs={{0,3},{1,2},{2,1},{3,0},{4,7},{5,6},{6,5},{7,4},{8,11},{9,10},{10,... | collective-permute-start | bytes 98312 | tf_op jit(solution)/shard_map/ppermute | solution.py:545
  47.3 7.6 %collective-permute-start.17 = (f32[2,4,2,8,128]{4,3,2,1,0:T(8,128)S(1)}, f32[2,4,2,8,128]{4,3,2,1,0:T(8,128)S(1)}, u32[]{:S(2)}, u32[]{:S(2)}) collective-permute-start(f32[2,4,2,8,128]{4,3,2,1,0:T(8,128)S(1)} %pad_maximum_fusion.5), channel_id=1, source_target_pairs={{0,8},{4,12},{8,0},{12,4},{1,9},{5,13},{9,1},{13,5},{2,10},{6,14},... | collective-permute-start | bytes 196616 | tf_op jit(solution)/shard_map/ppermute | solution.py:545
  50.6 4.3 %collective-permute-start.16 = (f32[2,4,2,8,128]{4,3,2,1,0:T(8,128)S(1)}, f32[2,4,2,8,128]{4,3,2,1,0:T(8,128)S(1)}, u32[]{:S(2)}, u32[]{:S(2)}) collective-permute-start(f32[2,4,2,8,128]{4,3,2,1,0:T(8,128)S(1)} %pad_maximum_fusion.4), channel_id=1, source_target_pairs={{0,8},{4,12},{8,0},{12,4},{1,9},{5,13},{9,1},{13,5},{2,10},{6,14},... | collective-permute-start | bytes 196616 | tf_op jit(solution)/shard_map/ppermute | solution.py:545
  54.9 1.6 %collective-permute-start.18 = (f32[8,4,2,8,128]{4,3,2,1,0:T(8,128)S(1)}, f32[8,4,2,8,128]{4,3,2,1,0:T(8,128)S(1)}, u32[]{:S(2)}, u32[]{:S(2)}) collective-permute-start(f32[8,4,2,8,128]{4,3,2,1,0:T(8,128)S(1)} %constant_dynamic-update-slice_fusion.6.refs_0_), channel_id=1, source_target_pairs={{0,4},{4,0},{8,12},{12,8},{1,5},{5,1},{9,13},{13,9},{2,6},{6,2},{1... | collective-permute-start | bytes 786440 | tf_op jit(solution)/shard_map/ppermute | solution.py:545

commit v8 on v7

--- a/solution.py
+++ b/solution.py
@@ -407,17 +407,27 @@
     return terms[0] + (terms[1] + terms[2])
 
 
+def split_lanes(values):
+    size_x, size_z, size_y = values.shape
+    flat = values.reshape(size_x * size_z, size_y)
+    split = permuted(flat, lambda y, l: y == (l % LANES) * 4 + l // LANES)
+    return [
+        split[:, p * LANES : (p + 1) * LANES].reshape(size_x, size_z, LANES) for p in range(4)
+    ]
+
+
 def lanes_kernel(where_ref, charges_ref, rows_ref, one_ref, two_ref):
     odd = where_ref[1] % 2
-    width = charges_ref.shape[2]
-    flat = charges_ref[...].reshape(BRICK_X * BRICK_Z, width)
-    split = permuted(flat, lambda y, l: y == (l % LANES) * 4 + l // LANES)
-    for p in range(4):
-        tile = split[:, p * LANES : (p + 1) * LANES].reshape(BRICK_X, BRICK_Z, LANES)
+    for p, tile in enumerate(split_lanes(charges_ref[...])):
         rows_ref[:, p] = tile
         first, last = tile[:, 0:8], tile[:, 8:16]
         one_ref[:, p] = jnp.where(odd == 0, last, first)
         two_ref[:, p] = jnp.where(odd == 0, first, last)
+
+
+def far_lanes_kernel(where_ref, charges_ref, rows_ref):
+    for p, tile in enumerate(split_lanes(charges_ref[...])):
+        rows_ref[:, p] = tile
 
 
 def down_kernel(count_x, count_z, where_ref, mid_ref, mid_rim_ref, one_ref, one_rim_ref, two_ref,
@@ -562,17 +572,17 @@
     at_x, at_z = lax.axis_index("gx"), lax.axis_index("gz")
     where = jnp.stack([at_x, at_z]).astype(jnp.int32)
     brick, rim = (BRICK_X, 4, BRICK_Z, LANES), (BRICK_X, 4, RIM, LANES)
+    x_far = pairs_shifted(count_x)
+    (far,) = call(far_lanes_kernel, [brick], [])(where, lax.ppermute(charges, "gx", x_far))
     middle, one, two = call(lanes_kernel, [brick, rim, rim], [])(where, charges)
     z_one = pairs_apart(count_z, 1)
     z_two = pairs_shifted(count_z)
-    x_far = pairs_shifted(count_x)
     even = at_z % 2 == 0
 
     def both_rims(from_one, from_two):
         after, before = jnp.where(even, from_one, from_two), jnp.where(even, from_two, from_one)
         return jnp.concatenate([after, before], axis=2)
 
-    far = lax.ppermute(middle, "gx", x_far)
     far_rim = both_rims(
         lax.ppermute(one, ("gx", "gz"), across(x_far, z_one, count_z)),
         lax.ppermute(two, ("gx", "gz"), across(x_far, z_two, count_z)),

time: 61.5 us -> 61.6 us (level)
  Pallas kernels: 14.4 us -> 15.7 us
  local copies, waits for them, and re-layouts: 1.01 us -> 0.06 us
    pallas_call x4 -> x5, Pallas kernels: 14.4 us -> 15.7 us  [run(): pl.pallas_call(kernel, out_shape=shapes, in_specs=[pl.BlockSpec(memory_sp...]
    unnamed x12 -> x10, local copies, waits for them, and re-layouts: 0.99 us -> 0.04 us
    ppermute x14, starting transfers between devices: 28.1 us -> 27.4 us  [swap(): lax.ppermute(values, axis, pairs_apart(lax.axis_size(axis), distance))]
  transfers between devices with their start and end apart: 19 -> 19, of which waited for: 8 -> 7; matrix products, arithmetic and copies ran while one was open for 0% -> 0% of each run, Pallas kernels for 0% -> 2%
where the time goes in v8:
time: 61.6 us; the launch traced here: 61.4 us
  starting transfers between devices  33.2 us (54%)
  Pallas kernels  15.7 us (25%)
  waiting for transfers between devices  12.1 us (20%)
    ppermute x14, starting transfers between devices, swap(): lax.ppermute(values, axis, pairs_apart(lax.axis_size(axis), distance))  27.4 us
    pallas_call x5, Pallas kernels, run(): pl.pallas_call(kernel, out_shape=shapes, in_specs=[pl.BlockSpec(memory_sp...  15.7 us
    ppermute x14, waiting for transfers between devices, swap(): lax.ppermute(values, axis, pairs_apart(lax.axis_size(axis), distance))  11.3 us
    ppermute x1, starting transfers between devices, per_device(): lax.ppermute(one, 'gz', z_one)  3.09 us
  transfers between devices with their start and end apart: 19, of which 7 were waited for; matrix products, arithmetic and copies ran while one was open for 0% of the time, Pallas kernels for 2%

profile of v8, /device:TPU:0, one launch (start us, length us, event | category | flops | bytes accessed | tf_op | source)
XLA Modules:
  0.0 61.4 jit_solution(8874013698311846499)
XLA Ops:
  0.0 0.1 pad_add_fusion.where_ref
  0.1 1.4 %shard_map.17 = (f32[8,4,16,128]{3,2,1,0:T(8,128)S(1)}, f32[8,4,8,128]{3,2,1,0:T(8,128)S(1)}, f32[8,4,8,128]{3,2,1,0:T(8,128)S(1)}) custom-call(s32[2]{0:T(128)S(1)} %pad_add_fusion.where_ref, f32[8,16,512]{2,1,0:T(8,128)} %charges_ref.1), custom_call_target="tpu_custom_call" | custom-call | tf_op jit(solution)/shard_map/pallas_call | solution.py:524
  1.5 3.1 %collective-permute-start = (f32[8,4,8,128]{3,2,1,0:T(8,128)S(1)}, f32[8,4,8,128]{3,2,1,0:T(8,128)S(1)}, u32[]{:S(2)}, u32[]{:S(2)}) collective-permute-start(f32[8,4,8,128]{3,2,1,0:T(8,128)S(1)} %get-tuple-element.14), channel_id=1, source_target_pairs={{0,1},{1,0},{2,3},{3,2},{4,5},{5,4},{6,7},{7,6},{8,9},{9,8},{10,11... | collective-permute-start | bytes 393224 | tf_op jit(solution)/shard_map/ppermute | solution.py:590
  4.6 0.7 %collective-permute-start.1 = (f32[8,4,8,128]{3,2,1,0:T(8,128)S(1)}, f32[8,4,8,128]{3,2,1,0:T(8,128)S(1)}, u32[]{:S(2)}, u32[]{:S(2)}) collective-permute-start(f32[8,4,8,128]{3,2,1,0:T(8,128)S(1)} %get-tuple-element.15), channel_id=1, source_target_pairs={{1,2},{2,1},{5,6},{6,5},{9,10},{10,9},{13,14},{14,13},{17,18},{18,... | collective-permute-start | bytes 393224 | tf_op jit(solution)/shard_map/ppermute | solution.py:590
  5.2 0.7 %collective-permute-start.4 = (f32[8,16,512]{2,1,0:T(8,128)}, f32[8,16,512]{2,1,0:T(8,128)S(1)}, u32[]{:S(2)}, u32[]{:S(2)}) collective-permute-start(f32[8,16,512]{2,1,0:T(8,128)} %charges_ref.1), channel_id=1, source_target_pairs={{4,8},{8,4},{5,9},{9,5},{6,10},{10,6},{7,11},{11,7},{20,24},{24,20... | collective-permute-start | bytes 786440 | tf_op jit(solution)/shard_map/ppermute | solution.py:576
  5.9 0.7 %collective-permute-start.5 = (f32[8,4,8,128]{3,2,1,0:T(8,128)S(1)}, f32[8,4,8,128]{3,2,1,0:T(8,128)S(1)}, u32[]{:S(2)}, u32[]{:S(2)}) collective-permute-start(f32[8,4,8,128]{3,2,1,0:T(8,128)S(1)} %get-tuple-element.14), channel_id=1, source_target_pairs={{4,9},{5,8},{6,11},{7,10},{8,5},{9,4},{10,7},{11,6},{20,25},{21,24... | collective-permute-start | bytes 393224 | tf_op jit(solution)/shard_map/ppermute | solution.py:587
  6.6 0.7 %collective-permute-start.6 = (f32[8,4,8,128]{3,2,1,0:T(8,128)S(1)}, f32[8,4,8,128]{3,2,1,0:T(8,128)S(1)}, u32[]{:S(2)}, u32[]{:S(2)}) collective-permute-start(f32[8,4,8,128]{3,2,1,0:T(8,128)S(1)} %get-tuple-element.15), channel_id=1, source_target_pairs={{5,10},{6,9},{9,6},{10,5},{21,26},{22,25},{25,22},{26,21}} | collective-permute-start | bytes 393224 | tf_op jit(solution)/shard_map/ppermute | solution.py:588
  7.3 0.8 %collective-permute-done = f32[8,4,8,128]{3,2,1,0:T(8,128)S(1)} collective-permute-done((f32[8,4,8,128]{3,2,1,0:T(8,128)S(1)}, f32[8,4,8,128]{3,2,1,0:T(8,128)S(1)}, u32[]{:S(2)}, u32[]{:S(2)}) %collective-permute-start) | collective-permute-done | bytes 131104 | tf_op jit(solution)/shard_map/ppermute | solution.py:590
  8.1 7.2 %collective-permute-start.2 = (f32[8,4,16,128]{3,2,1,0:T(8,128)S(1)}, f32[8,4,16,128]{3,2,1,0:T(8,128)S(1)}, u32[]{:S(2)}, u32[]{:S(2)}) collective-permute-start(f32[8,4,16,128]{3,2,1,0:T(8,128)S(1)} %get-tuple-element.13.mid_ref), channel_id=1, source_target_pairs={{0,4},{4,0},{8,12},{12,8},{1,5},{5,1},{9,13},{13,9},{2,6},{6,2},{1... | collective-permute-start | bytes 786440 | tf_op jit(solution)/shard_map/ppermute | solution.py:555
  15.3 0.0 collective-permute-done.1
  15.4 0.1 collective-permute-start.3
  15.5 0.0 collective-permute-done.5
  15.5 0.0 collective-permute-done.6
  15.5 0.0 collective-permute-done.4.charges_ref
  15.5 1.0 %shard_map.18.two_ref = f32[8,4,16,128]{3,2,1,0:T(8,128)S(1)} custom-call(s32[2]{0:T(128)S(1)} %pad_add_fusion.where_ref, f32[8,16,512]{2,1,0:T(8,128)S(1)} %collective-permute-done.4.charges_ref), custom_call_target="tpu_custom_call" | custom-call | tf_op jit(solution)/shard_map/pallas_call | solution.py:524
  16.5 0.0 collective-permute-done.2.one_ref
  16.5 0.4 collective-permute-done.3.one_rim_ref
  17.0 2.5 %shard_map.19 = (f32[24,4,4,8,128]{4,3,2,1,0:T(8,128)S(1)}, f32[24,4,4,8,128]{4,3,2,1,0:T(8,128)S(1)}, f32[4,2,8,128]{3,2,1,0:T(8,128)S(1)}) custom-call(s32[2]{0:T(128)S(1)} %pad_add_fusion.where_ref, f32[8,4,16,128]{3,2,1,0:T(8,128)S(1)} %get-tuple-element.13.mid_ref, f32[8,4,16,128]{3,2,1,0:T(8,128)S(1)} %pad_maximum_fusion.mid_rim_ref, ...), custom_call_target="tpu_custom_call" | custom-call | tf_op jit(solution)/shard_map/pallas_call | solution.py:524
  19.5 1.9 %collective-permute-start.9 = (f32[1,4,2,8,128]{4,3,2,1,0:T(8,128)S(1)}, f32[1,4,2,8,128]{4,3,2,1,0:T(8,128)S(1)}, u32[]{:S(2)}, u32[]{:S(2)}) collective-permute-start(f32[1,4,2,8,128]{4,3,2,1,0:T(8,128)S(1)} %bitcast.6), channel_id=1, source_target_pairs={{0,1},{1,0},{2,3},{3,2},{4,5},{5,4},{6,7},{7,6},{8,9},{9,8},{10,11... | collective-permute-start | bytes 98312 | tf_op jit(solution)/shard_map/ppermute | solution.py:555
  21.3 1.0 %collective-permute-start.8 = (f32[1,4,2,8,128]{4,3,2,1,0:T(8,128)S(1)}, f32[1,4,2,8,128]{4,3,2,1,0:T(8,128)S(1)}, u32[]{:S(2)}, u32[]{:S(2)}) collective-permute-start(f32[1,4,2,8,128]{4,3,2,1,0:T(8,128)S(1)} %bitcast.7), channel_id=1, source_target_pairs={{0,2},{1,3},{2,0},{3,1},{4,6},{5,7},{6,4},{7,5},{8,10},{9,11},{10,... | collective-permute-start | bytes 98312 | tf_op jit(solution)/shard_map/ppermute | solution.py:555
  22.3 1.6 %collective-permute-start.7 = (f32[1,4,2,8,128]{4,3,2,1,0:T(8,128)S(1)}, f32[1,4,2,8,128]{4,3,2,1,0:T(8,128)S(1)}, u32[]{:S(2)}, u32[]{:S(2)}) collective-permute-start(f32[1,4,2,8,128]{4,3,2,1,0:T(8,128)S(1)} %bitcast.8), channel_id=1, source_target_pairs={{0,3},{1,2},{2,1},{3,0},{4,7},{5,6},{6,5},{7,4},{8,11},{9,10},{10,... | collective-permute-start | bytes 98312 | tf_op jit(solution)/shard_map/ppermute | solution.py:555
  23.9 0.0 collective-permute-done.9
  23.9 4.4 %collective-permute-start.11 = (f32[2,4,2,8,128]{4,3,2,1,0:T(8,128)S(1)}, f32[2,4,2,8,128]{4,3,2,1,0:T(8,128)S(1)}, u32[]{:S(2)}, u32[]{:S(2)}) collective-permute-start(f32[2,4,2,8,128]{4,3,2,1,0:T(8,128)S(1)} %pad_maximum_fusion.3), channel_id=1, source_target_pairs={{0,8},{4,12},{8,0},{12,4},{1,9},{5,13},{9,1},{13,5},{2,10},{6,14},... | collective-permute-start | bytes 196616 | tf_op jit(solution)/shard_map/ppermute | solution.py:555
  28.3 0.0 collective-permute-done.8
  28.4 0.0 collective-permute-done.7
  28.4 3.3 %collective-permute-start.10 = (f32[2,4,2,8,128]{4,3,2,1,0:T(8,128)S(1)}, f32[2,4,2,8,128]{4,3,2,1,0:T(8,128)S(1)}, u32[]{:S(2)}, u32[]{:S(2)}) collective-permute-start(f32[2,4,2,8,128]{4,3,2,1,0:T(8,128)S(1)} %pad_maximum_fusion.2), channel_id=1, source_target_pairs={{0,8},{4,12},{8,0},{12,4},{1,9},{5,13},{9,1},{13,5},{2,10},{6,14},... | collective-permute-start | bytes 196616 | tf_op jit(solution)/shard_map/ppermute | solution.py:555
  31.7 2.6 %collective-permute-done.10 = f32[2,4,2,8,128]{4,3,2,1,0:T(8,128)S(1)} collective-permute-done((f32[2,4,2,8,128]{4,3,2,1,0:T(8,128)S(1)}, f32[2,4,2,8,128]{4,3,2,1,0:T(8,128)S(1)}, u32[]{:S(2)}, u32[]{:S(2)}) %collective-permute-start.10) | collective-permute-done | bytes 65568 | tf_op jit(solution)/shard_map/ppermute | solution.py:555
  34.2 0.0 collective-permute-done.11
  34.3 0.1 collective-permute-start.12
  34.3 1.5 %collective-permute-done.12.refs_1_ = f32[8,4,2,8,128]{4,3,2,1,0:T(8,128)S(1)} collective-permute-done((f32[8,4,2,8,128]{4,3,2,1,0:T(8,128)S(1)}, f32[8,4,2,8,128]{4,3,2,1,0:T(8,128)S(1)}, u32[]{:S(2)}, u32[]{:S(2)}) %collective-permute-start.12) | collective-permute-done | bytes 262176 | tf_op jit(solution)/shard_map/ppermute | solution.py:555
  35.9 6.0 %shard_map.20 = (f32[24,4,4,8,128]{4,3,2,1,0:T(8,128)S(1)}, f32[4,2,8,128]{3,2,1,0:T(8,128)S(1)}) custom-call(s32[2]{0:T(128)S(1)} %pad_add_fusion.where_ref, f32[8,4,2,8,128]{4,3,2,1,0:T(8,128)S(1)} %constant_dynamic-update-slice_fusion.refs_0_, f32[8,4,2,8,128]{4,3,2,1,0:T(8,128)S(1)} %collective-permute-done.12.refs_1_, ...), custom_call_target="tpu_custom_call" | custom-call | tf_op jit(solution)/shard_map/pallas_call | solution.py:524
  41.8 0.2 collective-permute-start.15
  42.1 2.8 %collective-permute-start.14 = (f32[1,4,2,8,128]{4,3,2,1,0:T(8,128)S(1)}, f32[1,4,2,8,128]{4,3,2,1,0:T(8,128)S(1)}, u32[]{:S(2)}, u32[]{:S(2)}) collective-permute-start(f32[1,4,2,8,128]{4,3,2,1,0:T(8,128)S(1)} %bitcast.11), channel_id=1, source_target_pairs={{0,2},{1,3},{2,0},{3,1},{4,6},{5,7},{6,4},{7,5},{8,10},{9,11},{10,... | collective-permute-start | bytes 98312 | tf_op jit(solution)/shard_map/ppermute | solution.py:555
  44.9 1.4 %collective-permute-start.13 = (f32[1,4,2,8,128]{4,3,2,1,0:T(8,128)S(1)}, f32[1,4,2,8,128]{4,3,2,1,0:T(8,128)S(1)}, u32[]{:S(2)}, u32[]{:S(2)}) collective-permute-start(f32[1,4,2,8,128]{4,3,2,1,0:T(8,128)S(1)} %bitcast.12), channel_id=1, source_target_pairs={{0,3},{1,2},{2,1},{3,0},{4,7},{5,6},{6,5},{7,4},{8,11},{9,10},{10,... | collective-permute-start | bytes 98312 | tf_op jit(solution)/shard_map/ppermute | solution.py:555
  46.3 0.0 collective-permute-done.15
  46.3 1.7 %collective-permute-start.17 = (f32[2,4,2,8,128]{4,3,2,1,0:T(8,128)S(1)}, f32[2,4,2,8,128]{4,3,2,1,0:T(8,128)S(1)}, u32[]{:S(2)}, u32[]{:S(2)}) collective-permute-start(f32[2,4,2,8,128]{4,3,2,1,0:T(8,128)S(1)} %pad_maximum_fusion.5), channel_id=1, source_target_pairs={{0,8},{4,12},{8,0},{12,4},{1,9},{5,13},{9,1},{13,5},{2,10},{6,14},... | collective-permute-start | bytes 196616 | tf_op jit(solution)/shard_map/ppermute | solution.py:555
  48.0 0.0 collective-permute-done.14
  48.0 2.6 %collective-permute-done.13 = f32[1,4,2,8,128]{4,3,2,1,0:T(8,128)S(1)} collective-permute-done((f32[1,4,2,8,128]{4,3,2,1,0:T(8,128)S(1)}, f32[1,4,2,8,128]{4,3,2,1,0:T(8,128)S(1)}, u32[]{:S(2)}, u32[]{:S(2)}) %collective-permute-start.13) | collective-permute-done | bytes 32800 | tf_op jit(solution)/shard_map/ppermute | solution.py:555
  50.6 1.6 %collective-permute-start.16 = (f32[2,4,2,8,128]{4,3,2,1,0:T(8,128)S(1)}, f32[2,4,2,8,128]{4,3,2,1,0:T(8,128)S(1)}, u32[]{:S(2)}, u32[]{:S(2)}) collective-permute-start(f32[2,4,2,8,128]{4,3,2,1,0:T(8,128)S(1)} %pad_maximum_fusion.4), channel_id=1, source_target_pairs={{0,8},{4,12},{8,0},{12,4},{1,9},{5,13},{9,1},{13,5},{2,10},{6,14},... | collective-permute-start | bytes 196616 | tf_op jit(solution)/shard_map/ppermute | solution.py:555
  52.2 2.6 %collective-permute-done.16 = f32[2,4,2,8,128]{4,3,2,1,0:T(8,128)S(1)} collective-permute-done((f32[2,4,2,8,128]{4,3,2,1,0:T(8,128)S(1)}, f32[2,4,2,8,128]{4,3,2,1,0:T(8,128)S(1)}, u32[]{:S(2)}, u32[]{:S(2)}) %collective-permute-start.16) | collective-permute-done | bytes 65568 | tf_op jit(solution)/shard_map/ppermute | solution.py:555
  54.9 0.0 collective-permute-done.17
  54.9 0.1 collective-permute-start.18
  55.0 1.5 %collective-permute-done.18.refs_1_ = f32[8,4,2,8,128]{4,3,2,1,0:T(8,128)S(1)} collective-permute-done((f32[8,4,2,8,128]{4,3,2,1,0:T(8,128)S(1)}, f32[8,4,2,8,128]{4,3,2,1,0:T(8,128)S(1)}, u32[]{:S(2)}, u32[]{:S(2)}) %collective-permute-start.18) | collective-permute-done | bytes 262176 | tf_op jit(solution)/shard_map/ppermute | solution.py:555
  56.5 4.9 %shard_map.21 = f32[8,16,512]{2,1,0:T(8,128)} custom-call(s32[2]{0:T(128)S(1)} %pad_add_fusion.where_ref, f32[8,4,2,8,128]{4,3,2,1,0:T(8,128)S(1)} %constant_dynamic-update-slice_fusion.6.refs_0_, f32[8,4,2,8,128]{4,3,2,1,0:T(8,128)S(1)} %collective-permute-done.18.refs_1_, f32[24,4,4,8,128]{4,3,2,1,0:T(8,128)S(1)} %get-tuple-element.20.refs_2_, ...), custom_call_target="tpu_custom_call" | custom-call | tf_op jit(solution)/shard_map/pallas_call | solution.py:524
  (20 shorter events, 0.2 us)
Async XLA Ops:
  1.5 6.6 %collective-permute-start = (f32[8,4,8,128]{3,2,1,0:T(8,128)S(1)}, f32[8,4,8,128]{3,2,1,0:T(8,128)S(1)}, u32[]{:S(2)}, u32[]{:S(2)}) collective-permute-start(f32[8,4,8,128]{3,2,1,0:T(8,128)S(1)} %get-tuple-element.14), channel_id=1, source_target_pairs={{0,1},{1,0},{2,3},{3,2},{4,5},{5,4},{6,7},{7,6},{8,9},{9,8},{10,11... | collective-permute-start | bytes 393224 | tf_op jit(solution)/shard_map/ppermute | solution.py:590
  4.6 10.7 %collective-permute-start.1 = (f32[8,4,8,128]{3,2,1,0:T(8,128)S(1)}, f32[8,4,8,128]{3,2,1,0:T(8,128)S(1)}, u32[]{:S(2)}, u32[]{:S(2)}) collective-permute-start(f32[8,4,8,128]{3,2,1,0:T(8,128)S(1)} %get-tuple-element.15), channel_id=1, source_target_pairs={{1,2},{2,1},{5,6},{6,5},{9,10},{10,9},{13,14},{14,13},{17,18},{18,... | collective-permute-start | bytes 393224 | tf_op jit(solution)/shard_map/ppermute | solution.py:590
  5.2 10.3 %collective-permute-start.4 = (f32[8,16,512]{2,1,0:T(8,128)}, f32[8,16,512]{2,1,0:T(8,128)S(1)}, u32[]{:S(2)}, u32[]{:S(2)}) collective-permute-start(f32[8,16,512]{2,1,0:T(8,128)} %charges_ref.1), channel_id=1, source_target_pairs={{4,8},{8,4},{5,9},{9,5},{6,10},{10,6},{7,11},{11,7},{20,24},{24,20... | collective-permute-start | bytes 786440 | tf_op jit(solution)/shard_map/ppermute | solution.py:576
  5.9 9.5 %collective-permute-start.5 = (f32[8,4,8,128]{3,2,1,0:T(8,128)S(1)}, f32[8,4,8,128]{3,2,1,0:T(8,128)S(1)}, u32[]{:S(2)}, u32[]{:S(2)}) collective-permute-start(f32[8,4,8,128]{3,2,1,0:T(8,128)S(1)} %get-tuple-element.14), channel_id=1, source_target_pairs={{4,9},{5,8},{6,11},{7,10},{8,5},{9,4},{10,7},{11,6},{20,25},{21,24... | collective-permute-start | bytes 393224 | tf_op jit(solution)/shard_map/ppermute | solution.py:587
  6.6 8.9 %collective-permute-start.6 = (f32[8,4,8,128]{3,2,1,0:T(8,128)S(1)}, f32[8,4,8,128]{3,2,1,0:T(8,128)S(1)}, u32[]{:S(2)}, u32[]{:S(2)}) collective-permute-start(f32[8,4,8,128]{3,2,1,0:T(8,128)S(1)} %get-tuple-element.15), channel_id=1, source_target_pairs={{5,10},{6,9},{9,6},{10,5},{21,26},{22,25},{25,22},{26,21}} | collective-permute-start | bytes 393224 | tf_op jit(solution)/shard_map/ppermute | solution.py:588
  8.1 8.5 %collective-permute-start.2 = (f32[8,4,16,128]{3,2,1,0:T(8,128)S(1)}, f32[8,4,16,128]{3,2,1,0:T(8,128)S(1)}, u32[]{:S(2)}, u32[]{:S(2)}) collective-permute-start(f32[8,4,16,128]{3,2,1,0:T(8,128)S(1)} %get-tuple-element.13.mid_ref), channel_id=1, source_target_pairs={{0,4},{4,0},{8,12},{12,8},{1,5},{5,1},{9,13},{13,9},{2,6},{6,2},{1... | collective-permute-start | bytes 786440 | tf_op jit(solution)/shard_map/ppermute | solution.py:555
  15.4 1.6 %collective-permute-start.3 = (f32[8,4,16,128]{3,2,1,0:T(8,128)S(1)}, f32[8,4,16,128]{3,2,1,0:T(8,128)S(1)}, u32[]{:S(2)}, u32[]{:S(2)}) collective-permute-start(f32[8,4,16,128]{3,2,1,0:T(8,128)S(1)} %pad_maximum_fusion.mid_rim_ref), channel_id=1, source_target_pairs={{0,4},{4,0},{8,12},{12,8},{1,5},{5,1},{9,13},{13,9},{2,6},{6,2},{1... | collective-permute-start | bytes 786440 | tf_op jit(solution)/shard_map/ppermute | solution.py:555
  19.5 4.5 %collective-permute-start.9 = (f32[1,4,2,8,128]{4,3,2,1,0:T(8,128)S(1)}, f32[1,4,2,8,128]{4,3,2,1,0:T(8,128)S(1)}, u32[]{:S(2)}, u32[]{:S(2)}) collective-permute-start(f32[1,4,2,8,128]{4,3,2,1,0:T(8,128)S(1)} %bitcast.6), channel_id=1, source_target_pairs={{0,1},{1,0},{2,3},{3,2},{4,5},{5,4},{6,7},{7,6},{8,9},{9,8},{10,11... | collective-permute-start | bytes 98312 | tf_op jit(solution)/shard_map/ppermute | solution.py:555
  21.3 7.0 %collective-permute-start.8 = (f32[1,4,2,8,128]{4,3,2,1,0:T(8,128)S(1)}, f32[1,4,2,8,128]{4,3,2,1,0:T(8,128)S(1)}, u32[]{:S(2)}, u32[]{:S(2)}) collective-permute-start(f32[1,4,2,8,128]{4,3,2,1,0:T(8,128)S(1)} %bitcast.7), channel_id=1, source_target_pairs={{0,2},{1,3},{2,0},{3,1},{4,6},{5,7},{6,4},{7,5},{8,10},{9,11},{10,... | collective-permute-start | bytes 98312 | tf_op jit(solution)/shard_map/ppermute | solution.py:555
  22.3 6.0 %collective-permute-start.7 = (f32[1,4,2,8,128]{4,3,2,1,0:T(8,128)S(1)}, f32[1,4,2,8,128]{4,3,2,1,0:T(8,128)S(1)}, u32[]{:S(2)}, u32[]{:S(2)}) collective-permute-start(f32[1,4,2,8,128]{4,3,2,1,0:T(8,128)S(1)} %bitcast.8), channel_id=1, source_target_pairs={{0,3},{1,2},{2,1},{3,0},{4,7},{5,6},{6,5},{7,4},{8,11},{9,10},{10,... | collective-permute-start | bytes 98312 | tf_op jit(solution)/shard_map/ppermute | solution.py:555
  23.9 10.3 %collective-permute-start.11 = (f32[2,4,2,8,128]{4,3,2,1,0:T(8,128)S(1)}, f32[2,4,2,8,128]{4,3,2,1,0:T(8,128)S(1)}, u32[]{:S(2)}, u32[]{:S(2)}) collective-permute-start(f32[2,4,2,8,128]{4,3,2,1,0:T(8,128)S(1)} %pad_maximum_fusion.3), channel_id=1, source_target_pairs={{0,8},{4,12},{8,0},{12,4},{1,9},{5,13},{9,1},{13,5},{2,10},{6,14},... | collective-permute-start | bytes 196616 | tf_op jit(solution)/shard_map/ppermute | solution.py:555
  28.4 5.9 %collective-permute-start.10 = (f32[2,4,2,8,128]{4,3,2,1,0:T(8,128)S(1)}, f32[2,4,2,8,128]{4,3,2,1,0:T(8,128)S(1)}, u32[]{:S(2)}, u32[]{:S(2)}) collective-permute-start(f32[2,4,2,8,128]{4,3,2,1,0:T(8,128)S(1)} %pad_maximum_fusion.2), channel_id=1, source_target_pairs={{0,8},{4,12},{8,0},{12,4},{1,9},{5,13},{9,1},{13,5},{2,10},{6,14},... | collective-permute-start | bytes 196616 | tf_op jit(solution)/shard_map/ppermute | solution.py:555
  34.3 1.6 %collective-permute-start.12 = (f32[8,4,2,8,128]{4,3,2,1,0:T(8,128)S(1)}, f32[8,4,2,8,128]{4,3,2,1,0:T(8,128)S(1)}, u32[]{:S(2)}, u32[]{:S(2)}) collective-permute-start(f32[8,4,2,8,128]{4,3,2,1,0:T(8,128)S(1)} %constant_dynamic-update-slice_fusion.refs_0_), channel_id=1, source_target_pairs={{0,4},{4,0},{8,12},{12,8},{1,5},{5,1},{9,13},{13,9},{2,6},{6,2},{1... | collective-permute-start | bytes 786440 | tf_op jit(solution)/shard_map/ppermute | solution.py:555
  41.8 4.5 %collective-permute-start.15 = (f32[1,4,2,8,128]{4,3,2,1,0:T(8,128)S(1)}, f32[1,4,2,8,128]{4,3,2,1,0:T(8,128)S(1)}, u32[]{:S(2)}, u32[]{:S(2)}) collective-permute-start(f32[1,4,2,8,128]{4,3,2,1,0:T(8,128)S(1)} %bitcast.10), channel_id=1, source_target_pairs={{0,1},{1,0},{2,3},{3,2},{4,5},{5,4},{6,7},{7,6},{8,9},{9,8},{10,11... | collective-permute-start | bytes 98312 | tf_op jit(solution)/shard_map/ppermute | solution.py:555
  42.1 6.0 %collective-permute-start.14 = (f32[1,4,2,8,128]{4,3,2,1,0:T(8,128)S(1)}, f32[1,4,2,8,128]{4,3,2,1,0:T(8,128)S(1)}, u32[]{:S(2)}, u32[]{:S(2)}) collective-permute-start(f32[1,4,2,8,128]{4,3,2,1,0:T(8,128)S(1)} %bitcast.11), channel_id=1, source_target_pairs={{0,2},{1,3},{2,0},{3,1},{4,6},{5,7},{6,4},{7,5},{8,10},{9,11},{10,... | collective-permute-start | bytes 98312 | tf_op jit(solution)/shard_map/ppermute | solution.py:555
  44.9 5.7 %collective-permute-start.13 = (f32[1,4,2,8,128]{4,3,2,1,0:T(8,128)S(1)}, f32[1,4,2,8,128]{4,3,2,1,0:T(8,128)S(1)}, u32[]{:S(2)}, u32[]{:S(2)}) collective-permute-start(f32[1,4,2,8,128]{4,3,2,1,0:T(8,128)S(1)} %bitcast.12), channel_id=1, source_target_pairs={{0,3},{1,2},{2,1},{3,0},{4,7},{5,6},{6,5},{7,4},{8,11},{9,10},{10,... | collective-permute-start | bytes 98312 | tf_op jit(solution)/shard_map/ppermute | solution.py:555
  46.3 8.6 %collective-permute-start.17 = (f32[2,4,2,8,128]{4,3,2,1,0:T(8,128)S(1)}, f32[2,4,2,8,128]{4,3,2,1,0:T(8,128)S(1)}, u32[]{:S(2)}, u32[]{:S(2)}) collective-permute-start(f32[2,4,2,8,128]{4,3,2,1,0:T(8,128)S(1)} %pad_maximum_fusion.5), channel_id=1, source_target_pairs={{0,8},{4,12},{8,0},{12,4},{1,9},{5,13},{9,1},{13,5},{2,10},{6,14},... | collective-permute-start | bytes 196616 | tf_op jit(solution)/shard_map/ppermute | solution.py:555
  50.6 4.3 %collective-permute-start.16 = (f32[2,4,2,8,128]{4,3,2,1,0:T(8,128)S(1)}, f32[2,4,2,8,128]{4,3,2,1,0:T(8,128)S(1)}, u32[]{:S(2)}, u32[]{:S(2)}) collective-permute-start(f32[2,4,2,8,128]{4,3,2,1,0:T(8,128)S(1)} %pad_maximum_fusion.4), channel_id=1, source_target_pairs={{0,8},{4,12},{8,0},{12,4},{1,9},{5,13},{9,1},{13,5},{2,10},{6,14},... | collective-permute-start | bytes 196616 | tf_op jit(solution)/shard_map/ppermute | solution.py:555
  54.9 1.6 %collective-permute-start.18 = (f32[8,4,2,8,128]{4,3,2,1,0:T(8,128)S(1)}, f32[8,4,2,8,128]{4,3,2,1,0:T(8,128)S(1)}, u32[]{:S(2)}, u32[]{:S(2)}) collective-permute-start(f32[8,4,2,8,128]{4,3,2,1,0:T(8,128)S(1)} %constant_dynamic-update-slice_fusion.6.refs_0_), channel_id=1, source_target_pairs={{0,4},{4,0},{8,12},{12,8},{1,5},{5,1},{9,13},{13,9},{2,6},{6,2},{1... | collective-permute-start | bytes 786440 | tf_op jit(solution)/shard_map/ppermute | solution.py:555

commit v9 on v7

--- a/solution.py
+++ b/solution.py
@@ -130,6 +130,17 @@
         ]
 
 
+class Held:
+    def __init__(self, rows, zero_at=()):
+        self.tiles = {(x, 0, 0): jnp.zeros((rows, LANES), jnp.float32) for x in zero_at}
+
+    def __getitem__(self, place):
+        return self.tiles[place]
+
+    def __setitem__(self, place, tile):
+        self.tiles[place] = tile
+
+
 def add_planes(one, other):
     return [[a + b for a, b in zip(l, m)] for l, m in zip(one, other)]
 
@@ -186,25 +197,32 @@
 def coarse_grids(count_x, count_z):
     rows = count_z * BRICK_Z // 4
     shapes = []
-    for planes, count in ((4 * count_x + 2 * PAD, 2), (2 * count_x + 2 * PAD_2, 1), (count_x + 2, 1)):
+    for planes, count in ((4 * count_x + 2 * PAD, 2), (2 * count_x + 2 * PAD_2, 1)):
         shapes += [pltpu.VMEM((planes, count, count, rows, LANES), jnp.float32)] * 5
     return shapes
 
 
 def coarse_solve(count_x, count_z, where_ref, pieces, grids):
-    (ua1, ub1, ga1, gb1, b1), (ua2, ub2, ga2, gb2, b2), (ua3, ub3, ga3, gb3, b3) = (
-        grids[0:5],
-        grids[5:10],
-        grids[10:15],
-    )
+    ua1, ub1, ga1, gb1, b1 = grids[0:5]
+    kept_2 = grids[5]
     size_1, size_2, size_3 = 4 * count_x, 2 * count_x, count_x
-    for refs, pad, size in (
-        ((ua1, ub1, ga1, gb1, b1), PAD, size_1),
-        ((ua2, ub2, ga2, gb2), PAD_2, size_2),
-        ((ua3, ub3, ga3, gb3), 1, size_3),
-    ):
-        for ref in refs:
-            zero_planes(ref, list(range(pad)) + list(range(pad + size, pad + size + pad)))
+    rows = b1.shape[3]
+
+    def ends(pad, size):
+        return list(range(pad)) + list(range(pad + size, pad + size + pad))
+
+    for ref in (ua1, ub1, ga1, gb1, b1):
+        zero_planes(ref, ends(PAD, size_1))
+    zero_planes(kept_2, ends(PAD_2, size_2))
+    if size_2 <= 8:
+        step_2 = size_2
+        ua2, ub2, ga2, gb2, b2 = (Held(rows, ends(PAD_2, size_2)) for _ in range(5))
+    else:
+        step_2 = 8
+        ua2, ub2, ga2, gb2, b2 = grids[5:10]
+        for ref in (ub2, ga2, gb2):
+            zero_planes(ref, ends(PAD_2, size_2))
+    ua3, ub3, ga3, gb3, b3 = (Held(rows, ends(1, size_3)) for _ in range(5))
     third = 1.0 / 30.0
 
     at_x, at_z = where_ref[0], where_ref[1]
@@ -220,8 +238,7 @@
                     even.append(jnp.where(first, one, pltpu.roll(two, 4, 0)))
                     odd.append(jnp.where(first, pltpu.roll(one, 4, 0), two))
                 plane.append([jnp.concatenate(even, axis=0), jnp.concatenate(odd, axis=0)])
-            store_plane(b1, x + i, plane)
-            LEVEL_1.put(ub1, gb1, x + i, plane)
+            LEVEL_1.put(b1, gb1, x + i, plane)
 
     if len(pieces) == 1:
 
@@ -241,7 +258,7 @@
     def sweep(level, u_in, g_in, u_out, g_out, b):
         return lambda x: level.put(u_out, g_out, x, level.sweep(u_in, g_in, b, x, third))
 
-    each(PAD, PAD + size_1, sweep(LEVEL_1, ub1, gb1, ua1, ga1, b1), 16)
+    each(PAD, PAD + size_1, sweep(LEVEL_1, b1, gb1, ua1, ga1, b1), 16)
 
     def restrict_1(x):
         fine = PAD + 2 * x
@@ -252,9 +269,9 @@
         store_plane(b2, PAD_2 + x, plane)
         LEVEL_2.put(ub2, gb2, PAD_2 + x, plane)
 
-    each(0, size_2, restrict_1, 8)
+    each(0, size_2, restrict_1, step_2)
     all_2 = (PAD_2, PAD_2 + size_2)
-    each(*all_2, sweep(LEVEL_2, ub2, gb2, ua2, ga2, b2), 8)
+    each(*all_2, sweep(LEVEL_2, ub2, gb2, ua2, ga2, b2), step_2)
 
     def restrict_2(x):
         fine = PAD_2 + 2 * x
@@ -265,10 +282,10 @@
         store_plane(b3, 1 + x, plane)
         LEVEL_3.put(ub3, gb3, 1 + x, plane)
 
-    each(0, size_3, restrict_2, 4)
+    each(0, size_3, restrict_2, size_3)
     now, later = (ub3, gb3), (ua3, ga3)
     for _ in range(COARSE_SWEEPS - 1):
-        each(1, 1 + size_3, sweep(LEVEL_3, *now, *later, b3), 4)
+        each(1, 1 + size_3, sweep(LEVEL_3, *now, *later, b3), size_3)
         now, later = later, now
 
     def prolong_3(x):
@@ -276,10 +293,14 @@
             fine = PAD_2 + 2 * x + d
             LEVEL_2.put(ua2, ga2, fine, [[ua2[fine, 0, 0] + now[0][1 + x, 0, 0]]])
 
-    each(0, size_3, prolong_3, 4)
-    each(*all_2, sweep(LEVEL_2, ua2, ga2, ub2, gb2, b2), 8)
-    each(*all_2, sweep(LEVEL_2, ub2, gb2, ua2, ga2, b2), 8)
-    return ua1, ua2, b1
+    each(0, size_3, prolong_3, size_3)
+    each(*all_2, sweep(LEVEL_2, ua2, ga2, ub2, gb2, b2), step_2)
+
+    def last_sweep(x):
+        store_plane(kept_2, x, LEVEL_2.sweep(ub2, gb2, b2, x, third))
+
+    each(*all_2, last_sweep, step_2)
+    return ua1, kept_2, b1
 
 
 def coarse_finish(count_x, grids):
@@ -302,7 +323,11 @@
 
     each(0, size_2, prolong_2, 8)
     each(PAD, PAD + size_1, sweep(ua1, ga1, ub1, gb1), 16)
-    each(PAD, PAD + size_1, sweep(ub1, gb1, ua1, ga1), 16)
+
+    def last_sweep(x):
+        store_plane(ua1, x, LEVEL_1.sweep(ub1, gb1, b1, x, 1.0 / 30.0))
+
+    each(PAD, PAD + size_1, last_sweep, 16)
     return ua1
 
 
@@ -328,14 +353,14 @@
 
     each(1, 11, take, 5)
 
-    def sweep(u_in, g_in, u_out, g_out):
-        def body(i, weight):
-            NEAR_1.put(u_out, g_out, i, NEAR_1.sweep(u_in, g_in, b, i, weight))
-
-        return body
-
-    in_segments(2, 10, sweep(ua, ga, ub, gb), masks, 1.0 / 30.0, 4, PAD, BRICK_X // 2)
-    in_segments(3, 9, sweep(ub, gb, ua, ga), masks, 1.0 / 30.0, 4, PAD, BRICK_X // 2)
+    def sweep(i, weight):
+        NEAR_1.put(ub, gb, i, NEAR_1.sweep(ua, ga, b, i, weight))
+
+    def last_sweep(i, weight):
+        store_plane(ua, i, NEAR_1.sweep(ub, gb, b, i, weight))
+
+    in_segments(2, 10, sweep, masks, 1.0 / 30.0, 4, PAD, BRICK_X // 2)
+    in_segments(3, 9, last_sweep, masks, 1.0 / 30.0, 4, PAD, BRICK_X // 2)
     return ua
 
 
@@ -394,12 +419,13 @@
     each(0, BRICK_X // 2, body, BRICK_X // 2)
 
 
-def permuted(values, places):
-    shape = (values.shape[1], values.shape[1])
-    row, column = (lax.broadcasted_iota(jnp.int32, shape, d) for d in range(2))
-    matrix = places(row, column).astype(jnp.float32).astype(jnp.bfloat16)
-    total, rest = None, values
-    terms = []
+def places(size, joins):
+    row, column = (lax.broadcasted_iota(jnp.int32, (size, size), d) for d in range(2))
+    return joins(row, column).astype(jnp.float32).astype(jnp.bfloat16)
+
+
+def permuted(values, matrix):
+    rest, terms = values, []
     for _ in range(3):
         term = rest.astype(jnp.bfloat16)
         rest = rest - term.astype(jnp.float32)
@@ -410,8 +436,8 @@
 def lanes_kernel(where_ref, charges_ref, rows_ref, one_ref, two_ref):
     odd = where_ref[1] % 2
     width = charges_ref.shape[2]
-    flat = charges_ref[...].reshape(BRICK_X * BRICK_Z, width)
-    split = permuted(flat, lambda y, l: y == (l % LANES) * 4 + l // LANES)
+    matrix = places(width, lambda y, l: y == (l % LANES) * 4 + l // LANES)
+    split = permuted(charges_ref[...].reshape(BRICK_X * BRICK_Z, width), matrix)
     for p in range(4):
         tile = split[:, p * LANES : (p + 1) * LANES].reshape(BRICK_X, BRICK_Z, LANES)
         rows_ref[:, p] = tile
@@ -483,7 +509,7 @@
 
 def up_kernel(count_x, count_z, count_pieces, where_ref, *refs):
     pieces, refs = refs[:count_pieces], refs[count_pieces:]
-    u_ref, b_ref, out_ref, ga_ref, gb_ref, ua_ref, ub_ref, rows_ref, *refs = refs
+    u_ref, b_ref, out_ref, ga_ref, gb_ref, ua_ref, ub_ref, rows_ref, held_ref, semaphores, *refs = refs
     near, grids = refs[:5], refs[5:]
     masks = rim_masks(count_x, count_z, where_ref)
     coarse = coarse_solve(count_x, count_z, where_ref, pieces, grids)
@@ -497,26 +523,41 @@
             for p in range(4):
                 rows_ref[x - RIM, p, pl.ds(q, 4, stride=4), :] = plane[q][p][0:4]
 
-    each(RIM, RIM + BRICK_X, body, 2)
-    tiles = [rows_ref[:, p].reshape(BRICK_X * BRICK_Z, LANES) for p in range(4)]
-    whole = permuted(
-        jnp.concatenate(tiles, axis=1), lambda l, y: y == (l % LANES) * 4 + l // LANES
-    )
-    out_ref[...] = whole.reshape(out_ref.shape)
-
-
-def call(kernel, outputs, scratch):
+    width = out_ref.shape[2]
+    matrix = places(width, lambda l, y: y == (l % LANES) * 4 + l // LANES)
+    half = BRICK_X // 2
+    copies = []
+    for start in (0, half):
+        each(RIM + start, RIM + start + half, body, 2)
+        tiles = [
+            rows_ref[start : start + half, p].reshape(half * BRICK_Z, LANES) for p in range(4)
+        ]
+        whole = permuted(jnp.concatenate(tiles, axis=1), matrix)
+        planes = pl.ds(start, half)
+        held_ref[planes] = whole.reshape(half, BRICK_Z, width)
+        copies.append(
+            pltpu.make_async_copy(
+                held_ref.at[planes], out_ref.at[planes], semaphores.at[start // half]
+            )
+        )
+        copies[-1].start()
+    for copy in copies:
+        copy.wait()
+
+
+def call(kernel, outputs, scratch, far_out=False):
     shapes = [jax.ShapeDtypeStruct(shape, jnp.float32) for shape in outputs]
-    held = sum(4 * math.prod(shape.shape) for shape in scratch)
+    held = sum(4 * math.prod(shape.shape) for shape in scratch if hasattr(shape, "memory_space"))
 
     def run(where, *arrays):
         moved = sum(4 * math.prod(array.shape) for array in arrays + tuple(shapes))
+        inside = pl.BlockSpec(memory_space=pltpu.VMEM)
+        outside = pl.BlockSpec(memory_space=pltpu.HBM if far_out else pltpu.VMEM)
         return pl.pallas_call(
             kernel,
             out_shape=shapes,
-            in_specs=[pl.BlockSpec(memory_space=pltpu.SMEM)]
-            + [pl.BlockSpec(memory_space=pltpu.VMEM)] * len(arrays),
-            out_specs=[pl.BlockSpec(memory_space=pltpu.VMEM)] * len(shapes),
+            in_specs=[pl.BlockSpec(memory_space=pltpu.SMEM)] + [inside] * len(arrays),
+            out_specs=[outside] * len(shapes),
             scratch_shapes=scratch,
             compiler_params=pltpu.CompilerParams(vmem_limit_bytes=held + moved + SPARE_BYTES),
         )(where, *arrays)
@@ -531,14 +572,6 @@
 def pairs_shifted(count):
     pairs = [(i, i + 1) for i in range(1, count - 1, 2)]
     return pairs + [(target, source) for source, target in pairs]
-
-
-def across(pairs_x, pairs_z, count_z):
-    return [
-        (x_from * count_z + z_from, x_to * count_z + z_to)
-        for x_from, x_to in pairs_x
-        for z_from, z_to in pairs_z
-    ]
 
 
 def swap(axis, values, distance):
@@ -562,23 +595,15 @@
     at_x, at_z = lax.axis_index("gx"), lax.axis_index("gz")
     where = jnp.stack([at_x, at_z]).astype(jnp.int32)
     brick, rim = (BRICK_X, 4, BRICK_Z, LANES), (BRICK_X, 4, RIM, LANES)
+    held = pltpu.VMEM(charges.shape, jnp.float32)
     middle, one, two = call(lanes_kernel, [brick, rim, rim], [])(where, charges)
-    z_one = pairs_apart(count_z, 1)
-    z_two = pairs_shifted(count_z)
-    x_far = pairs_shifted(count_x)
+    x_far, z_two = pairs_shifted(count_x), pairs_shifted(count_z)
+    far = lax.ppermute(middle, "gx", x_far)
+    near = swap("gx", middle, 1)
+    one, two = swap("gz", one, 1), lax.ppermute(two, "gz", z_two)
     even = at_z % 2 == 0
-
-    def both_rims(from_one, from_two):
-        after, before = jnp.where(even, from_one, from_two), jnp.where(even, from_two, from_one)
-        return jnp.concatenate([after, before], axis=2)
-
-    far = lax.ppermute(middle, "gx", x_far)
-    far_rim = both_rims(
-        lax.ppermute(one, ("gx", "gz"), across(x_far, z_one, count_z)),
-        lax.ppermute(two, ("gx", "gz"), across(x_far, z_two, count_z)),
-    )
-    middle_rim = both_rims(lax.ppermute(one, "gz", z_one), lax.ppermute(two, "gz", z_two))
-    near = swap("gx", middle, 1)
+    middle_rim = jnp.concatenate([jnp.where(even, one, two), jnp.where(even, two, one)], axis=2)
+    far_rim = lax.ppermute(middle_rim, "gx", x_far)
     near_rim = swap("gx", middle_rim, 1)
 
     wide = (WIDE_X, 4, 4, 8, LANES)
@@ -604,7 +629,8 @@
     (potential,) = call(
         functools.partial(up_kernel, count_x, count_z, len(pieces)),
         [charges.shape],
-        [fine] * 4 + [rows_out] + [close] * 5 + grids,
+        [fine] * 4 + [rows_out, held, pltpu.SemaphoreType.DMA((2,))] + [close] * 5 + grids,
+        far_out=True,
     )(where, *pieces, u, b)
     return potential
 

time: 61.5 us -> 60.9 us (level)
  waiting for transfers between devices: 11.8 us -> 9.85 us
  starting transfers between devices: 33.8 us -> 35.1 us
    ppermute x14 -> x15, starting transfers between devices: 28.1 us -> 33.1 us  [swap(): lax.ppermute(values, axis, pairs_apart(lax.axis_size(axis), distance))]
    ppermute x4 -> x2, starting transfers between devices: 5.09 us -> 1.33 us  [the longest x1 0.68 us: per_device(): far_rim = lax.ppermute(middle_rim, 'gx', x_far)]
    ppermute x14 -> x15, waiting for transfers between devices: 11 us -> 9.84 us  [swap(): lax.ppermute(values, axis, pairs_apart(lax.axis_size(axis), distance))]
    ppermute x4 -> x2, waiting for transfers between devices: 0.79 us -> 0.01 us  [the longest x1 0.01 us: per_device(): far_rim = lax.ppermute(middle_rim, 'gx', x_far)]
  transfers between devices with their start and end apart: 19 -> 18, of which waited for: 8 -> 6; matrix products, arithmetic and copies ran while one was open for 0% -> 0% of each run, Pallas kernels for 0% -> 0%
where the time goes in v9:
time: 60.9 us; the launch traced here: 60.7 us
  starting transfers between devices  35.1 us (58%)
  Pallas kernels  14.5 us (24%)
  waiting for transfers between devices  9.85 us (16%)
  local copies, waits for them, and re-layouts  1.01 us (2%)
    ppermute x15, starting transfers between devices, swap(): lax.ppermute(values, axis, pairs_apart(lax.axis_size(axis), distance))  33.1 us
    pallas_call x4, Pallas kernels, run(): pl.pallas_call(kernel, out_shape=shapes, in_specs=[pl.BlockSpec(memory_sp...  14.5 us
    ppermute x15, waiting for transfers between devices, swap(): lax.ppermute(values, axis, pairs_apart(lax.axis_size(axis), distance))  9.84 us
  transfers between devices with their start and end apart: 18, of which 6 were waited for; matrix products, arithmetic and copies ran while one was open for 0% of the time, Pallas kernels for 0%

profile of v9, /device:TPU:0, one launch (start us, length us, event | category | flops | bytes accessed | tf_op | source)
XLA Modules:
  0.0 60.7 jit_solution(13163086460852432365)
XLA Ops:
  0.0 0.1 pad_add_fusion.where_ref
  0.1 0.0 copy-start
  0.1 0.9 %copy-done = f32[8,16,512]{2,1,0:T(8,128)S(1)} copy-done((f32[8,16,512]{2,1,0:T(8,128)S(1)}, f32[8,16,512]{2,1,0:T(8,128)}, u32[]{:S(2)}) %copy-start) | copy-done | bytes 262168
  1.0 1.0 %shard_map.17 = (f32[8,4,16,128]{3,2,1,0:T(8,128)S(1)}, f32[8,4,8,128]{3,2,1,0:T(8,128)S(1)}, f32[8,4,8,128]{3,2,1,0:T(8,128)S(1)}) custom-call(s32[2]{0:T(128)S(1)} %pad_add_fusion.where_ref, f32[8,16,512]{2,1,0:T(8,128)S(1)} %copy-done), custom_call_target="tpu_custom_call" | custom-call | tf_op jit(solution)/shard_map/pallas_call | solution.py:556
  2.0 3.1 %collective-permute-start = (f32[8,4,8,128]{3,2,1,0:T(8,128)S(1)}, f32[8,4,8,128]{3,2,1,0:T(8,128)S(1)}, u32[]{:S(2)}, u32[]{:S(2)}) collective-permute-start(f32[8,4,8,128]{3,2,1,0:T(8,128)S(1)} %get-tuple-element.14), channel_id=1, source_target_pairs={{0,1},{1,0},{2,3},{3,2},{4,5},{5,4},{6,7},{7,6},{8,9},{9,8},{10,11... | collective-permute-start | bytes 393224 | tf_op jit(solution)/shard_map/ppermute | solution.py:578
  5.1 0.7 %collective-permute-start.1 = (f32[8,4,8,128]{3,2,1,0:T(8,128)S(1)}, f32[8,4,8,128]{3,2,1,0:T(8,128)S(1)}, u32[]{:S(2)}, u32[]{:S(2)}) collective-permute-start(f32[8,4,8,128]{3,2,1,0:T(8,128)S(1)} %get-tuple-element.15), channel_id=1, source_target_pairs={{1,2},{2,1},{5,6},{6,5},{9,10},{10,9},{13,14},{14,13},{17,18},{18,... | collective-permute-start | bytes 393224 | tf_op jit(solution)/shard_map/ppermute | solution.py:603
  5.8 0.7 %collective-permute-start.4 = (f32[8,4,16,128]{3,2,1,0:T(8,128)S(1)}, f32[8,4,16,128]{3,2,1,0:T(8,128)S(1)}, u32[]{:S(2)}, u32[]{:S(2)}) collective-permute-start(f32[8,4,16,128]{3,2,1,0:T(8,128)S(1)} %get-tuple-element.13.mid_ref), channel_id=1, source_target_pairs={{4,8},{8,4},{5,9},{9,5},{6,10},{10,6},{7,11},{11,7},{20,24},{24,20... | collective-permute-start | bytes 786440 | tf_op jit(solution)/shard_map/ppermute | solution.py:601
  6.5 2.9 %collective-permute-start.2 = (f32[8,4,16,128]{3,2,1,0:T(8,128)S(1)}, f32[8,4,16,128]{3,2,1,0:T(8,128)S(1)}, u32[]{:S(2)}, u32[]{:S(2)}) collective-permute-start(f32[8,4,16,128]{3,2,1,0:T(8,128)S(1)} %get-tuple-element.13.mid_ref), channel_id=1, source_target_pairs={{0,4},{4,0},{8,12},{12,8},{1,5},{5,1},{9,13},{13,9},{2,6},{6,2},{1... | collective-permute-start | bytes 786440 | tf_op jit(solution)/shard_map/ppermute | solution.py:578
  9.4 0.0 collective-permute-done
  9.4 0.0 collective-permute-done.1
  9.4 0.7 %collective-permute-start.5 = (f32[8,4,16,128]{3,2,1,0:T(8,128)S(1)}, f32[8,4,16,128]{3,2,1,0:T(8,128)S(1)}, u32[]{:S(2)}, u32[]{:S(2)}) collective-permute-start(f32[8,4,16,128]{3,2,1,0:T(8,128)S(1)} %pad_maximum_fusion.mid_rim_ref), channel_id=1, source_target_pairs={{4,8},{8,4},{5,9},{9,5},{6,10},{10,6},{7,11},{11,7},{20,24},{24,20... | collective-permute-start | bytes 786440 | tf_op jit(solution)/shard_map/ppermute | solution.py:606
  10.1 2.3 %collective-permute-start.3 = (f32[8,4,16,128]{3,2,1,0:T(8,128)S(1)}, f32[8,4,16,128]{3,2,1,0:T(8,128)S(1)}, u32[]{:S(2)}, u32[]{:S(2)}) collective-permute-start(f32[8,4,16,128]{3,2,1,0:T(8,128)S(1)} %pad_maximum_fusion.mid_rim_ref), channel_id=1, source_target_pairs={{0,4},{4,0},{8,12},{12,8},{1,5},{5,1},{9,13},{13,9},{2,6},{6,2},{1... | collective-permute-start | bytes 786440 | tf_op jit(solution)/shard_map/ppermute | solution.py:578
  12.4 0.0 collective-permute-done.4.two_ref
  12.4 0.0 collective-permute-done.2.one_ref
  12.4 0.0 collective-permute-done.5.two_rim_ref
  12.5 1.1 %collective-permute-done.3.one_rim_ref = f32[8,4,16,128]{3,2,1,0:T(8,128)S(1)} collective-permute-done((f32[8,4,16,128]{3,2,1,0:T(8,128)S(1)}, f32[8,4,16,128]{3,2,1,0:T(8,128)S(1)}, u32[]{:S(2)}, u32[]{:S(2)}) %collective-permute-start.3) | collective-permute-done | bytes 262176 | tf_op jit(solution)/shard_map/ppermute | solution.py:578
  13.6 2.5 %shard_map.18 = (f32[24,4,4,8,128]{4,3,2,1,0:T(8,128)S(1)}, f32[24,4,4,8,128]{4,3,2,1,0:T(8,128)S(1)}, f32[4,2,8,128]{3,2,1,0:T(8,128)S(1)}) custom-call(s32[2]{0:T(128)S(1)} %pad_add_fusion.where_ref, f32[8,4,16,128]{3,2,1,0:T(8,128)S(1)} %get-tuple-element.13.mid_ref, f32[8,4,16,128]{3,2,1,0:T(8,128)S(1)} %pad_maximum_fusion.mid_rim_ref, ...), custom_call_target="tpu_custom_call" | custom-call | tf_op jit(solution)/shard_map/pallas_call | solution.py:556
  16.1 4.7 %collective-permute-start.8 = (f32[1,4,2,8,128]{4,3,2,1,0:T(8,128)S(1)}, f32[1,4,2,8,128]{4,3,2,1,0:T(8,128)S(1)}, u32[]{:S(2)}, u32[]{:S(2)}) collective-permute-start(f32[1,4,2,8,128]{4,3,2,1,0:T(8,128)S(1)} %bitcast.6), channel_id=1, source_target_pairs={{0,1},{1,0},{2,3},{3,2},{4,5},{5,4},{6,7},{7,6},{8,9},{9,8},{10,11... | collective-permute-start | bytes 98312 | tf_op jit(solution)/shard_map/ppermute | solution.py:578
  20.8 1.3 %collective-permute-start.7 = (f32[1,4,2,8,128]{4,3,2,1,0:T(8,128)S(1)}, f32[1,4,2,8,128]{4,3,2,1,0:T(8,128)S(1)}, u32[]{:S(2)}, u32[]{:S(2)}) collective-permute-start(f32[1,4,2,8,128]{4,3,2,1,0:T(8,128)S(1)} %bitcast.7), channel_id=1, source_target_pairs={{0,2},{1,3},{2,0},{3,1},{4,6},{5,7},{6,4},{7,5},{8,10},{9,11},{10,... | collective-permute-start | bytes 98312 | tf_op jit(solution)/shard_map/ppermute | solution.py:578
  22.1 1.4 %collective-permute-start.6 = (f32[1,4,2,8,128]{4,3,2,1,0:T(8,128)S(1)}, f32[1,4,2,8,128]{4,3,2,1,0:T(8,128)S(1)}, u32[]{:S(2)}, u32[]{:S(2)}) collective-permute-start(f32[1,4,2,8,128]{4,3,2,1,0:T(8,128)S(1)} %bitcast.8), channel_id=1, source_target_pairs={{0,3},{1,2},{2,1},{3,0},{4,7},{5,6},{6,5},{7,4},{8,11},{9,10},{10,... | collective-permute-start | bytes 98312 | tf_op jit(solution)/shard_map/ppermute | solution.py:578
  23.4 0.0 collective-permute-done.8
  23.4 4.5 %collective-permute-start.10 = (f32[2,4,2,8,128]{4,3,2,1,0:T(8,128)S(1)}, f32[2,4,2,8,128]{4,3,2,1,0:T(8,128)S(1)}, u32[]{:S(2)}, u32[]{:S(2)}) collective-permute-start(f32[2,4,2,8,128]{4,3,2,1,0:T(8,128)S(1)} %pad_maximum_fusion.2), channel_id=1, source_target_pairs={{0,8},{4,12},{8,0},{12,4},{1,9},{5,13},{9,1},{13,5},{2,10},{6,14},... | collective-permute-start | bytes 196616 | tf_op jit(solution)/shard_map/ppermute | solution.py:578
  28.0 0.0 collective-permute-done.7
  28.0 0.0 collective-permute-done.6
  28.0 4.2 %collective-permute-start.9 = (f32[2,4,2,8,128]{4,3,2,1,0:T(8,128)S(1)}, f32[2,4,2,8,128]{4,3,2,1,0:T(8,128)S(1)}, u32[]{:S(2)}, u32[]{:S(2)}) collective-permute-start(f32[2,4,2,8,128]{4,3,2,1,0:T(8,128)S(1)} %pad_maximum_fusion.1), channel_id=1, source_target_pairs={{0,8},{4,12},{8,0},{12,4},{1,9},{5,13},{9,1},{13,5},{2,10},{6,14},... | collective-permute-start | bytes 196616 | tf_op jit(solution)/shard_map/ppermute | solution.py:578
  32.2 2.2 %collective-permute-done.9 = f32[2,4,2,8,128]{4,3,2,1,0:T(8,128)S(1)} collective-permute-done((f32[2,4,2,8,128]{4,3,2,1,0:T(8,128)S(1)}, f32[2,4,2,8,128]{4,3,2,1,0:T(8,128)S(1)}, u32[]{:S(2)}, u32[]{:S(2)}) %collective-permute-start.9) | collective-permute-done | bytes 65568 | tf_op jit(solution)/shard_map/ppermute | solution.py:578
  34.5 0.0 collective-permute-done.10
  34.5 0.1 collective-permute-start.11
  34.6 1.5 %collective-permute-done.11.refs_1_ = f32[8,4,2,8,128]{4,3,2,1,0:T(8,128)S(1)} collective-permute-done((f32[8,4,2,8,128]{4,3,2,1,0:T(8,128)S(1)}, f32[8,4,2,8,128]{4,3,2,1,0:T(8,128)S(1)}, u32[]{:S(2)}, u32[]{:S(2)}) %collective-permute-start.11) | collective-permute-done | bytes 262176 | tf_op jit(solution)/shard_map/ppermute | solution.py:578
  36.1 5.8 %shard_map.19 = (f32[24,4,4,8,128]{4,3,2,1,0:T(8,128)S(1)}, f32[4,2,8,128]{3,2,1,0:T(8,128)S(1)}) custom-call(s32[2]{0:T(128)S(1)} %pad_add_fusion.where_ref, f32[8,4,2,8,128]{4,3,2,1,0:T(8,128)S(1)} %constant_dynamic-update-slice_fusion.refs_0_, f32[8,4,2,8,128]{4,3,2,1,0:T(8,128)S(1)} %collective-permute-done.11.refs_1_, ...), custom_call_target="tpu_custom_call" | custom-call | tf_op jit(solution)/shard_map/pallas_call | solution.py:556
  41.8 0.2 collective-permute-start.14
  42.0 1.8 %collective-permute-start.13 = (f32[1,4,2,8,128]{4,3,2,1,0:T(8,128)S(1)}, f32[1,4,2,8,128]{4,3,2,1,0:T(8,128)S(1)}, u32[]{:S(2)}, u32[]{:S(2)}) collective-permute-start(f32[1,4,2,8,128]{4,3,2,1,0:T(8,128)S(1)} %bitcast.11), channel_id=1, source_target_pairs={{0,2},{1,3},{2,0},{3,1},{4,6},{5,7},{6,4},{7,5},{8,10},{9,11},{10,... | collective-permute-start | bytes 98312 | tf_op jit(solution)/shard_map/ppermute | solution.py:578
  43.8 2.4 %collective-permute-start.12 = (f32[1,4,2,8,128]{4,3,2,1,0:T(8,128)S(1)}, f32[1,4,2,8,128]{4,3,2,1,0:T(8,128)S(1)}, u32[]{:S(2)}, u32[]{:S(2)}) collective-permute-start(f32[1,4,2,8,128]{4,3,2,1,0:T(8,128)S(1)} %bitcast.12), channel_id=1, source_target_pairs={{0,3},{1,2},{2,1},{3,0},{4,7},{5,6},{6,5},{7,4},{8,11},{9,10},{10,... | collective-permute-start | bytes 98312 | tf_op jit(solution)/shard_map/ppermute | solution.py:578
  46.3 0.0 collective-permute-done.14
  46.3 2.1 %collective-permute-start.16 = (f32[2,4,2,8,128]{4,3,2,1,0:T(8,128)S(1)}, f32[2,4,2,8,128]{4,3,2,1,0:T(8,128)S(1)}, u32[]{:S(2)}, u32[]{:S(2)}) collective-permute-start(f32[2,4,2,8,128]{4,3,2,1,0:T(8,128)S(1)} %pad_maximum_fusion.4), channel_id=1, source_target_pairs={{0,8},{4,12},{8,0},{12,4},{1,9},{5,13},{9,1},{13,5},{2,10},{6,14},... | collective-permute-start | bytes 196616 | tf_op jit(solution)/shard_map/ppermute | solution.py:578
  48.4 0.0 collective-permute-done.13
  48.4 1.2 %collective-permute-done.12 = f32[1,4,2,8,128]{4,3,2,1,0:T(8,128)S(1)} collective-permute-done((f32[1,4,2,8,128]{4,3,2,1,0:T(8,128)S(1)}, f32[1,4,2,8,128]{4,3,2,1,0:T(8,128)S(1)}, u32[]{:S(2)}, u32[]{:S(2)}) %collective-permute-start.12) | collective-permute-done | bytes 32800 | tf_op jit(solution)/shard_map/ppermute | solution.py:578
  49.6 2.0 %collective-permute-start.15 = (f32[2,4,2,8,128]{4,3,2,1,0:T(8,128)S(1)}, f32[2,4,2,8,128]{4,3,2,1,0:T(8,128)S(1)}, u32[]{:S(2)}, u32[]{:S(2)}) collective-permute-start(f32[2,4,2,8,128]{4,3,2,1,0:T(8,128)S(1)} %pad_maximum_fusion.3), channel_id=1, source_target_pairs={{0,8},{4,12},{8,0},{12,4},{1,9},{5,13},{9,1},{13,5},{2,10},{6,14},... | collective-permute-start | bytes 196616 | tf_op jit(solution)/shard_map/ppermute | solution.py:578
  51.6 2.2 %collective-permute-done.15 = f32[2,4,2,8,128]{4,3,2,1,0:T(8,128)S(1)} collective-permute-done((f32[2,4,2,8,128]{4,3,2,1,0:T(8,128)S(1)}, f32[2,4,2,8,128]{4,3,2,1,0:T(8,128)S(1)}, u32[]{:S(2)}, u32[]{:S(2)}) %collective-permute-start.15) | collective-permute-done | bytes 65568 | tf_op jit(solution)/shard_map/ppermute | solution.py:578
  53.8 0.0 collective-permute-done.16
  53.9 0.1 collective-permute-start.17
  53.9 1.5 %collective-permute-done.17.refs_1_ = f32[8,4,2,8,128]{4,3,2,1,0:T(8,128)S(1)} collective-permute-done((f32[8,4,2,8,128]{4,3,2,1,0:T(8,128)S(1)}, f32[8,4,2,8,128]{4,3,2,1,0:T(8,128)S(1)}, u32[]{:S(2)}, u32[]{:S(2)}) %collective-permute-start.17) | collective-permute-done | bytes 262176 | tf_op jit(solution)/shard_map/ppermute | solution.py:578
  55.5 5.2 %shard_map.20 = f32[8,16,512]{2,1,0:T(8,128)} custom-call(s32[2]{0:T(128)S(1)} %pad_add_fusion.where_ref, f32[8,4,2,8,128]{4,3,2,1,0:T(8,128)S(1)} %constant_dynamic-update-slice_fusion.6.refs_0_, f32[8,4,2,8,128]{4,3,2,1,0:T(8,128)S(1)} %collective-permute-done.17.refs_1_, f32[24,4,4,8,128]{4,3,2,1,0:T(8,128)S(1)} %get-tuple-element.20.refs_2_, ...), custom_call_target="tpu_custom_call" | custom-call | tf_op jit(solution)/shard_map/pallas_call | solution.py:556
  (18 shorter events, 0.1 us)
Async XLA Ops:
  0.1 0.9 %copy-start = (f32[8,16,512]{2,1,0:T(8,128)S(1)}, f32[8,16,512]{2,1,0:T(8,128)}, u32[]{:S(2)}) copy-start(f32[8,16,512]{2,1,0:T(8,128)} %charges_ref.1) | copy-start | bytes 786436
  2.0 7.4 %collective-permute-start = (f32[8,4,8,128]{3,2,1,0:T(8,128)S(1)}, f32[8,4,8,128]{3,2,1,0:T(8,128)S(1)}, u32[]{:S(2)}, u32[]{:S(2)}) collective-permute-start(f32[8,4,8,128]{3,2,1,0:T(8,128)S(1)} %get-tuple-element.14), channel_id=1, source_target_pairs={{0,1},{1,0},{2,3},{3,2},{4,5},{5,4},{6,7},{7,6},{8,9},{9,8},{10,11... | collective-permute-start | bytes 393224 | tf_op jit(solution)/shard_map/ppermute | solution.py:578
  5.1 4.3 %collective-permute-start.1 = (f32[8,4,8,128]{3,2,1,0:T(8,128)S(1)}, f32[8,4,8,128]{3,2,1,0:T(8,128)S(1)}, u32[]{:S(2)}, u32[]{:S(2)}) collective-permute-start(f32[8,4,8,128]{3,2,1,0:T(8,128)S(1)} %get-tuple-element.15), channel_id=1, source_target_pairs={{1,2},{2,1},{5,6},{6,5},{9,10},{10,9},{13,14},{14,13},{17,18},{18,... | collective-permute-start | bytes 393224 | tf_op jit(solution)/shard_map/ppermute | solution.py:603
  5.8 6.7 %collective-permute-start.4 = (f32[8,4,16,128]{3,2,1,0:T(8,128)S(1)}, f32[8,4,16,128]{3,2,1,0:T(8,128)S(1)}, u32[]{:S(2)}, u32[]{:S(2)}) collective-permute-start(f32[8,4,16,128]{3,2,1,0:T(8,128)S(1)} %get-tuple-element.13.mid_ref), channel_id=1, source_target_pairs={{4,8},{8,4},{5,9},{9,5},{6,10},{10,6},{7,11},{11,7},{20,24},{24,20... | collective-permute-start | bytes 786440 | tf_op jit(solution)/shard_map/ppermute | solution.py:601
  6.5 6.0 %collective-permute-start.2 = (f32[8,4,16,128]{3,2,1,0:T(8,128)S(1)}, f32[8,4,16,128]{3,2,1,0:T(8,128)S(1)}, u32[]{:S(2)}, u32[]{:S(2)}) collective-permute-start(f32[8,4,16,128]{3,2,1,0:T(8,128)S(1)} %get-tuple-element.13.mid_ref), channel_id=1, source_target_pairs={{0,4},{4,0},{8,12},{12,8},{1,5},{5,1},{9,13},{13,9},{2,6},{6,2},{1... | collective-permute-start | bytes 786440 | tf_op jit(solution)/shard_map/ppermute | solution.py:578
  9.4 3.0 %collective-permute-start.5 = (f32[8,4,16,128]{3,2,1,0:T(8,128)S(1)}, f32[8,4,16,128]{3,2,1,0:T(8,128)S(1)}, u32[]{:S(2)}, u32[]{:S(2)}) collective-permute-start(f32[8,4,16,128]{3,2,1,0:T(8,128)S(1)} %pad_maximum_fusion.mid_rim_ref), channel_id=1, source_target_pairs={{4,8},{8,4},{5,9},{9,5},{6,10},{10,6},{7,11},{11,7},{20,24},{24,20... | collective-permute-start | bytes 786440 | tf_op jit(solution)/shard_map/ppermute | solution.py:606
  10.1 3.5 %collective-permute-start.3 = (f32[8,4,16,128]{3,2,1,0:T(8,128)S(1)}, f32[8,4,16,128]{3,2,1,0:T(8,128)S(1)}, u32[]{:S(2)}, u32[]{:S(2)}) collective-permute-start(f32[8,4,16,128]{3,2,1,0:T(8,128)S(1)} %pad_maximum_fusion.mid_rim_ref), channel_id=1, source_target_pairs={{0,4},{4,0},{8,12},{12,8},{1,5},{5,1},{9,13},{13,9},{2,6},{6,2},{1... | collective-permute-start | bytes 786440 | tf_op jit(solution)/shard_map/ppermute | solution.py:578
  16.1 7.3 %collective-permute-start.8 = (f32[1,4,2,8,128]{4,3,2,1,0:T(8,128)S(1)}, f32[1,4,2,8,128]{4,3,2,1,0:T(8,128)S(1)}, u32[]{:S(2)}, u32[]{:S(2)}) collective-permute-start(f32[1,4,2,8,128]{4,3,2,1,0:T(8,128)S(1)} %bitcast.6), channel_id=1, source_target_pairs={{0,1},{1,0},{2,3},{3,2},{4,5},{5,4},{6,7},{7,6},{8,9},{9,8},{10,11... | collective-permute-start | bytes 98312 | tf_op jit(solution)/shard_map/ppermute | solution.py:578
  20.8 7.2 %collective-permute-start.7 = (f32[1,4,2,8,128]{4,3,2,1,0:T(8,128)S(1)}, f32[1,4,2,8,128]{4,3,2,1,0:T(8,128)S(1)}, u32[]{:S(2)}, u32[]{:S(2)}) collective-permute-start(f32[1,4,2,8,128]{4,3,2,1,0:T(8,128)S(1)} %bitcast.7), channel_id=1, source_target_pairs={{0,2},{1,3},{2,0},{3,1},{4,6},{5,7},{6,4},{7,5},{8,10},{9,11},{10,... | collective-permute-start | bytes 98312 | tf_op jit(solution)/shard_map/ppermute | solution.py:578
  22.1 5.9 %collective-permute-start.6 = (f32[1,4,2,8,128]{4,3,2,1,0:T(8,128)S(1)}, f32[1,4,2,8,128]{4,3,2,1,0:T(8,128)S(1)}, u32[]{:S(2)}, u32[]{:S(2)}) collective-permute-start(f32[1,4,2,8,128]{4,3,2,1,0:T(8,128)S(1)} %bitcast.8), channel_id=1, source_target_pairs={{0,3},{1,2},{2,1},{3,0},{4,7},{5,6},{6,5},{7,4},{8,11},{9,10},{10,... | collective-permute-start | bytes 98312 | tf_op jit(solution)/shard_map/ppermute | solution.py:578
  23.4 11.0 %collective-permute-start.10 = (f32[2,4,2,8,128]{4,3,2,1,0:T(8,128)S(1)}, f32[2,4,2,8,128]{4,3,2,1,0:T(8,128)S(1)}, u32[]{:S(2)}, u32[]{:S(2)}) collective-permute-start(f32[2,4,2,8,128]{4,3,2,1,0:T(8,128)S(1)} %pad_maximum_fusion.2), channel_id=1, source_target_pairs={{0,8},{4,12},{8,0},{12,4},{1,9},{5,13},{9,1},{13,5},{2,10},{6,14},... | collective-permute-start | bytes 196616 | tf_op jit(solution)/shard_map/ppermute | solution.py:578
  28.0 6.5 %collective-permute-start.9 = (f32[2,4,2,8,128]{4,3,2,1,0:T(8,128)S(1)}, f32[2,4,2,8,128]{4,3,2,1,0:T(8,128)S(1)}, u32[]{:S(2)}, u32[]{:S(2)}) collective-permute-start(f32[2,4,2,8,128]{4,3,2,1,0:T(8,128)S(1)} %pad_maximum_fusion.1), channel_id=1, source_target_pairs={{0,8},{4,12},{8,0},{12,4},{1,9},{5,13},{9,1},{13,5},{2,10},{6,14},... | collective-permute-start | bytes 196616 | tf_op jit(solution)/shard_map/ppermute | solution.py:578
  34.5 1.6 %collective-permute-start.11 = (f32[8,4,2,8,128]{4,3,2,1,0:T(8,128)S(1)}, f32[8,4,2,8,128]{4,3,2,1,0:T(8,128)S(1)}, u32[]{:S(2)}, u32[]{:S(2)}) collective-permute-start(f32[8,4,2,8,128]{4,3,2,1,0:T(8,128)S(1)} %constant_dynamic-update-slice_fusion.refs_0_), channel_id=1, source_target_pairs={{0,4},{4,0},{8,12},{12,8},{1,5},{5,1},{9,13},{13,9},{2,6},{6,2},{1... | collective-permute-start | bytes 786440 | tf_op jit(solution)/shard_map/ppermute | solution.py:578
  41.8 4.5 %collective-permute-start.14 = (f32[1,4,2,8,128]{4,3,2,1,0:T(8,128)S(1)}, f32[1,4,2,8,128]{4,3,2,1,0:T(8,128)S(1)}, u32[]{:S(2)}, u32[]{:S(2)}) collective-permute-start(f32[1,4,2,8,128]{4,3,2,1,0:T(8,128)S(1)} %bitcast.10), channel_id=1, source_target_pairs={{0,1},{1,0},{2,3},{3,2},{4,5},{5,4},{6,7},{7,6},{8,9},{9,8},{10,11... | collective-permute-start | bytes 98312 | tf_op jit(solution)/shard_map/ppermute | solution.py:578
  42.0 6.3 %collective-permute-start.13 = (f32[1,4,2,8,128]{4,3,2,1,0:T(8,128)S(1)}, f32[1,4,2,8,128]{4,3,2,1,0:T(8,128)S(1)}, u32[]{:S(2)}, u32[]{:S(2)}) collective-permute-start(f32[1,4,2,8,128]{4,3,2,1,0:T(8,128)S(1)} %bitcast.11), channel_id=1, source_target_pairs={{0,2},{1,3},{2,0},{3,1},{4,6},{5,7},{6,4},{7,5},{8,10},{9,11},{10,... | collective-permute-start | bytes 98312 | tf_op jit(solution)/shard_map/ppermute | solution.py:578
  43.8 5.7 %collective-permute-start.12 = (f32[1,4,2,8,128]{4,3,2,1,0:T(8,128)S(1)}, f32[1,4,2,8,128]{4,3,2,1,0:T(8,128)S(1)}, u32[]{:S(2)}, u32[]{:S(2)}) collective-permute-start(f32[1,4,2,8,128]{4,3,2,1,0:T(8,128)S(1)} %bitcast.12), channel_id=1, source_target_pairs={{0,3},{1,2},{2,1},{3,0},{4,7},{5,6},{6,5},{7,4},{8,11},{9,10},{10,... | collective-permute-start | bytes 98312 | tf_op jit(solution)/shard_map/ppermute | solution.py:578
  46.3 7.5 %collective-permute-start.16 = (f32[2,4,2,8,128]{4,3,2,1,0:T(8,128)S(1)}, f32[2,4,2,8,128]{4,3,2,1,0:T(8,128)S(1)}, u32[]{:S(2)}, u32[]{:S(2)}) collective-permute-start(f32[2,4,2,8,128]{4,3,2,1,0:T(8,128)S(1)} %pad_maximum_fusion.4), channel_id=1, source_target_pairs={{0,8},{4,12},{8,0},{12,4},{1,9},{5,13},{9,1},{13,5},{2,10},{6,14},... | collective-permute-start | bytes 196616 | tf_op jit(solution)/shard_map/ppermute | solution.py:578
  49.6 4.3 %collective-permute-start.15 = (f32[2,4,2,8,128]{4,3,2,1,0:T(8,128)S(1)}, f32[2,4,2,8,128]{4,3,2,1,0:T(8,128)S(1)}, u32[]{:S(2)}, u32[]{:S(2)}) collective-permute-start(f32[2,4,2,8,128]{4,3,2,1,0:T(8,128)S(1)} %pad_maximum_fusion.3), channel_id=1, source_target_pairs={{0,8},{4,12},{8,0},{12,4},{1,9},{5,13},{9,1},{13,5},{2,10},{6,14},... | collective-permute-start | bytes 196616 | tf_op jit(solution)/shard_map/ppermute | solution.py:578
  53.9 1.6 %collective-permute-start.17 = (f32[8,4,2,8,128]{4,3,2,1,0:T(8,128)S(1)}, f32[8,4,2,8,128]{4,3,2,1,0:T(8,128)S(1)}, u32[]{:S(2)}, u32[]{:S(2)}) collective-permute-start(f32[8,4,2,8,128]{4,3,2,1,0:T(8,128)S(1)} %constant_dynamic-update-slice_fusion.6.refs_0_), channel_id=1, source_target_pairs={{0,4},{4,0},{8,12},{12,8},{1,5},{5,1},{9,13},{13,9},{2,6},{6,2},{1... | collective-permute-start | bytes 786440 | tf_op jit(solution)/shard_map/ppermute | solution.py:578

commit v10 on v9

--- a/solution.py
+++ b/solution.py
@@ -303,10 +303,11 @@
     return ua1, kept_2, b1
 
 
-def coarse_finish(count_x, grids):
+def coarse_finish(count_x, where_ref, grids):
     ua1, ub1, ga1, gb1, b1 = grids[0:5]
     ua2 = grids[5]
     size_1, size_2 = 4 * count_x, 2 * count_x
+    third = 1.0 / 30.0
 
     def prolong_2(x):
         error = ua2[PAD_2 + x, 0, 0]
@@ -316,18 +317,25 @@
                 ua1, ga1, fine, [[t + error for t in line] for line in LEVEL_1.load(ua1, fine)]
             )
 
-    def sweep(u_in, g_in, u_out, g_out):
-        return lambda x: LEVEL_1.put(
-            u_out, g_out, x, LEVEL_1.sweep(u_in, g_in, b1, x, 1.0 / 30.0)
-        )
+    def window(rim):
+        count = min(BRICK_X // 2 + 2 * rim, size_1)
+        return PAD + jnp.clip(4 * where_ref[0] - rim, 0, size_1 - count), count
+
+    start, count = window(4)
+
+    def sweep(i):
+        x = start + i
+        LEVEL_1.put(ub1, gb1, x, LEVEL_1.sweep(ua1, ga1, b1, x, third))
+
+    last_start, last_count = window(3)
+
+    def last_sweep(i):
+        x = last_start + i
+        store_plane(ua1, x, LEVEL_1.sweep(ub1, gb1, b1, x, third))
 
     each(0, size_2, prolong_2, 8)
-    each(PAD, PAD + size_1, sweep(ua1, ga1, ub1, gb1), 16)
-
-    def last_sweep(x):
-        store_plane(ua1, x, LEVEL_1.sweep(ub1, gb1, b1, x, 1.0 / 30.0))
-
-    each(PAD, PAD + size_1, last_sweep, 16)
+    each(0, count, sweep, 12)
+    each(0, last_count, last_sweep, 10)
     return ua1
 
 
@@ -433,17 +441,27 @@
     return terms[0] + (terms[1] + terms[2])
 
 
+def split_lanes(values):
+    size_x, size_z, size_y = values.shape
+    matrix = places(size_y, lambda y, l: y == (l % LANES) * 4 + l // LANES)
+    split = permuted(values.reshape(size_x * size_z, size_y), matrix)
+    return [
+        split[:, p * LANES : (p + 1) * LANES].reshape(size_x, size_z, LANES) for p in range(4)
+    ]
+
+
 def lanes_kernel(where_ref, charges_ref, rows_ref, one_ref, two_ref):
     odd = where_ref[1] % 2
-    width = charges_ref.shape[2]
-    matrix = places(width, lambda y, l: y == (l % LANES) * 4 + l // LANES)
-    split = permuted(charges_ref[...].reshape(BRICK_X * BRICK_Z, width), matrix)
-    for p in range(4):
-        tile = split[:, p * LANES : (p + 1) * LANES].reshape(BRICK_X, BRICK_Z, LANES)
+    for p, tile in enumerate(split_lanes(charges_ref[...])):
         rows_ref[:, p] = tile
         first, last = tile[:, 0:8], tile[:, 8:16]
         one_ref[:, p] = jnp.where(odd == 0, last, first)
         two_ref[:, p] = jnp.where(odd == 0, first, last)
+
+
+def near_lanes_kernel(where_ref, charges_ref, rows_ref):
+    for p, tile in enumerate(split_lanes(charges_ref[...])):
+        rows_ref[:, p] = tile
 
 
 def down_kernel(count_x, count_z, where_ref, mid_ref, mid_rim_ref, one_ref, one_rim_ref, two_ref,
@@ -492,7 +510,7 @@
     u_ref, b_ref, v_ref, out_ref, ga_ref, gb_ref, ua_ref, *grids = refs
     masks = rim_masks(count_x, count_z, where_ref)
     coarse_solve(count_x, count_z, where_ref, pieces, grids)
-    coarse_ref = coarse_finish(count_x, grids)
+    coarse_ref = coarse_finish(count_x, where_ref, grids)
     at_x, at_z = where_ref[0], where_ref[1]
 
     def error_of(i):
@@ -509,7 +527,7 @@
 
 def up_kernel(count_x, count_z, count_pieces, where_ref, *refs):
     pieces, refs = refs[:count_pieces], refs[count_pieces:]
-    u_ref, b_ref, out_ref, ga_ref, gb_ref, ua_ref, ub_ref, rows_ref, held_ref, semaphores, *refs = refs
+    u_ref, b_ref, out_ref, ga_ref, gb_ref, ua_ref, ub_ref, rows_ref, *refs = refs
     near, grids = refs[:5], refs[5:]
     masks = rim_masks(count_x, count_z, where_ref)
     coarse = coarse_solve(count_x, count_z, where_ref, pieces, grids)
@@ -523,41 +541,24 @@
             for p in range(4):
                 rows_ref[x - RIM, p, pl.ds(q, 4, stride=4), :] = plane[q][p][0:4]
 
-    width = out_ref.shape[2]
-    matrix = places(width, lambda l, y: y == (l % LANES) * 4 + l // LANES)
-    half = BRICK_X // 2
-    copies = []
-    for start in (0, half):
-        each(RIM + start, RIM + start + half, body, 2)
-        tiles = [
-            rows_ref[start : start + half, p].reshape(half * BRICK_Z, LANES) for p in range(4)
-        ]
-        whole = permuted(jnp.concatenate(tiles, axis=1), matrix)
-        planes = pl.ds(start, half)
-        held_ref[planes] = whole.reshape(half, BRICK_Z, width)
-        copies.append(
-            pltpu.make_async_copy(
-                held_ref.at[planes], out_ref.at[planes], semaphores.at[start // half]
-            )
-        )
-        copies[-1].start()
-    for copy in copies:
-        copy.wait()
-
-
-def call(kernel, outputs, scratch, far_out=False):
+    each(RIM, RIM + BRICK_X, body, 2)
+    tiles = [rows_ref[:, p].reshape(BRICK_X * BRICK_Z, LANES) for p in range(4)]
+    matrix = places(out_ref.shape[2], lambda l, y: y == (l % LANES) * 4 + l // LANES)
+    out_ref[...] = permuted(jnp.concatenate(tiles, axis=1), matrix).reshape(out_ref.shape)
+
+
+def call(kernel, outputs, scratch):
     shapes = [jax.ShapeDtypeStruct(shape, jnp.float32) for shape in outputs]
-    held = sum(4 * math.prod(shape.shape) for shape in scratch if hasattr(shape, "memory_space"))
+    held = sum(4 * math.prod(shape.shape) for shape in scratch)
 
     def run(where, *arrays):
         moved = sum(4 * math.prod(array.shape) for array in arrays + tuple(shapes))
-        inside = pl.BlockSpec(memory_space=pltpu.VMEM)
-        outside = pl.BlockSpec(memory_space=pltpu.HBM if far_out else pltpu.VMEM)
+        whole = pl.BlockSpec(memory_space=pltpu.VMEM)
         return pl.pallas_call(
             kernel,
             out_shape=shapes,
-            in_specs=[pl.BlockSpec(memory_space=pltpu.SMEM)] + [inside] * len(arrays),
-            out_specs=[outside] * len(shapes),
+            in_specs=[pl.BlockSpec(memory_space=pltpu.SMEM)] + [whole] * len(arrays),
+            out_specs=[whole] * len(shapes),
             scratch_shapes=scratch,
             compiler_params=pltpu.CompilerParams(vmem_limit_bytes=held + moved + SPARE_BYTES),
         )(where, *arrays)
@@ -595,11 +596,10 @@
     at_x, at_z = lax.axis_index("gx"), lax.axis_index("gz")
     where = jnp.stack([at_x, at_z]).astype(jnp.int32)
     brick, rim = (BRICK_X, 4, BRICK_Z, LANES), (BRICK_X, 4, RIM, LANES)
-    held = pltpu.VMEM(charges.shape, jnp.float32)
     middle, one, two = call(lanes_kernel, [brick, rim, rim], [])(where, charges)
     x_far, z_two = pairs_shifted(count_x), pairs_shifted(count_z)
     far = lax.ppermute(middle, "gx", x_far)
-    near = swap("gx", middle, 1)
+    (near,) = call(near_lanes_kernel, [brick], [])(where, swap("gx", charges, 1))
     one, two = swap("gz", one, 1), lax.ppermute(two, "gz", z_two)
     even = at_z % 2 == 0
     middle_rim = jnp.concatenate([jnp.where(even, one, two), jnp.where(even, two, one)], axis=2)
@@ -629,8 +629,7 @@
     (potential,) = call(
         functools.partial(up_kernel, count_x, count_z, len(pieces)),
         [charges.shape],
-        [fine] * 4 + [rows_out, held, pltpu.SemaphoreType.DMA((2,))] + [close] * 5 + grids,
-        far_out=True,
+        [fine] * 4 + [rows_out] + [close] * 5 + grids,
     )(where, *pieces, u, b)
     return potential
 

time: 60.9 us -> 59.9 us (0.984)
  starting transfers between devices: 35.1 us -> 33 us
  waiting for transfers between devices: 9.85 us -> 10.9 us
  Pallas kernels: 14.5 us -> 15.5 us
  local copies, waits for them, and re-layouts: 1.01 us -> 0.06 us
    ppermute x15, starting transfers between devices: 33.1 us -> 31 us  [swap(): lax.ppermute(values, axis, pairs_apart(lax.axis_size(axis), distance))]
    ppermute x15, waiting for transfers between devices: 9.84 us -> 10.9 us  [swap(): lax.ppermute(values, axis, pairs_apart(lax.axis_size(axis), distance))]
    pallas_call x4 -> x5, Pallas kernels: 14.5 us -> 15.5 us  [run(): pl.pallas_call(kernel, out_shape=shapes, in_specs=[pl.BlockSpec(memory_sp...]
    unnamed x12 -> x10, local copies, waits for them, and re-layouts: 0.99 us -> 0.04 us
  transfers between devices with their start and end apart: 18 -> 18, of which waited for: 6 -> 7; matrix products, arithmetic and copies ran while one was open for 0% -> 0% of each run, Pallas kernels for 0% -> 2%
where the time goes in v10:
time: 59.9 us; the launch traced here: 59.7 us
  starting transfers between devices  33 us (55%)
  Pallas kernels  15.5 us (26%)
  waiting for transfers between devices  10.9 us (18%)
    ppermute x15, starting transfers between devices, swap(): lax.ppermute(values, axis, pairs_apart(lax.axis_size(axis), distance))  31 us
    pallas_call x5, Pallas kernels, run(): pl.pallas_call(kernel, out_shape=shapes, in_specs=[pl.BlockSpec(memory_sp...  15.5 us
    ppermute x15, waiting for transfers between devices, swap(): lax.ppermute(values, axis, pairs_apart(lax.axis_size(axis), distance))  10.9 us
  transfers between devices with their start and end apart: 18, of which 7 were waited for; matrix products, arithmetic and copies ran while one was open for 0% of the time, Pallas kernels for 2%

profile of v10, /device:TPU:0, one launch (start us, length us, event | category | flops | bytes accessed | tf_op | source)
XLA Modules:
  0.0 59.7 jit_solution(1485620086159840110)
XLA Ops:
  0.0 0.1 pad_add_fusion.where_ref
  0.1 1.4 %shard_map.17 = (f32[8,4,16,128]{3,2,1,0:T(8,128)S(1)}, f32[8,4,8,128]{3,2,1,0:T(8,128)S(1)}, f32[8,4,8,128]{3,2,1,0:T(8,128)S(1)}) custom-call(s32[2]{0:T(128)S(1)} %pad_add_fusion.where_ref, f32[8,16,512]{2,1,0:T(8,128)} %charges_ref.1), custom_call_target="tpu_custom_call" | custom-call | tf_op jit(solution)/shard_map/pallas_call | solution.py:557
  1.5 3.1 %collective-permute-start = (f32[8,4,8,128]{3,2,1,0:T(8,128)S(1)}, f32[8,4,8,128]{3,2,1,0:T(8,128)S(1)}, u32[]{:S(2)}, u32[]{:S(2)}) collective-permute-start(f32[8,4,8,128]{3,2,1,0:T(8,128)S(1)} %get-tuple-element.14), channel_id=1, source_target_pairs={{0,1},{1,0},{2,3},{3,2},{4,5},{5,4},{6,7},{7,6},{8,9},{9,8},{10,11... | collective-permute-start | bytes 393224 | tf_op jit(solution)/shard_map/ppermute | solution.py:579
  4.6 0.7 %collective-permute-start.1 = (f32[8,4,8,128]{3,2,1,0:T(8,128)S(1)}, f32[8,4,8,128]{3,2,1,0:T(8,128)S(1)}, u32[]{:S(2)}, u32[]{:S(2)}) collective-permute-start(f32[8,4,8,128]{3,2,1,0:T(8,128)S(1)} %get-tuple-element.15), channel_id=1, source_target_pairs={{1,2},{2,1},{5,6},{6,5},{9,10},{10,9},{13,14},{14,13},{17,18},{18,... | collective-permute-start | bytes 393224 | tf_op jit(solution)/shard_map/ppermute | solution.py:603
  5.2 0.1 collective-permute-start.2
  5.3 0.7 %collective-permute-start.4 = (f32[8,4,16,128]{3,2,1,0:T(8,128)S(1)}, f32[8,4,16,128]{3,2,1,0:T(8,128)S(1)}, u32[]{:S(2)}, u32[]{:S(2)}) collective-permute-start(f32[8,4,16,128]{3,2,1,0:T(8,128)S(1)} %get-tuple-element.13.mid_ref), channel_id=1, source_target_pairs={{4,8},{8,4},{5,9},{9,5},{6,10},{10,6},{7,11},{11,7},{20,24},{24,20... | collective-permute-start | bytes 786440 | tf_op jit(solution)/shard_map/ppermute | solution.py:601
  6.0 2.1 %collective-permute-done = f32[8,4,8,128]{3,2,1,0:T(8,128)S(1)} collective-permute-done((f32[8,4,8,128]{3,2,1,0:T(8,128)S(1)}, f32[8,4,8,128]{3,2,1,0:T(8,128)S(1)}, u32[]{:S(2)}, u32[]{:S(2)}) %collective-permute-start) | collective-permute-done | bytes 131104 | tf_op jit(solution)/shard_map/ppermute | solution.py:579
  8.1 0.0 collective-permute-done.1
  8.1 0.7 %collective-permute-start.5 = (f32[8,4,16,128]{3,2,1,0:T(8,128)S(1)}, f32[8,4,16,128]{3,2,1,0:T(8,128)S(1)}, u32[]{:S(2)}, u32[]{:S(2)}) collective-permute-start(f32[8,4,16,128]{3,2,1,0:T(8,128)S(1)} %pad_maximum_fusion.mid_rim_ref), channel_id=1, source_target_pairs={{4,8},{8,4},{5,9},{9,5},{6,10},{10,6},{7,11},{11,7},{20,24},{24,20... | collective-permute-start | bytes 786440 | tf_op jit(solution)/shard_map/ppermute | solution.py:606
  8.8 3.1 %collective-permute-start.3 = (f32[8,4,16,128]{3,2,1,0:T(8,128)S(1)}, f32[8,4,16,128]{3,2,1,0:T(8,128)S(1)}, u32[]{:S(2)}, u32[]{:S(2)}) collective-permute-start(f32[8,4,16,128]{3,2,1,0:T(8,128)S(1)} %pad_maximum_fusion.mid_rim_ref), channel_id=1, source_target_pairs={{0,4},{4,0},{8,12},{12,8},{1,5},{5,1},{9,13},{13,9},{2,6},{6,2},{1... | collective-permute-start | bytes 786440 | tf_op jit(solution)/shard_map/ppermute | solution.py:579
  11.9 0.0 collective-permute-done.2.charges_ref
  11.9 1.0 %shard_map.18.one_ref = f32[8,4,16,128]{3,2,1,0:T(8,128)S(1)} custom-call(s32[2]{0:T(128)S(1)} %pad_add_fusion.where_ref, f32[8,16,512]{2,1,0:T(8,128)S(1)} %collective-permute-done.2.charges_ref), custom_call_target="tpu_custom_call" | custom-call | tf_op jit(solution)/shard_map/pallas_call | solution.py:557
  12.9 0.0 collective-permute-done.4.two_ref
  12.9 0.0 collective-permute-done.5.two_rim_ref
  12.9 0.1 collective-permute-done.3.one_rim_ref
  13.1 2.5 %shard_map.19 = (f32[24,4,4,8,128]{4,3,2,1,0:T(8,128)S(1)}, f32[24,4,4,8,128]{4,3,2,1,0:T(8,128)S(1)}, f32[4,2,8,128]{3,2,1,0:T(8,128)S(1)}) custom-call(s32[2]{0:T(128)S(1)} %pad_add_fusion.where_ref, f32[8,4,16,128]{3,2,1,0:T(8,128)S(1)} %get-tuple-element.13.mid_ref, f32[8,4,16,128]{3,2,1,0:T(8,128)S(1)} %pad_maximum_fusion.mid_rim_ref, ...), custom_call_target="tpu_custom_call" | custom-call | tf_op jit(solution)/shard_map/pallas_call | solution.py:557
  15.6 4.7 %collective-permute-start.8 = (f32[1,4,2,8,128]{4,3,2,1,0:T(8,128)S(1)}, f32[1,4,2,8,128]{4,3,2,1,0:T(8,128)S(1)}, u32[]{:S(2)}, u32[]{:S(2)}) collective-permute-start(f32[1,4,2,8,128]{4,3,2,1,0:T(8,128)S(1)} %bitcast.6), channel_id=1, source_target_pairs={{0,1},{1,0},{2,3},{3,2},{4,5},{5,4},{6,7},{7,6},{8,9},{9,8},{10,11... | collective-permute-start | bytes 98312 | tf_op jit(solution)/shard_map/ppermute | solution.py:579
  20.2 1.3 %collective-permute-start.7 = (f32[1,4,2,8,128]{4,3,2,1,0:T(8,128)S(1)}, f32[1,4,2,8,128]{4,3,2,1,0:T(8,128)S(1)}, u32[]{:S(2)}, u32[]{:S(2)}) collective-permute-start(f32[1,4,2,8,128]{4,3,2,1,0:T(8,128)S(1)} %bitcast.7), channel_id=1, source_target_pairs={{0,2},{1,3},{2,0},{3,1},{4,6},{5,7},{6,4},{7,5},{8,10},{9,11},{10,... | collective-permute-start | bytes 98312 | tf_op jit(solution)/shard_map/ppermute | solution.py:579
  21.5 1.4 %collective-permute-start.6 = (f32[1,4,2,8,128]{4,3,2,1,0:T(8,128)S(1)}, f32[1,4,2,8,128]{4,3,2,1,0:T(8,128)S(1)}, u32[]{:S(2)}, u32[]{:S(2)}) collective-permute-start(f32[1,4,2,8,128]{4,3,2,1,0:T(8,128)S(1)} %bitcast.8), channel_id=1, source_target_pairs={{0,3},{1,2},{2,1},{3,0},{4,7},{5,6},{6,5},{7,4},{8,11},{9,10},{10,... | collective-permute-start | bytes 98312 | tf_op jit(solution)/shard_map/ppermute | solution.py:579
  22.9 0.0 collective-permute-done.8
  22.9 4.5 %collective-permute-start.10 = (f32[2,4,2,8,128]{4,3,2,1,0:T(8,128)S(1)}, f32[2,4,2,8,128]{4,3,2,1,0:T(8,128)S(1)}, u32[]{:S(2)}, u32[]{:S(2)}) collective-permute-start(f32[2,4,2,8,128]{4,3,2,1,0:T(8,128)S(1)} %pad_maximum_fusion.2), channel_id=1, source_target_pairs={{0,8},{4,12},{8,0},{12,4},{1,9},{5,13},{9,1},{13,5},{2,10},{6,14},... | collective-permute-start | bytes 196616 | tf_op jit(solution)/shard_map/ppermute | solution.py:579
  27.4 0.0 collective-permute-done.7
  27.4 0.0 collective-permute-done.6
  27.4 4.2 %collective-permute-start.9 = (f32[2,4,2,8,128]{4,3,2,1,0:T(8,128)S(1)}, f32[2,4,2,8,128]{4,3,2,1,0:T(8,128)S(1)}, u32[]{:S(2)}, u32[]{:S(2)}) collective-permute-start(f32[2,4,2,8,128]{4,3,2,1,0:T(8,128)S(1)} %pad_maximum_fusion.1), channel_id=1, source_target_pairs={{0,8},{4,12},{8,0},{12,4},{1,9},{5,13},{9,1},{13,5},{2,10},{6,14},... | collective-permute-start | bytes 196616 | tf_op jit(solution)/shard_map/ppermute | solution.py:579
  31.7 2.2 %collective-permute-done.9 = f32[2,4,2,8,128]{4,3,2,1,0:T(8,128)S(1)} collective-permute-done((f32[2,4,2,8,128]{4,3,2,1,0:T(8,128)S(1)}, f32[2,4,2,8,128]{4,3,2,1,0:T(8,128)S(1)}, u32[]{:S(2)}, u32[]{:S(2)}) %collective-permute-start.9) | collective-permute-done | bytes 65568 | tf_op jit(solution)/shard_map/ppermute | solution.py:579
  33.9 0.0 collective-permute-done.10
  33.9 0.1 collective-permute-start.11
  34.0 1.5 %collective-permute-done.11.refs_1_ = f32[8,4,2,8,128]{4,3,2,1,0:T(8,128)S(1)} collective-permute-done((f32[8,4,2,8,128]{4,3,2,1,0:T(8,128)S(1)}, f32[8,4,2,8,128]{4,3,2,1,0:T(8,128)S(1)}, u32[]{:S(2)}, u32[]{:S(2)}) %collective-permute-start.11) | collective-permute-done | bytes 262176 | tf_op jit(solution)/shard_map/ppermute | solution.py:579
  35.5 5.7 %shard_map.20 = (f32[24,4,4,8,128]{4,3,2,1,0:T(8,128)S(1)}, f32[4,2,8,128]{3,2,1,0:T(8,128)S(1)}) custom-call(s32[2]{0:T(128)S(1)} %pad_add_fusion.where_ref, f32[8,4,2,8,128]{4,3,2,1,0:T(8,128)S(1)} %constant_dynamic-update-slice_fusion.refs_0_, f32[8,4,2,8,128]{4,3,2,1,0:T(8,128)S(1)} %collective-permute-done.11.refs_1_, ...), custom_call_target="tpu_custom_call" | custom-call | tf_op jit(solution)/shard_map/pallas_call | solution.py:557
  41.3 0.2 collective-permute-start.14
  41.5 1.8 %collective-permute-start.13 = (f32[1,4,2,8,128]{4,3,2,1,0:T(8,128)S(1)}, f32[1,4,2,8,128]{4,3,2,1,0:T(8,128)S(1)}, u32[]{:S(2)}, u32[]{:S(2)}) collective-permute-start(f32[1,4,2,8,128]{4,3,2,1,0:T(8,128)S(1)} %bitcast.11), channel_id=1, source_target_pairs={{0,2},{1,3},{2,0},{3,1},{4,6},{5,7},{6,4},{7,5},{8,10},{9,11},{10,... | collective-permute-start | bytes 98312 | tf_op jit(solution)/shard_map/ppermute | solution.py:579
  43.3 2.4 %collective-permute-start.12 = (f32[1,4,2,8,128]{4,3,2,1,0:T(8,128)S(1)}, f32[1,4,2,8,128]{4,3,2,1,0:T(8,128)S(1)}, u32[]{:S(2)}, u32[]{:S(2)}) collective-permute-start(f32[1,4,2,8,128]{4,3,2,1,0:T(8,128)S(1)} %bitcast.12), channel_id=1, source_target_pairs={{0,3},{1,2},{2,1},{3,0},{4,7},{5,6},{6,5},{7,4},{8,11},{9,10},{10,... | collective-permute-start | bytes 98312 | tf_op jit(solution)/shard_map/ppermute | solution.py:579
  45.7 0.0 collective-permute-done.14
  45.7 2.1 %collective-permute-start.16 = (f32[2,4,2,8,128]{4,3,2,1,0:T(8,128)S(1)}, f32[2,4,2,8,128]{4,3,2,1,0:T(8,128)S(1)}, u32[]{:S(2)}, u32[]{:S(2)}) collective-permute-start(f32[2,4,2,8,128]{4,3,2,1,0:T(8,128)S(1)} %pad_maximum_fusion.4), channel_id=1, source_target_pairs={{0,8},{4,12},{8,0},{12,4},{1,9},{5,13},{9,1},{13,5},{2,10},{6,14},... | collective-permute-start | bytes 196616 | tf_op jit(solution)/shard_map/ppermute | solution.py:579
  47.8 0.0 collective-permute-done.13
  47.8 1.2 %collective-permute-done.12 = f32[1,4,2,8,128]{4,3,2,1,0:T(8,128)S(1)} collective-permute-done((f32[1,4,2,8,128]{4,3,2,1,0:T(8,128)S(1)}, f32[1,4,2,8,128]{4,3,2,1,0:T(8,128)S(1)}, u32[]{:S(2)}, u32[]{:S(2)}) %collective-permute-start.12) | collective-permute-done | bytes 32800 | tf_op jit(solution)/shard_map/ppermute | solution.py:579
  49.0 2.0 %collective-permute-start.15 = (f32[2,4,2,8,128]{4,3,2,1,0:T(8,128)S(1)}, f32[2,4,2,8,128]{4,3,2,1,0:T(8,128)S(1)}, u32[]{:S(2)}, u32[]{:S(2)}) collective-permute-start(f32[2,4,2,8,128]{4,3,2,1,0:T(8,128)S(1)} %pad_maximum_fusion.3), channel_id=1, source_target_pairs={{0,8},{4,12},{8,0},{12,4},{1,9},{5,13},{9,1},{13,5},{2,10},{6,14},... | collective-permute-start | bytes 196616 | tf_op jit(solution)/shard_map/ppermute | solution.py:579
  51.1 2.2 %collective-permute-done.15 = f32[2,4,2,8,128]{4,3,2,1,0:T(8,128)S(1)} collective-permute-done((f32[2,4,2,8,128]{4,3,2,1,0:T(8,128)S(1)}, f32[2,4,2,8,128]{4,3,2,1,0:T(8,128)S(1)}, u32[]{:S(2)}, u32[]{:S(2)}) %collective-permute-start.15) | collective-permute-done | bytes 65568 | tf_op jit(solution)/shard_map/ppermute | solution.py:579
  53.3 0.0 collective-permute-done.16
  53.3 0.1 collective-permute-start.17
  53.4 1.5 %collective-permute-done.17.refs_1_ = f32[8,4,2,8,128]{4,3,2,1,0:T(8,128)S(1)} collective-permute-done((f32[8,4,2,8,128]{4,3,2,1,0:T(8,128)S(1)}, f32[8,4,2,8,128]{4,3,2,1,0:T(8,128)S(1)}, u32[]{:S(2)}, u32[]{:S(2)}) %collective-permute-start.17) | collective-permute-done | bytes 262176 | tf_op jit(solution)/shard_map/ppermute | solution.py:579
  54.9 4.8 %shard_map.21 = f32[8,16,512]{2,1,0:T(8,128)} custom-call(s32[2]{0:T(128)S(1)} %pad_add_fusion.where_ref, f32[8,4,2,8,128]{4,3,2,1,0:T(8,128)S(1)} %constant_dynamic-update-slice_fusion.6.refs_0_, f32[8,4,2,8,128]{4,3,2,1,0:T(8,128)S(1)} %collective-permute-done.17.refs_1_, f32[24,4,4,8,128]{4,3,2,1,0:T(8,128)S(1)} %get-tuple-element.20.refs_2_, ...), custom_call_target="tpu_custom_call" | custom-call | tf_op jit(solution)/shard_map/pallas_call | solution.py:557
  (18 shorter events, 0.1 us)
Async XLA Ops:
  1.5 6.6 %collective-permute-start = (f32[8,4,8,128]{3,2,1,0:T(8,128)S(1)}, f32[8,4,8,128]{3,2,1,0:T(8,128)S(1)}, u32[]{:S(2)}, u32[]{:S(2)}) collective-permute-start(f32[8,4,8,128]{3,2,1,0:T(8,128)S(1)} %get-tuple-element.14), channel_id=1, source_target_pairs={{0,1},{1,0},{2,3},{3,2},{4,5},{5,4},{6,7},{7,6},{8,9},{9,8},{10,11... | collective-permute-start | bytes 393224 | tf_op jit(solution)/shard_map/ppermute | solution.py:579
  4.6 3.5 %collective-permute-start.1 = (f32[8,4,8,128]{3,2,1,0:T(8,128)S(1)}, f32[8,4,8,128]{3,2,1,0:T(8,128)S(1)}, u32[]{:S(2)}, u32[]{:S(2)}) collective-permute-start(f32[8,4,8,128]{3,2,1,0:T(8,128)S(1)} %get-tuple-element.15), channel_id=1, source_target_pairs={{1,2},{2,1},{5,6},{6,5},{9,10},{10,9},{13,14},{14,13},{17,18},{18,... | collective-permute-start | bytes 393224 | tf_op jit(solution)/shard_map/ppermute | solution.py:603
  5.2 6.7 %collective-permute-start.2 = (f32[8,16,512]{2,1,0:T(8,128)}, f32[8,16,512]{2,1,0:T(8,128)S(1)}, u32[]{:S(2)}, u32[]{:S(2)}) collective-permute-start(f32[8,16,512]{2,1,0:T(8,128)} %charges_ref.1), channel_id=1, source_target_pairs={{0,4},{4,0},{8,12},{12,8},{1,5},{5,1},{9,13},{13,9},{2,6},{6,2},{1... | collective-permute-start | bytes 786440 | tf_op jit(solution)/shard_map/ppermute | solution.py:579
  5.3 7.6 %collective-permute-start.4 = (f32[8,4,16,128]{3,2,1,0:T(8,128)S(1)}, f32[8,4,16,128]{3,2,1,0:T(8,128)S(1)}, u32[]{:S(2)}, u32[]{:S(2)}) collective-permute-start(f32[8,4,16,128]{3,2,1,0:T(8,128)S(1)} %get-tuple-element.13.mid_ref), channel_id=1, source_target_pairs={{4,8},{8,4},{5,9},{9,5},{6,10},{10,6},{7,11},{11,7},{20,24},{24,20... | collective-permute-start | bytes 786440 | tf_op jit(solution)/shard_map/ppermute | solution.py:601
  8.1 4.8 %collective-permute-start.5 = (f32[8,4,16,128]{3,2,1,0:T(8,128)S(1)}, f32[8,4,16,128]{3,2,1,0:T(8,128)S(1)}, u32[]{:S(2)}, u32[]{:S(2)}) collective-permute-start(f32[8,4,16,128]{3,2,1,0:T(8,128)S(1)} %pad_maximum_fusion.mid_rim_ref), channel_id=1, source_target_pairs={{4,8},{8,4},{5,9},{9,5},{6,10},{10,6},{7,11},{11,7},{20,24},{24,20... | collective-permute-start | bytes 786440 | tf_op jit(solution)/shard_map/ppermute | solution.py:606
  8.8 4.3 %collective-permute-start.3 = (f32[8,4,16,128]{3,2,1,0:T(8,128)S(1)}, f32[8,4,16,128]{3,2,1,0:T(8,128)S(1)}, u32[]{:S(2)}, u32[]{:S(2)}) collective-permute-start(f32[8,4,16,128]{3,2,1,0:T(8,128)S(1)} %pad_maximum_fusion.mid_rim_ref), channel_id=1, source_target_pairs={{0,4},{4,0},{8,12},{12,8},{1,5},{5,1},{9,13},{13,9},{2,6},{6,2},{1... | collective-permute-start | bytes 786440 | tf_op jit(solution)/shard_map/ppermute | solution.py:579
  15.6 7.3 %collective-permute-start.8 = (f32[1,4,2,8,128]{4,3,2,1,0:T(8,128)S(1)}, f32[1,4,2,8,128]{4,3,2,1,0:T(8,128)S(1)}, u32[]{:S(2)}, u32[]{:S(2)}) collective-permute-start(f32[1,4,2,8,128]{4,3,2,1,0:T(8,128)S(1)} %bitcast.6), channel_id=1, source_target_pairs={{0,1},{1,0},{2,3},{3,2},{4,5},{5,4},{6,7},{7,6},{8,9},{9,8},{10,11... | collective-permute-start | bytes 98312 | tf_op jit(solution)/shard_map/ppermute | solution.py:579
  20.2 7.2 %collective-permute-start.7 = (f32[1,4,2,8,128]{4,3,2,1,0:T(8,128)S(1)}, f32[1,4,2,8,128]{4,3,2,1,0:T(8,128)S(1)}, u32[]{:S(2)}, u32[]{:S(2)}) collective-permute-start(f32[1,4,2,8,128]{4,3,2,1,0:T(8,128)S(1)} %bitcast.7), channel_id=1, source_target_pairs={{0,2},{1,3},{2,0},{3,1},{4,6},{5,7},{6,4},{7,5},{8,10},{9,11},{10,... | collective-permute-start | bytes 98312 | tf_op jit(solution)/shard_map/ppermute | solution.py:579
  21.5 5.9 %collective-permute-start.6 = (f32[1,4,2,8,128]{4,3,2,1,0:T(8,128)S(1)}, f32[1,4,2,8,128]{4,3,2,1,0:T(8,128)S(1)}, u32[]{:S(2)}, u32[]{:S(2)}) collective-permute-start(f32[1,4,2,8,128]{4,3,2,1,0:T(8,128)S(1)} %bitcast.8), channel_id=1, source_target_pairs={{0,3},{1,2},{2,1},{3,0},{4,7},{5,6},{6,5},{7,4},{8,11},{9,10},{10,... | collective-permute-start | bytes 98312 | tf_op jit(solution)/shard_map/ppermute | solution.py:579
  22.9 11.0 %collective-permute-start.10 = (f32[2,4,2,8,128]{4,3,2,1,0:T(8,128)S(1)}, f32[2,4,2,8,128]{4,3,2,1,0:T(8,128)S(1)}, u32[]{:S(2)}, u32[]{:S(2)}) collective-permute-start(f32[2,4,2,8,128]{4,3,2,1,0:T(8,128)S(1)} %pad_maximum_fusion.2), channel_id=1, source_target_pairs={{0,8},{4,12},{8,0},{12,4},{1,9},{5,13},{9,1},{13,5},{2,10},{6,14},... | collective-permute-start | bytes 196616 | tf_op jit(solution)/shard_map/ppermute | solution.py:579
  27.4 6.5 %collective-permute-start.9 = (f32[2,4,2,8,128]{4,3,2,1,0:T(8,128)S(1)}, f32[2,4,2,8,128]{4,3,2,1,0:T(8,128)S(1)}, u32[]{:S(2)}, u32[]{:S(2)}) collective-permute-start(f32[2,4,2,8,128]{4,3,2,1,0:T(8,128)S(1)} %pad_maximum_fusion.1), channel_id=1, source_target_pairs={{0,8},{4,12},{8,0},{12,4},{1,9},{5,13},{9,1},{13,5},{2,10},{6,14},... | collective-permute-start | bytes 196616 | tf_op jit(solution)/shard_map/ppermute | solution.py:579
  33.9 1.6 %collective-permute-start.11 = (f32[8,4,2,8,128]{4,3,2,1,0:T(8,128)S(1)}, f32[8,4,2,8,128]{4,3,2,1,0:T(8,128)S(1)}, u32[]{:S(2)}, u32[]{:S(2)}) collective-permute-start(f32[8,4,2,8,128]{4,3,2,1,0:T(8,128)S(1)} %constant_dynamic-update-slice_fusion.refs_0_), channel_id=1, source_target_pairs={{0,4},{4,0},{8,12},{12,8},{1,5},{5,1},{9,13},{13,9},{2,6},{6,2},{1... | collective-permute-start | bytes 786440 | tf_op jit(solution)/shard_map/ppermute | solution.py:579
  41.3 4.5 %collective-permute-start.14 = (f32[1,4,2,8,128]{4,3,2,1,0:T(8,128)S(1)}, f32[1,4,2,8,128]{4,3,2,1,0:T(8,128)S(1)}, u32[]{:S(2)}, u32[]{:S(2)}) collective-permute-start(f32[1,4,2,8,128]{4,3,2,1,0:T(8,128)S(1)} %bitcast.10), channel_id=1, source_target_pairs={{0,1},{1,0},{2,3},{3,2},{4,5},{5,4},{6,7},{7,6},{8,9},{9,8},{10,11... | collective-permute-start | bytes 98312 | tf_op jit(solution)/shard_map/ppermute | solution.py:579
  41.5 6.3 %collective-permute-start.13 = (f32[1,4,2,8,128]{4,3,2,1,0:T(8,128)S(1)}, f32[1,4,2,8,128]{4,3,2,1,0:T(8,128)S(1)}, u32[]{:S(2)}, u32[]{:S(2)}) collective-permute-start(f32[1,4,2,8,128]{4,3,2,1,0:T(8,128)S(1)} %bitcast.11), channel_id=1, source_target_pairs={{0,2},{1,3},{2,0},{3,1},{4,6},{5,7},{6,4},{7,5},{8,10},{9,11},{10,... | collective-permute-start | bytes 98312 | tf_op jit(solution)/shard_map/ppermute | solution.py:579
  43.3 5.7 %collective-permute-start.12 = (f32[1,4,2,8,128]{4,3,2,1,0:T(8,128)S(1)}, f32[1,4,2,8,128]{4,3,2,1,0:T(8,128)S(1)}, u32[]{:S(2)}, u32[]{:S(2)}) collective-permute-start(f32[1,4,2,8,128]{4,3,2,1,0:T(8,128)S(1)} %bitcast.12), channel_id=1, source_target_pairs={{0,3},{1,2},{2,1},{3,0},{4,7},{5,6},{6,5},{7,4},{8,11},{9,10},{10,... | collective-permute-start | bytes 98312 | tf_op jit(solution)/shard_map/ppermute | solution.py:579
  45.7 7.5 %collective-permute-start.16 = (f32[2,4,2,8,128]{4,3,2,1,0:T(8,128)S(1)}, f32[2,4,2,8,128]{4,3,2,1,0:T(8,128)S(1)}, u32[]{:S(2)}, u32[]{:S(2)}) collective-permute-start(f32[2,4,2,8,128]{4,3,2,1,0:T(8,128)S(1)} %pad_maximum_fusion.4), channel_id=1, source_target_pairs={{0,8},{4,12},{8,0},{12,4},{1,9},{5,13},{9,1},{13,5},{2,10},{6,14},... | collective-permute-start | bytes 196616 | tf_op jit(solution)/shard_map/ppermute | solution.py:579
  49.0 4.3 %collective-permute-start.15 = (f32[2,4,2,8,128]{4,3,2,1,0:T(8,128)S(1)}, f32[2,4,2,8,128]{4,3,2,1,0:T(8,128)S(1)}, u32[]{:S(2)}, u32[]{:S(2)}) collective-permute-start(f32[2,4,2,8,128]{4,3,2,1,0:T(8,128)S(1)} %pad_maximum_fusion.3), channel_id=1, source_target_pairs={{0,8},{4,12},{8,0},{12,4},{1,9},{5,13},{9,1},{13,5},{2,10},{6,14},... | collective-permute-start | bytes 196616 | tf_op jit(solution)/shard_map/ppermute | solution.py:579
  53.3 1.6 %collective-permute-start.17 = (f32[8,4,2,8,128]{4,3,2,1,0:T(8,128)S(1)}, f32[8,4,2,8,128]{4,3,2,1,0:T(8,128)S(1)}, u32[]{:S(2)}, u32[]{:S(2)}) collective-permute-start(f32[8,4,2,8,128]{4,3,2,1,0:T(8,128)S(1)} %constant_dynamic-update-slice_fusion.6.refs_0_), channel_id=1, source_target_pairs={{0,4},{4,0},{8,12},{12,8},{1,5},{5,1},{9,13},{13,9},{2,6},{6,2},{1... | collective-permute-start | bytes 786440 | tf_op jit(solution)/shard_map/ppermute | solution.py:579

commit v11 on v10

--- a/solution.py
+++ b/solution.py
@@ -602,8 +602,13 @@
     (near,) = call(near_lanes_kernel, [brick], [])(where, swap("gx", charges, 1))
     one, two = swap("gz", one, 1), lax.ppermute(two, "gz", z_two)
     even = at_z % 2 == 0
-    middle_rim = jnp.concatenate([jnp.where(even, one, two), jnp.where(even, two, one)], axis=2)
-    far_rim = lax.ppermute(middle_rim, "gx", x_far)
+
+    def both_rims(from_one, from_two):
+        after, before = jnp.where(even, from_one, from_two), jnp.where(even, from_two, from_one)
+        return jnp.concatenate([after, before], axis=2)
+
+    middle_rim = both_rims(one, two)
+    far_rim = both_rims(lax.ppermute(one, "gx", x_far), lax.ppermute(two, "gx", x_far))
     near_rim = swap("gx", middle_rim, 1)
 
     wide = (WIDE_X, 4, 4, 8, LANES)

time: 59.9 us -> 60.8 us (1.015)
  waiting for transfers between devices: 10.9 us -> 12.1 us
    ppermute x15, waiting for transfers between devices: 10.9 us -> 12.1 us  [swap(): lax.ppermute(values, axis, pairs_apart(lax.axis_size(axis), distance))]
    ppermute x15, starting transfers between devices: 31 us -> 29.9 us  [swap(): lax.ppermute(values, axis, pairs_apart(lax.axis_size(axis), distance))]
    ppermute x1 -> x2, starting transfers between devices: 0.68 us -> 1.33 us  [the longest x1 0.67 us: per_device(): lax.ppermute(two, 'gx', x_far)]
  transfers between devices with their start and end apart: 18 -> 19, of which waited for: 7 -> 8; matrix products, arithmetic and copies ran while one was open for 0% -> 0% of each run, Pallas kernels for 2% -> 2%
where the time goes in v11:
time: 60.8 us; the launch traced here: 60.6 us
  starting transfers between devices  32.6 us (54%)
  Pallas kernels  15.4 us (25%)
  waiting for transfers between devices  12.1 us (20%)
    ppermute x15, starting transfers between devices, swap(): lax.ppermute(values, axis, pairs_apart(lax.axis_size(axis), distance))  29.9 us
    pallas_call x5, Pallas kernels, run(): pl.pallas_call(kernel, out_shape=shapes, in_specs=[pl.BlockSpec(memory_sp...  15.4 us
    ppermute x15, waiting for transfers between devices, swap(): lax.ppermute(values, axis, pairs_apart(lax.axis_size(axis), distance))  12.1 us
  transfers between devices with their start and end apart: 19, of which 8 were waited for; matrix products, arithmetic and copies ran while one was open for 0% of the time, Pallas kernels for 2%

profile of v11, /device:TPU:0, one launch (start us, length us, event | category | flops | bytes accessed | tf_op | source)
XLA Modules:
  0.0 60.6 jit_solution(1562365625356170923)
XLA Ops:
  0.0 0.1 pad_add_fusion.where_ref
  0.1 1.4 %shard_map.17 = (f32[8,4,16,128]{3,2,1,0:T(8,128)S(1)}, f32[8,4,8,128]{3,2,1,0:T(8,128)S(1)}, f32[8,4,8,128]{3,2,1,0:T(8,128)S(1)}) custom-call(s32[2]{0:T(128)S(1)} %pad_add_fusion.where_ref, f32[8,16,512]{2,1,0:T(8,128)} %charges_ref.1), custom_call_target="tpu_custom_call" | custom-call | tf_op jit(solution)/shard_map/pallas_call | solution.py:557
  1.5 3.1 %collective-permute-start = (f32[8,4,8,128]{3,2,1,0:T(8,128)S(1)}, f32[8,4,8,128]{3,2,1,0:T(8,128)S(1)}, u32[]{:S(2)}, u32[]{:S(2)}) collective-permute-start(f32[8,4,8,128]{3,2,1,0:T(8,128)S(1)} %get-tuple-element.14), channel_id=1, source_target_pairs={{0,1},{1,0},{2,3},{3,2},{4,5},{5,4},{6,7},{7,6},{8,9},{9,8},{10,11... | collective-permute-start | bytes 393224 | tf_op jit(solution)/shard_map/ppermute | solution.py:579
  4.6 0.7 %collective-permute-start.1 = (f32[8,4,8,128]{3,2,1,0:T(8,128)S(1)}, f32[8,4,8,128]{3,2,1,0:T(8,128)S(1)}, u32[]{:S(2)}, u32[]{:S(2)}) collective-permute-start(f32[8,4,8,128]{3,2,1,0:T(8,128)S(1)} %get-tuple-element.15), channel_id=1, source_target_pairs={{1,2},{2,1},{5,6},{6,5},{9,10},{10,9},{13,14},{14,13},{17,18},{18,... | collective-permute-start | bytes 393224 | tf_op jit(solution)/shard_map/ppermute | solution.py:603
  5.2 0.1 collective-permute-start.2
  5.3 0.7 %collective-permute-start.4 = (f32[8,4,16,128]{3,2,1,0:T(8,128)S(1)}, f32[8,4,16,128]{3,2,1,0:T(8,128)S(1)}, u32[]{:S(2)}, u32[]{:S(2)}) collective-permute-start(f32[8,4,16,128]{3,2,1,0:T(8,128)S(1)} %get-tuple-element.13.mid_ref), channel_id=1, source_target_pairs={{4,8},{8,4},{5,9},{9,5},{6,10},{10,6},{7,11},{11,7},{20,24},{24,20... | collective-permute-start | bytes 786440 | tf_op jit(solution)/shard_map/ppermute | solution.py:601
  6.0 2.1 %collective-permute-done = f32[8,4,8,128]{3,2,1,0:T(8,128)S(1)} collective-permute-done((f32[8,4,8,128]{3,2,1,0:T(8,128)S(1)}, f32[8,4,8,128]{3,2,1,0:T(8,128)S(1)}, u32[]{:S(2)}, u32[]{:S(2)}) %collective-permute-start) | collective-permute-done | bytes 131104 | tf_op jit(solution)/shard_map/ppermute | solution.py:579
  8.1 0.7 %collective-permute-start.5 = (f32[8,4,8,128]{3,2,1,0:T(8,128)S(1)}, f32[8,4,8,128]{3,2,1,0:T(8,128)S(1)}, u32[]{:S(2)}, u32[]{:S(2)}) collective-permute-start(f32[8,4,8,128]{3,2,1,0:T(8,128)S(1)} %collective-permute-done), channel_id=1, source_target_pairs={{4,8},{8,4},{5,9},{9,5},{6,10},{10,6},{7,11},{11,7},{20,24},{24,20... | collective-permute-start | bytes 393224 | tf_op jit(solution)/shard_map/ppermute | solution.py:611
  8.7 0.0 collective-permute-done.1
  8.7 0.7 %collective-permute-start.6 = (f32[8,4,8,128]{3,2,1,0:T(8,128)S(1)}, f32[8,4,8,128]{3,2,1,0:T(8,128)S(1)}, u32[]{:S(2)}, u32[]{:S(2)}) collective-permute-start(f32[8,4,8,128]{3,2,1,0:T(8,128)S(1)} %collective-permute-done.1), channel_id=1, source_target_pairs={{4,8},{8,4},{5,9},{9,5},{6,10},{10,6},{7,11},{11,7},{20,24},{24,20... | collective-permute-start | bytes 393224 | tf_op jit(solution)/shard_map/ppermute | solution.py:611
  9.5 5.1 %collective-permute-start.3 = (f32[8,4,16,128]{3,2,1,0:T(8,128)S(1)}, f32[8,4,16,128]{3,2,1,0:T(8,128)S(1)}, u32[]{:S(2)}, u32[]{:S(2)}) collective-permute-start(f32[8,4,16,128]{3,2,1,0:T(8,128)S(1)} %pad_maximum_fusion.mid_rim_ref), channel_id=1, source_target_pairs={{0,4},{4,0},{8,12},{12,8},{1,5},{5,1},{9,13},{13,9},{2,6},{6,2},{1... | collective-permute-start | bytes 786440 | tf_op jit(solution)/shard_map/ppermute | solution.py:579
  14.6 0.0 collective-permute-done.2.charges_ref
  14.6 1.0 %shard_map.18.one_ref = f32[8,4,16,128]{3,2,1,0:T(8,128)S(1)} custom-call(s32[2]{0:T(128)S(1)} %pad_add_fusion.where_ref, f32[8,16,512]{2,1,0:T(8,128)S(1)} %collective-permute-done.2.charges_ref), custom_call_target="tpu_custom_call" | custom-call | tf_op jit(solution)/shard_map/pallas_call | solution.py:557
  15.6 0.0 collective-permute-done.5
  15.6 0.0 collective-permute-done.6
  15.7 0.0 collective-permute-done.4.two_ref
  15.7 0.1 collective-permute-done.3.one_rim_ref
  15.8 2.5 %shard_map.19 = (f32[24,4,4,8,128]{4,3,2,1,0:T(8,128)S(1)}, f32[24,4,4,8,128]{4,3,2,1,0:T(8,128)S(1)}, f32[4,2,8,128]{3,2,1,0:T(8,128)S(1)}) custom-call(s32[2]{0:T(128)S(1)} %pad_add_fusion.where_ref, f32[8,4,16,128]{3,2,1,0:T(8,128)S(1)} %get-tuple-element.13.mid_ref, f32[8,4,16,128]{3,2,1,0:T(8,128)S(1)} %pad_maximum_fusion.mid_rim_ref, ...), custom_call_target="tpu_custom_call" | custom-call | tf_op jit(solution)/shard_map/pallas_call | solution.py:557
  18.3 4.5 %collective-permute-start.9 = (f32[1,4,2,8,128]{4,3,2,1,0:T(8,128)S(1)}, f32[1,4,2,8,128]{4,3,2,1,0:T(8,128)S(1)}, u32[]{:S(2)}, u32[]{:S(2)}) collective-permute-start(f32[1,4,2,8,128]{4,3,2,1,0:T(8,128)S(1)} %bitcast.6), channel_id=1, source_target_pairs={{0,1},{1,0},{2,3},{3,2},{4,5},{5,4},{6,7},{7,6},{8,9},{9,8},{10,11... | collective-permute-start | bytes 98312 | tf_op jit(solution)/shard_map/ppermute | solution.py:579
  22.7 0.0 collective-permute-start.8
  22.7 2.4 %collective-permute-start.7 = (f32[1,4,2,8,128]{4,3,2,1,0:T(8,128)S(1)}, f32[1,4,2,8,128]{4,3,2,1,0:T(8,128)S(1)}, u32[]{:S(2)}, u32[]{:S(2)}) collective-permute-start(f32[1,4,2,8,128]{4,3,2,1,0:T(8,128)S(1)} %bitcast.8), channel_id=1, source_target_pairs={{0,3},{1,2},{2,1},{3,0},{4,7},{5,6},{6,5},{7,4},{8,11},{9,10},{10,... | collective-permute-start | bytes 98312 | tf_op jit(solution)/shard_map/ppermute | solution.py:579
  25.2 0.0 collective-permute-done.9
  25.2 3.1 %collective-permute-start.11 = (f32[2,4,2,8,128]{4,3,2,1,0:T(8,128)S(1)}, f32[2,4,2,8,128]{4,3,2,1,0:T(8,128)S(1)}, u32[]{:S(2)}, u32[]{:S(2)}) collective-permute-start(f32[2,4,2,8,128]{4,3,2,1,0:T(8,128)S(1)} %pad_maximum_fusion.3), channel_id=1, source_target_pairs={{0,8},{4,12},{8,0},{12,4},{1,9},{5,13},{9,1},{13,5},{2,10},{6,14},... | collective-permute-start | bytes 196616 | tf_op jit(solution)/shard_map/ppermute | solution.py:579
  28.3 0.0 collective-permute-done.8
  28.3 0.3 collective-permute-done.7
  28.6 2.9 %collective-permute-start.10 = (f32[2,4,2,8,128]{4,3,2,1,0:T(8,128)S(1)}, f32[2,4,2,8,128]{4,3,2,1,0:T(8,128)S(1)}, u32[]{:S(2)}, u32[]{:S(2)}) collective-permute-start(f32[2,4,2,8,128]{4,3,2,1,0:T(8,128)S(1)} %pad_maximum_fusion.2), channel_id=1, source_target_pairs={{0,8},{4,12},{8,0},{12,4},{1,9},{5,13},{9,1},{13,5},{2,10},{6,14},... | collective-permute-start | bytes 196616 | tf_op jit(solution)/shard_map/ppermute | solution.py:579
  31.5 2.2 %collective-permute-done.10 = f32[2,4,2,8,128]{4,3,2,1,0:T(8,128)S(1)} collective-permute-done((f32[2,4,2,8,128]{4,3,2,1,0:T(8,128)S(1)}, f32[2,4,2,8,128]{4,3,2,1,0:T(8,128)S(1)}, u32[]{:S(2)}, u32[]{:S(2)}) %collective-permute-start.10) | collective-permute-done | bytes 65568 | tf_op jit(solution)/shard_map/ppermute | solution.py:579
  33.8 0.0 collective-permute-done.11
  33.8 0.1 collective-permute-start.12
  33.9 1.5 %collective-permute-done.12.refs_1_ = f32[8,4,2,8,128]{4,3,2,1,0:T(8,128)S(1)} collective-permute-done((f32[8,4,2,8,128]{4,3,2,1,0:T(8,128)S(1)}, f32[8,4,2,8,128]{4,3,2,1,0:T(8,128)S(1)}, u32[]{:S(2)}, u32[]{:S(2)}) %collective-permute-start.12) | collective-permute-done | bytes 262176 | tf_op jit(solution)/shard_map/ppermute | solution.py:579
  35.4 5.7 %shard_map.20 = (f32[24,4,4,8,128]{4,3,2,1,0:T(8,128)S(1)}, f32[4,2,8,128]{3,2,1,0:T(8,128)S(1)}) custom-call(s32[2]{0:T(128)S(1)} %pad_add_fusion.where_ref, f32[8,4,2,8,128]{4,3,2,1,0:T(8,128)S(1)} %constant_dynamic-update-slice_fusion.refs_0_, f32[8,4,2,8,128]{4,3,2,1,0:T(8,128)S(1)} %collective-permute-done.12.refs_1_, ...), custom_call_target="tpu_custom_call" | custom-call | tf_op jit(solution)/shard_map/pallas_call | solution.py:557
  41.1 0.4 collective-permute-start.15
  41.5 2.7 %collective-permute-start.14 = (f32[1,4,2,8,128]{4,3,2,1,0:T(8,128)S(1)}, f32[1,4,2,8,128]{4,3,2,1,0:T(8,128)S(1)}, u32[]{:S(2)}, u32[]{:S(2)}) collective-permute-start(f32[1,4,2,8,128]{4,3,2,1,0:T(8,128)S(1)} %bitcast.11), channel_id=1, source_target_pairs={{0,2},{1,3},{2,0},{3,1},{4,6},{5,7},{6,4},{7,5},{8,10},{9,11},{10,... | collective-permute-start | bytes 98312 | tf_op jit(solution)/shard_map/ppermute | solution.py:579
  44.2 1.4 %collective-permute-start.13 = (f32[1,4,2,8,128]{4,3,2,1,0:T(8,128)S(1)}, f32[1,4,2,8,128]{4,3,2,1,0:T(8,128)S(1)}, u32[]{:S(2)}, u32[]{:S(2)}) collective-permute-start(f32[1,4,2,8,128]{4,3,2,1,0:T(8,128)S(1)} %bitcast.12), channel_id=1, source_target_pairs={{0,3},{1,2},{2,1},{3,0},{4,7},{5,6},{6,5},{7,4},{8,11},{9,10},{10,... | collective-permute-start | bytes 98312 | tf_op jit(solution)/shard_map/ppermute | solution.py:579
  45.6 0.0 collective-permute-done.15
  45.6 2.1 %collective-permute-start.17 = (f32[2,4,2,8,128]{4,3,2,1,0:T(8,128)S(1)}, f32[2,4,2,8,128]{4,3,2,1,0:T(8,128)S(1)}, u32[]{:S(2)}, u32[]{:S(2)}) collective-permute-start(f32[2,4,2,8,128]{4,3,2,1,0:T(8,128)S(1)} %pad_maximum_fusion.5), channel_id=1, source_target_pairs={{0,8},{4,12},{8,0},{12,4},{1,9},{5,13},{9,1},{13,5},{2,10},{6,14},... | collective-permute-start | bytes 196616 | tf_op jit(solution)/shard_map/ppermute | solution.py:579
  47.7 0.0 collective-permute-done.14
  47.7 2.2 %collective-permute-done.13 = f32[1,4,2,8,128]{4,3,2,1,0:T(8,128)S(1)} collective-permute-done((f32[1,4,2,8,128]{4,3,2,1,0:T(8,128)S(1)}, f32[1,4,2,8,128]{4,3,2,1,0:T(8,128)S(1)}, u32[]{:S(2)}, u32[]{:S(2)}) %collective-permute-start.13) | collective-permute-done | bytes 32800 | tf_op jit(solution)/shard_map/ppermute | solution.py:579
  49.9 2.0 %collective-permute-start.16 = (f32[2,4,2,8,128]{4,3,2,1,0:T(8,128)S(1)}, f32[2,4,2,8,128]{4,3,2,1,0:T(8,128)S(1)}, u32[]{:S(2)}, u32[]{:S(2)}) collective-permute-start(f32[2,4,2,8,128]{4,3,2,1,0:T(8,128)S(1)} %pad_maximum_fusion.4), channel_id=1, source_target_pairs={{0,8},{4,12},{8,0},{12,4},{1,9},{5,13},{9,1},{13,5},{2,10},{6,14},... | collective-permute-start | bytes 196616 | tf_op jit(solution)/shard_map/ppermute | solution.py:579
  52.0 2.2 %collective-permute-done.16 = f32[2,4,2,8,128]{4,3,2,1,0:T(8,128)S(1)} collective-permute-done((f32[2,4,2,8,128]{4,3,2,1,0:T(8,128)S(1)}, f32[2,4,2,8,128]{4,3,2,1,0:T(8,128)S(1)}, u32[]{:S(2)}, u32[]{:S(2)}) %collective-permute-start.16) | collective-permute-done | bytes 65568 | tf_op jit(solution)/shard_map/ppermute | solution.py:579
  54.2 0.0 collective-permute-done.17
  54.2 0.1 collective-permute-start.18
  54.3 1.5 %collective-permute-done.18.refs_1_ = f32[8,4,2,8,128]{4,3,2,1,0:T(8,128)S(1)} collective-permute-done((f32[8,4,2,8,128]{4,3,2,1,0:T(8,128)S(1)}, f32[8,4,2,8,128]{4,3,2,1,0:T(8,128)S(1)}, u32[]{:S(2)}, u32[]{:S(2)}) %collective-permute-start.18) | collective-permute-done | bytes 262176 | tf_op jit(solution)/shard_map/ppermute | solution.py:579
  55.8 4.8 %shard_map.21 = f32[8,16,512]{2,1,0:T(8,128)} custom-call(s32[2]{0:T(128)S(1)} %pad_add_fusion.where_ref, f32[8,4,2,8,128]{4,3,2,1,0:T(8,128)S(1)} %constant_dynamic-update-slice_fusion.6.refs_0_, f32[8,4,2,8,128]{4,3,2,1,0:T(8,128)S(1)} %collective-permute-done.18.refs_1_, f32[24,4,4,8,128]{4,3,2,1,0:T(8,128)S(1)} %get-tuple-element.20.refs_2_, ...), custom_call_target="tpu_custom_call" | custom-call | tf_op jit(solution)/shard_map/pallas_call | solution.py:557
  (20 shorter events, 0.2 us)
Async XLA Ops:
  1.5 6.6 %collective-permute-start = (f32[8,4,8,128]{3,2,1,0:T(8,128)S(1)}, f32[8,4,8,128]{3,2,1,0:T(8,128)S(1)}, u32[]{:S(2)}, u32[]{:S(2)}) collective-permute-start(f32[8,4,8,128]{3,2,1,0:T(8,128)S(1)} %get-tuple-element.14), channel_id=1, source_target_pairs={{0,1},{1,0},{2,3},{3,2},{4,5},{5,4},{6,7},{7,6},{8,9},{9,8},{10,11... | collective-permute-start | bytes 393224 | tf_op jit(solution)/shard_map/ppermute | solution.py:579
  4.6 4.2 %collective-permute-start.1 = (f32[8,4,8,128]{3,2,1,0:T(8,128)S(1)}, f32[8,4,8,128]{3,2,1,0:T(8,128)S(1)}, u32[]{:S(2)}, u32[]{:S(2)}) collective-permute-start(f32[8,4,8,128]{3,2,1,0:T(8,128)S(1)} %get-tuple-element.15), channel_id=1, source_target_pairs={{1,2},{2,1},{5,6},{6,5},{9,10},{10,9},{13,14},{14,13},{17,18},{18,... | collective-permute-start | bytes 393224 | tf_op jit(solution)/shard_map/ppermute | solution.py:603
  5.2 9.4 %collective-permute-start.2 = (f32[8,16,512]{2,1,0:T(8,128)}, f32[8,16,512]{2,1,0:T(8,128)S(1)}, u32[]{:S(2)}, u32[]{:S(2)}) collective-permute-start(f32[8,16,512]{2,1,0:T(8,128)} %charges_ref.1), channel_id=1, source_target_pairs={{0,4},{4,0},{8,12},{12,8},{1,5},{5,1},{9,13},{13,9},{2,6},{6,2},{1... | collective-permute-start | bytes 786440 | tf_op jit(solution)/shard_map/ppermute | solution.py:579
  5.3 10.4 %collective-permute-start.4 = (f32[8,4,16,128]{3,2,1,0:T(8,128)S(1)}, f32[8,4,16,128]{3,2,1,0:T(8,128)S(1)}, u32[]{:S(2)}, u32[]{:S(2)}) collective-permute-start(f32[8,4,16,128]{3,2,1,0:T(8,128)S(1)} %get-tuple-element.13.mid_ref), channel_id=1, source_target_pairs={{4,8},{8,4},{5,9},{9,5},{6,10},{10,6},{7,11},{11,7},{20,24},{24,20... | collective-permute-start | bytes 786440 | tf_op jit(solution)/shard_map/ppermute | solution.py:601
  8.1 7.5 %collective-permute-start.5 = (f32[8,4,8,128]{3,2,1,0:T(8,128)S(1)}, f32[8,4,8,128]{3,2,1,0:T(8,128)S(1)}, u32[]{:S(2)}, u32[]{:S(2)}) collective-permute-start(f32[8,4,8,128]{3,2,1,0:T(8,128)S(1)} %collective-permute-done), channel_id=1, source_target_pairs={{4,8},{8,4},{5,9},{9,5},{6,10},{10,6},{7,11},{11,7},{20,24},{24,20... | collective-permute-start | bytes 393224 | tf_op jit(solution)/shard_map/ppermute | solution.py:611
  8.7 6.9 %collective-permute-start.6 = (f32[8,4,8,128]{3,2,1,0:T(8,128)S(1)}, f32[8,4,8,128]{3,2,1,0:T(8,128)S(1)}, u32[]{:S(2)}, u32[]{:S(2)}) collective-permute-start(f32[8,4,8,128]{3,2,1,0:T(8,128)S(1)} %collective-permute-done.1), channel_id=1, source_target_pairs={{4,8},{8,4},{5,9},{9,5},{6,10},{10,6},{7,11},{11,7},{20,24},{24,20... | collective-permute-start | bytes 393224 | tf_op jit(solution)/shard_map/ppermute | solution.py:611
  9.5 6.3 %collective-permute-start.3 = (f32[8,4,16,128]{3,2,1,0:T(8,128)S(1)}, f32[8,4,16,128]{3,2,1,0:T(8,128)S(1)}, u32[]{:S(2)}, u32[]{:S(2)}) collective-permute-start(f32[8,4,16,128]{3,2,1,0:T(8,128)S(1)} %pad_maximum_fusion.mid_rim_ref), channel_id=1, source_target_pairs={{0,4},{4,0},{8,12},{12,8},{1,5},{5,1},{9,13},{13,9},{2,6},{6,2},{1... | collective-permute-start | bytes 786440 | tf_op jit(solution)/shard_map/ppermute | solution.py:579
  18.3 6.9 %collective-permute-start.9 = (f32[1,4,2,8,128]{4,3,2,1,0:T(8,128)S(1)}, f32[1,4,2,8,128]{4,3,2,1,0:T(8,128)S(1)}, u32[]{:S(2)}, u32[]{:S(2)}) collective-permute-start(f32[1,4,2,8,128]{4,3,2,1,0:T(8,128)S(1)} %bitcast.6), channel_id=1, source_target_pairs={{0,1},{1,0},{2,3},{3,2},{4,5},{5,4},{6,7},{7,6},{8,9},{9,8},{10,11... | collective-permute-start | bytes 98312 | tf_op jit(solution)/shard_map/ppermute | solution.py:579
  22.7 5.6 %collective-permute-start.8 = (f32[1,4,2,8,128]{4,3,2,1,0:T(8,128)S(1)}, f32[1,4,2,8,128]{4,3,2,1,0:T(8,128)S(1)}, u32[]{:S(2)}, u32[]{:S(2)}) collective-permute-start(f32[1,4,2,8,128]{4,3,2,1,0:T(8,128)S(1)} %bitcast.7), channel_id=1, source_target_pairs={{0,2},{1,3},{2,0},{3,1},{4,6},{5,7},{6,4},{7,5},{8,10},{9,11},{10,... | collective-permute-start | bytes 98312 | tf_op jit(solution)/shard_map/ppermute | solution.py:579
  22.7 5.8 %collective-permute-start.7 = (f32[1,4,2,8,128]{4,3,2,1,0:T(8,128)S(1)}, f32[1,4,2,8,128]{4,3,2,1,0:T(8,128)S(1)}, u32[]{:S(2)}, u32[]{:S(2)}) collective-permute-start(f32[1,4,2,8,128]{4,3,2,1,0:T(8,128)S(1)} %bitcast.8), channel_id=1, source_target_pairs={{0,3},{1,2},{2,1},{3,0},{4,7},{5,6},{6,5},{7,4},{8,11},{9,10},{10,... | collective-permute-start | bytes 98312 | tf_op jit(solution)/shard_map/ppermute | solution.py:579
  25.2 8.6 %collective-permute-start.11 = (f32[2,4,2,8,128]{4,3,2,1,0:T(8,128)S(1)}, f32[2,4,2,8,128]{4,3,2,1,0:T(8,128)S(1)}, u32[]{:S(2)}, u32[]{:S(2)}) collective-permute-start(f32[2,4,2,8,128]{4,3,2,1,0:T(8,128)S(1)} %pad_maximum_fusion.3), channel_id=1, source_target_pairs={{0,8},{4,12},{8,0},{12,4},{1,9},{5,13},{9,1},{13,5},{2,10},{6,14},... | collective-permute-start | bytes 196616 | tf_op jit(solution)/shard_map/ppermute | solution.py:579
  28.6 5.2 %collective-permute-start.10 = (f32[2,4,2,8,128]{4,3,2,1,0:T(8,128)S(1)}, f32[2,4,2,8,128]{4,3,2,1,0:T(8,128)S(1)}, u32[]{:S(2)}, u32[]{:S(2)}) collective-permute-start(f32[2,4,2,8,128]{4,3,2,1,0:T(8,128)S(1)} %pad_maximum_fusion.2), channel_id=1, source_target_pairs={{0,8},{4,12},{8,0},{12,4},{1,9},{5,13},{9,1},{13,5},{2,10},{6,14},... | collective-permute-start | bytes 196616 | tf_op jit(solution)/shard_map/ppermute | solution.py:579
  33.8 1.6 %collective-permute-start.12 = (f32[8,4,2,8,128]{4,3,2,1,0:T(8,128)S(1)}, f32[8,4,2,8,128]{4,3,2,1,0:T(8,128)S(1)}, u32[]{:S(2)}, u32[]{:S(2)}) collective-permute-start(f32[8,4,2,8,128]{4,3,2,1,0:T(8,128)S(1)} %constant_dynamic-update-slice_fusion.refs_0_), channel_id=1, source_target_pairs={{0,4},{4,0},{8,12},{12,8},{1,5},{5,1},{9,13},{13,9},{2,6},{6,2},{1... | collective-permute-start | bytes 786440 | tf_op jit(solution)/shard_map/ppermute | solution.py:579
  41.1 4.5 %collective-permute-start.15 = (f32[1,4,2,8,128]{4,3,2,1,0:T(8,128)S(1)}, f32[1,4,2,8,128]{4,3,2,1,0:T(8,128)S(1)}, u32[]{:S(2)}, u32[]{:S(2)}) collective-permute-start(f32[1,4,2,8,128]{4,3,2,1,0:T(8,128)S(1)} %bitcast.10), channel_id=1, source_target_pairs={{0,1},{1,0},{2,3},{3,2},{4,5},{5,4},{6,7},{7,6},{8,9},{9,8},{10,11... | collective-permute-start | bytes 98312 | tf_op jit(solution)/shard_map/ppermute | solution.py:579
  41.5 6.2 %collective-permute-start.14 = (f32[1,4,2,8,128]{4,3,2,1,0:T(8,128)S(1)}, f32[1,4,2,8,128]{4,3,2,1,0:T(8,128)S(1)}, u32[]{:S(2)}, u32[]{:S(2)}) collective-permute-start(f32[1,4,2,8,128]{4,3,2,1,0:T(8,128)S(1)} %bitcast.11), channel_id=1, source_target_pairs={{0,2},{1,3},{2,0},{3,1},{4,6},{5,7},{6,4},{7,5},{8,10},{9,11},{10,... | collective-permute-start | bytes 98312 | tf_op jit(solution)/shard_map/ppermute | solution.py:579
  44.2 5.7 %collective-permute-start.13 = (f32[1,4,2,8,128]{4,3,2,1,0:T(8,128)S(1)}, f32[1,4,2,8,128]{4,3,2,1,0:T(8,128)S(1)}, u32[]{:S(2)}, u32[]{:S(2)}) collective-permute-start(f32[1,4,2,8,128]{4,3,2,1,0:T(8,128)S(1)} %bitcast.12), channel_id=1, source_target_pairs={{0,3},{1,2},{2,1},{3,0},{4,7},{5,6},{6,5},{7,4},{8,11},{9,10},{10,... | collective-permute-start | bytes 98312 | tf_op jit(solution)/shard_map/ppermute | solution.py:579
  45.6 8.6 %collective-permute-start.17 = (f32[2,4,2,8,128]{4,3,2,1,0:T(8,128)S(1)}, f32[2,4,2,8,128]{4,3,2,1,0:T(8,128)S(1)}, u32[]{:S(2)}, u32[]{:S(2)}) collective-permute-start(f32[2,4,2,8,128]{4,3,2,1,0:T(8,128)S(1)} %pad_maximum_fusion.5), channel_id=1, source_target_pairs={{0,8},{4,12},{8,0},{12,4},{1,9},{5,13},{9,1},{13,5},{2,10},{6,14},... | collective-permute-start | bytes 196616 | tf_op jit(solution)/shard_map/ppermute | solution.py:579
  49.9 4.3 %collective-permute-start.16 = (f32[2,4,2,8,128]{4,3,2,1,0:T(8,128)S(1)}, f32[2,4,2,8,128]{4,3,2,1,0:T(8,128)S(1)}, u32[]{:S(2)}, u32[]{:S(2)}) collective-permute-start(f32[2,4,2,8,128]{4,3,2,1,0:T(8,128)S(1)} %pad_maximum_fusion.4), channel_id=1, source_target_pairs={{0,8},{4,12},{8,0},{12,4},{1,9},{5,13},{9,1},{13,5},{2,10},{6,14},... | collective-permute-start | bytes 196616 | tf_op jit(solution)/shard_map/ppermute | solution.py:579
  54.2 1.6 %collective-permute-start.18 = (f32[8,4,2,8,128]{4,3,2,1,0:T(8,128)S(1)}, f32[8,4,2,8,128]{4,3,2,1,0:T(8,128)S(1)}, u32[]{:S(2)}, u32[]{:S(2)}) collective-permute-start(f32[8,4,2,8,128]{4,3,2,1,0:T(8,128)S(1)} %constant_dynamic-update-slice_fusion.6.refs_0_), channel_id=1, source_target_pairs={{0,4},{4,0},{8,12},{12,8},{1,5},{5,1},{9,13},{13,9},{2,6},{6,2},{1... | collective-permute-start | bytes 786440 | tf_op jit(solution)/shard_map/ppermute | solution.py:579

commit v12 on v10

--- a/solution.py
+++ b/solution.py
@@ -459,16 +459,7 @@
         two_ref[:, p] = jnp.where(odd == 0, first, last)
 
 
-def near_lanes_kernel(where_ref, charges_ref, rows_ref):
-    for p, tile in enumerate(split_lanes(charges_ref[...])):
-        rows_ref[:, p] = tile
-
-
-def down_kernel(count_x, count_z, where_ref, mid_ref, mid_rim_ref, one_ref, one_rim_ref, two_ref,
-                two_rim_ref, u_ref, b_ref, out_ref, c_ref, g_ref, h_ref, rows_ref):
-    masks = rim_masks(count_x, count_z, where_ref)
-    odd = where_ref[0] % 2
-
+def row_splitter(rows_ref, c_ref):
     def split_rows(ref, rim_ref, part):
         def split(x):
             for p in range(4):
@@ -479,11 +470,14 @@
 
         each(0, BRICK_X, split, 2)
 
-    split_rows(mid_ref, mid_rim_ref, 1)
-    split_rows(one_ref, one_rim_ref, 2 - 2 * odd)
-    split_rows(two_ref, two_rim_ref, 2 * odd)
-
-    def source(x, weight):
+    return split_rows
+
+
+def source_on(c_ref, b_ref, g_ref, start, count, mask):
+    weight = mask * (0.2 / 12.0)
+
+    def body(i):
+        x = start + i
         here = FINE.load(c_ref, x)
         sums = along_z(here, 1, True)
         plane = []
@@ -496,12 +490,61 @@
             plane.append(line)
         FINE.put(b_ref, g_ref, x, plane)
 
-    in_segments(1, WIDE_X - 1, source, masks, 0.2 / 12.0, 4)
-
-    def body(x, weight):
+    each(0, count, body, 4)
+
+
+def first_sweep_on(b_ref, g_ref, u_ref, h_ref, start, count, mask):
+    weight = mask * (1.0 / 30.0)
+
+    def body(i):
+        x = start + i
         FINE.put(u_ref, h_ref, x, FINE.sweep(b_ref, g_ref, b_ref, x, weight))
 
-    in_segments(2, WIDE_X - 2, body, masks, 1.0 / 30.0, 4)
+    each(0, count, body, 4)
+
+
+def early_kernel(count_x, count_z, where_ref, mid_ref, mid_rim_ref, near_ref, far_ref, c_ref,
+                 b_ref, g_ref, u_ref, h_ref, lanes_ref, rows_ref):
+    inner = rim_masks(count_x, count_z, where_ref)[0]
+    odd = where_ref[0] % 2
+    for p, tile in enumerate(split_lanes(near_ref[...])):
+        lanes_ref[:, p] = tile
+    split_rows = row_splitter(rows_ref, c_ref)
+    split_rows(mid_ref, mid_rim_ref, 1)
+    split_rows(lanes_ref, mid_rim_ref, 2 - 2 * odd)
+    split_rows(far_ref, mid_rim_ref, 2 * odd)
+    source_on(c_ref, b_ref, g_ref, 9, 6, inner)
+    first_sweep_on(b_ref, g_ref, u_ref, h_ref, 10, 4, inner)
+
+
+def down_kernel(count_x, count_z, where_ref, near_rim_ref, far_rim_ref, c_in, b_in, g_in, u_in, h_in,
+                c_ref, b_ref, g_ref, u_ref, h_ref, out_ref):
+    del c_in, b_in, g_in, u_in, h_in
+    inner, below, above = rim_masks(count_x, count_z, where_ref)
+    odd = where_ref[0] % 2
+    far = inner * jnp.where(odd == 0, below, above)
+    first = row_of((8, LANES)) < 4
+
+    def join_rows(rim_ref, start):
+        def join_plane(i):
+            for p in range(4):
+                for q in range(4):
+                    rim = rim_ref[i, p, pl.ds(q, 4, stride=4), :]
+                    rim = jnp.concatenate([rim, rim], axis=0)
+                    c_ref[start + i, q, p] = jnp.where(first, c_ref[start + i, q, p], rim)
+
+        each(0, BRICK_X, join_plane, 2)
+
+    join_rows(near_rim_ref, 2 * BRICK_X * (1 - odd))
+    join_rows(far_rim_ref, 2 * BRICK_X * odd)
+    source_on(c_ref, b_ref, g_ref, 1 + 15 * odd, 7, far)
+    source_on(c_ref, b_ref, g_ref, 16 - 15 * odd, 7, inner)
+    source_on(c_ref, b_ref, g_ref, 8, 1, inner)
+    source_on(c_ref, b_ref, g_ref, 15, 1, inner)
+    first_sweep_on(b_ref, g_ref, u_ref, h_ref, 2 + 14 * odd, 6, far)
+    first_sweep_on(b_ref, g_ref, u_ref, h_ref, 16 - 14 * odd, 6, inner)
+    first_sweep_on(b_ref, g_ref, u_ref, h_ref, 8, 2, inner)
+    first_sweep_on(b_ref, g_ref, u_ref, h_ref, 14, 2, inner)
     send_residual(u_ref, h_ref, b_ref, out_ref)
 
 
@@ -547,7 +590,7 @@
     out_ref[...] = permuted(jnp.concatenate(tiles, axis=1), matrix).reshape(out_ref.shape)
 
 
-def call(kernel, outputs, scratch):
+def call(kernel, outputs, scratch, in_place=None):
     shapes = [jax.ShapeDtypeStruct(shape, jnp.float32) for shape in outputs]
     held = sum(4 * math.prod(shape.shape) for shape in scratch)
 
@@ -560,6 +603,7 @@
             in_specs=[pl.BlockSpec(memory_space=pltpu.SMEM)] + [whole] * len(arrays),
             out_specs=[whole] * len(shapes),
             scratch_shapes=scratch,
+            input_output_aliases=in_place or {},
             compiler_params=pltpu.CompilerParams(vmem_limit_bytes=held + moved + SPARE_BYTES),
         )(where, *arrays)
 
@@ -599,7 +643,7 @@
     middle, one, two = call(lanes_kernel, [brick, rim, rim], [])(where, charges)
     x_far, z_two = pairs_shifted(count_x), pairs_shifted(count_z)
     far = lax.ppermute(middle, "gx", x_far)
-    (near,) = call(near_lanes_kernel, [brick], [])(where, swap("gx", charges, 1))
+    near = swap("gx", charges, 1)
     one, two = swap("gz", one, 1), lax.ppermute(two, "gz", z_two)
     even = at_z % 2 == 0
     middle_rim = jnp.concatenate([jnp.where(even, one, two), jnp.where(even, two, one)], axis=2)
@@ -614,11 +658,17 @@
     close = pltpu.VMEM((WIDE_X // 2, 2, 2, 8, LANES), jnp.float32)
     rows_out = pltpu.VMEM((BRICK_X, 4, BRICK_Z, LANES), jnp.float32)
 
-    u, b, piece = call(
+    early = call(
+        functools.partial(early_kernel, count_x, count_z),
+        [wide] * 5,
+        [pltpu.VMEM(brick, jnp.float32), rows_in],
+    )(where, middle, middle_rim, near, far)
+    _, b, _, u, _, piece = call(
         functools.partial(down_kernel, count_x, count_z),
-        [wide, wide, piece_shape],
-        [fine] * 3 + [rows_in],
-    )(where, middle, middle_rim, near, near_rim, far, far_rim)
+        [wide] * 5 + [piece_shape],
+        [],
+        in_place={3 + i: i for i in range(5)},
+    )(where, near_rim, far_rim, *early)
     pieces = every_piece(piece)
     u, piece = call(
         functools.partial(middle_kernel, count_x, count_z, len(pieces)),

time: 59.9 us -> 59.6 us (level)
  starting transfers between devices: 33 us -> 32.1 us
    ppermute x15, starting transfers between devices: 31 us -> 30.1 us  [swap(): lax.ppermute(values, axis, pairs_apart(lax.axis_size(axis), distance))]
  transfers between devices with their start and end apart: 18 -> 18, of which waited for: 7 -> 7; matrix products, arithmetic and copies ran while one was open for 0% -> 0% of each run, Pallas kernels for 2% -> 3%
where the time goes in v12:
time: 59.6 us; the launch traced here: 59.4 us
  starting transfers between devices  32.1 us (54%)
  Pallas kernels  15.8 us (27%)
  waiting for transfers between devices  11.1 us (19%)
    ppermute x15, starting transfers between devices, swap(): lax.ppermute(values, axis, pairs_apart(lax.axis_size(axis), distance))  30.1 us
    pallas_call x5, Pallas kernels, run(): pl.pallas_call(kernel, out_shape=shapes, in_specs=[pl.BlockSpec(memory_sp...  15.8 us
    ppermute x15, waiting for transfers between devices, swap(): lax.ppermute(values, axis, pairs_apart(lax.axis_size(axis), distance))  11.1 us
  transfers between devices with their start and end apart: 18, of which 7 were waited for; matrix products, arithmetic and copies ran while one was open for 0% of the time, Pallas kernels for 3%

profile of v12, /device:TPU:0, one launch (start us, length us, event | category | flops | bytes accessed | tf_op | source)
XLA Modules:
  0.0 59.4 jit_solution(14863549713842883878)
XLA Ops:
  0.0 0.1 pad_add_fusion.where_ref
  0.1 1.4 %shard_map.17 = (f32[8,4,16,128]{3,2,1,0:T(8,128)S(1)}, f32[8,4,8,128]{3,2,1,0:T(8,128)S(1)}, f32[8,4,8,128]{3,2,1,0:T(8,128)S(1)}) custom-call(s32[2]{0:T(128)S(1)} %pad_add_fusion.where_ref, f32[8,16,512]{2,1,0:T(8,128)} %charges_ref.1), custom_call_target="tpu_custom_call" | custom-call | tf_op jit(solution)/shard_map/pallas_call | solution.py:600
  1.5 3.1 %collective-permute-start = (f32[8,4,8,128]{3,2,1,0:T(8,128)S(1)}, f32[8,4,8,128]{3,2,1,0:T(8,128)S(1)}, u32[]{:S(2)}, u32[]{:S(2)}) collective-permute-start(f32[8,4,8,128]{3,2,1,0:T(8,128)S(1)} %get-tuple-element.18), channel_id=1, source_target_pairs={{0,1},{1,0},{2,3},{3,2},{4,5},{5,4},{6,7},{7,6},{8,9},{9,8},{10,11... | collective-permute-start | bytes 393224 | tf_op jit(solution)/shard_map/ppermute | solution.py:623
  4.6 0.7 %collective-permute-start.1 = (f32[8,4,8,128]{3,2,1,0:T(8,128)S(1)}, f32[8,4,8,128]{3,2,1,0:T(8,128)S(1)}, u32[]{:S(2)}, u32[]{:S(2)}) collective-permute-start(f32[8,4,8,128]{3,2,1,0:T(8,128)S(1)} %get-tuple-element.19), channel_id=1, source_target_pairs={{1,2},{2,1},{5,6},{6,5},{9,10},{10,9},{13,14},{14,13},{17,18},{18,... | collective-permute-start | bytes 393224 | tf_op jit(solution)/shard_map/ppermute | solution.py:647
  5.2 0.1 collective-permute-start.4
  5.3 0.7 %collective-permute-start.5 = (f32[8,4,16,128]{3,2,1,0:T(8,128)S(1)}, f32[8,4,16,128]{3,2,1,0:T(8,128)S(1)}, u32[]{:S(2)}, u32[]{:S(2)}) collective-permute-start(f32[8,4,16,128]{3,2,1,0:T(8,128)S(1)} %get-tuple-element.20.mid_ref), channel_id=1, source_target_pairs={{4,8},{8,4},{5,9},{9,5},{6,10},{10,6},{7,11},{11,7},{20,24},{24,20... | collective-permute-start | bytes 786440 | tf_op jit(solution)/shard_map/ppermute | solution.py:645
  6.0 2.1 %collective-permute-done = f32[8,4,8,128]{3,2,1,0:T(8,128)S(1)} collective-permute-done((f32[8,4,8,128]{3,2,1,0:T(8,128)S(1)}, f32[8,4,8,128]{3,2,1,0:T(8,128)S(1)}, u32[]{:S(2)}, u32[]{:S(2)}) %collective-permute-start) | collective-permute-done | bytes 131104 | tf_op jit(solution)/shard_map/ppermute | solution.py:623
  8.1 0.0 collective-permute-done.1
  8.1 0.7 %collective-permute-start.3 = (f32[8,4,16,128]{3,2,1,0:T(8,128)S(1)}, f32[8,4,16,128]{3,2,1,0:T(8,128)S(1)}, u32[]{:S(2)}, u32[]{:S(2)}) collective-permute-start(f32[8,4,16,128]{3,2,1,0:T(8,128)S(1)} %pad_maximum_fusion.mid_rim_ref), channel_id=1, source_target_pairs={{4,8},{8,4},{5,9},{9,5},{6,10},{10,6},{7,11},{11,7},{20,24},{24,20... | collective-permute-start | bytes 786440 | tf_op jit(solution)/shard_map/ppermute | solution.py:650
  8.8 3.1 %collective-permute-start.2 = (f32[8,4,16,128]{3,2,1,0:T(8,128)S(1)}, f32[8,4,16,128]{3,2,1,0:T(8,128)S(1)}, u32[]{:S(2)}, u32[]{:S(2)}) collective-permute-start(f32[8,4,16,128]{3,2,1,0:T(8,128)S(1)} %pad_maximum_fusion.mid_rim_ref), channel_id=1, source_target_pairs={{0,4},{4,0},{8,12},{12,8},{1,5},{5,1},{9,13},{13,9},{2,6},{6,2},{1... | collective-permute-start | bytes 786440 | tf_op jit(solution)/shard_map/ppermute | solution.py:623
  11.9 0.0 collective-permute-done.4.near_ref
  11.9 0.0 collective-permute-done.5.far_ref
  11.9 1.7 %shard_map.18 = (f32[24,4,4,8,128]{4,3,2,1,0:T(8,128)S(1)}, f32[24,4,4,8,128]{4,3,2,1,0:T(8,128)S(1)}, f32[24,4,4,8,128]{4,3,2,1,0:T(8,128)S(1)}, f32[24,4,4,8,1...) custom-call(s32[2]{0:T(128)S(1)} %pad_add_fusion.where_ref, f32[8,4,16,128]{3,2,1,0:T(8,128)S(1)} %get-tuple-element.20.mid_ref, ...), custom_call_target="tpu_custom_call" | custom-call | tf_op jit(solution)/shard_map/pallas_call | solution.py:600
  13.6 0.0 collective-permute-done.3.far_rim_ref
  13.6 0.0 collective-permute-done.2.near_rim_ref
  13.6 2.2 %shard_map.19 = (f32[24,4,4,8,128]{4,3,2,1,0:T(8,128)S(1)}, f32[24,4,4,8,128]{4,3,2,1,0:T(8,128)S(1)}, f32[24,4,4,8,128]{4,3,2,1,0:T(8,128)S(1)}, f32[24,4,4,8,1...) custom-call(s32[2]{0:T(128)S(1)} %pad_add_fusion.where_ref, ...), custom_call_target="tpu_custom_call", output_to_operand_aliasing={{0}: (3, {}), {1}: (4, {}), {2}: (5, {}), {3}: (6, {}), {4}... | custom-call | tf_op jit(solution)/shard_map/pallas_call | solution.py:600
  15.8 4.7 %collective-permute-start.8 = (f32[1,4,2,8,128]{4,3,2,1,0:T(8,128)S(1)}, f32[1,4,2,8,128]{4,3,2,1,0:T(8,128)S(1)}, u32[]{:S(2)}, u32[]{:S(2)}) collective-permute-start(f32[1,4,2,8,128]{4,3,2,1,0:T(8,128)S(1)} %bitcast.6), channel_id=1, source_target_pairs={{0,1},{1,0},{2,3},{3,2},{4,5},{5,4},{6,7},{7,6},{8,9},{9,8},{10,11... | collective-permute-start | bytes 98312 | tf_op jit(solution)/shard_map/ppermute | solution.py:623
  20.5 1.3 %collective-permute-start.7 = (f32[1,4,2,8,128]{4,3,2,1,0:T(8,128)S(1)}, f32[1,4,2,8,128]{4,3,2,1,0:T(8,128)S(1)}, u32[]{:S(2)}, u32[]{:S(2)}) collective-permute-start(f32[1,4,2,8,128]{4,3,2,1,0:T(8,128)S(1)} %bitcast.7), channel_id=1, source_target_pairs={{0,2},{1,3},{2,0},{3,1},{4,6},{5,7},{6,4},{7,5},{8,10},{9,11},{10,... | collective-permute-start | bytes 98312 | tf_op jit(solution)/shard_map/ppermute | solution.py:623
  21.7 1.4 %collective-permute-start.6 = (f32[1,4,2,8,128]{4,3,2,1,0:T(8,128)S(1)}, f32[1,4,2,8,128]{4,3,2,1,0:T(8,128)S(1)}, u32[]{:S(2)}, u32[]{:S(2)}) collective-permute-start(f32[1,4,2,8,128]{4,3,2,1,0:T(8,128)S(1)} %bitcast.8), channel_id=1, source_target_pairs={{0,3},{1,2},{2,1},{3,0},{4,7},{5,6},{6,5},{7,4},{8,11},{9,10},{10,... | collective-permute-start | bytes 98312 | tf_op jit(solution)/shard_map/ppermute | solution.py:623
  23.1 0.0 collective-permute-done.8
  23.1 4.0 %collective-permute-start.10 = (f32[2,4,2,8,128]{4,3,2,1,0:T(8,128)S(1)}, f32[2,4,2,8,128]{4,3,2,1,0:T(8,128)S(1)}, u32[]{:S(2)}, u32[]{:S(2)}) collective-permute-start(f32[2,4,2,8,128]{4,3,2,1,0:T(8,128)S(1)} %pad_maximum_fusion.2), channel_id=1, source_target_pairs={{0,8},{4,12},{8,0},{12,4},{1,9},{5,13},{9,1},{13,5},{2,10},{6,14},... | collective-permute-start | bytes 196616 | tf_op jit(solution)/shard_map/ppermute | solution.py:623
  27.1 0.0 collective-permute-done.7
  27.1 0.4 collective-permute-done.6
  27.5 3.9 %collective-permute-start.9 = (f32[2,4,2,8,128]{4,3,2,1,0:T(8,128)S(1)}, f32[2,4,2,8,128]{4,3,2,1,0:T(8,128)S(1)}, u32[]{:S(2)}, u32[]{:S(2)}) collective-permute-start(f32[2,4,2,8,128]{4,3,2,1,0:T(8,128)S(1)} %pad_maximum_fusion.1), channel_id=1, source_target_pairs={{0,8},{4,12},{8,0},{12,4},{1,9},{5,13},{9,1},{13,5},{2,10},{6,14},... | collective-permute-start | bytes 196616 | tf_op jit(solution)/shard_map/ppermute | solution.py:623
  31.4 2.2 %collective-permute-done.9 = f32[2,4,2,8,128]{4,3,2,1,0:T(8,128)S(1)} collective-permute-done((f32[2,4,2,8,128]{4,3,2,1,0:T(8,128)S(1)}, f32[2,4,2,8,128]{4,3,2,1,0:T(8,128)S(1)}, u32[]{:S(2)}, u32[]{:S(2)}) %collective-permute-start.9) | collective-permute-done | bytes 65568 | tf_op jit(solution)/shard_map/ppermute | solution.py:623
  33.6 0.0 collective-permute-done.10
  33.6 0.1 collective-permute-start.11
  33.7 1.5 %collective-permute-done.11.refs_1_ = f32[8,4,2,8,128]{4,3,2,1,0:T(8,128)S(1)} collective-permute-done((f32[8,4,2,8,128]{4,3,2,1,0:T(8,128)S(1)}, f32[8,4,2,8,128]{4,3,2,1,0:T(8,128)S(1)}, u32[]{:S(2)}, u32[]{:S(2)}) %collective-permute-start.11) | collective-permute-done | bytes 262176 | tf_op jit(solution)/shard_map/ppermute | solution.py:623
  35.2 5.7 %shard_map.20 = (f32[24,4,4,8,128]{4,3,2,1,0:T(8,128)S(1)}, f32[4,2,8,128]{3,2,1,0:T(8,128)S(1)}) custom-call(s32[2]{0:T(128)S(1)} %pad_add_fusion.where_ref, f32[8,4,2,8,128]{4,3,2,1,0:T(8,128)S(1)} %constant_dynamic-update-slice_fusion.refs_0_, f32[8,4,2,8,128]{4,3,2,1,0:T(8,128)S(1)} %collective-permute-done.11.refs_1_, ...), custom_call_target="tpu_custom_call" | custom-call | tf_op jit(solution)/shard_map/pallas_call | solution.py:600
  40.9 0.2 collective-permute-start.14
  41.2 1.8 %collective-permute-start.13 = (f32[1,4,2,8,128]{4,3,2,1,0:T(8,128)S(1)}, f32[1,4,2,8,128]{4,3,2,1,0:T(8,128)S(1)}, u32[]{:S(2)}, u32[]{:S(2)}) collective-permute-start(f32[1,4,2,8,128]{4,3,2,1,0:T(8,128)S(1)} %bitcast.11), channel_id=1, source_target_pairs={{0,2},{1,3},{2,0},{3,1},{4,6},{5,7},{6,4},{7,5},{8,10},{9,11},{10,... | collective-permute-start | bytes 98312 | tf_op jit(solution)/shard_map/ppermute | solution.py:623
  43.0 2.4 %collective-permute-start.12 = (f32[1,4,2,8,128]{4,3,2,1,0:T(8,128)S(1)}, f32[1,4,2,8,128]{4,3,2,1,0:T(8,128)S(1)}, u32[]{:S(2)}, u32[]{:S(2)}) collective-permute-start(f32[1,4,2,8,128]{4,3,2,1,0:T(8,128)S(1)} %bitcast.12), channel_id=1, source_target_pairs={{0,3},{1,2},{2,1},{3,0},{4,7},{5,6},{6,5},{7,4},{8,11},{9,10},{10,... | collective-permute-start | bytes 98312 | tf_op jit(solution)/shard_map/ppermute | solution.py:623
  45.4 0.0 collective-permute-done.14
  45.4 2.1 %collective-permute-start.16 = (f32[2,4,2,8,128]{4,3,2,1,0:T(8,128)S(1)}, f32[2,4,2,8,128]{4,3,2,1,0:T(8,128)S(1)}, u32[]{:S(2)}, u32[]{:S(2)}) collective-permute-start(f32[2,4,2,8,128]{4,3,2,1,0:T(8,128)S(1)} %pad_maximum_fusion.4), channel_id=1, source_target_pairs={{0,8},{4,12},{8,0},{12,4},{1,9},{5,13},{9,1},{13,5},{2,10},{6,14},... | collective-permute-start | bytes 196616 | tf_op jit(solution)/shard_map/ppermute | solution.py:623
  47.5 0.0 collective-permute-done.13
  47.5 1.2 %collective-permute-done.12 = f32[1,4,2,8,128]{4,3,2,1,0:T(8,128)S(1)} collective-permute-done((f32[1,4,2,8,128]{4,3,2,1,0:T(8,128)S(1)}, f32[1,4,2,8,128]{4,3,2,1,0:T(8,128)S(1)}, u32[]{:S(2)}, u32[]{:S(2)}) %collective-permute-start.12) | collective-permute-done | bytes 32800 | tf_op jit(solution)/shard_map/ppermute | solution.py:623
  48.7 2.0 %collective-permute-start.15 = (f32[2,4,2,8,128]{4,3,2,1,0:T(8,128)S(1)}, f32[2,4,2,8,128]{4,3,2,1,0:T(8,128)S(1)}, u32[]{:S(2)}, u32[]{:S(2)}) collective-permute-start(f32[2,4,2,8,128]{4,3,2,1,0:T(8,128)S(1)} %pad_maximum_fusion.3), channel_id=1, source_target_pairs={{0,8},{4,12},{8,0},{12,4},{1,9},{5,13},{9,1},{13,5},{2,10},{6,14},... | collective-permute-start | bytes 196616 | tf_op jit(solution)/shard_map/ppermute | solution.py:623
  50.7 2.2 %collective-permute-done.15 = f32[2,4,2,8,128]{4,3,2,1,0:T(8,128)S(1)} collective-permute-done((f32[2,4,2,8,128]{4,3,2,1,0:T(8,128)S(1)}, f32[2,4,2,8,128]{4,3,2,1,0:T(8,128)S(1)}, u32[]{:S(2)}, u32[]{:S(2)}) %collective-permute-start.15) | collective-permute-done | bytes 65568 | tf_op jit(solution)/shard_map/ppermute | solution.py:623
  53.0 0.0 collective-permute-done.16
  53.0 0.1 collective-permute-start.17
  53.1 1.5 %collective-permute-done.17.refs_1_ = f32[8,4,2,8,128]{4,3,2,1,0:T(8,128)S(1)} collective-permute-done((f32[8,4,2,8,128]{4,3,2,1,0:T(8,128)S(1)}, f32[8,4,2,8,128]{4,3,2,1,0:T(8,128)S(1)}, u32[]{:S(2)}, u32[]{:S(2)}) %collective-permute-start.17) | collective-permute-done | bytes 262176 | tf_op jit(solution)/shard_map/ppermute | solution.py:623
  54.6 4.8 %shard_map.21 = f32[8,16,512]{2,1,0:T(8,128)} custom-call(s32[2]{0:T(128)S(1)} %pad_add_fusion.where_ref, f32[8,4,2,8,128]{4,3,2,1,0:T(8,128)S(1)} %constant_dynamic-update-slice_fusion.6.refs_0_, f32[8,4,2,8,128]{4,3,2,1,0:T(8,128)S(1)} %collective-permute-done.17.refs_1_, f32[24,4,4,8,128]{4,3,2,1,0:T(8,128)S(1)} %get-tuple-element.30.refs_2_, ...), custom_call_target="tpu_custom_call" | custom-call | tf_op jit(solution)/shard_map/pallas_call | solution.py:600
  (18 shorter events, 0.1 us)
Async XLA Ops:
  1.5 6.6 %collective-permute-start = (f32[8,4,8,128]{3,2,1,0:T(8,128)S(1)}, f32[8,4,8,128]{3,2,1,0:T(8,128)S(1)}, u32[]{:S(2)}, u32[]{:S(2)}) collective-permute-start(f32[8,4,8,128]{3,2,1,0:T(8,128)S(1)} %get-tuple-element.18), channel_id=1, source_target_pairs={{0,1},{1,0},{2,3},{3,2},{4,5},{5,4},{6,7},{7,6},{8,9},{9,8},{10,11... | collective-permute-start | bytes 393224 | tf_op jit(solution)/shard_map/ppermute | solution.py:623
  4.6 3.5 %collective-permute-start.1 = (f32[8,4,8,128]{3,2,1,0:T(8,128)S(1)}, f32[8,4,8,128]{3,2,1,0:T(8,128)S(1)}, u32[]{:S(2)}, u32[]{:S(2)}) collective-permute-start(f32[8,4,8,128]{3,2,1,0:T(8,128)S(1)} %get-tuple-element.19), channel_id=1, source_target_pairs={{1,2},{2,1},{5,6},{6,5},{9,10},{10,9},{13,14},{14,13},{17,18},{18,... | collective-permute-start | bytes 393224 | tf_op jit(solution)/shard_map/ppermute | solution.py:647
  5.2 6.7 %collective-permute-start.4 = (f32[8,16,512]{2,1,0:T(8,128)}, f32[8,16,512]{2,1,0:T(8,128)S(1)}, u32[]{:S(2)}, u32[]{:S(2)}) collective-permute-start(f32[8,16,512]{2,1,0:T(8,128)} %charges_ref.1), channel_id=1, source_target_pairs={{0,4},{4,0},{8,12},{12,8},{1,5},{5,1},{9,13},{13,9},{2,6},{6,2},{1... | collective-permute-start | bytes 786440 | tf_op jit(solution)/shard_map/ppermute | solution.py:623
  5.3 6.6 %collective-permute-start.5 = (f32[8,4,16,128]{3,2,1,0:T(8,128)S(1)}, f32[8,4,16,128]{3,2,1,0:T(8,128)S(1)}, u32[]{:S(2)}, u32[]{:S(2)}) collective-permute-start(f32[8,4,16,128]{3,2,1,0:T(8,128)S(1)} %get-tuple-element.20.mid_ref), channel_id=1, source_target_pairs={{4,8},{8,4},{5,9},{9,5},{6,10},{10,6},{7,11},{11,7},{20,24},{24,20... | collective-permute-start | bytes 786440 | tf_op jit(solution)/shard_map/ppermute | solution.py:645
  8.1 5.5 %collective-permute-start.3 = (f32[8,4,16,128]{3,2,1,0:T(8,128)S(1)}, f32[8,4,16,128]{3,2,1,0:T(8,128)S(1)}, u32[]{:S(2)}, u32[]{:S(2)}) collective-permute-start(f32[8,4,16,128]{3,2,1,0:T(8,128)S(1)} %pad_maximum_fusion.mid_rim_ref), channel_id=1, source_target_pairs={{4,8},{8,4},{5,9},{9,5},{6,10},{10,6},{7,11},{11,7},{20,24},{24,20... | collective-permute-start | bytes 786440 | tf_op jit(solution)/shard_map/ppermute | solution.py:650
  8.8 4.8 %collective-permute-start.2 = (f32[8,4,16,128]{3,2,1,0:T(8,128)S(1)}, f32[8,4,16,128]{3,2,1,0:T(8,128)S(1)}, u32[]{:S(2)}, u32[]{:S(2)}) collective-permute-start(f32[8,4,16,128]{3,2,1,0:T(8,128)S(1)} %pad_maximum_fusion.mid_rim_ref), channel_id=1, source_target_pairs={{0,4},{4,0},{8,12},{12,8},{1,5},{5,1},{9,13},{13,9},{2,6},{6,2},{1... | collective-permute-start | bytes 786440 | tf_op jit(solution)/shard_map/ppermute | solution.py:623
  15.8 7.3 %collective-permute-start.8 = (f32[1,4,2,8,128]{4,3,2,1,0:T(8,128)S(1)}, f32[1,4,2,8,128]{4,3,2,1,0:T(8,128)S(1)}, u32[]{:S(2)}, u32[]{:S(2)}) collective-permute-start(f32[1,4,2,8,128]{4,3,2,1,0:T(8,128)S(1)} %bitcast.6), channel_id=1, source_target_pairs={{0,1},{1,0},{2,3},{3,2},{4,5},{5,4},{6,7},{7,6},{8,9},{9,8},{10,11... | collective-permute-start | bytes 98312 | tf_op jit(solution)/shard_map/ppermute | solution.py:623
  20.5 6.6 %collective-permute-start.7 = (f32[1,4,2,8,128]{4,3,2,1,0:T(8,128)S(1)}, f32[1,4,2,8,128]{4,3,2,1,0:T(8,128)S(1)}, u32[]{:S(2)}, u32[]{:S(2)}) collective-permute-start(f32[1,4,2,8,128]{4,3,2,1,0:T(8,128)S(1)} %bitcast.7), channel_id=1, source_target_pairs={{0,2},{1,3},{2,0},{3,1},{4,6},{5,7},{6,4},{7,5},{8,10},{9,11},{10,... | collective-permute-start | bytes 98312 | tf_op jit(solution)/shard_map/ppermute | solution.py:623
  21.7 5.7 %collective-permute-start.6 = (f32[1,4,2,8,128]{4,3,2,1,0:T(8,128)S(1)}, f32[1,4,2,8,128]{4,3,2,1,0:T(8,128)S(1)}, u32[]{:S(2)}, u32[]{:S(2)}) collective-permute-start(f32[1,4,2,8,128]{4,3,2,1,0:T(8,128)S(1)} %bitcast.8), channel_id=1, source_target_pairs={{0,3},{1,2},{2,1},{3,0},{4,7},{5,6},{6,5},{7,4},{8,11},{9,10},{10,... | collective-permute-start | bytes 98312 | tf_op jit(solution)/shard_map/ppermute | solution.py:623
  23.1 10.5 %collective-permute-start.10 = (f32[2,4,2,8,128]{4,3,2,1,0:T(8,128)S(1)}, f32[2,4,2,8,128]{4,3,2,1,0:T(8,128)S(1)}, u32[]{:S(2)}, u32[]{:S(2)}) collective-permute-start(f32[2,4,2,8,128]{4,3,2,1,0:T(8,128)S(1)} %pad_maximum_fusion.2), channel_id=1, source_target_pairs={{0,8},{4,12},{8,0},{12,4},{1,9},{5,13},{9,1},{13,5},{2,10},{6,14},... | collective-permute-start | bytes 196616 | tf_op jit(solution)/shard_map/ppermute | solution.py:623
  27.5 6.1 %collective-permute-start.9 = (f32[2,4,2,8,128]{4,3,2,1,0:T(8,128)S(1)}, f32[2,4,2,8,128]{4,3,2,1,0:T(8,128)S(1)}, u32[]{:S(2)}, u32[]{:S(2)}) collective-permute-start(f32[2,4,2,8,128]{4,3,2,1,0:T(8,128)S(1)} %pad_maximum_fusion.1), channel_id=1, source_target_pairs={{0,8},{4,12},{8,0},{12,4},{1,9},{5,13},{9,1},{13,5},{2,10},{6,14},... | collective-permute-start | bytes 196616 | tf_op jit(solution)/shard_map/ppermute | solution.py:623
  33.6 1.6 %collective-permute-start.11 = (f32[8,4,2,8,128]{4,3,2,1,0:T(8,128)S(1)}, f32[8,4,2,8,128]{4,3,2,1,0:T(8,128)S(1)}, u32[]{:S(2)}, u32[]{:S(2)}) collective-permute-start(f32[8,4,2,8,128]{4,3,2,1,0:T(8,128)S(1)} %constant_dynamic-update-slice_fusion.refs_0_), channel_id=1, source_target_pairs={{0,4},{4,0},{8,12},{12,8},{1,5},{5,1},{9,13},{13,9},{2,6},{6,2},{1... | collective-permute-start | bytes 786440 | tf_op jit(solution)/shard_map/ppermute | solution.py:623
  40.9 4.5 %collective-permute-start.14 = (f32[1,4,2,8,128]{4,3,2,1,0:T(8,128)S(1)}, f32[1,4,2,8,128]{4,3,2,1,0:T(8,128)S(1)}, u32[]{:S(2)}, u32[]{:S(2)}) collective-permute-start(f32[1,4,2,8,128]{4,3,2,1,0:T(8,128)S(1)} %bitcast.10), channel_id=1, source_target_pairs={{0,1},{1,0},{2,3},{3,2},{4,5},{5,4},{6,7},{7,6},{8,9},{9,8},{10,11... | collective-permute-start | bytes 98312 | tf_op jit(solution)/shard_map/ppermute | solution.py:623
  41.2 6.3 %collective-permute-start.13 = (f32[1,4,2,8,128]{4,3,2,1,0:T(8,128)S(1)}, f32[1,4,2,8,128]{4,3,2,1,0:T(8,128)S(1)}, u32[]{:S(2)}, u32[]{:S(2)}) collective-permute-start(f32[1,4,2,8,128]{4,3,2,1,0:T(8,128)S(1)} %bitcast.11), channel_id=1, source_target_pairs={{0,2},{1,3},{2,0},{3,1},{4,6},{5,7},{6,4},{7,5},{8,10},{9,11},{10,... | collective-permute-start | bytes 98312 | tf_op jit(solution)/shard_map/ppermute | solution.py:623
  43.0 5.7 %collective-permute-start.12 = (f32[1,4,2,8,128]{4,3,2,1,0:T(8,128)S(1)}, f32[1,4,2,8,128]{4,3,2,1,0:T(8,128)S(1)}, u32[]{:S(2)}, u32[]{:S(2)}) collective-permute-start(f32[1,4,2,8,128]{4,3,2,1,0:T(8,128)S(1)} %bitcast.12), channel_id=1, source_target_pairs={{0,3},{1,2},{2,1},{3,0},{4,7},{5,6},{6,5},{7,4},{8,11},{9,10},{10,... | collective-permute-start | bytes 98312 | tf_op jit(solution)/shard_map/ppermute | solution.py:623
  45.4 7.5 %collective-permute-start.16 = (f32[2,4,2,8,128]{4,3,2,1,0:T(8,128)S(1)}, f32[2,4,2,8,128]{4,3,2,1,0:T(8,128)S(1)}, u32[]{:S(2)}, u32[]{:S(2)}) collective-permute-start(f32[2,4,2,8,128]{4,3,2,1,0:T(8,128)S(1)} %pad_maximum_fusion.4), channel_id=1, source_target_pairs={{0,8},{4,12},{8,0},{12,4},{1,9},{5,13},{9,1},{13,5},{2,10},{6,14},... | collective-permute-start | bytes 196616 | tf_op jit(solution)/shard_map/ppermute | solution.py:623
  48.7 4.3 %collective-permute-start.15 = (f32[2,4,2,8,128]{4,3,2,1,0:T(8,128)S(1)}, f32[2,4,2,8,128]{4,3,2,1,0:T(8,128)S(1)}, u32[]{:S(2)}, u32[]{:S(2)}) collective-permute-start(f32[2,4,2,8,128]{4,3,2,1,0:T(8,128)S(1)} %pad_maximum_fusion.3), channel_id=1, source_target_pairs={{0,8},{4,12},{8,0},{12,4},{1,9},{5,13},{9,1},{13,5},{2,10},{6,14},... | collective-permute-start | bytes 196616 | tf_op jit(solution)/shard_map/ppermute | solution.py:623
  53.0 1.6 %collective-permute-start.17 = (f32[8,4,2,8,128]{4,3,2,1,0:T(8,128)S(1)}, f32[8,4,2,8,128]{4,3,2,1,0:T(8,128)S(1)}, u32[]{:S(2)}, u32[]{:S(2)}) collective-permute-start(f32[8,4,2,8,128]{4,3,2,1,0:T(8,128)S(1)} %constant_dynamic-update-slice_fusion.6.refs_0_), channel_id=1, source_target_pairs={{0,4},{4,0},{8,12},{12,8},{1,5},{5,1},{9,13},{13,9},{2,6},{6,2},{1... | collective-permute-start | bytes 786440 | tf_op jit(solution)/shard_map/ppermute | solution.py:623

commit v13 on v12

--- a/solution.py
+++ b/solution.py
@@ -253,7 +253,7 @@
                 x = PAD + 4 * ((2 * n + core) ^ at_x)
                 place(x, lambda z, i, q: pieces[core][n * count_z + (z ^ at_z ^ (count_z - 1)), i, q])
 
-        each(0, count_x // 2, gather, 1)
+        each(0, count_x // 2, gather, 2)
 
     def sweep(level, u_in, g_in, u_out, g_out, b):
         return lambda x: level.put(u_out, g_out, x, level.sweep(u_in, g_in, b, x, third))
@@ -441,18 +441,25 @@
     return terms[0] + (terms[1] + terms[2])
 
 
-def split_lanes(values):
+def lane_places(size):
+    return places(size, lambda y, l: y == (l % LANES) * 4 + l // LANES)
+
+
+def split_lanes(values, matrix):
     size_x, size_z, size_y = values.shape
-    matrix = places(size_y, lambda y, l: y == (l % LANES) * 4 + l // LANES)
     split = permuted(values.reshape(size_x * size_z, size_y), matrix)
     return [
         split[:, p * LANES : (p + 1) * LANES].reshape(size_x, size_z, LANES) for p in range(4)
     ]
 
 
-def lanes_kernel(where_ref, charges_ref, rows_ref, one_ref, two_ref):
+def lanes_kernel(where_ref, charges_ref, rows_ref, one_ref, two_ref, held_ref, semaphore):
+    copy = pltpu.make_async_copy(charges_ref, held_ref, semaphore)
+    copy.start()
     odd = where_ref[1] % 2
-    for p, tile in enumerate(split_lanes(charges_ref[...])):
+    matrix = lane_places(charges_ref.shape[2])
+    copy.wait()
+    for p, tile in enumerate(split_lanes(held_ref[...], matrix)):
         rows_ref[:, p] = tile
         first, last = tile[:, 0:8], tile[:, 8:16]
         one_ref[:, p] = jnp.where(odd == 0, last, first)
@@ -504,11 +511,13 @@
 
 
 def early_kernel(count_x, count_z, where_ref, mid_ref, mid_rim_ref, near_ref, far_ref, c_ref,
-                 b_ref, g_ref, u_ref, h_ref, lanes_ref, rows_ref):
+                 b_ref, g_ref, u_ref, h_ref, matrix_ref, lanes_ref, rows_ref):
     inner = rim_masks(count_x, count_z, where_ref)[0]
     odd = where_ref[0] % 2
-    for p, tile in enumerate(split_lanes(near_ref[...])):
+    size = near_ref.shape[2]
+    for p, tile in enumerate(split_lanes(near_ref[...], lane_places(size))):
         lanes_ref[:, p] = tile
+    matrix_ref[...] = places(size, lambda l, y: y == (l % LANES) * 4 + l // LANES)
     split_rows = row_splitter(rows_ref, c_ref)
     split_rows(mid_ref, mid_rim_ref, 1)
     split_rows(lanes_ref, mid_rim_ref, 2 - 2 * odd)
@@ -570,7 +579,7 @@
 
 def up_kernel(count_x, count_z, count_pieces, where_ref, *refs):
     pieces, refs = refs[:count_pieces], refs[count_pieces:]
-    u_ref, b_ref, out_ref, ga_ref, gb_ref, ua_ref, ub_ref, rows_ref, *refs = refs
+    u_ref, b_ref, matrix_ref, out_ref, ga_ref, gb_ref, ua_ref, ub_ref, rows_ref, *refs = refs
     near, grids = refs[:5], refs[5:]
     masks = rim_masks(count_x, count_z, where_ref)
     coarse = coarse_solve(count_x, count_z, where_ref, pieces, grids)
@@ -586,13 +595,16 @@
 
     each(RIM, RIM + BRICK_X, body, 2)
     tiles = [rows_ref[:, p].reshape(BRICK_X * BRICK_Z, LANES) for p in range(4)]
-    matrix = places(out_ref.shape[2], lambda l, y: y == (l % LANES) * 4 + l // LANES)
-    out_ref[...] = permuted(jnp.concatenate(tiles, axis=1), matrix).reshape(out_ref.shape)
-
-
-def call(kernel, outputs, scratch, in_place=None):
-    shapes = [jax.ShapeDtypeStruct(shape, jnp.float32) for shape in outputs]
-    held = sum(4 * math.prod(shape.shape) for shape in scratch)
+    whole = permuted(jnp.concatenate(tiles, axis=1), matrix_ref[...])
+    out_ref[...] = whole.reshape(out_ref.shape)
+
+
+def call(kernel, outputs, scratch, in_place=None, far_in=False):
+    shapes = [
+        shape if hasattr(shape, "dtype") else jax.ShapeDtypeStruct(shape, jnp.float32)
+        for shape in outputs
+    ]
+    held = sum(4 * math.prod(shape.shape) for shape in scratch if hasattr(shape, "shape"))
 
     def run(where, *arrays):
         moved = sum(4 * math.prod(array.shape) for array in arrays + tuple(shapes))
@@ -600,7 +612,8 @@
         return pl.pallas_call(
             kernel,
             out_shape=shapes,
-            in_specs=[pl.BlockSpec(memory_space=pltpu.SMEM)] + [whole] * len(arrays),
+            in_specs=[pl.BlockSpec(memory_space=pltpu.SMEM)]
+            + [pl.BlockSpec(memory_space=pltpu.HBM) if far_in else whole] * len(arrays),
             out_specs=[whole] * len(shapes),
             scratch_shapes=scratch,
             input_output_aliases=in_place or {},
@@ -640,7 +653,12 @@
     at_x, at_z = lax.axis_index("gx"), lax.axis_index("gz")
     where = jnp.stack([at_x, at_z]).astype(jnp.int32)
     brick, rim = (BRICK_X, 4, BRICK_Z, LANES), (BRICK_X, 4, RIM, LANES)
-    middle, one, two = call(lanes_kernel, [brick, rim, rim], [])(where, charges)
+    middle, one, two = call(
+        lanes_kernel,
+        [brick, rim, rim],
+        [pltpu.VMEM(charges.shape, jnp.float32), pltpu.SemaphoreType.DMA],
+        far_in=True,
+    )(where, charges)
     x_far, z_two = pairs_shifted(count_x), pairs_shifted(count_z)
     far = lax.ppermute(middle, "gx", x_far)
     near = swap("gx", charges, 1)
@@ -658,9 +676,10 @@
     close = pltpu.VMEM((WIDE_X // 2, 2, 2, 8, LANES), jnp.float32)
     rows_out = pltpu.VMEM((BRICK_X, 4, BRICK_Z, LANES), jnp.float32)
 
-    early = call(
+    size = charges.shape[2]
+    *early, matrix = call(
         functools.partial(early_kernel, count_x, count_z),
-        [wide] * 5,
+        [wide] * 5 + [jax.ShapeDtypeStruct((size, size), jnp.bfloat16)],
         [pltpu.VMEM(brick, jnp.float32), rows_in],
     )(where, middle, middle_rim, near, far)
     _, b, _, u, _, piece = call(
@@ -680,7 +699,7 @@
         functools.partial(up_kernel, count_x, count_z, len(pieces)),
         [charges.shape],
         [fine] * 4 + [rows_out] + [close] * 5 + grids,
-    )(where, *pieces, u, b)
+    )(where, *pieces, u, b, matrix)
     return potential
 
 

time: 59.6 us -> 60 us (level)
  no operation moved by 1% of the time
where the time goes in v13:
time: 60 us; the launch traced here: 59.8 us
  starting transfers between devices  31.8 us (53%)
  Pallas kernels  16.3 us (27%)
  waiting for transfers between devices  11.3 us (19%)
    ppermute x15, starting transfers between devices, swap(): lax.ppermute(values, axis, pairs_apart(lax.axis_size(axis), distance))  29.7 us
    pallas_call x5, Pallas kernels, run(): pl.pallas_call(kernel, out_shape=shapes, in_specs=[pl.BlockSpec(memory_sp...  16.3 us
    ppermute x15, waiting for transfers between devices, swap(): lax.ppermute(values, axis, pairs_apart(lax.axis_size(axis), distance))  11.3 us
  transfers between devices with their start and end apart: 18, of which 7 were waited for; matrix products, arithmetic and copies ran while one was open for 0% of the time, Pallas kernels for 3%

profile of v13, /device:TPU:0, one launch (start us, length us, event | category | flops | bytes accessed | tf_op | source)
XLA Modules:
  0.0 59.8 jit_solution(8294531090061194852)
XLA Ops:
  0.0 0.1 pad_add_fusion.where_ref
  0.1 1.9 %shard_map.17 = (f32[8,4,16,128]{3,2,1,0:T(8,128)S(1)}, f32[8,4,8,128]{3,2,1,0:T(8,128)S(1)}, f32[8,4,8,128]{3,2,1,0:T(8,128)S(1)}) custom-call(s32[2]{0:T(128)S(1)} %pad_add_fusion.where_ref, f32[8,16,512]{2,1,0:T(8,128)} %charges_ref.1), custom_call_target="tpu_custom_call" | custom-call | tf_op jit(solution)/shard_map/pallas_call | solution.py:612
  2.0 3.1 %collective-permute-start = (f32[8,4,8,128]{3,2,1,0:T(8,128)S(1)}, f32[8,4,8,128]{3,2,1,0:T(8,128)S(1)}, u32[]{:S(2)}, u32[]{:S(2)}) collective-permute-start(f32[8,4,8,128]{3,2,1,0:T(8,128)S(1)} %get-tuple-element.19), channel_id=1, source_target_pairs={{0,1},{1,0},{2,3},{3,2},{4,5},{5,4},{6,7},{7,6},{8,9},{9,8},{10,11... | collective-permute-start | bytes 393224 | tf_op jit(solution)/shard_map/ppermute | solution.py:636
  5.1 0.7 %collective-permute-start.1 = (f32[8,4,8,128]{3,2,1,0:T(8,128)S(1)}, f32[8,4,8,128]{3,2,1,0:T(8,128)S(1)}, u32[]{:S(2)}, u32[]{:S(2)}) collective-permute-start(f32[8,4,8,128]{3,2,1,0:T(8,128)S(1)} %get-tuple-element.20), channel_id=1, source_target_pairs={{1,2},{2,1},{5,6},{6,5},{9,10},{10,9},{13,14},{14,13},{17,18},{18,... | collective-permute-start | bytes 393224 | tf_op jit(solution)/shard_map/ppermute | solution.py:665
  5.7 0.1 collective-permute-start.4
  5.8 0.7 %collective-permute-start.5 = (f32[8,4,16,128]{3,2,1,0:T(8,128)S(1)}, f32[8,4,16,128]{3,2,1,0:T(8,128)S(1)}, u32[]{:S(2)}, u32[]{:S(2)}) collective-permute-start(f32[8,4,16,128]{3,2,1,0:T(8,128)S(1)} %get-tuple-element.21.mid_ref), channel_id=1, source_target_pairs={{4,8},{8,4},{5,9},{9,5},{6,10},{10,6},{7,11},{11,7},{20,24},{24,20... | collective-permute-start | bytes 786440 | tf_op jit(solution)/shard_map/ppermute | solution.py:663
  6.5 2.1 %collective-permute-done = f32[8,4,8,128]{3,2,1,0:T(8,128)S(1)} collective-permute-done((f32[8,4,8,128]{3,2,1,0:T(8,128)S(1)}, f32[8,4,8,128]{3,2,1,0:T(8,128)S(1)}, u32[]{:S(2)}, u32[]{:S(2)}) %collective-permute-start) | collective-permute-done | bytes 131104 | tf_op jit(solution)/shard_map/ppermute | solution.py:636
  8.6 0.0 collective-permute-done.1
  8.6 0.7 %collective-permute-start.3 = (f32[8,4,16,128]{3,2,1,0:T(8,128)S(1)}, f32[8,4,16,128]{3,2,1,0:T(8,128)S(1)}, u32[]{:S(2)}, u32[]{:S(2)}) collective-permute-start(f32[8,4,16,128]{3,2,1,0:T(8,128)S(1)} %pad_maximum_fusion.mid_rim_ref), channel_id=1, source_target_pairs={{4,8},{8,4},{5,9},{9,5},{6,10},{10,6},{7,11},{11,7},{20,24},{24,20... | collective-permute-start | bytes 786440 | tf_op jit(solution)/shard_map/ppermute | solution.py:668
  9.3 3.1 %collective-permute-start.2 = (f32[8,4,16,128]{3,2,1,0:T(8,128)S(1)}, f32[8,4,16,128]{3,2,1,0:T(8,128)S(1)}, u32[]{:S(2)}, u32[]{:S(2)}) collective-permute-start(f32[8,4,16,128]{3,2,1,0:T(8,128)S(1)} %pad_maximum_fusion.mid_rim_ref), channel_id=1, source_target_pairs={{0,4},{4,0},{8,12},{12,8},{1,5},{5,1},{9,13},{13,9},{2,6},{6,2},{1... | collective-permute-start | bytes 786440 | tf_op jit(solution)/shard_map/ppermute | solution.py:636
  12.4 0.0 collective-permute-done.4.near_ref
  12.4 0.0 collective-permute-done.5.far_ref
  12.4 1.8 %shard_map.18 = (f32[24,4,4,8,128]{4,3,2,1,0:T(8,128)S(1)}, f32[24,4,4,8,128]{4,3,2,1,0:T(8,128)S(1)}, f32[24,4,4,8,128]{4,3,2,1,0:T(8,128)S(1)}, f32[24,4,4,8,1...) custom-call(s32[2]{0:T(128)S(1)} %pad_add_fusion.where_ref, ...), custom_call_target="tpu_custom_call" | custom-call | tf_op jit(solution)/shard_map/pallas_call | solution.py:612
  14.2 0.0 collective-permute-done.3.far_rim_ref
  14.2 0.0 collective-permute-done.2.near_rim_ref
  14.2 2.2 %shard_map.19 = (f32[24,4,4,8,128]{4,3,2,1,0:T(8,128)S(1)}, f32[24,4,4,8,128]{4,3,2,1,0:T(8,128)S(1)}, f32[24,4,4,8,128]{4,3,2,1,0:T(8,128)S(1)}, f32[24,4,4,8,1...) custom-call(s32[2]{0:T(128)S(1)} %pad_add_fusion.where_ref, ...), custom_call_target="tpu_custom_call", output_to_operand_aliasing={{0}: (3, {}), {1}: (4, {}), {2}: (5, {}), {3}: (6, {}), {4}... | custom-call | tf_op jit(solution)/shard_map/pallas_call | solution.py:612
  16.4 4.7 %collective-permute-start.8 = (f32[1,4,2,8,128]{4,3,2,1,0:T(8,128)S(1)}, f32[1,4,2,8,128]{4,3,2,1,0:T(8,128)S(1)}, u32[]{:S(2)}, u32[]{:S(2)}) collective-permute-start(f32[1,4,2,8,128]{4,3,2,1,0:T(8,128)S(1)} %bitcast.6), channel_id=1, source_target_pairs={{0,1},{1,0},{2,3},{3,2},{4,5},{5,4},{6,7},{7,6},{8,9},{9,8},{10,11... | collective-permute-start | bytes 98312 | tf_op jit(solution)/shard_map/ppermute | solution.py:636
  21.1 1.3 %collective-permute-start.7 = (f32[1,4,2,8,128]{4,3,2,1,0:T(8,128)S(1)}, f32[1,4,2,8,128]{4,3,2,1,0:T(8,128)S(1)}, u32[]{:S(2)}, u32[]{:S(2)}) collective-permute-start(f32[1,4,2,8,128]{4,3,2,1,0:T(8,128)S(1)} %bitcast.7), channel_id=1, source_target_pairs={{0,2},{1,3},{2,0},{3,1},{4,6},{5,7},{6,4},{7,5},{8,10},{9,11},{10,... | collective-permute-start | bytes 98312 | tf_op jit(solution)/shard_map/ppermute | solution.py:636
  22.3 1.4 %collective-permute-start.6 = (f32[1,4,2,8,128]{4,3,2,1,0:T(8,128)S(1)}, f32[1,4,2,8,128]{4,3,2,1,0:T(8,128)S(1)}, u32[]{:S(2)}, u32[]{:S(2)}) collective-permute-start(f32[1,4,2,8,128]{4,3,2,1,0:T(8,128)S(1)} %bitcast.8), channel_id=1, source_target_pairs={{0,3},{1,2},{2,1},{3,0},{4,7},{5,6},{6,5},{7,4},{8,11},{9,10},{10,... | collective-permute-start | bytes 98312 | tf_op jit(solution)/shard_map/ppermute | solution.py:636
  23.7 0.0 collective-permute-done.8
  23.7 3.8 %collective-permute-start.10 = (f32[2,4,2,8,128]{4,3,2,1,0:T(8,128)S(1)}, f32[2,4,2,8,128]{4,3,2,1,0:T(8,128)S(1)}, u32[]{:S(2)}, u32[]{:S(2)}) collective-permute-start(f32[2,4,2,8,128]{4,3,2,1,0:T(8,128)S(1)} %pad_maximum_fusion.2), channel_id=1, source_target_pairs={{0,8},{4,12},{8,0},{12,4},{1,9},{5,13},{9,1},{13,5},{2,10},{6,14},... | collective-permute-start | bytes 196616 | tf_op jit(solution)/shard_map/ppermute | solution.py:636
  27.6 0.0 collective-permute-done.7
  27.6 0.6 collective-permute-done.6
  28.2 3.6 %collective-permute-start.9 = (f32[2,4,2,8,128]{4,3,2,1,0:T(8,128)S(1)}, f32[2,4,2,8,128]{4,3,2,1,0:T(8,128)S(1)}, u32[]{:S(2)}, u32[]{:S(2)}) collective-permute-start(f32[2,4,2,8,128]{4,3,2,1,0:T(8,128)S(1)} %pad_maximum_fusion.1), channel_id=1, source_target_pairs={{0,8},{4,12},{8,0},{12,4},{1,9},{5,13},{9,1},{13,5},{2,10},{6,14},... | collective-permute-start | bytes 196616 | tf_op jit(solution)/shard_map/ppermute | solution.py:636
  31.9 2.2 %collective-permute-done.9 = f32[2,4,2,8,128]{4,3,2,1,0:T(8,128)S(1)} collective-permute-done((f32[2,4,2,8,128]{4,3,2,1,0:T(8,128)S(1)}, f32[2,4,2,8,128]{4,3,2,1,0:T(8,128)S(1)}, u32[]{:S(2)}, u32[]{:S(2)}) %collective-permute-start.9) | collective-permute-done | bytes 65568 | tf_op jit(solution)/shard_map/ppermute | solution.py:636
  34.1 0.0 collective-permute-done.10
  34.1 0.1 collective-permute-start.11
  34.2 1.5 %collective-permute-done.11.refs_1_ = f32[8,4,2,8,128]{4,3,2,1,0:T(8,128)S(1)} collective-permute-done((f32[8,4,2,8,128]{4,3,2,1,0:T(8,128)S(1)}, f32[8,4,2,8,128]{4,3,2,1,0:T(8,128)S(1)}, u32[]{:S(2)}, u32[]{:S(2)}) %collective-permute-start.11) | collective-permute-done | bytes 262176 | tf_op jit(solution)/shard_map/ppermute | solution.py:636
  35.7 5.7 %shard_map.20 = (f32[24,4,4,8,128]{4,3,2,1,0:T(8,128)S(1)}, f32[4,2,8,128]{3,2,1,0:T(8,128)S(1)}) custom-call(s32[2]{0:T(128)S(1)} %pad_add_fusion.where_ref, f32[8,4,2,8,128]{4,3,2,1,0:T(8,128)S(1)} %constant_dynamic-update-slice_fusion.refs_0_, f32[8,4,2,8,128]{4,3,2,1,0:T(8,128)S(1)} %collective-permute-done.11.refs_1_, ...), custom_call_target="tpu_custom_call" | custom-call | tf_op jit(solution)/shard_map/pallas_call | solution.py:612
  41.4 0.2 collective-permute-start.14
  41.6 1.8 %collective-permute-start.13 = (f32[1,4,2,8,128]{4,3,2,1,0:T(8,128)S(1)}, f32[1,4,2,8,128]{4,3,2,1,0:T(8,128)S(1)}, u32[]{:S(2)}, u32[]{:S(2)}) collective-permute-start(f32[1,4,2,8,128]{4,3,2,1,0:T(8,128)S(1)} %bitcast.11), channel_id=1, source_target_pairs={{0,2},{1,3},{2,0},{3,1},{4,6},{5,7},{6,4},{7,5},{8,10},{9,11},{10,... | collective-permute-start | bytes 98312 | tf_op jit(solution)/shard_map/ppermute | solution.py:636
  43.4 2.4 %collective-permute-start.12 = (f32[1,4,2,8,128]{4,3,2,1,0:T(8,128)S(1)}, f32[1,4,2,8,128]{4,3,2,1,0:T(8,128)S(1)}, u32[]{:S(2)}, u32[]{:S(2)}) collective-permute-start(f32[1,4,2,8,128]{4,3,2,1,0:T(8,128)S(1)} %bitcast.12), channel_id=1, source_target_pairs={{0,3},{1,2},{2,1},{3,0},{4,7},{5,6},{6,5},{7,4},{8,11},{9,10},{10,... | collective-permute-start | bytes 98312 | tf_op jit(solution)/shard_map/ppermute | solution.py:636
  45.9 0.0 collective-permute-done.14
  45.9 2.1 %collective-permute-start.16 = (f32[2,4,2,8,128]{4,3,2,1,0:T(8,128)S(1)}, f32[2,4,2,8,128]{4,3,2,1,0:T(8,128)S(1)}, u32[]{:S(2)}, u32[]{:S(2)}) collective-permute-start(f32[2,4,2,8,128]{4,3,2,1,0:T(8,128)S(1)} %pad_maximum_fusion.4), channel_id=1, source_target_pairs={{0,8},{4,12},{8,0},{12,4},{1,9},{5,13},{9,1},{13,5},{2,10},{6,14},... | collective-permute-start | bytes 196616 | tf_op jit(solution)/shard_map/ppermute | solution.py:636
  48.0 0.0 collective-permute-done.13
  48.0 1.2 %collective-permute-done.12 = f32[1,4,2,8,128]{4,3,2,1,0:T(8,128)S(1)} collective-permute-done((f32[1,4,2,8,128]{4,3,2,1,0:T(8,128)S(1)}, f32[1,4,2,8,128]{4,3,2,1,0:T(8,128)S(1)}, u32[]{:S(2)}, u32[]{:S(2)}) %collective-permute-start.12) | collective-permute-done | bytes 32800 | tf_op jit(solution)/shard_map/ppermute | solution.py:636
  49.2 2.0 %collective-permute-start.15 = (f32[2,4,2,8,128]{4,3,2,1,0:T(8,128)S(1)}, f32[2,4,2,8,128]{4,3,2,1,0:T(8,128)S(1)}, u32[]{:S(2)}, u32[]{:S(2)}) collective-permute-start(f32[2,4,2,8,128]{4,3,2,1,0:T(8,128)S(1)} %pad_maximum_fusion.3), channel_id=1, source_target_pairs={{0,8},{4,12},{8,0},{12,4},{1,9},{5,13},{9,1},{13,5},{2,10},{6,14},... | collective-permute-start | bytes 196616 | tf_op jit(solution)/shard_map/ppermute | solution.py:636
  51.2 2.2 %collective-permute-done.15 = f32[2,4,2,8,128]{4,3,2,1,0:T(8,128)S(1)} collective-permute-done((f32[2,4,2,8,128]{4,3,2,1,0:T(8,128)S(1)}, f32[2,4,2,8,128]{4,3,2,1,0:T(8,128)S(1)}, u32[]{:S(2)}, u32[]{:S(2)}) %collective-permute-start.15) | collective-permute-done | bytes 65568 | tf_op jit(solution)/shard_map/ppermute | solution.py:636
  53.4 0.0 collective-permute-done.16
  53.5 0.1 collective-permute-start.17
  53.5 1.5 %collective-permute-done.17.refs_1_ = f32[8,4,2,8,128]{4,3,2,1,0:T(8,128)S(1)} collective-permute-done((f32[8,4,2,8,128]{4,3,2,1,0:T(8,128)S(1)}, f32[8,4,2,8,128]{4,3,2,1,0:T(8,128)S(1)}, u32[]{:S(2)}, u32[]{:S(2)}) %collective-permute-start.17) | collective-permute-done | bytes 262176 | tf_op jit(solution)/shard_map/ppermute | solution.py:636
  55.1 4.7 %shard_map.21 = f32[8,16,512]{2,1,0:T(8,128)} custom-call(s32[2]{0:T(128)S(1)} %pad_add_fusion.where_ref, f32[8,4,2,8,128]{4,3,2,1,0:T(8,128)S(1)} %constant_dynamic-update-slice_fusion.6.refs_0_, f32[8,4,2,8,128]{4,3,2,1,0:T(8,128)S(1)} %collective-permute-done.17.refs_1_, f32[24,4,4,8,128]{4,3,2,1,0:T(8,128)S(1)} %get-tuple-element.31.refs_2_, ...), custom_call_target="tpu_custom_call" | custom-call | tf_op jit(solution)/shard_map/pallas_call | solution.py:612
  (18 shorter events, 0.1 us)
Async XLA Ops:
  2.0 6.6 %collective-permute-start = (f32[8,4,8,128]{3,2,1,0:T(8,128)S(1)}, f32[8,4,8,128]{3,2,1,0:T(8,128)S(1)}, u32[]{:S(2)}, u32[]{:S(2)}) collective-permute-start(f32[8,4,8,128]{3,2,1,0:T(8,128)S(1)} %get-tuple-element.19), channel_id=1, source_target_pairs={{0,1},{1,0},{2,3},{3,2},{4,5},{5,4},{6,7},{7,6},{8,9},{9,8},{10,11... | collective-permute-start | bytes 393224 | tf_op jit(solution)/shard_map/ppermute | solution.py:636
  5.1 3.5 %collective-permute-start.1 = (f32[8,4,8,128]{3,2,1,0:T(8,128)S(1)}, f32[8,4,8,128]{3,2,1,0:T(8,128)S(1)}, u32[]{:S(2)}, u32[]{:S(2)}) collective-permute-start(f32[8,4,8,128]{3,2,1,0:T(8,128)S(1)} %get-tuple-element.20), channel_id=1, source_target_pairs={{1,2},{2,1},{5,6},{6,5},{9,10},{10,9},{13,14},{14,13},{17,18},{18,... | collective-permute-start | bytes 393224 | tf_op jit(solution)/shard_map/ppermute | solution.py:665
  5.7 6.7 %collective-permute-start.4 = (f32[8,16,512]{2,1,0:T(8,128)}, f32[8,16,512]{2,1,0:T(8,128)S(1)}, u32[]{:S(2)}, u32[]{:S(2)}) collective-permute-start(f32[8,16,512]{2,1,0:T(8,128)} %charges_ref.1), channel_id=1, source_target_pairs={{0,4},{4,0},{8,12},{12,8},{1,5},{5,1},{9,13},{13,9},{2,6},{6,2},{1... | collective-permute-start | bytes 786440 | tf_op jit(solution)/shard_map/ppermute | solution.py:636
  5.8 6.6 %collective-permute-start.5 = (f32[8,4,16,128]{3,2,1,0:T(8,128)S(1)}, f32[8,4,16,128]{3,2,1,0:T(8,128)S(1)}, u32[]{:S(2)}, u32[]{:S(2)}) collective-permute-start(f32[8,4,16,128]{3,2,1,0:T(8,128)S(1)} %get-tuple-element.21.mid_ref), channel_id=1, source_target_pairs={{4,8},{8,4},{5,9},{9,5},{6,10},{10,6},{7,11},{11,7},{20,24},{24,20... | collective-permute-start | bytes 786440 | tf_op jit(solution)/shard_map/ppermute | solution.py:663
  8.6 5.6 %collective-permute-start.3 = (f32[8,4,16,128]{3,2,1,0:T(8,128)S(1)}, f32[8,4,16,128]{3,2,1,0:T(8,128)S(1)}, u32[]{:S(2)}, u32[]{:S(2)}) collective-permute-start(f32[8,4,16,128]{3,2,1,0:T(8,128)S(1)} %pad_maximum_fusion.mid_rim_ref), channel_id=1, source_target_pairs={{4,8},{8,4},{5,9},{9,5},{6,10},{10,6},{7,11},{11,7},{20,24},{24,20... | collective-permute-start | bytes 786440 | tf_op jit(solution)/shard_map/ppermute | solution.py:668
  9.3 4.9 %collective-permute-start.2 = (f32[8,4,16,128]{3,2,1,0:T(8,128)S(1)}, f32[8,4,16,128]{3,2,1,0:T(8,128)S(1)}, u32[]{:S(2)}, u32[]{:S(2)}) collective-permute-start(f32[8,4,16,128]{3,2,1,0:T(8,128)S(1)} %pad_maximum_fusion.mid_rim_ref), channel_id=1, source_target_pairs={{0,4},{4,0},{8,12},{12,8},{1,5},{5,1},{9,13},{13,9},{2,6},{6,2},{1... | collective-permute-start | bytes 786440 | tf_op jit(solution)/shard_map/ppermute | solution.py:636
  16.4 7.3 %collective-permute-start.8 = (f32[1,4,2,8,128]{4,3,2,1,0:T(8,128)S(1)}, f32[1,4,2,8,128]{4,3,2,1,0:T(8,128)S(1)}, u32[]{:S(2)}, u32[]{:S(2)}) collective-permute-start(f32[1,4,2,8,128]{4,3,2,1,0:T(8,128)S(1)} %bitcast.6), channel_id=1, source_target_pairs={{0,1},{1,0},{2,3},{3,2},{4,5},{5,4},{6,7},{7,6},{8,9},{9,8},{10,11... | collective-permute-start | bytes 98312 | tf_op jit(solution)/shard_map/ppermute | solution.py:636
  21.1 6.5 %collective-permute-start.7 = (f32[1,4,2,8,128]{4,3,2,1,0:T(8,128)S(1)}, f32[1,4,2,8,128]{4,3,2,1,0:T(8,128)S(1)}, u32[]{:S(2)}, u32[]{:S(2)}) collective-permute-start(f32[1,4,2,8,128]{4,3,2,1,0:T(8,128)S(1)} %bitcast.7), channel_id=1, source_target_pairs={{0,2},{1,3},{2,0},{3,1},{4,6},{5,7},{6,4},{7,5},{8,10},{9,11},{10,... | collective-permute-start | bytes 98312 | tf_op jit(solution)/shard_map/ppermute | solution.py:636
  22.3 5.8 %collective-permute-start.6 = (f32[1,4,2,8,128]{4,3,2,1,0:T(8,128)S(1)}, f32[1,4,2,8,128]{4,3,2,1,0:T(8,128)S(1)}, u32[]{:S(2)}, u32[]{:S(2)}) collective-permute-start(f32[1,4,2,8,128]{4,3,2,1,0:T(8,128)S(1)} %bitcast.8), channel_id=1, source_target_pairs={{0,3},{1,2},{2,1},{3,0},{4,7},{5,6},{6,5},{7,4},{8,11},{9,10},{10,... | collective-permute-start | bytes 98312 | tf_op jit(solution)/shard_map/ppermute | solution.py:636
  23.7 10.3 %collective-permute-start.10 = (f32[2,4,2,8,128]{4,3,2,1,0:T(8,128)S(1)}, f32[2,4,2,8,128]{4,3,2,1,0:T(8,128)S(1)}, u32[]{:S(2)}, u32[]{:S(2)}) collective-permute-start(f32[2,4,2,8,128]{4,3,2,1,0:T(8,128)S(1)} %pad_maximum_fusion.2), channel_id=1, source_target_pairs={{0,8},{4,12},{8,0},{12,4},{1,9},{5,13},{9,1},{13,5},{2,10},{6,14},... | collective-permute-start | bytes 196616 | tf_op jit(solution)/shard_map/ppermute | solution.py:636
  28.2 5.9 %collective-permute-start.9 = (f32[2,4,2,8,128]{4,3,2,1,0:T(8,128)S(1)}, f32[2,4,2,8,128]{4,3,2,1,0:T(8,128)S(1)}, u32[]{:S(2)}, u32[]{:S(2)}) collective-permute-start(f32[2,4,2,8,128]{4,3,2,1,0:T(8,128)S(1)} %pad_maximum_fusion.1), channel_id=1, source_target_pairs={{0,8},{4,12},{8,0},{12,4},{1,9},{5,13},{9,1},{13,5},{2,10},{6,14},... | collective-permute-start | bytes 196616 | tf_op jit(solution)/shard_map/ppermute | solution.py:636
  34.1 1.6 %collective-permute-start.11 = (f32[8,4,2,8,128]{4,3,2,1,0:T(8,128)S(1)}, f32[8,4,2,8,128]{4,3,2,1,0:T(8,128)S(1)}, u32[]{:S(2)}, u32[]{:S(2)}) collective-permute-start(f32[8,4,2,8,128]{4,3,2,1,0:T(8,128)S(1)} %constant_dynamic-update-slice_fusion.refs_0_), channel_id=1, source_target_pairs={{0,4},{4,0},{8,12},{12,8},{1,5},{5,1},{9,13},{13,9},{2,6},{6,2},{1... | collective-permute-start | bytes 786440 | tf_op jit(solution)/shard_map/ppermute | solution.py:636
  41.4 4.5 %collective-permute-start.14 = (f32[1,4,2,8,128]{4,3,2,1,0:T(8,128)S(1)}, f32[1,4,2,8,128]{4,3,2,1,0:T(8,128)S(1)}, u32[]{:S(2)}, u32[]{:S(2)}) collective-permute-start(f32[1,4,2,8,128]{4,3,2,1,0:T(8,128)S(1)} %bitcast.10), channel_id=1, source_target_pairs={{0,1},{1,0},{2,3},{3,2},{4,5},{5,4},{6,7},{7,6},{8,9},{9,8},{10,11... | collective-permute-start | bytes 98312 | tf_op jit(solution)/shard_map/ppermute | solution.py:636
  41.6 6.3 %collective-permute-start.13 = (f32[1,4,2,8,128]{4,3,2,1,0:T(8,128)S(1)}, f32[1,4,2,8,128]{4,3,2,1,0:T(8,128)S(1)}, u32[]{:S(2)}, u32[]{:S(2)}) collective-permute-start(f32[1,4,2,8,128]{4,3,2,1,0:T(8,128)S(1)} %bitcast.11), channel_id=1, source_target_pairs={{0,2},{1,3},{2,0},{3,1},{4,6},{5,7},{6,4},{7,5},{8,10},{9,11},{10,... | collective-permute-start | bytes 98312 | tf_op jit(solution)/shard_map/ppermute | solution.py:636
  43.4 5.7 %collective-permute-start.12 = (f32[1,4,2,8,128]{4,3,2,1,0:T(8,128)S(1)}, f32[1,4,2,8,128]{4,3,2,1,0:T(8,128)S(1)}, u32[]{:S(2)}, u32[]{:S(2)}) collective-permute-start(f32[1,4,2,8,128]{4,3,2,1,0:T(8,128)S(1)} %bitcast.12), channel_id=1, source_target_pairs={{0,3},{1,2},{2,1},{3,0},{4,7},{5,6},{6,5},{7,4},{8,11},{9,10},{10,... | collective-permute-start | bytes 98312 | tf_op jit(solution)/shard_map/ppermute | solution.py:636
  45.9 7.5 %collective-permute-start.16 = (f32[2,4,2,8,128]{4,3,2,1,0:T(8,128)S(1)}, f32[2,4,2,8,128]{4,3,2,1,0:T(8,128)S(1)}, u32[]{:S(2)}, u32[]{:S(2)}) collective-permute-start(f32[2,4,2,8,128]{4,3,2,1,0:T(8,128)S(1)} %pad_maximum_fusion.4), channel_id=1, source_target_pairs={{0,8},{4,12},{8,0},{12,4},{1,9},{5,13},{9,1},{13,5},{2,10},{6,14},... | collective-permute-start | bytes 196616 | tf_op jit(solution)/shard_map/ppermute | solution.py:636
  49.2 4.3 %collective-permute-start.15 = (f32[2,4,2,8,128]{4,3,2,1,0:T(8,128)S(1)}, f32[2,4,2,8,128]{4,3,2,1,0:T(8,128)S(1)}, u32[]{:S(2)}, u32[]{:S(2)}) collective-permute-start(f32[2,4,2,8,128]{4,3,2,1,0:T(8,128)S(1)} %pad_maximum_fusion.3), channel_id=1, source_target_pairs={{0,8},{4,12},{8,0},{12,4},{1,9},{5,13},{9,1},{13,5},{2,10},{6,14},... | collective-permute-start | bytes 196616 | tf_op jit(solution)/shard_map/ppermute | solution.py:636
  53.5 1.6 %collective-permute-start.17 = (f32[8,4,2,8,128]{4,3,2,1,0:T(8,128)S(1)}, f32[8,4,2,8,128]{4,3,2,1,0:T(8,128)S(1)}, u32[]{:S(2)}, u32[]{:S(2)}) collective-permute-start(f32[8,4,2,8,128]{4,3,2,1,0:T(8,128)S(1)} %constant_dynamic-update-slice_fusion.6.refs_0_), channel_id=1, source_target_pairs={{0,4},{4,0},{8,12},{12,8},{1,5},{5,1},{9,13},{13,9},{2,6},{6,2},{1... | collective-permute-start | bytes 786440 | tf_op jit(solution)/shard_map/ppermute | solution.py:636

commit v14 on v12

--- a/solution.py
+++ b/solution.py
@@ -399,7 +399,7 @@
     def body(x, weight):
         FINE.put(u_out, g_out, x, FINE.sweep(u_in, g_in, b_ref, x, weight))
 
-    in_segments(margin, WIDE_X - margin, body, masks, 1.0 / 30.0, 4)
+    in_segments(margin, WIDE_X - margin, body, masks, 1.0 / 30.0, 8)
 
 
 def add_correction(error_of, u_in, u_out, g_out, margin):
@@ -412,7 +412,7 @@
             ]
             FINE.put(u_out, g_out, x, plane)
 
-    each(margin // 2, (WIDE_X - margin) // 2, body, 2)
+    each(margin // 2, (WIDE_X - margin) // 2, body, 6)
 
 
 def send_residual(u_ref, g_ref, b_ref, out_ref):
@@ -490,7 +490,7 @@
             plane.append(line)
         FINE.put(b_ref, g_ref, x, plane)
 
-    each(0, count, body, 4)
+    each(0, count, body, 8)
 
 
 def first_sweep_on(b_ref, g_ref, u_ref, h_ref, start, count, mask):
@@ -500,7 +500,7 @@
         x = start + i
         FINE.put(u_ref, h_ref, x, FINE.sweep(b_ref, g_ref, b_ref, x, weight))
 
-    each(0, count, body, 4)
+    each(0, count, body, 8)
 
 
 def early_kernel(count_x, count_z, where_ref, mid_ref, mid_rim_ref, near_ref, far_ref, c_ref,
@@ -584,7 +584,7 @@
             for p in range(4):
                 rows_ref[x - RIM, p, pl.ds(q, 4, stride=4), :] = plane[q][p][0:4]
 
-    each(RIM, RIM + BRICK_X, body, 2)
+    each(RIM, RIM + BRICK_X, body, 4)
     tiles = [rows_ref[:, p].reshape(BRICK_X * BRICK_Z, LANES) for p in range(4)]
     matrix = places(out_ref.shape[2], lambda l, y: y == (l % LANES) * 4 + l // LANES)
     out_ref[...] = permuted(jnp.concatenate(tiles, axis=1), matrix).reshape(out_ref.shape)

time: 59.6 us -> 59.3 us (level)
  no operation moved by 1% of the time
where the time goes in v14:
time: 59.3 us; the launch traced here: 59.1 us
  starting transfers between devices  32.1 us (54%)
  Pallas kernels  15.5 us (26%)
  waiting for transfers between devices  11.1 us (19%)
    ppermute x15, starting transfers between devices, swap(): lax.ppermute(values, axis, pairs_apart(lax.axis_size(axis), distance))  30.1 us
    pallas_call x5, Pallas kernels, run(): pl.pallas_call(kernel, out_shape=shapes, in_specs=[pl.BlockSpec(memory_sp...  15.5 us
    ppermute x15, waiting for transfers between devices, swap(): lax.ppermute(values, axis, pairs_apart(lax.axis_size(axis), distance))  11.1 us
  transfers between devices with their start and end apart: 18, of which 7 were waited for; matrix products, arithmetic and copies ran while one was open for 0% of the time, Pallas kernels for 3%

profile of v14, /device:TPU:0, one launch (start us, length us, event | category | flops | bytes accessed | tf_op | source)
XLA Modules:
  0.0 59.1 jit_solution(14071284044882387684)
XLA Ops:
  0.0 0.1 pad_add_fusion.where_ref
  0.1 1.4 %shard_map.17 = (f32[8,4,16,128]{3,2,1,0:T(8,128)S(1)}, f32[8,4,8,128]{3,2,1,0:T(8,128)S(1)}, f32[8,4,8,128]{3,2,1,0:T(8,128)S(1)}) custom-call(s32[2]{0:T(128)S(1)} %pad_add_fusion.where_ref, f32[8,16,512]{2,1,0:T(8,128)} %charges_ref.1), custom_call_target="tpu_custom_call" | custom-call | tf_op jit(solution)/shard_map/pallas_call | solution.py:600
  1.5 3.1 %collective-permute-start = (f32[8,4,8,128]{3,2,1,0:T(8,128)S(1)}, f32[8,4,8,128]{3,2,1,0:T(8,128)S(1)}, u32[]{:S(2)}, u32[]{:S(2)}) collective-permute-start(f32[8,4,8,128]{3,2,1,0:T(8,128)S(1)} %get-tuple-element.18), channel_id=1, source_target_pairs={{0,1},{1,0},{2,3},{3,2},{4,5},{5,4},{6,7},{7,6},{8,9},{9,8},{10,11... | collective-permute-start | bytes 393224 | tf_op jit(solution)/shard_map/ppermute | solution.py:623
  4.6 0.7 %collective-permute-start.1 = (f32[8,4,8,128]{3,2,1,0:T(8,128)S(1)}, f32[8,4,8,128]{3,2,1,0:T(8,128)S(1)}, u32[]{:S(2)}, u32[]{:S(2)}) collective-permute-start(f32[8,4,8,128]{3,2,1,0:T(8,128)S(1)} %get-tuple-element.19), channel_id=1, source_target_pairs={{1,2},{2,1},{5,6},{6,5},{9,10},{10,9},{13,14},{14,13},{17,18},{18,... | collective-permute-start | bytes 393224 | tf_op jit(solution)/shard_map/ppermute | solution.py:647
  5.2 0.1 collective-permute-start.4
  5.3 0.7 %collective-permute-start.5 = (f32[8,4,16,128]{3,2,1,0:T(8,128)S(1)}, f32[8,4,16,128]{3,2,1,0:T(8,128)S(1)}, u32[]{:S(2)}, u32[]{:S(2)}) collective-permute-start(f32[8,4,16,128]{3,2,1,0:T(8,128)S(1)} %get-tuple-element.20.mid_ref), channel_id=1, source_target_pairs={{4,8},{8,4},{5,9},{9,5},{6,10},{10,6},{7,11},{11,7},{20,24},{24,20... | collective-permute-start | bytes 786440 | tf_op jit(solution)/shard_map/ppermute | solution.py:645
  6.0 2.1 %collective-permute-done = f32[8,4,8,128]{3,2,1,0:T(8,128)S(1)} collective-permute-done((f32[8,4,8,128]{3,2,1,0:T(8,128)S(1)}, f32[8,4,8,128]{3,2,1,0:T(8,128)S(1)}, u32[]{:S(2)}, u32[]{:S(2)}) %collective-permute-start) | collective-permute-done | bytes 131104 | tf_op jit(solution)/shard_map/ppermute | solution.py:623
  8.1 0.0 collective-permute-done.1
  8.1 0.7 %collective-permute-start.3 = (f32[8,4,16,128]{3,2,1,0:T(8,128)S(1)}, f32[8,4,16,128]{3,2,1,0:T(8,128)S(1)}, u32[]{:S(2)}, u32[]{:S(2)}) collective-permute-start(f32[8,4,16,128]{3,2,1,0:T(8,128)S(1)} %pad_maximum_fusion.mid_rim_ref), channel_id=1, source_target_pairs={{4,8},{8,4},{5,9},{9,5},{6,10},{10,6},{7,11},{11,7},{20,24},{24,20... | collective-permute-start | bytes 786440 | tf_op jit(solution)/shard_map/ppermute | solution.py:650
  8.8 3.1 %collective-permute-start.2 = (f32[8,4,16,128]{3,2,1,0:T(8,128)S(1)}, f32[8,4,16,128]{3,2,1,0:T(8,128)S(1)}, u32[]{:S(2)}, u32[]{:S(2)}) collective-permute-start(f32[8,4,16,128]{3,2,1,0:T(8,128)S(1)} %pad_maximum_fusion.mid_rim_ref), channel_id=1, source_target_pairs={{0,4},{4,0},{8,12},{12,8},{1,5},{5,1},{9,13},{13,9},{2,6},{6,2},{1... | collective-permute-start | bytes 786440 | tf_op jit(solution)/shard_map/ppermute | solution.py:623
  11.9 0.0 collective-permute-done.4.near_ref
  11.9 0.0 collective-permute-done.5.far_ref
  11.9 1.7 %shard_map.18 = (f32[24,4,4,8,128]{4,3,2,1,0:T(8,128)S(1)}, f32[24,4,4,8,128]{4,3,2,1,0:T(8,128)S(1)}, f32[24,4,4,8,128]{4,3,2,1,0:T(8,128)S(1)}, f32[24,4,4,8,1...) custom-call(s32[2]{0:T(128)S(1)} %pad_add_fusion.where_ref, f32[8,4,16,128]{3,2,1,0:T(8,128)S(1)} %get-tuple-element.20.mid_ref, ...), custom_call_target="tpu_custom_call" | custom-call | tf_op jit(solution)/shard_map/pallas_call | solution.py:600
  13.6 0.0 collective-permute-done.3.far_rim_ref
  13.6 0.0 collective-permute-done.2.near_rim_ref
  13.6 2.2 %shard_map.19 = (f32[24,4,4,8,128]{4,3,2,1,0:T(8,128)S(1)}, f32[24,4,4,8,128]{4,3,2,1,0:T(8,128)S(1)}, f32[24,4,4,8,128]{4,3,2,1,0:T(8,128)S(1)}, f32[24,4,4,8,1...) custom-call(s32[2]{0:T(128)S(1)} %pad_add_fusion.where_ref, ...), custom_call_target="tpu_custom_call", output_to_operand_aliasing={{0}: (3, {}), {1}: (4, {}), {2}: (5, {}), {3}: (6, {}), {4}... | custom-call | tf_op jit(solution)/shard_map/pallas_call | solution.py:600
  15.8 4.7 %collective-permute-start.8 = (f32[1,4,2,8,128]{4,3,2,1,0:T(8,128)S(1)}, f32[1,4,2,8,128]{4,3,2,1,0:T(8,128)S(1)}, u32[]{:S(2)}, u32[]{:S(2)}) collective-permute-start(f32[1,4,2,8,128]{4,3,2,1,0:T(8,128)S(1)} %bitcast.6), channel_id=1, source_target_pairs={{0,1},{1,0},{2,3},{3,2},{4,5},{5,4},{6,7},{7,6},{8,9},{9,8},{10,11... | collective-permute-start | bytes 98312 | tf_op jit(solution)/shard_map/ppermute | solution.py:623
  20.5 1.3 %collective-permute-start.7 = (f32[1,4,2,8,128]{4,3,2,1,0:T(8,128)S(1)}, f32[1,4,2,8,128]{4,3,2,1,0:T(8,128)S(1)}, u32[]{:S(2)}, u32[]{:S(2)}) collective-permute-start(f32[1,4,2,8,128]{4,3,2,1,0:T(8,128)S(1)} %bitcast.7), channel_id=1, source_target_pairs={{0,2},{1,3},{2,0},{3,1},{4,6},{5,7},{6,4},{7,5},{8,10},{9,11},{10,... | collective-permute-start | bytes 98312 | tf_op jit(solution)/shard_map/ppermute | solution.py:623
  21.7 1.4 %collective-permute-start.6 = (f32[1,4,2,8,128]{4,3,2,1,0:T(8,128)S(1)}, f32[1,4,2,8,128]{4,3,2,1,0:T(8,128)S(1)}, u32[]{:S(2)}, u32[]{:S(2)}) collective-permute-start(f32[1,4,2,8,128]{4,3,2,1,0:T(8,128)S(1)} %bitcast.8), channel_id=1, source_target_pairs={{0,3},{1,2},{2,1},{3,0},{4,7},{5,6},{6,5},{7,4},{8,11},{9,10},{10,... | collective-permute-start | bytes 98312 | tf_op jit(solution)/shard_map/ppermute | solution.py:623
  23.1 0.0 collective-permute-done.8
  23.1 4.0 %collective-permute-start.10 = (f32[2,4,2,8,128]{4,3,2,1,0:T(8,128)S(1)}, f32[2,4,2,8,128]{4,3,2,1,0:T(8,128)S(1)}, u32[]{:S(2)}, u32[]{:S(2)}) collective-permute-start(f32[2,4,2,8,128]{4,3,2,1,0:T(8,128)S(1)} %pad_maximum_fusion.2), channel_id=1, source_target_pairs={{0,8},{4,12},{8,0},{12,4},{1,9},{5,13},{9,1},{13,5},{2,10},{6,14},... | collective-permute-start | bytes 196616 | tf_op jit(solution)/shard_map/ppermute | solution.py:623
  27.1 0.0 collective-permute-done.7
  27.1 0.4 collective-permute-done.6
  27.5 3.9 %collective-permute-start.9 = (f32[2,4,2,8,128]{4,3,2,1,0:T(8,128)S(1)}, f32[2,4,2,8,128]{4,3,2,1,0:T(8,128)S(1)}, u32[]{:S(2)}, u32[]{:S(2)}) collective-permute-start(f32[2,4,2,8,128]{4,3,2,1,0:T(8,128)S(1)} %pad_maximum_fusion.1), channel_id=1, source_target_pairs={{0,8},{4,12},{8,0},{12,4},{1,9},{5,13},{9,1},{13,5},{2,10},{6,14},... | collective-permute-start | bytes 196616 | tf_op jit(solution)/shard_map/ppermute | solution.py:623
  31.4 2.2 %collective-permute-done.9 = f32[2,4,2,8,128]{4,3,2,1,0:T(8,128)S(1)} collective-permute-done((f32[2,4,2,8,128]{4,3,2,1,0:T(8,128)S(1)}, f32[2,4,2,8,128]{4,3,2,1,0:T(8,128)S(1)}, u32[]{:S(2)}, u32[]{:S(2)}) %collective-permute-start.9) | collective-permute-done | bytes 65568 | tf_op jit(solution)/shard_map/ppermute | solution.py:623
  33.6 0.0 collective-permute-done.10
  33.6 0.1 collective-permute-start.11
  33.7 1.5 %collective-permute-done.11.refs_1_ = f32[8,4,2,8,128]{4,3,2,1,0:T(8,128)S(1)} collective-permute-done((f32[8,4,2,8,128]{4,3,2,1,0:T(8,128)S(1)}, f32[8,4,2,8,128]{4,3,2,1,0:T(8,128)S(1)}, u32[]{:S(2)}, u32[]{:S(2)}) %collective-permute-start.11) | collective-permute-done | bytes 262176 | tf_op jit(solution)/shard_map/ppermute | solution.py:623
  35.2 5.7 %shard_map.20 = (f32[24,4,4,8,128]{4,3,2,1,0:T(8,128)S(1)}, f32[4,2,8,128]{3,2,1,0:T(8,128)S(1)}) custom-call(s32[2]{0:T(128)S(1)} %pad_add_fusion.where_ref, f32[8,4,2,8,128]{4,3,2,1,0:T(8,128)S(1)} %constant_dynamic-update-slice_fusion.refs_0_, f32[8,4,2,8,128]{4,3,2,1,0:T(8,128)S(1)} %collective-permute-done.11.refs_1_, ...), custom_call_target="tpu_custom_call" | custom-call | tf_op jit(solution)/shard_map/pallas_call | solution.py:600
  40.9 0.2 collective-permute-start.14
  41.2 1.8 %collective-permute-start.13 = (f32[1,4,2,8,128]{4,3,2,1,0:T(8,128)S(1)}, f32[1,4,2,8,128]{4,3,2,1,0:T(8,128)S(1)}, u32[]{:S(2)}, u32[]{:S(2)}) collective-permute-start(f32[1,4,2,8,128]{4,3,2,1,0:T(8,128)S(1)} %bitcast.11), channel_id=1, source_target_pairs={{0,2},{1,3},{2,0},{3,1},{4,6},{5,7},{6,4},{7,5},{8,10},{9,11},{10,... | collective-permute-start | bytes 98312 | tf_op jit(solution)/shard_map/ppermute | solution.py:623
  43.0 2.4 %collective-permute-start.12 = (f32[1,4,2,8,128]{4,3,2,1,0:T(8,128)S(1)}, f32[1,4,2,8,128]{4,3,2,1,0:T(8,128)S(1)}, u32[]{:S(2)}, u32[]{:S(2)}) collective-permute-start(f32[1,4,2,8,128]{4,3,2,1,0:T(8,128)S(1)} %bitcast.12), channel_id=1, source_target_pairs={{0,3},{1,2},{2,1},{3,0},{4,7},{5,6},{6,5},{7,4},{8,11},{9,10},{10,... | collective-permute-start | bytes 98312 | tf_op jit(solution)/shard_map/ppermute | solution.py:623
  45.4 0.0 collective-permute-done.14
  45.4 2.1 %collective-permute-start.16 = (f32[2,4,2,8,128]{4,3,2,1,0:T(8,128)S(1)}, f32[2,4,2,8,128]{4,3,2,1,0:T(8,128)S(1)}, u32[]{:S(2)}, u32[]{:S(2)}) collective-permute-start(f32[2,4,2,8,128]{4,3,2,1,0:T(8,128)S(1)} %pad_maximum_fusion.4), channel_id=1, source_target_pairs={{0,8},{4,12},{8,0},{12,4},{1,9},{5,13},{9,1},{13,5},{2,10},{6,14},... | collective-permute-start | bytes 196616 | tf_op jit(solution)/shard_map/ppermute | solution.py:623
  47.5 0.0 collective-permute-done.13
  47.5 1.2 %collective-permute-done.12 = f32[1,4,2,8,128]{4,3,2,1,0:T(8,128)S(1)} collective-permute-done((f32[1,4,2,8,128]{4,3,2,1,0:T(8,128)S(1)}, f32[1,4,2,8,128]{4,3,2,1,0:T(8,128)S(1)}, u32[]{:S(2)}, u32[]{:S(2)}) %collective-permute-start.12) | collective-permute-done | bytes 32800 | tf_op jit(solution)/shard_map/ppermute | solution.py:623
  48.7 2.0 %collective-permute-start.15 = (f32[2,4,2,8,128]{4,3,2,1,0:T(8,128)S(1)}, f32[2,4,2,8,128]{4,3,2,1,0:T(8,128)S(1)}, u32[]{:S(2)}, u32[]{:S(2)}) collective-permute-start(f32[2,4,2,8,128]{4,3,2,1,0:T(8,128)S(1)} %pad_maximum_fusion.3), channel_id=1, source_target_pairs={{0,8},{4,12},{8,0},{12,4},{1,9},{5,13},{9,1},{13,5},{2,10},{6,14},... | collective-permute-start | bytes 196616 | tf_op jit(solution)/shard_map/ppermute | solution.py:623
  50.7 2.2 %collective-permute-done.15 = f32[2,4,2,8,128]{4,3,2,1,0:T(8,128)S(1)} collective-permute-done((f32[2,4,2,8,128]{4,3,2,1,0:T(8,128)S(1)}, f32[2,4,2,8,128]{4,3,2,1,0:T(8,128)S(1)}, u32[]{:S(2)}, u32[]{:S(2)}) %collective-permute-start.15) | collective-permute-done | bytes 65568 | tf_op jit(solution)/shard_map/ppermute | solution.py:623
  53.0 0.0 collective-permute-done.16
  53.0 0.1 collective-permute-start.17
  53.1 1.5 %collective-permute-done.17.refs_1_ = f32[8,4,2,8,128]{4,3,2,1,0:T(8,128)S(1)} collective-permute-done((f32[8,4,2,8,128]{4,3,2,1,0:T(8,128)S(1)}, f32[8,4,2,8,128]{4,3,2,1,0:T(8,128)S(1)}, u32[]{:S(2)}, u32[]{:S(2)}) %collective-permute-start.17) | collective-permute-done | bytes 262176 | tf_op jit(solution)/shard_map/ppermute | solution.py:623
  54.6 4.5 %shard_map.21 = f32[8,16,512]{2,1,0:T(8,128)} custom-call(s32[2]{0:T(128)S(1)} %pad_add_fusion.where_ref, f32[8,4,2,8,128]{4,3,2,1,0:T(8,128)S(1)} %constant_dynamic-update-slice_fusion.6.refs_0_, f32[8,4,2,8,128]{4,3,2,1,0:T(8,128)S(1)} %collective-permute-done.17.refs_1_, f32[24,4,4,8,128]{4,3,2,1,0:T(8,128)S(1)} %get-tuple-element.30.refs_2_, ...), custom_call_target="tpu_custom_call" | custom-call | tf_op jit(solution)/shard_map/pallas_call | solution.py:600
  (18 shorter events, 0.1 us)
Async XLA Ops:
  1.5 6.6 %collective-permute-start = (f32[8,4,8,128]{3,2,1,0:T(8,128)S(1)}, f32[8,4,8,128]{3,2,1,0:T(8,128)S(1)}, u32[]{:S(2)}, u32[]{:S(2)}) collective-permute-start(f32[8,4,8,128]{3,2,1,0:T(8,128)S(1)} %get-tuple-element.18), channel_id=1, source_target_pairs={{0,1},{1,0},{2,3},{3,2},{4,5},{5,4},{6,7},{7,6},{8,9},{9,8},{10,11... | collective-permute-start | bytes 393224 | tf_op jit(solution)/shard_map/ppermute | solution.py:623
  4.6 3.5 %collective-permute-start.1 = (f32[8,4,8,128]{3,2,1,0:T(8,128)S(1)}, f32[8,4,8,128]{3,2,1,0:T(8,128)S(1)}, u32[]{:S(2)}, u32[]{:S(2)}) collective-permute-start(f32[8,4,8,128]{3,2,1,0:T(8,128)S(1)} %get-tuple-element.19), channel_id=1, source_target_pairs={{1,2},{2,1},{5,6},{6,5},{9,10},{10,9},{13,14},{14,13},{17,18},{18,... | collective-permute-start | bytes 393224 | tf_op jit(solution)/shard_map/ppermute | solution.py:647
  5.2 6.7 %collective-permute-start.4 = (f32[8,16,512]{2,1,0:T(8,128)}, f32[8,16,512]{2,1,0:T(8,128)S(1)}, u32[]{:S(2)}, u32[]{:S(2)}) collective-permute-start(f32[8,16,512]{2,1,0:T(8,128)} %charges_ref.1), channel_id=1, source_target_pairs={{0,4},{4,0},{8,12},{12,8},{1,5},{5,1},{9,13},{13,9},{2,6},{6,2},{1... | collective-permute-start | bytes 786440 | tf_op jit(solution)/shard_map/ppermute | solution.py:623
  5.3 6.6 %collective-permute-start.5 = (f32[8,4,16,128]{3,2,1,0:T(8,128)S(1)}, f32[8,4,16,128]{3,2,1,0:T(8,128)S(1)}, u32[]{:S(2)}, u32[]{:S(2)}) collective-permute-start(f32[8,4,16,128]{3,2,1,0:T(8,128)S(1)} %get-tuple-element.20.mid_ref), channel_id=1, source_target_pairs={{4,8},{8,4},{5,9},{9,5},{6,10},{10,6},{7,11},{11,7},{20,24},{24,20... | collective-permute-start | bytes 786440 | tf_op jit(solution)/shard_map/ppermute | solution.py:645
  8.1 5.5 %collective-permute-start.3 = (f32[8,4,16,128]{3,2,1,0:T(8,128)S(1)}, f32[8,4,16,128]{3,2,1,0:T(8,128)S(1)}, u32[]{:S(2)}, u32[]{:S(2)}) collective-permute-start(f32[8,4,16,128]{3,2,1,0:T(8,128)S(1)} %pad_maximum_fusion.mid_rim_ref), channel_id=1, source_target_pairs={{4,8},{8,4},{5,9},{9,5},{6,10},{10,6},{7,11},{11,7},{20,24},{24,20... | collective-permute-start | bytes 786440 | tf_op jit(solution)/shard_map/ppermute | solution.py:650
  8.8 4.8 %collective-permute-start.2 = (f32[8,4,16,128]{3,2,1,0:T(8,128)S(1)}, f32[8,4,16,128]{3,2,1,0:T(8,128)S(1)}, u32[]{:S(2)}, u32[]{:S(2)}) collective-permute-start(f32[8,4,16,128]{3,2,1,0:T(8,128)S(1)} %pad_maximum_fusion.mid_rim_ref), channel_id=1, source_target_pairs={{0,4},{4,0},{8,12},{12,8},{1,5},{5,1},{9,13},{13,9},{2,6},{6,2},{1... | collective-permute-start | bytes 786440 | tf_op jit(solution)/shard_map/ppermute | solution.py:623
  15.8 7.3 %collective-permute-start.8 = (f32[1,4,2,8,128]{4,3,2,1,0:T(8,128)S(1)}, f32[1,4,2,8,128]{4,3,2,1,0:T(8,128)S(1)}, u32[]{:S(2)}, u32[]{:S(2)}) collective-permute-start(f32[1,4,2,8,128]{4,3,2,1,0:T(8,128)S(1)} %bitcast.6), channel_id=1, source_target_pairs={{0,1},{1,0},{2,3},{3,2},{4,5},{5,4},{6,7},{7,6},{8,9},{9,8},{10,11... | collective-permute-start | bytes 98312 | tf_op jit(solution)/shard_map/ppermute | solution.py:623
  20.5 6.6 %collective-permute-start.7 = (f32[1,4,2,8,128]{4,3,2,1,0:T(8,128)S(1)}, f32[1,4,2,8,128]{4,3,2,1,0:T(8,128)S(1)}, u32[]{:S(2)}, u32[]{:S(2)}) collective-permute-start(f32[1,4,2,8,128]{4,3,2,1,0:T(8,128)S(1)} %bitcast.7), channel_id=1, source_target_pairs={{0,2},{1,3},{2,0},{3,1},{4,6},{5,7},{6,4},{7,5},{8,10},{9,11},{10,... | collective-permute-start | bytes 98312 | tf_op jit(solution)/shard_map/ppermute | solution.py:623
  21.7 5.7 %collective-permute-start.6 = (f32[1,4,2,8,128]{4,3,2,1,0:T(8,128)S(1)}, f32[1,4,2,8,128]{4,3,2,1,0:T(8,128)S(1)}, u32[]{:S(2)}, u32[]{:S(2)}) collective-permute-start(f32[1,4,2,8,128]{4,3,2,1,0:T(8,128)S(1)} %bitcast.8), channel_id=1, source_target_pairs={{0,3},{1,2},{2,1},{3,0},{4,7},{5,6},{6,5},{7,4},{8,11},{9,10},{10,... | collective-permute-start | bytes 98312 | tf_op jit(solution)/shard_map/ppermute | solution.py:623
  23.1 10.5 %collective-permute-start.10 = (f32[2,4,2,8,128]{4,3,2,1,0:T(8,128)S(1)}, f32[2,4,2,8,128]{4,3,2,1,0:T(8,128)S(1)}, u32[]{:S(2)}, u32[]{:S(2)}) collective-permute-start(f32[2,4,2,8,128]{4,3,2,1,0:T(8,128)S(1)} %pad_maximum_fusion.2), channel_id=1, source_target_pairs={{0,8},{4,12},{8,0},{12,4},{1,9},{5,13},{9,1},{13,5},{2,10},{6,14},... | collective-permute-start | bytes 196616 | tf_op jit(solution)/shard_map/ppermute | solution.py:623
  27.5 6.1 %collective-permute-start.9 = (f32[2,4,2,8,128]{4,3,2,1,0:T(8,128)S(1)}, f32[2,4,2,8,128]{4,3,2,1,0:T(8,128)S(1)}, u32[]{:S(2)}, u32[]{:S(2)}) collective-permute-start(f32[2,4,2,8,128]{4,3,2,1,0:T(8,128)S(1)} %pad_maximum_fusion.1), channel_id=1, source_target_pairs={{0,8},{4,12},{8,0},{12,4},{1,9},{5,13},{9,1},{13,5},{2,10},{6,14},... | collective-permute-start | bytes 196616 | tf_op jit(solution)/shard_map/ppermute | solution.py:623
  33.6 1.6 %collective-permute-start.11 = (f32[8,4,2,8,128]{4,3,2,1,0:T(8,128)S(1)}, f32[8,4,2,8,128]{4,3,2,1,0:T(8,128)S(1)}, u32[]{:S(2)}, u32[]{:S(2)}) collective-permute-start(f32[8,4,2,8,128]{4,3,2,1,0:T(8,128)S(1)} %constant_dynamic-update-slice_fusion.refs_0_), channel_id=1, source_target_pairs={{0,4},{4,0},{8,12},{12,8},{1,5},{5,1},{9,13},{13,9},{2,6},{6,2},{1... | collective-permute-start | bytes 786440 | tf_op jit(solution)/shard_map/ppermute | solution.py:623
  40.9 4.5 %collective-permute-start.14 = (f32[1,4,2,8,128]{4,3,2,1,0:T(8,128)S(1)}, f32[1,4,2,8,128]{4,3,2,1,0:T(8,128)S(1)}, u32[]{:S(2)}, u32[]{:S(2)}) collective-permute-start(f32[1,4,2,8,128]{4,3,2,1,0:T(8,128)S(1)} %bitcast.10), channel_id=1, source_target_pairs={{0,1},{1,0},{2,3},{3,2},{4,5},{5,4},{6,7},{7,6},{8,9},{9,8},{10,11... | collective-permute-start | bytes 98312 | tf_op jit(solution)/shard_map/ppermute | solution.py:623
  41.2 6.3 %collective-permute-start.13 = (f32[1,4,2,8,128]{4,3,2,1,0:T(8,128)S(1)}, f32[1,4,2,8,128]{4,3,2,1,0:T(8,128)S(1)}, u32[]{:S(2)}, u32[]{:S(2)}) collective-permute-start(f32[1,4,2,8,128]{4,3,2,1,0:T(8,128)S(1)} %bitcast.11), channel_id=1, source_target_pairs={{0,2},{1,3},{2,0},{3,1},{4,6},{5,7},{6,4},{7,5},{8,10},{9,11},{10,... | collective-permute-start | bytes 98312 | tf_op jit(solution)/shard_map/ppermute | solution.py:623
  43.0 5.7 %collective-permute-start.12 = (f32[1,4,2,8,128]{4,3,2,1,0:T(8,128)S(1)}, f32[1,4,2,8,128]{4,3,2,1,0:T(8,128)S(1)}, u32[]{:S(2)}, u32[]{:S(2)}) collective-permute-start(f32[1,4,2,8,128]{4,3,2,1,0:T(8,128)S(1)} %bitcast.12), channel_id=1, source_target_pairs={{0,3},{1,2},{2,1},{3,0},{4,7},{5,6},{6,5},{7,4},{8,11},{9,10},{10,... | collective-permute-start | bytes 98312 | tf_op jit(solution)/shard_map/ppermute | solution.py:623
  45.4 7.5 %collective-permute-start.16 = (f32[2,4,2,8,128]{4,3,2,1,0:T(8,128)S(1)}, f32[2,4,2,8,128]{4,3,2,1,0:T(8,128)S(1)}, u32[]{:S(2)}, u32[]{:S(2)}) collective-permute-start(f32[2,4,2,8,128]{4,3,2,1,0:T(8,128)S(1)} %pad_maximum_fusion.4), channel_id=1, source_target_pairs={{0,8},{4,12},{8,0},{12,4},{1,9},{5,13},{9,1},{13,5},{2,10},{6,14},... | collective-permute-start | bytes 196616 | tf_op jit(solution)/shard_map/ppermute | solution.py:623
  48.7 4.3 %collective-permute-start.15 = (f32[2,4,2,8,128]{4,3,2,1,0:T(8,128)S(1)}, f32[2,4,2,8,128]{4,3,2,1,0:T(8,128)S(1)}, u32[]{:S(2)}, u32[]{:S(2)}) collective-permute-start(f32[2,4,2,8,128]{4,3,2,1,0:T(8,128)S(1)} %pad_maximum_fusion.3), channel_id=1, source_target_pairs={{0,8},{4,12},{8,0},{12,4},{1,9},{5,13},{9,1},{13,5},{2,10},{6,14},... | collective-permute-start | bytes 196616 | tf_op jit(solution)/shard_map/ppermute | solution.py:623
  53.0 1.6 %collective-permute-start.17 = (f32[8,4,2,8,128]{4,3,2,1,0:T(8,128)S(1)}, f32[8,4,2,8,128]{4,3,2,1,0:T(8,128)S(1)}, u32[]{:S(2)}, u32[]{:S(2)}) collective-permute-start(f32[8,4,2,8,128]{4,3,2,1,0:T(8,128)S(1)} %constant_dynamic-update-slice_fusion.6.refs_0_), channel_id=1, source_target_pairs={{0,4},{4,0},{8,12},{12,8},{1,5},{5,1},{9,13},{13,9},{2,6},{6,2},{1... | collective-permute-start | bytes 786440 | tf_op jit(solution)/shard_map/ppermute | solution.py:623

commit v15 on v14

--- a/solution.py
+++ b/solution.py
@@ -626,8 +626,8 @@
 def every_piece(piece):
     count_x, count_z = lax.axis_size("gx"), lax.axis_size("gz")
     line = [swap("gz", piece[None], count_z - 1 - n) for n in range(count_z - 1)] + [piece[None]]
-    halves = [jnp.concatenate(half) for half in (line[: count_z // 2], line[count_z // 2 :])]
-    held = jnp.concatenate(halves + [swap("gx", half, 2) for half in halves])
+    parts = [jnp.concatenate(part) for part in (line[:1], line[1:])]
+    held = jnp.concatenate(parts + [swap("gx", part, 2) for part in parts])
     distance = 4
     while distance < count_x:
         held = jnp.concatenate([held, swap("gx", held, distance)])

time: 59.3 us -> 59.8 us (level)
  waiting for transfers between devices: 11.1 us -> 15.5 us
  starting transfers between devices: 32.1 us -> 28.1 us
    ppermute x15, waiting for transfers between devices: 11.1 us -> 15.5 us  [swap(): lax.ppermute(values, axis, pairs_apart(lax.axis_size(axis), distance))]
    ppermute x15, starting transfers between devices: 30.1 us -> 26.1 us  [swap(): lax.ppermute(values, axis, pairs_apart(lax.axis_size(axis), distance))]
  transfers between devices with their start and end apart: 18 -> 18, of which waited for: 7 -> 8; matrix products, arithmetic and copies ran while one was open for 0% -> 0% of each run, Pallas kernels for 3% -> 3%
where the time goes in v15:
time: 59.8 us; the launch traced here: 59.6 us
  starting transfers between devices  28.1 us (47%)
  Pallas kernels  15.5 us (26%)
  waiting for transfers between devices  15.5 us (26%)
    ppermute x15, starting transfers between devices, swap(): lax.ppermute(values, axis, pairs_apart(lax.axis_size(axis), distance))  26.1 us
    ppermute x15, waiting for transfers between devices, swap(): lax.ppermute(values, axis, pairs_apart(lax.axis_size(axis), distance))  15.5 us
    pallas_call x5, Pallas kernels, run(): pl.pallas_call(kernel, out_shape=shapes, in_specs=[pl.BlockSpec(memory_sp...  15.5 us
  transfers between devices with their start and end apart: 18, of which 8 were waited for; matrix products, arithmetic and copies ran while one was open for 0% of the time, Pallas kernels for 3%

profile of v15, /device:TPU:0, one launch (start us, length us, event | category | flops | bytes accessed | tf_op | source)
XLA Modules:
  0.0 59.6 jit_solution(12535945387627956472)
XLA Ops:
  0.0 0.1 pad_add_fusion.where_ref
  0.1 1.4 %shard_map.17 = (f32[8,4,16,128]{3,2,1,0:T(8,128)S(1)}, f32[8,4,8,128]{3,2,1,0:T(8,128)S(1)}, f32[8,4,8,128]{3,2,1,0:T(8,128)S(1)}) custom-call(s32[2]{0:T(128)S(1)} %pad_add_fusion.where_ref, f32[8,16,512]{2,1,0:T(8,128)} %charges_ref.1), custom_call_target="tpu_custom_call" | custom-call | tf_op jit(solution)/shard_map/pallas_call | solution.py:600
  1.5 3.1 %collective-permute-start = (f32[8,4,8,128]{3,2,1,0:T(8,128)S(1)}, f32[8,4,8,128]{3,2,1,0:T(8,128)S(1)}, u32[]{:S(2)}, u32[]{:S(2)}) collective-permute-start(f32[8,4,8,128]{3,2,1,0:T(8,128)S(1)} %get-tuple-element.18), channel_id=1, source_target_pairs={{0,1},{1,0},{2,3},{3,2},{4,5},{5,4},{6,7},{7,6},{8,9},{9,8},{10,11... | collective-permute-start | bytes 393224 | tf_op jit(solution)/shard_map/ppermute | solution.py:623
  4.6 0.7 %collective-permute-start.1 = (f32[8,4,8,128]{3,2,1,0:T(8,128)S(1)}, f32[8,4,8,128]{3,2,1,0:T(8,128)S(1)}, u32[]{:S(2)}, u32[]{:S(2)}) collective-permute-start(f32[8,4,8,128]{3,2,1,0:T(8,128)S(1)} %get-tuple-element.19), channel_id=1, source_target_pairs={{1,2},{2,1},{5,6},{6,5},{9,10},{10,9},{13,14},{14,13},{17,18},{18,... | collective-permute-start | bytes 393224 | tf_op jit(solution)/shard_map/ppermute | solution.py:647
  5.2 0.1 collective-permute-start.4
  5.3 0.7 %collective-permute-start.5 = (f32[8,4,16,128]{3,2,1,0:T(8,128)S(1)}, f32[8,4,16,128]{3,2,1,0:T(8,128)S(1)}, u32[]{:S(2)}, u32[]{:S(2)}) collective-permute-start(f32[8,4,16,128]{3,2,1,0:T(8,128)S(1)} %get-tuple-element.20.mid_ref), channel_id=1, source_target_pairs={{4,8},{8,4},{5,9},{9,5},{6,10},{10,6},{7,11},{11,7},{20,24},{24,20... | collective-permute-start | bytes 786440 | tf_op jit(solution)/shard_map/ppermute | solution.py:645
  6.0 2.1 %collective-permute-done = f32[8,4,8,128]{3,2,1,0:T(8,128)S(1)} collective-permute-done((f32[8,4,8,128]{3,2,1,0:T(8,128)S(1)}, f32[8,4,8,128]{3,2,1,0:T(8,128)S(1)}, u32[]{:S(2)}, u32[]{:S(2)}) %collective-permute-start) | collective-permute-done | bytes 131104 | tf_op jit(solution)/shard_map/ppermute | solution.py:623
  8.1 0.0 collective-permute-done.1
  8.1 0.7 %collective-permute-start.3 = (f32[8,4,16,128]{3,2,1,0:T(8,128)S(1)}, f32[8,4,16,128]{3,2,1,0:T(8,128)S(1)}, u32[]{:S(2)}, u32[]{:S(2)}) collective-permute-start(f32[8,4,16,128]{3,2,1,0:T(8,128)S(1)} %pad_maximum_fusion.mid_rim_ref), channel_id=1, source_target_pairs={{4,8},{8,4},{5,9},{9,5},{6,10},{10,6},{7,11},{11,7},{20,24},{24,20... | collective-permute-start | bytes 786440 | tf_op jit(solution)/shard_map/ppermute | solution.py:650
  8.8 3.1 %collective-permute-start.2 = (f32[8,4,16,128]{3,2,1,0:T(8,128)S(1)}, f32[8,4,16,128]{3,2,1,0:T(8,128)S(1)}, u32[]{:S(2)}, u32[]{:S(2)}) collective-permute-start(f32[8,4,16,128]{3,2,1,0:T(8,128)S(1)} %pad_maximum_fusion.mid_rim_ref), channel_id=1, source_target_pairs={{0,4},{4,0},{8,12},{12,8},{1,5},{5,1},{9,13},{13,9},{2,6},{6,2},{1... | collective-permute-start | bytes 786440 | tf_op jit(solution)/shard_map/ppermute | solution.py:623
  11.9 0.0 collective-permute-done.4.near_ref
  11.9 0.0 collective-permute-done.5.far_ref
  11.9 1.7 %shard_map.18 = (f32[24,4,4,8,128]{4,3,2,1,0:T(8,128)S(1)}, f32[24,4,4,8,128]{4,3,2,1,0:T(8,128)S(1)}, f32[24,4,4,8,128]{4,3,2,1,0:T(8,128)S(1)}, f32[24,4,4,8,1...) custom-call(s32[2]{0:T(128)S(1)} %pad_add_fusion.where_ref, f32[8,4,16,128]{3,2,1,0:T(8,128)S(1)} %get-tuple-element.20.mid_ref, ...), custom_call_target="tpu_custom_call" | custom-call | tf_op jit(solution)/shard_map/pallas_call | solution.py:600
  13.6 0.0 collective-permute-done.3.far_rim_ref
  13.6 0.0 collective-permute-done.2.near_rim_ref
  13.6 2.2 %shard_map.19 = (f32[24,4,4,8,128]{4,3,2,1,0:T(8,128)S(1)}, f32[24,4,4,8,128]{4,3,2,1,0:T(8,128)S(1)}, f32[24,4,4,8,128]{4,3,2,1,0:T(8,128)S(1)}, f32[24,4,4,8,1...) custom-call(s32[2]{0:T(128)S(1)} %pad_add_fusion.where_ref, ...), custom_call_target="tpu_custom_call", output_to_operand_aliasing={{0}: (3, {}), {1}: (4, {}), {2}: (5, {}), {3}: (6, {}), {4}... | custom-call | tf_op jit(solution)/shard_map/pallas_call | solution.py:600
  15.8 4.7 %collective-permute-start.8 = (f32[1,4,2,8,128]{4,3,2,1,0:T(8,128)S(1)}, f32[1,4,2,8,128]{4,3,2,1,0:T(8,128)S(1)}, u32[]{:S(2)}, u32[]{:S(2)}) collective-permute-start(f32[1,4,2,8,128]{4,3,2,1,0:T(8,128)S(1)} %bitcast.6), channel_id=1, source_target_pairs={{0,1},{1,0},{2,3},{3,2},{4,5},{5,4},{6,7},{7,6},{8,9},{9,8},{10,11... | collective-permute-start | bytes 98312 | tf_op jit(solution)/shard_map/ppermute | solution.py:623
  20.5 1.3 %collective-permute-start.7 = (f32[1,4,2,8,128]{4,3,2,1,0:T(8,128)S(1)}, f32[1,4,2,8,128]{4,3,2,1,0:T(8,128)S(1)}, u32[]{:S(2)}, u32[]{:S(2)}) collective-permute-start(f32[1,4,2,8,128]{4,3,2,1,0:T(8,128)S(1)} %bitcast.7), channel_id=1, source_target_pairs={{0,2},{1,3},{2,0},{3,1},{4,6},{5,7},{6,4},{7,5},{8,10},{9,11},{10,... | collective-permute-start | bytes 98312 | tf_op jit(solution)/shard_map/ppermute | solution.py:623
  21.7 1.4 %collective-permute-start.6 = (f32[1,4,2,8,128]{4,3,2,1,0:T(8,128)S(1)}, f32[1,4,2,8,128]{4,3,2,1,0:T(8,128)S(1)}, u32[]{:S(2)}, u32[]{:S(2)}) collective-permute-start(f32[1,4,2,8,128]{4,3,2,1,0:T(8,128)S(1)} %bitcast.8), channel_id=1, source_target_pairs={{0,3},{1,2},{2,1},{3,0},{4,7},{5,6},{6,5},{7,4},{8,11},{9,10},{10,... | collective-permute-start | bytes 98312 | tf_op jit(solution)/shard_map/ppermute | solution.py:623
  23.1 0.0 collective-permute-done.8
  23.1 2.5 %collective-permute-done.7 = f32[1,4,2,8,128]{4,3,2,1,0:T(8,128)S(1)} collective-permute-done((f32[1,4,2,8,128]{4,3,2,1,0:T(8,128)S(1)}, f32[1,4,2,8,128]{4,3,2,1,0:T(8,128)S(1)}, u32[]{:S(2)}, u32[]{:S(2)}) %collective-permute-start.7) | collective-permute-done | bytes 32800 | tf_op jit(solution)/shard_map/ppermute | solution.py:623
  25.6 4.0 %collective-permute-start.10 = (f32[3,4,2,8,128]{4,3,2,1,0:T(8,128)S(1)}, f32[3,4,2,8,128]{4,3,2,1,0:T(8,128)S(1)}, u32[]{:S(2)}, u32[]{:S(2)}) collective-permute-start(f32[3,4,2,8,128]{4,3,2,1,0:T(8,128)S(1)} %pad_maximum_fusion.1), channel_id=1, source_target_pairs={{0,8},{4,12},{8,0},{12,4},{1,9},{5,13},{9,1},{13,5},{2,10},{6,14},... | collective-permute-start | bytes 294920 | tf_op jit(solution)/shard_map/ppermute | solution.py:623
  29.6 0.0 collective-permute-done.6
  29.6 1.7 %collective-permute-start.9 = (f32[1,4,2,8,128]{4,3,2,1,0:T(8,128)S(1)}, f32[1,4,2,8,128]{4,3,2,1,0:T(8,128)S(1)}, u32[]{:S(2)}, u32[]{:S(2)}) collective-permute-start(f32[1,4,2,8,128]{4,3,2,1,0:T(8,128)S(1)} %collective-permute-done.6), channel_id=1, source_target_pairs={{0,8},{4,12},{8,0},{12,4},{1,9},{5,13},{9,1},{13,5},{2,10},{6,14},... | collective-permute-start | bytes 98312 | tf_op jit(solution)/shard_map/ppermute | solution.py:623
  31.4 2.2 %collective-permute-done.9 = f32[1,4,2,8,128]{4,3,2,1,0:T(8,128)S(1)} collective-permute-done((f32[1,4,2,8,128]{4,3,2,1,0:T(8,128)S(1)}, f32[1,4,2,8,128]{4,3,2,1,0:T(8,128)S(1)}, u32[]{:S(2)}, u32[]{:S(2)}) %collective-permute-start.9) | collective-permute-done | bytes 32800 | tf_op jit(solution)/shard_map/ppermute | solution.py:623
  33.5 0.0 collective-permute-done.10
  33.5 0.1 collective-permute-start.11
  33.6 1.5 %collective-permute-done.11.refs_1_ = f32[8,4,2,8,128]{4,3,2,1,0:T(8,128)S(1)} collective-permute-done((f32[8,4,2,8,128]{4,3,2,1,0:T(8,128)S(1)}, f32[8,4,2,8,128]{4,3,2,1,0:T(8,128)S(1)}, u32[]{:S(2)}, u32[]{:S(2)}) %collective-permute-start.11) | collective-permute-done | bytes 262176 | tf_op jit(solution)/shard_map/ppermute | solution.py:623
  35.1 5.7 %shard_map.20 = (f32[24,4,4,8,128]{4,3,2,1,0:T(8,128)S(1)}, f32[4,2,8,128]{3,2,1,0:T(8,128)S(1)}) custom-call(s32[2]{0:T(128)S(1)} %pad_add_fusion.where_ref, f32[8,4,2,8,128]{4,3,2,1,0:T(8,128)S(1)} %constant_dynamic-update-slice_fusion.refs_0_, f32[8,4,2,8,128]{4,3,2,1,0:T(8,128)S(1)} %collective-permute-done.11.refs_1_, ...), custom_call_target="tpu_custom_call" | custom-call | tf_op jit(solution)/shard_map/pallas_call | solution.py:600
  40.9 0.4 collective-permute-start.14
  41.3 2.5 %collective-permute-start.13 = (f32[1,4,2,8,128]{4,3,2,1,0:T(8,128)S(1)}, f32[1,4,2,8,128]{4,3,2,1,0:T(8,128)S(1)}, u32[]{:S(2)}, u32[]{:S(2)}) collective-permute-start(f32[1,4,2,8,128]{4,3,2,1,0:T(8,128)S(1)} %bitcast.11), channel_id=1, source_target_pairs={{0,2},{1,3},{2,0},{3,1},{4,6},{5,7},{6,4},{7,5},{8,10},{9,11},{10,... | collective-permute-start | bytes 98312 | tf_op jit(solution)/shard_map/ppermute | solution.py:623
  43.8 1.5 %collective-permute-start.12 = (f32[1,4,2,8,128]{4,3,2,1,0:T(8,128)S(1)}, f32[1,4,2,8,128]{4,3,2,1,0:T(8,128)S(1)}, u32[]{:S(2)}, u32[]{:S(2)}) collective-permute-start(f32[1,4,2,8,128]{4,3,2,1,0:T(8,128)S(1)} %bitcast.12), channel_id=1, source_target_pairs={{0,3},{1,2},{2,1},{3,0},{4,7},{5,6},{6,5},{7,4},{8,11},{9,10},{10,... | collective-permute-start | bytes 98312 | tf_op jit(solution)/shard_map/ppermute | solution.py:623
  45.3 0.0 collective-permute-done.14
  45.3 1.5 %collective-permute-done.13 = f32[1,4,2,8,128]{4,3,2,1,0:T(8,128)S(1)} collective-permute-done((f32[1,4,2,8,128]{4,3,2,1,0:T(8,128)S(1)}, f32[1,4,2,8,128]{4,3,2,1,0:T(8,128)S(1)}, u32[]{:S(2)}, u32[]{:S(2)}) %collective-permute-start.13) | collective-permute-done | bytes 32800 | tf_op jit(solution)/shard_map/ppermute | solution.py:623
  46.8 1.3 %collective-permute-start.16 = (f32[3,4,2,8,128]{4,3,2,1,0:T(8,128)S(1)}, f32[3,4,2,8,128]{4,3,2,1,0:T(8,128)S(1)}, u32[]{:S(2)}, u32[]{:S(2)}) collective-permute-start(f32[3,4,2,8,128]{4,3,2,1,0:T(8,128)S(1)} %pad_maximum_fusion.2), channel_id=1, source_target_pairs={{0,8},{4,12},{8,0},{12,4},{1,9},{5,13},{9,1},{13,5},{2,10},{6,14},... | collective-permute-start | bytes 294920 | tf_op jit(solution)/shard_map/ppermute | solution.py:623
  48.1 1.4 %collective-permute-done.12 = f32[1,4,2,8,128]{4,3,2,1,0:T(8,128)S(1)} collective-permute-done((f32[1,4,2,8,128]{4,3,2,1,0:T(8,128)S(1)}, f32[1,4,2,8,128]{4,3,2,1,0:T(8,128)S(1)}, u32[]{:S(2)}, u32[]{:S(2)}) %collective-permute-start.12) | collective-permute-done | bytes 32800 | tf_op jit(solution)/shard_map/ppermute | solution.py:623
  49.5 1.0 %collective-permute-start.15 = (f32[1,4,2,8,128]{4,3,2,1,0:T(8,128)S(1)}, f32[1,4,2,8,128]{4,3,2,1,0:T(8,128)S(1)}, u32[]{:S(2)}, u32[]{:S(2)}) collective-permute-start(f32[1,4,2,8,128]{4,3,2,1,0:T(8,128)S(1)} %collective-permute-done.12), channel_id=1, source_target_pairs={{0,8},{4,12},{8,0},{12,4},{1,9},{5,13},{9,1},{13,5},{2,10},{6,14},... | collective-permute-start | bytes 98312 | tf_op jit(solution)/shard_map/ppermute | solution.py:623
  50.6 2.8 %collective-permute-done.15 = f32[1,4,2,8,128]{4,3,2,1,0:T(8,128)S(1)} collective-permute-done((f32[1,4,2,8,128]{4,3,2,1,0:T(8,128)S(1)}, f32[1,4,2,8,128]{4,3,2,1,0:T(8,128)S(1)}, u32[]{:S(2)}, u32[]{:S(2)}) %collective-permute-start.15) | collective-permute-done | bytes 32800 | tf_op jit(solution)/shard_map/ppermute | solution.py:623
  53.4 0.0 collective-permute-done.16
  53.4 0.1 collective-permute-start.17
  53.5 1.5 %collective-permute-done.17.refs_1_ = f32[8,4,2,8,128]{4,3,2,1,0:T(8,128)S(1)} collective-permute-done((f32[8,4,2,8,128]{4,3,2,1,0:T(8,128)S(1)}, f32[8,4,2,8,128]{4,3,2,1,0:T(8,128)S(1)}, u32[]{:S(2)}, u32[]{:S(2)}) %collective-permute-start.17) | collective-permute-done | bytes 262176 | tf_op jit(solution)/shard_map/ppermute | solution.py:623
  55.1 4.5 %shard_map.21 = f32[8,16,512]{2,1,0:T(8,128)} custom-call(s32[2]{0:T(128)S(1)} %pad_add_fusion.where_ref, f32[8,4,2,8,128]{4,3,2,1,0:T(8,128)S(1)} %constant_dynamic-update-slice_fusion.6.refs_0_, f32[8,4,2,8,128]{4,3,2,1,0:T(8,128)S(1)} %collective-permute-done.17.refs_1_, f32[24,4,4,8,128]{4,3,2,1,0:T(8,128)S(1)} %get-tuple-element.30.refs_2_, ...), custom_call_target="tpu_custom_call" | custom-call | tf_op jit(solution)/shard_map/pallas_call | solution.py:600
  (16 shorter events, 0.1 us)
Async XLA Ops:
  1.5 6.6 %collective-permute-start = (f32[8,4,8,128]{3,2,1,0:T(8,128)S(1)}, f32[8,4,8,128]{3,2,1,0:T(8,128)S(1)}, u32[]{:S(2)}, u32[]{:S(2)}) collective-permute-start(f32[8,4,8,128]{3,2,1,0:T(8,128)S(1)} %get-tuple-element.18), channel_id=1, source_target_pairs={{0,1},{1,0},{2,3},{3,2},{4,5},{5,4},{6,7},{7,6},{8,9},{9,8},{10,11... | collective-permute-start | bytes 393224 | tf_op jit(solution)/shard_map/ppermute | solution.py:623
  4.6 3.5 %collective-permute-start.1 = (f32[8,4,8,128]{3,2,1,0:T(8,128)S(1)}, f32[8,4,8,128]{3,2,1,0:T(8,128)S(1)}, u32[]{:S(2)}, u32[]{:S(2)}) collective-permute-start(f32[8,4,8,128]{3,2,1,0:T(8,128)S(1)} %get-tuple-element.19), channel_id=1, source_target_pairs={{1,2},{2,1},{5,6},{6,5},{9,10},{10,9},{13,14},{14,13},{17,18},{18,... | collective-permute-start | bytes 393224 | tf_op jit(solution)/shard_map/ppermute | solution.py:647
  5.2 6.7 %collective-permute-start.4 = (f32[8,16,512]{2,1,0:T(8,128)}, f32[8,16,512]{2,1,0:T(8,128)S(1)}, u32[]{:S(2)}, u32[]{:S(2)}) collective-permute-start(f32[8,16,512]{2,1,0:T(8,128)} %charges_ref.1), channel_id=1, source_target_pairs={{0,4},{4,0},{8,12},{12,8},{1,5},{5,1},{9,13},{13,9},{2,6},{6,2},{1... | collective-permute-start | bytes 786440 | tf_op jit(solution)/shard_map/ppermute | solution.py:623
  5.3 6.6 %collective-permute-start.5 = (f32[8,4,16,128]{3,2,1,0:T(8,128)S(1)}, f32[8,4,16,128]{3,2,1,0:T(8,128)S(1)}, u32[]{:S(2)}, u32[]{:S(2)}) collective-permute-start(f32[8,4,16,128]{3,2,1,0:T(8,128)S(1)} %get-tuple-element.20.mid_ref), channel_id=1, source_target_pairs={{4,8},{8,4},{5,9},{9,5},{6,10},{10,6},{7,11},{11,7},{20,24},{24,20... | collective-permute-start | bytes 786440 | tf_op jit(solution)/shard_map/ppermute | solution.py:645
  8.1 5.5 %collective-permute-start.3 = (f32[8,4,16,128]{3,2,1,0:T(8,128)S(1)}, f32[8,4,16,128]{3,2,1,0:T(8,128)S(1)}, u32[]{:S(2)}, u32[]{:S(2)}) collective-permute-start(f32[8,4,16,128]{3,2,1,0:T(8,128)S(1)} %pad_maximum_fusion.mid_rim_ref), channel_id=1, source_target_pairs={{4,8},{8,4},{5,9},{9,5},{6,10},{10,6},{7,11},{11,7},{20,24},{24,20... | collective-permute-start | bytes 786440 | tf_op jit(solution)/shard_map/ppermute | solution.py:650
  8.8 4.8 %collective-permute-start.2 = (f32[8,4,16,128]{3,2,1,0:T(8,128)S(1)}, f32[8,4,16,128]{3,2,1,0:T(8,128)S(1)}, u32[]{:S(2)}, u32[]{:S(2)}) collective-permute-start(f32[8,4,16,128]{3,2,1,0:T(8,128)S(1)} %pad_maximum_fusion.mid_rim_ref), channel_id=1, source_target_pairs={{0,4},{4,0},{8,12},{12,8},{1,5},{5,1},{9,13},{13,9},{2,6},{6,2},{1... | collective-permute-start | bytes 786440 | tf_op jit(solution)/shard_map/ppermute | solution.py:623
  15.8 7.3 %collective-permute-start.8 = (f32[1,4,2,8,128]{4,3,2,1,0:T(8,128)S(1)}, f32[1,4,2,8,128]{4,3,2,1,0:T(8,128)S(1)}, u32[]{:S(2)}, u32[]{:S(2)}) collective-permute-start(f32[1,4,2,8,128]{4,3,2,1,0:T(8,128)S(1)} %bitcast.6), channel_id=1, source_target_pairs={{0,1},{1,0},{2,3},{3,2},{4,5},{5,4},{6,7},{7,6},{8,9},{9,8},{10,11... | collective-permute-start | bytes 98312 | tf_op jit(solution)/shard_map/ppermute | solution.py:623
  20.5 5.2 %collective-permute-start.7 = (f32[1,4,2,8,128]{4,3,2,1,0:T(8,128)S(1)}, f32[1,4,2,8,128]{4,3,2,1,0:T(8,128)S(1)}, u32[]{:S(2)}, u32[]{:S(2)}) collective-permute-start(f32[1,4,2,8,128]{4,3,2,1,0:T(8,128)S(1)} %bitcast.7), channel_id=1, source_target_pairs={{0,2},{1,3},{2,0},{3,1},{4,6},{5,7},{6,4},{7,5},{8,10},{9,11},{10,... | collective-permute-start | bytes 98312 | tf_op jit(solution)/shard_map/ppermute | solution.py:623
  21.7 7.9 %collective-permute-start.6 = (f32[1,4,2,8,128]{4,3,2,1,0:T(8,128)S(1)}, f32[1,4,2,8,128]{4,3,2,1,0:T(8,128)S(1)}, u32[]{:S(2)}, u32[]{:S(2)}) collective-permute-start(f32[1,4,2,8,128]{4,3,2,1,0:T(8,128)S(1)} %bitcast.8), channel_id=1, source_target_pairs={{0,3},{1,2},{2,1},{3,0},{4,7},{5,6},{6,5},{7,4},{8,11},{9,10},{10,... | collective-permute-start | bytes 98312 | tf_op jit(solution)/shard_map/ppermute | solution.py:623
  25.6 7.9 %collective-permute-start.10 = (f32[3,4,2,8,128]{4,3,2,1,0:T(8,128)S(1)}, f32[3,4,2,8,128]{4,3,2,1,0:T(8,128)S(1)}, u32[]{:S(2)}, u32[]{:S(2)}) collective-permute-start(f32[3,4,2,8,128]{4,3,2,1,0:T(8,128)S(1)} %pad_maximum_fusion.1), channel_id=1, source_target_pairs={{0,8},{4,12},{8,0},{12,4},{1,9},{5,13},{9,1},{13,5},{2,10},{6,14},... | collective-permute-start | bytes 294920 | tf_op jit(solution)/shard_map/ppermute | solution.py:623
  29.6 3.9 %collective-permute-start.9 = (f32[1,4,2,8,128]{4,3,2,1,0:T(8,128)S(1)}, f32[1,4,2,8,128]{4,3,2,1,0:T(8,128)S(1)}, u32[]{:S(2)}, u32[]{:S(2)}) collective-permute-start(f32[1,4,2,8,128]{4,3,2,1,0:T(8,128)S(1)} %collective-permute-done.6), channel_id=1, source_target_pairs={{0,8},{4,12},{8,0},{12,4},{1,9},{5,13},{9,1},{13,5},{2,10},{6,14},... | collective-permute-start | bytes 98312 | tf_op jit(solution)/shard_map/ppermute | solution.py:623
  33.5 1.6 %collective-permute-start.11 = (f32[8,4,2,8,128]{4,3,2,1,0:T(8,128)S(1)}, f32[8,4,2,8,128]{4,3,2,1,0:T(8,128)S(1)}, u32[]{:S(2)}, u32[]{:S(2)}) collective-permute-start(f32[8,4,2,8,128]{4,3,2,1,0:T(8,128)S(1)} %constant_dynamic-update-slice_fusion.refs_0_), channel_id=1, source_target_pairs={{0,4},{4,0},{8,12},{12,8},{1,5},{5,1},{9,13},{13,9},{2,6},{6,2},{1... | collective-permute-start | bytes 786440 | tf_op jit(solution)/shard_map/ppermute | solution.py:623
  40.9 4.5 %collective-permute-start.14 = (f32[1,4,2,8,128]{4,3,2,1,0:T(8,128)S(1)}, f32[1,4,2,8,128]{4,3,2,1,0:T(8,128)S(1)}, u32[]{:S(2)}, u32[]{:S(2)}) collective-permute-start(f32[1,4,2,8,128]{4,3,2,1,0:T(8,128)S(1)} %bitcast.10), channel_id=1, source_target_pairs={{0,1},{1,0},{2,3},{3,2},{4,5},{5,4},{6,7},{7,6},{8,9},{9,8},{10,11... | collective-permute-start | bytes 98312 | tf_op jit(solution)/shard_map/ppermute | solution.py:623
  41.3 5.5 %collective-permute-start.13 = (f32[1,4,2,8,128]{4,3,2,1,0:T(8,128)S(1)}, f32[1,4,2,8,128]{4,3,2,1,0:T(8,128)S(1)}, u32[]{:S(2)}, u32[]{:S(2)}) collective-permute-start(f32[1,4,2,8,128]{4,3,2,1,0:T(8,128)S(1)} %bitcast.11), channel_id=1, source_target_pairs={{0,2},{1,3},{2,0},{3,1},{4,6},{5,7},{6,4},{7,5},{8,10},{9,11},{10,... | collective-permute-start | bytes 98312 | tf_op jit(solution)/shard_map/ppermute | solution.py:623
  43.8 5.7 %collective-permute-start.12 = (f32[1,4,2,8,128]{4,3,2,1,0:T(8,128)S(1)}, f32[1,4,2,8,128]{4,3,2,1,0:T(8,128)S(1)}, u32[]{:S(2)}, u32[]{:S(2)}) collective-permute-start(f32[1,4,2,8,128]{4,3,2,1,0:T(8,128)S(1)} %bitcast.12), channel_id=1, source_target_pairs={{0,3},{1,2},{2,1},{3,0},{4,7},{5,6},{6,5},{7,4},{8,11},{9,10},{10,... | collective-permute-start | bytes 98312 | tf_op jit(solution)/shard_map/ppermute | solution.py:623
  46.8 6.6 %collective-permute-start.16 = (f32[3,4,2,8,128]{4,3,2,1,0:T(8,128)S(1)}, f32[3,4,2,8,128]{4,3,2,1,0:T(8,128)S(1)}, u32[]{:S(2)}, u32[]{:S(2)}) collective-permute-start(f32[3,4,2,8,128]{4,3,2,1,0:T(8,128)S(1)} %pad_maximum_fusion.2), channel_id=1, source_target_pairs={{0,8},{4,12},{8,0},{12,4},{1,9},{5,13},{9,1},{13,5},{2,10},{6,14},... | collective-permute-start | bytes 294920 | tf_op jit(solution)/shard_map/ppermute | solution.py:623
  49.5 3.9 %collective-permute-start.15 = (f32[1,4,2,8,128]{4,3,2,1,0:T(8,128)S(1)}, f32[1,4,2,8,128]{4,3,2,1,0:T(8,128)S(1)}, u32[]{:S(2)}, u32[]{:S(2)}) collective-permute-start(f32[1,4,2,8,128]{4,3,2,1,0:T(8,128)S(1)} %collective-permute-done.12), channel_id=1, source_target_pairs={{0,8},{4,12},{8,0},{12,4},{1,9},{5,13},{9,1},{13,5},{2,10},{6,14},... | collective-permute-start | bytes 98312 | tf_op jit(solution)/shard_map/ppermute | solution.py:623
  53.4 1.6 %collective-permute-start.17 = (f32[8,4,2,8,128]{4,3,2,1,0:T(8,128)S(1)}, f32[8,4,2,8,128]{4,3,2,1,0:T(8,128)S(1)}, u32[]{:S(2)}, u32[]{:S(2)}) collective-permute-start(f32[8,4,2,8,128]{4,3,2,1,0:T(8,128)S(1)} %constant_dynamic-update-slice_fusion.6.refs_0_), channel_id=1, source_target_pairs={{0,4},{4,0},{8,12},{12,8},{1,5},{5,1},{9,13},{13,9},{2,6},{6,2},{1... | collective-permute-start | bytes 786440 | tf_op jit(solution)/shard_map/ppermute | solution.py:623
